TPU v7x, 32 devices: a whole 2x2x4 slice. The times are simulated.
32 devices in a mesh: parts: 2 (over y), set: 4 (over x, core), seq: 4 (over z).
Axes of the slice: x: 2, y: 2, z: 4, core: 2. Of those that a mesh axis runs over, the one named last changes fastest.
Arguments:
- span_hidden: bfloat16 [512, 8192], P('parts', 'seq'), parts along dimension 0, may hold values from -500 to 500
- norm_gain: bfloat16 [8192], P('seq'), may hold values from 0.099609375 to 1.8984375
- key_value_weight: bfloat16 [8192, 2048], P('seq', 'set'), may hold values from -0.0625 to 0.0625
- prompt_key_value: bfloat16 [256, 2048], P(('parts', 'seq')), parts along dimension 0, may hold values from -6 to 6
- span_offset: int32 [2], P('parts'), parts along dimension 0, may hold values from 64 to 128
- cont_query: bfloat16 [32, 64, 8192], P(('parts', 'set', 'seq')), parts along dimension 0, may hold values from -24 to 24
- continuation_key_value: bfloat16 [32, 64, 2048], P(('parts', 'set', 'seq')), parts along dimension 0, may hold values from -6 to 6
- cont_lengths: int32 [32], P(('parts', 'set', 'seq')), parts along dimension 0, may hold values from 1 to 64
Outputs:
- span_key_value: bfloat16 [512, 2048], P(('parts', 'seq'), 'set'), parts along dimension 0
- attended: bfloat16 [32, 64, 8192], P(('parts', 'set', 'seq')), parts along dimension 0
There are 2 independent parts, one for each index of `parts`. A program takes and returns all parts, laid end to end along the dimension named above; an argument that names none is the same for every part. Nothing has to cross between parts.
All inputs are finite; a program needn't handle non-finite values.
Results may differ from a plain program's by a relative error of at most 0.02.
Values may be sent and summed in bfloat16 or wider, within the bound.
No kernel may reach another device: no remote copies, remote signals or barrier semaphores. Data moves between devices by JAX's collectives and lax.ppermute only.
A program may use at most 64 MiB of HBM per device.

v0:
```python
import math

import jax
import jax.numpy as jnp
from jax import lax
from jax.sharding import PartitionSpec as P

MODEL_WIDTH = 8192
QUERY_HEADS = 64
KEY_HEADS = 8
HEAD_SIZE = 128
SPAN_LENGTH = 256


EPS = 1e-05
NEGATIVE_LARGE = -1e30


def frequencies(count, width, dtype):
    base = 500000.0 ** (-(jnp.arange(count).astype(dtype) * 2.0) / width)
    wave = 2.0 * math.pi / base
    smooth = (8192.0 / wave - 1.0) / 3.0
    blended = (1.0 - smooth) * base / 8.0 + smooth * base
    return jnp.where(wave < 2048.0, base, jnp.where(wave > 8192.0, base / 8.0, blended))


def apply_rotary(value_matrix, positions):
    mid_point = value_matrix.shape[-1] // 2
    frequency = frequencies(mid_point, value_matrix.shape[-1], value_matrix.dtype)
    angles = positions.astype(value_matrix.dtype)[:, None] * frequency[None, :]
    cosine = jnp.concatenate([jnp.cos(angles), jnp.cos(angles)], -1)[:, None, :]
    sine_part = jnp.concatenate([jnp.sin(angles), jnp.sin(angles)], -1)[:, None, :]
    turned = jnp.concatenate([-value_matrix[..., mid_point:], value_matrix[..., :mid_point]], -1)
    return value_matrix * cosine + turned * sine_part


def attend(state, query_rows, key_matrix, value_matrix, valid):
    best, total, accum = state
    scores = jnp.einsum(
        "tgkd,ngd->tgkn", query_rows, key_matrix, preferred_element_type=jnp.float32
    ) * HEAD_SIZE ** (-0.5)
    valid_four = valid.reshape(valid.shape[0], 1, 1, valid.shape[1])
    masked = jnp.where(valid_four, scores, NEGATIVE_LARGE)
    new_best = jnp.maximum(best, jnp.max(masked, axis=-1))
    weights = jnp.where(valid_four, jnp.exp(masked - new_best[..., None]), 0.0)
    shrink = jnp.exp(best - new_best)
    total = total * shrink + jnp.sum(weights, axis=-1)
    accum = accum * shrink[..., None] + jnp.einsum(
        "tgkn,ngd->tgkd",
        weights.astype(jnp.bfloat16),
        value_matrix,
        preferred_element_type=jnp.float32,
    )
    return (new_best, total, accum)


def attend_rows(state, query_rows, slice_part, valid_rows):
    sequence_length = slice_part.shape[0]
    key_columns_width = KEY_HEADS * HEAD_SIZE
    key_matrix = slice_part[:, :key_columns_width].reshape(sequence_length, KEY_HEADS, HEAD_SIZE)
    value_matrix = slice_part[:, key_columns_width:].reshape(sequence_length, KEY_HEADS, HEAD_SIZE)
    if sequence_length <= 256 or sequence_length % 256 != 0:
        return attend(state, query_rows, key_matrix, value_matrix, valid_rows[None, :])

    def one_block(index, inner):
        begin = index * 256
        block_keys = lax.dynamic_slice_in_dim(key_matrix, begin, 256, 0)
        block_values = lax.dynamic_slice_in_dim(value_matrix, begin, 256, 0)
        block_valid = lax.dynamic_slice_in_dim(valid_rows, begin, 256, 0)
        return attend(inner, query_rows, block_keys, block_values, block_valid[None, :])

    return lax.fori_loop(0, sequence_length // 256, one_block, state)


def on_device(
    span_hidden,
    norm_gain,
    key_value_weight,
    prompt_key_value,
    span_offset,
    cont_query,
    continuation_key_value,
    cont_lengths,
):
    offset = span_offset[0]
    key_columns_width = KEY_HEADS * HEAD_SIZE
    group_factor = QUERY_HEADS // KEY_HEADS
    span_rows = span_hidden.shape[0] // lax.axis_size("seq")
    hidden = span_hidden.astype(jnp.float32)
    squares = lax.psum(jnp.sum(hidden * hidden, axis=1), "seq")
    normed = (
        hidden
        * lax.rsqrt(squares / MODEL_WIDTH + EPS)[:, None]
        * norm_gain.astype(jnp.float32)[None, :]
    ).astype(jnp.bfloat16)
    block = lax.psum_scatter(
        jnp.dot(normed, key_value_weight, preferred_element_type=jnp.float32).astype(jnp.bfloat16),
        "seq",
        scatter_dimension=0,
        tiled=True,
    ).astype(jnp.float32)
    width = key_value_weight.shape[1]
    col_start = lax.axis_index("set") * width
    row_pos = offset + lax.axis_index("seq") * span_rows + jnp.arange(span_rows, dtype=jnp.int32)
    turned = apply_rotary(block.reshape(span_rows, width // HEAD_SIZE, HEAD_SIZE), row_pos).reshape(
        span_rows, width
    )
    block_kv = jnp.where(col_start < key_columns_width, turned, block).astype(jnp.bfloat16)
    step_length = cont_query.shape[1]
    token_index = jnp.arange(step_length, dtype=jnp.int32)
    self_positions = offset + SPAN_LENGTH + token_index
    query_rows = apply_rotary(
        cont_query[0].astype(jnp.float32).reshape(step_length, QUERY_HEADS, HEAD_SIZE),
        self_positions,
    ).astype(jnp.bfloat16)
    query_rows = query_rows.reshape(step_length, KEY_HEADS, group_factor, HEAD_SIZE)
    self_key_rows = apply_rotary(
        continuation_key_value[0, :, :key_columns_width]
        .astype(jnp.float32)
        .reshape(step_length, KEY_HEADS, HEAD_SIZE),
        self_positions,
    ).astype(jnp.bfloat16)
    self_value_rows = continuation_key_value[0, :, key_columns_width:].reshape(
        step_length, KEY_HEADS, HEAD_SIZE
    )
    state = (
        jnp.full((step_length, KEY_HEADS, group_factor), NEGATIVE_LARGE, jnp.float32),
        jnp.zeros((step_length, KEY_HEADS, group_factor), jnp.float32),
        jnp.zeros((step_length, KEY_HEADS, group_factor, HEAD_SIZE), jnp.float32),
    )
    causal = token_index[:, None] >= token_index[None, :]
    state = attend(state, query_rows, self_key_rows, self_value_rows, causal)
    joined_rows = lax.all_gather(block_kv, "set", axis=1, tiled=True)
    local_rows = jnp.concatenate([prompt_key_value, joined_rows], 0)
    cache_rows = prompt_key_value.shape[0]
    shard_rows = local_rows.shape[0]
    slice_part = lax.all_gather(local_rows, "seq", axis=0, tiled=True)
    global_row = jnp.arange(slice_part.shape[0], dtype=jnp.int32)
    within = global_row % shard_rows
    rows_valid = (within >= cache_rows) | (global_row // shard_rows * cache_rows + within < offset)
    state = attend_rows(state, query_rows, slice_part, rows_valid)
    best, total, accum = state
    mixed = (accum / total[..., None]).reshape(step_length, QUERY_HEADS * HEAD_SIZE)
    live = token_index < cont_lengths[0]
    attended = jnp.where(live[:, None], mixed, 0.0).astype(jnp.bfloat16)[None]
    return (block_kv, attended)


def solution(mesh):
    placed = (
        P("parts", "seq"),
        P("seq"),
        P("seq", "set"),
        P(("parts", "seq"), None),
        P("parts"),
        P(("parts", "set", "seq"), None, None),
        P(("parts", "set", "seq"), None, None),
        P(("parts", "set", "seq")),
    )
    return jax.shard_map(
        on_device,
        mesh=mesh,
        in_specs=placed,
        out_specs=(P(("parts", "seq"), "set"), P(("parts", "set", "seq"), None, None)),
        check_vma=False,
    )
```

profile of v0, /device:TPU:0, one launch (start us, length us, event | category | flops | bytes accessed | tf_op | source)
XLA Modules:
  0.0 121.2 jit_solution(6057361284964646912)
XLA Ops:
  7.2 1.6 %fusion.6 = f32[256]{0:T(256)S(1)} fusion(bf16[256,2048]{1,0:T(8,128)(2,1)} %param.8), kind=kLoop, calls=%fused_computation.11 | loop fusion | flops 1572608 | bytes 1049600 | tf_op jit(solution)/shard_map/reduce_sum | solution.py:90
  8.9 13.5 %psum.7 = f32[256]{0:T(256)S(1)} all-reduce(f32[256]{0:T(256)S(1)} %fusion.6), channel_id=1, replica_groups=mesh['parts'=2,'set'=4,'seq'=4] {'seq'}, use_global_device_ids=true, to_apply=%region_1.0 | all-reduce | flops 256 | bytes 2048 | tf_op jit(solution)/shard_map/psum | solution.py:90
  22.3 0.7 convert_element_type.88
  23.0 2.7 %convolution_convert_fusion = bf16[256,512]{1,0:T(8,128)(2,1)} fusion(bf16[2048,512]{1,0:T(8,128)(2,1)S(1)} %copy-done, bf16[256,2048]{1,0:T(8,128)(2,1)} %param.8, f32[2048]{0:T(1024)S(1)} %convert_element_type.88, f32[256]{0:T(256)S(1)} %add_rsqrt_fusion), kind=kOutput, calls=%fused_computation.30 | convolution fusion | flops 539099136 | bytes 3417088 | tf_op jit(solution)/shard_map/dot_general | solution.py:97
  26.9 16.8 %reduce-scatter.2.cloned.1.call-done = bf16[64,512]{1,0:T(8,128)(2,1)} async-done(((bf16[256,512]{1,0:T(8,128)(2,1)}), bf16[64,512]{1,0:T(8,128)(2,1)}) %reduce-scatter.2.cloned.1.call-update) | async-done | bytes 65552 | tf_op jit(solution)/shard_map/reduce_scatter | solution.py:96
  43.7 0.9 reshape.175
  44.9 1.0 fusion.30
  45.8 0.6 copy-done.5
  46.5 5.8 %all_gather.6 = bf16[64,2048]{1,0:T(8,128)(2,1)S(1)} all-gather(bf16[64,512]{1,0:T(8,128)(2,1)S(1)} %fusion.30), channel_id=1, replica_groups=mesh['parts'=2,'set'=4,'seq'=4] {'set'}, dimensions={1}, use_global_device_ids=true | all-gather | bytes 327680 | tf_op jit(solution)/shard_map/all_gather | solution.py:133
  52.3 1.7 %pad_maximum_fusion = bf16[96,2048]{1,0:T(8,128)(2,1)} fusion(bf16[64,2048]{1,0:T(8,128)(2,1)S(1)} %all_gather.6, bf16[32,2048]{1,0:T(8,128)(2,1)} %param.11), kind=kLoop, calls=%fused_computation.38 | loop fusion | flops 786432 | bytes 786432 | tf_op jit(solution)/shard_map/concatenate | solution.py:134
  55.4 0.9 slice_negate_fusion
  56.2 1.2 %copy.27 = f32[64,64,64]{2,0,1:T(8,128)S(1)} copy(f32[64,64,64]{2,1,0:T(8,128)S(1)} %get-tuple-element.8) | data formatting | bytes 2097152 | tf_op jit(solution)/shard_map/neg | solution.py:33
  57.5 1.2 %copy.28 = f32[64,64,64]{2,0,1:T(8,128)S(1)} copy(f32[64,64,64]{2,1,0:T(8,128)S(1)} %get-tuple-element.9) | data formatting | bytes 2097152 | tf_op jit(solution)/shard_map/slice | solution.py:33
  59.0 1.5 %fusion.10 = bf16[64,8,8,128]{3,0,2,1:T(8,128)(2,1)S(1)} fusion(f32[64,8,8,64]{3,0,2,1:T(8,128)S(1)} %bitcast.95, f32[64,8,8,64]{3,0,2,1:T(8,128)S(1)} %bitcast.94, f32[64,8,8,128]{3,2,1,0:T(8,128)S(1)} %bitcast.93, f32[64,128]{1,0:T(8,128)S(1)} %get-tuple-element.34, f32[64,128]{1,0:T(8,128)S(1)} %get-tuple-element.33), kind=kLoop, calls=%fused_computation.17 | loop fusion | flops 2621440 | bytes 5308416 | tf_op jit(solution)/shard_map/convert_element_type | solution.py:115
  60.4 2.5 %fusion.13 = (f32[64,8,8]{0,2,1:T(8,128)S(1)}, f32[8,64,64,8]{2,1,3,0:T(8,128)}) fusion(pred[64,64]{0,1:T(8,128)(4,1)S(1)} %iota_compare_fusion, bf16[64,8,8,128]{3,0,2,1:T(8,128)(2,1)S(1)} %fusion.10, f32[64,8,64]{2,0,1:T(8,128)S(1)} %get-tuple-element.15, f32[64,8,64]{2,0,1:T(8,128)S(1)} %get-tuple-element.14, f32[64,128]{1,0:T(8,128)S(1)} %get-tuple-element.34, ...), kind=kOutput, calls=%fused_computation.27 | convolution fusion | flops 68218880 | bytes 2707456 | tf_op jit(solution)/shard_map/tgkd,ngd->tgkn/dot_general | solution.py:39
  62.9 26.6 %all-gather.2.cloned.1.call-done = bf16[384,2048]{1,0:T(8,128)(2,1)} async-done(((bf16[96,2048]{1,0:T(8,128)(2,1)}), bf16[384,2048]{1,0:T(8,128)(2,1)}) %all-gather.2.cloned.1.call-update) | async-done | bytes 1572880 | tf_op jit(solution)/shard_map/all_gather | solution.py:137
  89.6 1.5 %slice_bitcast_fusion = (bf16[48,8,8,128]{3,1,2,0:T(8,128)(2,1)S(1)}, bf16[48,8,8,128]{3,1,2,0:T(8,128)(2,1)S(1)}) fusion(bf16[384,2048]{1,0:T(8,128)(2,1)} %all-gather.2.cloned.1.call-done), kind=kLoop, calls=%fused_computation.33 | loop fusion | bytes 3145728
  91.1 1.1 copy.57
  92.3 1.2 bitcast_reduce_fusion
  93.5 0.6 exponential_multiply_fusion
  94.1 0.8 fusion.16
  94.9 3.3 %fusion.2 = (f32[64,8,8]{0,2,1:T(8,128)S(1)}, bf16[64,8,8,384]{3,0,2,1:T(8,128)(2,1)}) fusion(f32[8,384,64,8]{1,2,3,0:T(8,128)S(1)} %get-tuple-element.30, f32[64,8,8]{0,2,1:T(8,128)S(1)} %get-tuple-element.19, pred[384]{0:T(512)(128)(4,1)S(1)} %fusion.42), kind=kLoop, calls=%fused_computation.5 | loop fusion | flops 9433088 | bytes 9470336 | tf_op jit(solution)/shard_map/reduce_sum | solution.py:47
  98.2 0.6 multiply_add_fusion
  98.9 0.9 copy.36
  99.7 1.6 %copy.29 = f32[64,8,8]{2,0,1:T(8,128)} copy(f32[64,8,8]{0,2,1:T(8,128)} %get-tuple-element.18) | data formatting | bytes 32768 | tf_op jit(solution)/shard_map/mul;broadcast_in_dim | solution.py:48
  101.3 1.6 %copy.33 = f32[64,8,8]{2,0,1:T(8,128)} copy(f32[64,8,8]{0,2,1:T(8,128)} %get-tuple-element.3) | data formatting | bytes 32768 | tf_op jit(solution)/shard_map/exp | solution.py:46
  102.9 1.5 %copy.30 = bf16[64,8,8,64]{3,2,0,1:T(8,128)(2,1)} copy(bf16[64,8,8,64]{0,3,2,1:T(8,128)(2,1)S(1)} %get-tuple-element.7) | data formatting | bytes 1048576 | tf_op jit(solution)/shard_map/convert_element_type | solution.py:50
  104.4 1.8 %fusion.31 = f32[8,64,8,128]{3,2,1,0:T(8,128)S(1)} fusion(bf16[64,8,8,64]{3,2,0,1:T(8,128)(2,1)} %copy.30, bf16[64,8,128,1]{2,1,0,3:T(8,128)(2,1)S(1)} %bitcast.100), kind=kOutput, calls=%fused_computation.52 | convolution fusion | flops 67108864 | bytes 2752512 | tf_op jit(solution)/shard_map/tgkn,ngd->tgkd/dot_general | solution.py:48
  106.6 3.8 %fusion.11 = bf16[64,8,8,128]{3,2,0,1:T(8,128)(2,1)S(1)} fusion(f32[8,64,8,128]{3,2,1,0:T(8,128)S(1)} %fusion.31, bf16[64,8,8,384]{3,0,2,1:T(8,128)(2,1)S(1)} %copy-done.2, f32[64,8,8]{2,0,1:T(8,128)S(1)} %copy.36, f32[64,8,8]{2,0,1:T(8,128)} %copy.33, f32[64,8,8]{2,0,1:T(8,128)} %copy.29, bf16[384,8,128,1]{2,1,0,3:T(8,128)(2,1)} %bitcast.99), kind=kOutput, calls=%fused_computation.19 | convolution fusion | flops 405274624 | bytes 7127040 | tf_op jit(solution)/shard_map/tgkn,ngd->tgkd/dot_general | solution.py:48
  110.3 1.3 %copy.37 = bf16[64,8,8,128]{3,2,1,0:T(8,128)(2,1)} copy(bf16[64,8,8,128]{3,2,0,1:T(8,128)(2,1)S(1)} %fusion.11) | data formatting | bytes 2097152 | tf_op jit(solution)/shard_map/div | solution.py:143
  111.6 1.5 %reshape.178 = bf16[1,64,8192]{2,1,0:T(8,128)(2,1)S(1)} reshape(bf16[64,8,8,128]{3,2,1,0:T(8,128)(2,1)} %copy.37) | data formatting | bytes 2097152 | tf_op jit(solution)/shard_map/reshape | solution.py:143
  113.1 1.2 select_convert_fusion
  (36 shorter events, 2.4 us)
Async XLA Ops:
  7.2 15.9 %copy-start = (bf16[2048,512]{1,0:T(8,128)(2,1)S(1)}, bf16[2048,512]{1,0:T(8,128)(2,1)}, u32[]{:S(2)}) copy-start(bf16[2048,512]{1,0:T(8,128)(2,1)} %param.10) | copy-start | bytes 6291460
  7.2 36.5 %reduce-scatter.2.cloned.1.call-start = ((), (), s32[]{:S(2)}) async-start(), calls=%async_computation.1 | async-start | bytes 327680 | tf_op jit(solution)/shard_map/reduce_scatter | solution.py:96
  25.7 28.9 %copy-start.4 = (bf16[1,64,2048]{2,1,0:T(8,128)(2,1)S(1)}, bf16[1,64,2048]{2,1,0:T(8,128)(2,1)}, u32[]{:S(2)}) copy-start(bf16[1,64,2048]{2,1,0:T(8,128)(2,1)} %param.14) | copy-start | bytes 786436
  25.7 63.8 %all-gather.2.cloned.1.call-start = ((), (), s32[]{:S(2)}) async-start(), calls=%async_computation.2 | async-start | bytes 1966080 | tf_op jit(solution)/shard_map/all_gather | solution.py:137
  44.8 10.0 %copy-start.3 = (bf16[1,64,8192]{2,1,0:T(8,128)(2,1)S(1)}, bf16[1,64,8192]{2,1,0:T(8,128)(2,1)}, u32[]{:S(2)}) copy-start(bf16[1,64,8192]{2,1,0:T(8,128)(2,1)} %param.13) | copy-start | bytes 3145732
  45.8 0.6 copy-start.5
  92.3 1.8 %copy-start.1 = (f32[8,64,64,8]{2,1,3,0:T(8,128)S(1)}, f32[8,64,64,8]{2,1,3,0:T(8,128)}, u32[]{:S(2)}) copy-start(f32[8,64,64,8]{2,1,3,0:T(8,128)} %get-tuple-element.28) | copy-start | bytes 3145732
  104.4 2.2 %copy-start.2 = (bf16[64,8,8,384]{3,0,2,1:T(8,128)(2,1)S(1)}, bf16[64,8,8,384]{3,0,2,1:T(8,128)(2,1)}, u32[]{:S(2)}) copy-start(bf16[64,8,8,384]{3,0,2,1:T(8,128)(2,1)} %get-tuple-element.5) | copy-start | bytes 9437188
Sparse Core Ops, SparseCore 0:
  25.9 17.7 reduce-scatter.1
  54.1 35.4 all-gather.1
where the time goes:
time: 122 us; the launch traced here: 121 us
  waiting for transfers between devices  43.4 us (36%)
  blocking collectives  19.3 us (16%)
  local copies, waits for them, and re-layouts  15.9 us (13%)
  between operations  15.6 us (13%)
  other arithmetic  15 us (12%)
  matrix products  11.9 us (10%)
    all_gather x1, waiting for transfers between devices, on_device(): slice_part = lax.all_gather(local_rows, 'seq', axis=0, tiled=True)  26.6 us
    reduce_scatter x1, waiting for transfers between devices, on_device(): lax.psum_scatter(jnp.dot(normed, key_value_weight, preferred_element_type...  16.8 us
    psum x1, blocking collectives, on_device(): squares = lax.psum(jnp.sum(hidden * hidden, axis=1), 'seq')  13.5 us
    all_gather x1, blocking collectives, on_device(): joined_rows = lax.all_gather(block_kv, 'set', axis=1, tiled=True)  5.83 us
    dot_general x2, matrix products, attend(): jnp.einsum('tgkn,ngd->tgkd', weights.astype(jnp.bfloat16), value_matrix,...  5.55 us
    unnamed x18, local copies, waits for them, and re-layouts  4.21 us
    reduce_sum x2, other arithmetic, attend(): total = total * shrink + jnp.sum(weights, axis=-1)  4.09 us
    dot_general x2, matrix products, attend(): jnp.einsum('tgkd,ngd->tgkn', query_rows, key_matrix, preferred_element_ty...  3.65 us
  transfers between devices with their start and end apart: 2, of which 2 were waited for; matrix products, arithmetic and copies ran while one was open for 7% of the time, Pallas kernels for 0%

commit v1 on v0

v1 whole, which is shorter than its diff:
```python
import functools
import math

import jax
import jax.numpy as jnp
from jax import lax
from jax.experimental import pallas as pl
from jax.experimental.pallas import tpu as pltpu
from jax.sharding import PartitionSpec as P

MODEL_WIDTH = 8192
QUERY_HEADS = 64
KEY_HEADS = 8
HEAD_SIZE = 128
SPAN_LENGTH = 256
EPS = 1e-05
NEGATIVE_LARGE = -1e30
GROUP = QUERY_HEADS // KEY_HEADS
KEY_COLUMNS = KEY_HEADS * HEAD_SIZE
BF16 = jnp.bfloat16
F32 = jnp.float32
VMEM = pl.BlockSpec(memory_space=pltpu.VMEM)
SMEM = pl.BlockSpec(memory_space=pltpu.SMEM)


def peer(index, step, count):
    if count & (count - 1) == 0:
        return index ^ step
    return (index + step) % count


def source(index, step, count):
    if count & (count - 1) == 0:
        return index ^ step
    return (index + count - step) % count


def exchange(value, axis, step):
    count = lax.axis_size(axis)
    return lax.ppermute(value, axis, [(i, peer(i, step, count)) for i in range(count)])


def frequencies():
    base = 500000.0 ** (-(jnp.arange(HEAD_SIZE // 2).astype(F32) * 2.0) / HEAD_SIZE)
    wave = 2.0 * math.pi / base
    smooth = (8192.0 / wave - 1.0) / 3.0
    blended = (1.0 - smooth) * base / 8.0 + smooth * base
    return jnp.where(wave < 2048.0, base, jnp.where(wave > 8192.0, base / 8.0, blended))


def tables(positions):
    angles = positions.astype(F32)[:, None] * frequencies()[None, :]
    cosine, sine = jnp.cos(angles), jnp.sin(angles)
    return jnp.concatenate([cosine, cosine], -1), jnp.concatenate([-sine, sine], -1)


def turn(value, cosine, sine):
    return value * cosine + pltpu.roll(value, HEAD_SIZE // 2, 1) * sine


def diagonal(rows):
    shape = (rows, HEAD_SIZE)
    return lax.broadcasted_iota(jnp.int32, shape, 0) == lax.broadcasted_iota(jnp.int32, shape, 1)


def project_kernel(count, rows, heads, at_ref, hidden_ref, gain_ref, weight_ref, *rest):
    own_ref, square_ref = rest[:2]
    sends, (total, squares) = rest[2 : 1 + count], rest[1 + count :]
    step = pl.program_id(0)
    hidden = hidden_ref[...].astype(F32)
    scaled = (hidden * gain_ref[...].astype(F32)).astype(BF16)
    part = jnp.dot(scaled, weight_ref[...], preferred_element_type=F32)
    square = hidden * hidden
    folded = square[:, :HEAD_SIZE]
    for lane in range(1, square.shape[1] // HEAD_SIZE):
        folded = folded + square[:, lane * HEAD_SIZE : (lane + 1) * HEAD_SIZE]

    @pl.when(step == 0)
    def _():
        total[...] = part
        squares[...] = folded

    @pl.when(step > 0)
    def _():
        total[...] += part
        squares[...] += folded

    @pl.when(step == pl.num_programs(0) - 1)
    def _():
        me = at_ref[0]
        for k in range(count):
            to = pl.ds(pl.multiple_of(peer(me, k, count) * rows, rows), rows)
            column = jnp.sum(squares[to, :], axis=1, keepdims=True)
            if k == 0:
                square_ref[...] = jnp.broadcast_to(column, (rows, HEAD_SIZE))
                out = own_ref
            else:
                out = sends[k - 1]
                line = jnp.sum(jnp.where(diagonal(rows), column, 0.0), axis=0, keepdims=True)
                high = line.astype(BF16).astype(F32)
                low = line - high
                which = lax.broadcasted_iota(jnp.int32, (16, HEAD_SIZE), 0)
                tail = jnp.where(which == 0, high, jnp.where(which == 1, low, 0.0))
                out[heads * rows :, :] = tail.astype(BF16)
            for h in range(heads):
                piece = total[to, h * HEAD_SIZE : (h + 1) * HEAD_SIZE]
                out[h * rows : (h + 1) * rows, :] = piece.astype(out.dtype)


def project(at, span_hidden, norm_gain, key_value_weight, count):
    length, depth = span_hidden.shape
    width = key_value_weight.shape[1]
    rows, heads = length // count, width // HEAD_SIZE
    steps = 4 if depth % 512 == 0 else 1
    chunk = depth // steps
    whole = lambda i: (0, 0)
    outs = [
        jax.ShapeDtypeStruct((heads * rows, HEAD_SIZE), F32),
        jax.ShapeDtypeStruct((rows, HEAD_SIZE), F32),
    ] + [jax.ShapeDtypeStruct((heads * rows + 16, HEAD_SIZE), BF16)] * (count - 1)
    return pl.pallas_call(
        functools.partial(project_kernel, count, rows, heads),
        grid=(steps,),
        in_specs=[
            SMEM,
            pl.BlockSpec((length, chunk), lambda i: (0, i)),
            pl.BlockSpec((1, chunk), lambda i: (0, i)),
            pl.BlockSpec((chunk, width), lambda i: (i, 0)),
        ],
        out_shape=outs,
        out_specs=[pl.BlockSpec(o.shape, whole) for o in outs],
        scratch_shapes=[pltpu.VMEM((length, width), F32), pltpu.VMEM((length, HEAD_SIZE), F32)],
        compiler_params=pltpu.CompilerParams(vmem_limit_bytes=24 << 20),
        cost_estimate=pl.CostEstimate(
            flops=2 * length * depth * width, bytes_accessed=2 * depth * (length + width), transcendentals=0
        ),
        name="project",
    )(at, span_hidden, norm_gain[None, :], key_value_weight)


def combine_kernel(rows, heads, first_ref, own_ref, square_ref, cosine_ref, sine_ref, *rest):
    got, out_ref = rest[:-1], rest[-1]
    line = jnp.zeros((1, HEAD_SIZE), F32)
    for ref in got:
        tail = ref[heads * rows :, :].astype(F32)
        line = line + tail[0:1, :] + tail[1:2, :]
    column = jnp.sum(jnp.where(diagonal(rows), line, 0.0), axis=1, keepdims=True)
    scale = lax.rsqrt((square_ref[...] + column) / MODEL_WIDTH + EPS)
    cosine, sine = cosine_ref[...], sine_ref[...]
    for h in range(heads):
        span = slice(h * rows, (h + 1) * rows)
        value = own_ref[span, :]
        for ref in got:
            value = value + ref[span, :].astype(F32)
        value = value * scale
        is_key = first_ref[0] + h < KEY_HEADS
        out = jnp.where(is_key, turn(value, cosine, sine), value)
        out_ref[:, h * HEAD_SIZE : (h + 1) * HEAD_SIZE] = out.astype(BF16)


def combine(first, own, square, cosine, sine, got):
    rows = square.shape[0]
    heads = own.shape[0] // rows
    return pl.pallas_call(
        functools.partial(combine_kernel, rows, heads),
        in_specs=[SMEM] + [VMEM] * (4 + len(got)),
        out_shape=jax.ShapeDtypeStruct((rows, heads * HEAD_SIZE), BF16),
        out_specs=VMEM,
        name="combine",
    )(first, own, square, cosine, sine, *got)


def queries_kernel(query_ref, own_ref, cosine_ref, sine_ref, query_out, key_out):
    tokens = cosine_ref.shape[0]
    cosine, sine = cosine_ref[...], sine_ref[...]
    for h in range(KEY_HEADS):
        span = slice(h * HEAD_SIZE, (h + 1) * HEAD_SIZE)
        key_out[:, span] = turn(own_ref[:, span].astype(F32), cosine, sine).astype(BF16)
    factor = HEAD_SIZE**-0.5 * math.log2(math.e)
    cosine, sine = cosine * factor, sine * factor
    for h in range(QUERY_HEADS):
        span = slice(h * HEAD_SIZE, (h + 1) * HEAD_SIZE)
        turned = turn(query_ref[:, span].astype(F32), cosine, sine)
        query_out[h * tokens : (h + 1) * tokens, :] = turned.astype(BF16)


def queries(cont_query, own_rows, cosine, sine):
    tokens = cosine.shape[0]
    return pl.pallas_call(
        queries_kernel,
        in_specs=[VMEM] * 4,
        out_shape=[
            jax.ShapeDtypeStruct((QUERY_HEADS * tokens, HEAD_SIZE), BF16),
            jax.ShapeDtypeStruct((tokens, KEY_COLUMNS), BF16),
        ],
        out_specs=[VMEM, VMEM],
        compiler_params=pltpu.CompilerParams(vmem_limit_bytes=24 << 20),
        cost_estimate=pl.CostEstimate(flops=8 * cont_query.size, bytes_accessed=4 * cont_query.size, transcendentals=0),
        name="queries",
    )(cont_query, own_rows, cosine, sine)


def attend_kernel(sets, blocks, spots_ref, query_ref, key_ref, own_ref, prompt_refs, span_refs, out_ref, cache):
    me, offset, length = spots_ref[0], spots_ref[1], spots_ref[2]
    tokens = key_ref.shape[0]
    width = cache.shape[2]
    heads = width // HEAD_SIZE
    prompt_rows = prompt_refs[0].shape[0]
    span_rows = cache.shape[1] - prompt_rows - tokens
    for ref, (step, first) in zip(list(span_refs) + list(prompt_refs), blocks):
        cache[source(me, step, sets), first : first + ref.shape[0], :] = ref[...]
    for s in range(sets):
        columns = slice(s * width, (s + 1) * width)
        mine = key_ref if s * width < KEY_COLUMNS else own_ref
        cache[s, span_rows + prompt_rows :, :] = mine[:, columns]
    token = lax.broadcasted_iota(jnp.int32, (tokens, prompt_rows + tokens), 0)
    place = lax.broadcasted_iota(jnp.int32, (tokens, prompt_rows + tokens), 1)
    live = (place < offset) & (place < prompt_rows) | (place >= prompt_rows) & (place - prompt_rows <= token)
    bias = jnp.concatenate([jnp.where(live, 0.0, NEGATIVE_LARGE)] * GROUP, axis=0)
    keep = lax.broadcasted_iota(jnp.int32, (tokens, HEAD_SIZE), 0) < length
    for g in range(KEY_HEADS):
        lane = (g % heads) * HEAD_SIZE
        key = cache[g // heads, :, lane : lane + HEAD_SIZE]
        value = cache[sets // 2 + g // heads, :, lane : lane + HEAD_SIZE]
        query = query_ref[g * GROUP * tokens : (g + 1) * GROUP * tokens, :]
        scores = lax.dot_general(query, key, (((1,), (1,)), ((), ())), preferred_element_type=F32)
        scores = jnp.concatenate([scores[:, :span_rows], scores[:, span_rows:] + bias], axis=1)
        top = jnp.max(scores, axis=1, keepdims=True)
        weights = jnp.exp2(scores - top)
        total = jnp.sum(weights, axis=1, keepdims=True)
        mixed = jnp.dot(weights.astype(BF16), value, preferred_element_type=F32) / total
        for j in range(GROUP):
            column = (g * GROUP + j) * HEAD_SIZE
            piece = jnp.where(keep, mixed[j * tokens : (j + 1) * tokens, :], 0.0)
            out_ref[:, column : column + HEAD_SIZE] = piece.astype(BF16)


def attend(spots, query, key, own_rows, prompts, spans, sets, blocks, total_rows):
    tokens = key.shape[0]
    width = spans[0].shape[1]
    n_prompt = len(prompts)

    def kernel(spots_ref, query_ref, key_ref, own_ref, *rest):
        prompt_refs, span_refs = rest[:n_prompt], rest[n_prompt:-2]
        attend_kernel(
            sets, blocks, spots_ref, query_ref, key_ref, own_ref, prompt_refs, span_refs, rest[-2], rest[-1]
        )

    return pl.pallas_call(
        kernel,
        in_specs=[SMEM] + [VMEM] * (3 + len(prompts) + len(spans)),
        out_shape=jax.ShapeDtypeStruct((tokens, QUERY_HEADS * HEAD_SIZE), BF16),
        out_specs=VMEM,
        scratch_shapes=[pltpu.VMEM((sets, total_rows, width), BF16)],
        compiler_params=pltpu.CompilerParams(vmem_limit_bytes=40 << 20),
        cost_estimate=pl.CostEstimate(
            flops=4 * query.size * total_rows, bytes_accessed=4 * query.size, transcendentals=query.size
        ),
        name="attend",
    )(spots, query, key, own_rows, *prompts, *spans)


def on_device(
    span_hidden,
    norm_gain,
    key_value_weight,
    prompt_key_value,
    span_offset,
    cont_query,
    continuation_key_value,
    cont_lengths,
):
    offset = span_offset[0]
    sets, count = lax.axis_size("set"), lax.axis_size("seq")
    my_set, my_seq = lax.axis_index("set"), lax.axis_index("seq")
    width = key_value_weight.shape[1]
    rows = span_hidden.shape[0] // count
    tokens = cont_query.shape[1]
    low = 2 if sets % 2 == 0 else 1

    own, square, *sends = project(my_seq[None].astype(jnp.int32), span_hidden, norm_gain, key_value_weight, count)
    order = list(range(count - 1, 0, -1))
    got = [exchange(sends[k - 1], "seq", k) for k in order]

    span_cosine, span_sine = tables(offset + my_seq * rows + jnp.arange(rows, dtype=jnp.int32))
    self_cosine, self_sine = tables(offset + SPAN_LENGTH + jnp.arange(tokens, dtype=jnp.int32))
    query, key = queries(cont_query[0], continuation_key_value[0], self_cosine, self_sine)

    mine = lax.dynamic_slice_in_dim(prompt_key_value, my_set * width, width, 1)
    mine, *_ = lax.optimization_barrier((mine, own))
    parts = [mine] + [exchange(mine, "seq", k) for k in order]
    places = jnp.stack([my_seq] + [source(my_seq, k, count) for k in order])
    prompt = jnp.zeros((count,) + mine.shape, BF16)
    for part, place in zip(parts, [my_seq] + [source(my_seq, k, count) for k in order]):
        prompt = lax.dynamic_update_slice(prompt, part[None], (place, 0, 0))
    prompt = prompt.reshape(-1, width)
    prompts = [(0, prompt)]
    for step in range(low, sets, low):
        prompts.append((step, exchange(prompt, "set", step)))
    if low == 2:
        prompts += [(step ^ 1, exchange(value, "set", 1)) for step, value in prompts]

    first = (my_set * (width // HEAD_SIZE))[None].astype(jnp.int32)
    block = combine(first, own, square, span_cosine, span_sine, got)

    spans = [(0, 0, block)]
    for step in range(low, sets, low):
        spans.append((step, 0, exchange(block, "set", step)))
    across = [(k, exchange(block, "seq", k)) for k in order]
    for k, value in across:
        spans.append((0, k * rows, value))
        for step in range(low, sets, low):
            spans.append((step, k * rows, exchange(value, "set", step)))
    if low == 2:
        spans += [(step ^ 1, row, exchange(value, "set", 1)) for step, row, value in spans]

    span_total = count * rows
    blocks = [(step, row) for step, row, _ in spans] + [(step, span_total) for step, _ in prompts]
    spots = jnp.stack([my_set.astype(jnp.int32), offset, cont_lengths[0]])
    attended = attend(
        spots,
        query,
        key,
        continuation_key_value[0],
        [value for _, value in prompts],
        [value for _, _, value in spans],
        sets,
        blocks,
        span_total + prompt.shape[0] + tokens,
    )
    return block, attended[None]


def solution(mesh):
    placed = (
        P("parts", "seq"),
        P("seq"),
        P("seq", "set"),
        P(("parts", "seq"), None),
        P("parts"),
        P(("parts", "set", "seq"), None, None),
        P(("parts", "set", "seq"), None, None),
        P(("parts", "set", "seq")),
    )
    return jax.shard_map(
        on_device,
        mesh=mesh,
        in_specs=placed,
        out_specs=(P(("parts", "seq"), "set"), P(("parts", "set", "seq"), None, None)),
        check_vma=False,
    )
```

time: 122 us -> 52.3 us (0.43)
  waiting for transfers between devices: 43.4 us -> 10.6 us
  starting transfers between devices: 0.08 us -> 22.7 us
  blocking collectives: 19.3 us -> 0 us
  other arithmetic: 15 us -> 1.22 us
  between operations: 15.6 us -> 2.11 us
  matrix products: 11.9 us -> 0 us
  local copies, waits for them, and re-layouts: 15.9 us -> 6.51 us
  Pallas kernels: 0 us -> 8.79 us
    all_gather x1 -> x0, waiting for transfers between devices: 26.6 us -> none  [on_device(): slice_part = lax.all_gather(local_rows, 'seq', axis=0, tiled=True)]
    ppermute x0 -> x24, starting transfers between devices: none -> 22.7 us  [exchange(): lax.ppermute(value, axis, [(i, peer(i, step, count)) for i in range(count)])]
    reduce_scatter x1 -> x0, waiting for transfers between devices: 16.8 us -> none  [on_device(): lax.psum_scatter(jnp.dot(normed, key_value_weight, preferred_element_type...]
    psum x1 -> x0, blocking collectives: 13.5 us -> none  [on_device(): squares = lax.psum(jnp.sum(hidden * hidden, axis=1), 'seq')]
    dot_general x5 -> x0, matrix products: 11.9 us -> none  [the longest x2 5.55 us: attend(): jnp.einsum('tgkn,ngd->tgkd', weights.astype(jnp.bfloat16), value_matrix,...]
    ppermute x0 -> x24, waiting for transfers between devices: none -> 10.6 us  [exchange(): lax.ppermute(value, axis, [(i, peer(i, step, count)) for i in range(count)])]
    pallas_call x0 -> x4, Pallas kernels: none -> 8.79 us  [the longest x1 4.52 us: attend(): pl.pallas_call(kernel, in_specs=[SMEM] + [VMEM] * (3 + len(prompts) + len...]
    all_gather x1 -> x0, blocking collectives: 5.83 us -> none  [on_device(): joined_rows = lax.all_gather(block_kv, 'set', axis=1, tiled=True)]
  transfers between devices with their start and end apart: 2 -> 24, of which waited for: 2 -> 9; matrix products, arithmetic and copies ran while one was open for 7% -> 2% of each run, Pallas kernels for 0% -> 5%
where the time goes in v1:
time: 52.3 us; the launch traced here: 52 us
  starting transfers between devices  22.7 us (43%)
  waiting for transfers between devices  10.6 us (20%)
  Pallas kernels  8.79 us (17%)
  local copies, waits for them, and re-layouts  6.51 us (12%)
  between operations  2.11 us (4%)
  other arithmetic  1.22 us (2%)
    ppermute x24, starting transfers between devices, exchange(): lax.ppermute(value, axis, [(i, peer(i, step, count)) for i in range(count)])  22.7 us
    ppermute x24, waiting for transfers between devices, exchange(): lax.ppermute(value, axis, [(i, peer(i, step, count)) for i in range(count)])  10.6 us
    unnamed x22, local copies, waits for them, and re-layouts  5.74 us
    pallas_call x1, Pallas kernels, attend(): pl.pallas_call(kernel, in_specs=[SMEM] + [VMEM] * (3 + len(prompts) + len...  4.52 us
    pallas_call x1, Pallas kernels, combine(): pl.pallas_call(functools.partial(combine_kernel, rows, heads), in_specs=[...  1.9 us
    pallas_call x1, Pallas kernels, project(): pl.pallas_call(functools.partial(project_kernel, count, rows, heads), gri...  1.72 us
  transfers between devices with their start and end apart: 24, of which 9 were waited for; matrix products, arithmetic and copies ran while one was open for 2% of the time, Pallas kernels for 5%

profile of v1, /device:TPU:0, one launch (start us, length us, event | category | flops | bytes accessed | tf_op | source)
XLA Modules:
  0.0 52.0 jit_solution(14017531685890752809)
XLA Ops:
  0.7 0.7 %broadcast_in_dim.33.gain_ref = bf16[1,2048]{1,0:T(2,128)(2,1)S(1)} reshape(bf16[2048]{0:T(1024)(128)(2,1)} %param.9) | data formatting | bytes 8192 | tf_op jit(solution)/shard_map/broadcast_in_dim | solution.py:138
  1.6 1.6 %copy-done.1 = bf16[2048,512]{1,0:T(8,128)(2,1)S(1)} copy-done((bf16[2048,512]{1,0:T(8,128)(2,1)S(1)}, bf16[2048,512]{1,0:T(8,128)(2,1)}, u32[]{:S(2)}) %copy-start.1) | copy-done | bytes 2097176
  3.2 1.2 %copy-done.2 = bf16[256,2048]{1,0:T(8,128)(2,1)S(1)} copy-done((bf16[256,2048]{1,0:T(8,128)(2,1)S(1)}, bf16[256,2048]{1,0:T(8,128)(2,1)}, u32[]{:S(2)}) %copy-start.2) | copy-done | bytes 1048600
  4.4 1.7 %project.1 = (f32[256,128]{1,0:T(8,128)S(1)}, f32[64,128]{1,0:T(8,128)S(1)}, bf16[272,128]{1,0:T(8,128)(2,1)S(1)}, bf16[272,128]{1,0:T(8,128)(2,1)S(1)}, bf16[272,128]{1,0:T(8,128)(2,1)S(1)}) custom-call(s32[1]{0:T(128)} %bitcast.1.at_ref, bf16[256,2048]{1,0:T(8,128)(2,1)S(1)} %copy-done.2, bf16[1,2048]{1,0:T(2,128)(2,1)S(1)} %broadcast_in_dim.33.gain_ref, ...), custom_call_target="tpu_custom_call" | custom-call | flops 536870912 | bytes 3145728 | tf_op jit(solution)/shard_map/project/pallas_call | solution.py:121
  6.1 0.6 %copy-done.6 = f32[256,128]{1,0:T(8,128)} copy-done((f32[256,128]{1,0:T(8,128)}, f32[256,128]{1,0:T(8,128)S(1)}, u32[]{:S(2)}) %copy-start.6) | copy-done | bytes 131096
  6.8 0.6 %copy-done.7 = f32[64,128]{1,0:T(8,128)} copy-done((f32[64,128]{1,0:T(8,128)}, f32[64,128]{1,0:T(8,128)S(1)}, u32[]{:S(2)}) %copy-start.7) | copy-done | bytes 32792
  7.4 3.0 %collective-permute-start.5 = (bf16[32,512]{1,0:T(8,128)(2,1)S(1)}, bf16[32,512]{1,0:T(8,128)(2,1)S(1)}, u32[]{:S(2)}, u32[]{:S(2)}) collective-permute-start(bf16[32,512]{1,0:T(8,128)(2,1)S(1)} %constant_dynamic-slice_fusion), channel_id=1, source_target_pairs={{0,1},{1,0},{2,3},{3,2},{4,5},{5,4},{6,7},{7,6},{8,9},{9,8},{10,11... | collective-permute-start | bytes 98312 | tf_op jit(solution)/shard_map/ppermute | solution.py:40
  10.4 2.6 %collective-permute-start.4 = (bf16[32,512]{1,0:T(8,128)(2,1)S(1)}, bf16[32,512]{1,0:T(8,128)(2,1)S(1)}, u32[]{:S(2)}, u32[]{:S(2)}) collective-permute-start(bf16[32,512]{1,0:T(8,128)(2,1)S(1)} %constant_dynamic-slice_fusion), channel_id=1, source_target_pairs={{0,2},{1,3},{2,0},{3,1},{4,6},{5,7},{6,4},{7,5},{8,10},{9,11},{10,... | collective-permute-start | bytes 98312 | tf_op jit(solution)/shard_map/ppermute | solution.py:40
  13.0 3.8 %collective-permute-start = (bf16[272,128]{1,0:T(8,128)(2,1)S(1)}, bf16[272,128]{1,0:T(8,128)(2,1)S(1)}, u32[]{:S(2)}, u32[]{:S(2)}) collective-permute-start(bf16[272,128]{1,0:T(8,128)(2,1)S(1)} %get-tuple-element.12), channel_id=1, source_target_pairs={{0,3},{1,2},{2,1},{3,0},{4,7},{5,6},{6,5},{7,4},{8,11},{9,10},{10,... | collective-permute-start | bytes 208904 | tf_op jit(solution)/shard_map/ppermute | solution.py:40
  17.9 0.7 %pad_maximum_fusion = (f32[64,128]{1,0:T(8,128)}, f32[64,128]{1,0:T(8,128)}) fusion(f32[64,64]{1,0:T(8,128)S(1)} %get-tuple-element.24, f32[64,64]{1,0:T(8,128)S(1)} %get-tuple-element.25, f32[64,64]{1,0:T(8,128)S(1)} %get-tuple-element.26), kind=kLoop, calls=%fused_computation.4 | loop fusion | flops 16384 | bytes 114688 | tf_op jit(solution)/shard_map/concatenate | solution.py:54
  18.9 2.3 %collective-permute-start.2 = (bf16[272,128]{1,0:T(8,128)(2,1)S(1)}, bf16[272,128]{1,0:T(8,128)(2,1)S(1)}, u32[]{:S(2)}, u32[]{:S(2)}) collective-permute-start(bf16[272,128]{1,0:T(8,128)(2,1)S(1)} %get-tuple-element.14), channel_id=1, source_target_pairs={{0,1},{1,0},{2,3},{3,2},{4,5},{5,4},{6,7},{7,6},{8,9},{9,8},{10,11... | collective-permute-start | bytes 208904 | tf_op jit(solution)/shard_map/ppermute | solution.py:40
  21.3 1.5 %collective-permute-done.1.rest_1_ = bf16[272,128]{1,0:T(8,128)(2,1)S(1)} collective-permute-done((bf16[272,128]{1,0:T(8,128)(2,1)S(1)}, bf16[272,128]{1,0:T(8,128)(2,1)S(1)}, u32[]{:S(2)}, u32[]{:S(2)}) %collective-permute-start.1) | collective-permute-done | bytes 69664 | tf_op jit(solution)/shard_map/ppermute | solution.py:40
  22.8 0.7 %collective-permute-done.2.rest_2_ = bf16[272,128]{1,0:T(8,128)(2,1)S(1)} collective-permute-done((bf16[272,128]{1,0:T(8,128)(2,1)S(1)}, bf16[272,128]{1,0:T(8,128)(2,1)S(1)}, u32[]{:S(2)}, u32[]{:S(2)}) %collective-permute-start.2) | collective-permute-done | bytes 69664 | tf_op jit(solution)/shard_map/ppermute | solution.py:40
  23.6 0.6 %copy-done.10 = bf16[272,128]{1,0:T(8,128)(2,1)} copy-done((bf16[272,128]{1,0:T(8,128)(2,1)}, bf16[272,128]{1,0:T(8,128)(2,1)S(1)}, u32[]{:S(2)}) %copy-start.10) | copy-done | bytes 69656
  24.2 1.9 %combine.1.rest_4_ = bf16[64,512]{1,0:T(8,128)(2,1)} custom-call(s32[1]{0:T(128)} %bitcast.first_ref, f32[256,128]{1,0:T(8,128)} %copy-done.6, f32[64,128]{1,0:T(8,128)} %copy-done.7, f32[64,128]{1,0:T(8,128)} %get-tuple-element.27.cosine_ref, f32[64,128]{1,0:T(8,128)} %get-tuple-element.28.sine_ref, bf16[272,128]{1,0:T(8,128)(2,1)} %copy-done.8, ...), custom_call_target="tpu_custom_call" | custom-call | tf_op jit(solution)/shard_map/combine/pallas_call | solution.py:164
  26.1 2.0 %collective-permute-start.14 = (bf16[64,512]{1,0:T(8,128)(2,1)}, bf16[64,512]{1,0:T(8,128)(2,1)S(1)}, u32[]{:S(2)}, u32[]{:S(2)}) collective-permute-start(bf16[64,512]{1,0:T(8,128)(2,1)} %combine.1.rest_4_), channel_id=1, source_target_pairs={{0,1},{1,0},{2,3},{3,2},{4,5},{5,4},{6,7},{7,6},{8,9},{9,8},{10,11... | collective-permute-start | bytes 196616 | tf_op jit(solution)/shard_map/ppermute | solution.py:40
  28.4 1.5 %collective-permute-start.6 = (bf16[128,512]{1,0:T(8,128)(2,1)S(1)}, bf16[128,512]{1,0:T(8,128)(2,1)S(1)}, u32[]{:S(2)}, u32[]{:S(2)}) collective-permute-start(bf16[128,512]{1,0:T(8,128)(2,1)S(1)} %bitcast.22), channel_id=1, source_target_pairs={{0,8},{4,12},{8,0},{12,4},{1,9},{5,13},{9,1},{13,5},{2,10},{6,14},... | collective-permute-start | bytes 393224 | tf_op jit(solution)/shard_map/ppermute | solution.py:40
  29.9 0.7 %collective-permute-start.12 = (bf16[64,512]{1,0:T(8,128)(2,1)}, bf16[64,512]{1,0:T(8,128)(2,1)S(1)}, u32[]{:S(2)}, u32[]{:S(2)}) collective-permute-start(bf16[64,512]{1,0:T(8,128)(2,1)} %combine.1.rest_4_), channel_id=1, source_target_pairs={{0,2},{1,3},{2,0},{3,1},{4,6},{5,7},{6,4},{7,5},{8,10},{9,11},{10,... | collective-permute-start | bytes 196616 | tf_op jit(solution)/shard_map/ppermute | solution.py:40
  30.7 1.9 %collective-permute-start.10 = (bf16[64,512]{1,0:T(8,128)(2,1)}, bf16[64,512]{1,0:T(8,128)(2,1)S(1)}, u32[]{:S(2)}, u32[]{:S(2)}) collective-permute-start(bf16[64,512]{1,0:T(8,128)(2,1)} %combine.1.rest_4_), channel_id=1, source_target_pairs={{0,3},{1,2},{2,1},{3,0},{4,7},{5,6},{6,5},{7,4},{8,11},{9,10},{10,... | collective-permute-start | bytes 196616 | tf_op jit(solution)/shard_map/ppermute | solution.py:40
  32.6 0.5 %collective-permute-start.9 = (bf16[64,512]{1,0:T(8,128)(2,1)}, bf16[64,512]{1,0:T(8,128)(2,1)S(1)}, u32[]{:S(2)}, u32[]{:S(2)}) collective-permute-start(bf16[64,512]{1,0:T(8,128)(2,1)} %combine.1.rest_4_), channel_id=1, source_target_pairs={{0,8},{4,12},{8,0},{12,4},{1,9},{5,13},{9,1},{13,5},{2,10},{6,14},... | collective-permute-start | bytes 196616 | tf_op jit(solution)/shard_map/ppermute | solution.py:40
  33.1 4.8 %collective-permute-done.12.rest_8_ = bf16[64,512]{1,0:T(8,128)(2,1)S(1)} collective-permute-done((bf16[64,512]{1,0:T(8,128)(2,1)}, bf16[64,512]{1,0:T(8,128)(2,1)S(1)}, u32[]{:S(2)}, u32[]{:S(2)}) %collective-permute-start.12) | collective-permute-done | bytes 65568 | tf_op jit(solution)/shard_map/ppermute | solution.py:40
  37.9 0.4 collective-permute-start.15
  38.6 1.6 %collective-permute-start.13 = (bf16[64,512]{1,0:T(8,128)(2,1)S(1)}, bf16[64,512]{1,0:T(8,128)(2,1)S(1)}, u32[]{:S(2)}, u32[]{:S(2)}) collective-permute-start(bf16[64,512]{1,0:T(8,128)(2,1)S(1)} %collective-permute-done.12.rest_8_), channel_id=1, source_target_pairs={{0,8},{4,12},{8,0},{12,4},{1,9},{5,13},{9,1},{13,5},{2,10},{6,14},... | collective-permute-start | bytes 196616 | tf_op jit(solution)/shard_map/ppermute | solution.py:40
  40.2 0.5 collective-permute-start.11
  40.7 2.1 %collective-permute-done.15.rest_11_ = bf16[64,512]{1,0:T(8,128)(2,1)S(1)} collective-permute-done((bf16[64,512]{1,0:T(8,128)(2,1)S(1)}, bf16[64,512]{1,0:T(8,128)(2,1)S(1)}, u32[]{:S(2)}, u32[]{:S(2)}) %collective-permute-start.15) | collective-permute-done | bytes 65568 | tf_op jit(solution)/shard_map/ppermute | solution.py:40
  43.6 0.7 %queries.1 = (bf16[4096,128]{1,0:T(8,128)(2,1)S(1)}, bf16[64,1024]{1,0:T(8,128)(2,1)S(1)}) custom-call(bf16[64,8192]{1,0:T(8,128)(2,1)S(1)} %bitcast.18, bf16[64,2048]{1,0:T(8,128)(2,1)S(1)} %bitcast.19, f32[64,128]{1,0:T(8,128)S(1)} %get-tuple-element.29.cosine_ref, f32[64,128]{1,0:T(8,128)S(1)} %get-tuple-element.30.sine_ref), custom_call_target="tpu_custom_call" | custom-call | flops 4194304 | bytes 2097152 | tf_op jit(solution)/shard_map/queries/pallas_call | solution.py:189
  44.2 0.6 %collective-permute-start.17 = (bf16[64,512]{1,0:T(8,128)(2,1)S(1)}, bf16[64,512]{1,0:T(8,128)(2,1)S(1)}, u32[]{:S(2)}, u32[]{:S(2)}) collective-permute-start(bf16[64,512]{1,0:T(8,128)(2,1)S(1)} %collective-permute-done.9.rest_5_), channel_id=1, source_target_pairs={{0,4},{4,0},{8,12},{12,8},{1,5},{5,1},{9,13},{13,9},{2,6},{6,2},{1... | collective-permute-start | bytes 196616 | tf_op jit(solution)/shard_map/ppermute | solution.py:40
  44.9 0.4 collective-permute-start.21
  45.7 0.4 collective-permute-done.23.rest_19_
  46.2 0.4 collective-permute-done.19.rest_15_
  46.6 0.8 %copy-done.5 = bf16[64,512]{1,0:T(8,128)(2,1)S(1)} copy-done((bf16[64,512]{1,0:T(8,128)(2,1)S(1)}, bf16[64,512]{1,0:T(8,128)(2,1)}, u32[]{:S(2)}) %copy-start.5) | copy-done | bytes 65560
  47.4 4.5 %attend.1 = bf16[64,8192]{1,0:T(8,128)(2,1)} custom-call(s32[3]{0:T(128)S(1)} %pad_add_fusion.spots_ref, bf16[4096,128]{1,0:T(8,128)(2,1)S(1)} %get-tuple-element.15.query_ref, bf16[64,1024]{1,0:T(8,128)(2,1)S(1)} %get-tuple-element.16.key_ref, bf16[64,2048]{1,0:T(8,128)(2,1)S(1)} %bitcast.20, bf16[128,512]{1,0:T(8,128)(2,1)S(1)} %bitcast.23, ...), custom_call_target="tpu_custom_call" | custom-call | flops 939524096 | bytes 2097152 | tf_op jit(solution)/shard_map/attend/pallas_call | solution.py:249
  (56 shorter events, 2.2 us)
Async XLA Ops:
  0.6 0.9 %copy-start = (bf16[32,2048]{1,0:T(8,128)(2,1)S(1)}, bf16[32,2048]{1,0:T(8,128)(2,1)}, u32[]{:S(2)}) copy-start(bf16[32,2048]{1,0:T(8,128)(2,1)} %param.11) | copy-start | bytes 393220
  1.6 1.6 %copy-start.1 = (bf16[2048,512]{1,0:T(8,128)(2,1)S(1)}, bf16[2048,512]{1,0:T(8,128)(2,1)}, u32[]{:S(2)}) copy-start(bf16[2048,512]{1,0:T(8,128)(2,1)} %weight_ref.1) | copy-start | bytes 6291460
  3.2 1.2 %copy-start.2 = (bf16[256,2048]{1,0:T(8,128)(2,1)S(1)}, bf16[256,2048]{1,0:T(8,128)(2,1)}, u32[]{:S(2)}) copy-start(bf16[256,2048]{1,0:T(8,128)(2,1)} %hidden_ref.1) | copy-start | bytes 3145732
  4.4 39.2 %copy-start.3 = (bf16[1,64,8192]{2,1,0:T(8,128)(2,1)S(1)}, bf16[1,64,8192]{2,1,0:T(8,128)(2,1)}, u32[]{:S(2)}) copy-start(bf16[1,64,8192]{2,1,0:T(8,128)(2,1)} %param.13) | copy-start | bytes 3145732
  4.4 39.2 %copy-start.4 = (bf16[1,64,2048]{2,1,0:T(8,128)(2,1)S(1)}, bf16[1,64,2048]{2,1,0:T(8,128)(2,1)}, u32[]{:S(2)}) copy-start(bf16[1,64,2048]{2,1,0:T(8,128)(2,1)} %param.14) | copy-start | bytes 786436
  7.4 20.8 %collective-permute-start.5 = (bf16[32,512]{1,0:T(8,128)(2,1)S(1)}, bf16[32,512]{1,0:T(8,128)(2,1)S(1)}, u32[]{:S(2)}, u32[]{:S(2)}) collective-permute-start(bf16[32,512]{1,0:T(8,128)(2,1)S(1)} %constant_dynamic-slice_fusion), channel_id=1, source_target_pairs={{0,1},{1,0},{2,3},{3,2},{4,5},{5,4},{6,7},{7,6},{8,9},{9,8},{10,11... | collective-permute-start | bytes 98312 | tf_op jit(solution)/shard_map/ppermute | solution.py:40
  10.4 10.9 %collective-permute-start.4 = (bf16[32,512]{1,0:T(8,128)(2,1)S(1)}, bf16[32,512]{1,0:T(8,128)(2,1)S(1)}, u32[]{:S(2)}, u32[]{:S(2)}) collective-permute-start(bf16[32,512]{1,0:T(8,128)(2,1)S(1)} %constant_dynamic-slice_fusion), channel_id=1, source_target_pairs={{0,2},{1,3},{2,0},{3,1},{4,6},{5,7},{6,4},{7,5},{8,10},{9,11},{10,... | collective-permute-start | bytes 98312 | tf_op jit(solution)/shard_map/ppermute | solution.py:40
  13.0 6.0 %collective-permute-start.3 = (bf16[32,512]{1,0:T(8,128)(2,1)S(1)}, bf16[32,512]{1,0:T(8,128)(2,1)S(1)}, u32[]{:S(2)}, u32[]{:S(2)}) collective-permute-start(bf16[32,512]{1,0:T(8,128)(2,1)S(1)} %constant_dynamic-slice_fusion), channel_id=1, source_target_pairs={{0,3},{1,2},{2,1},{3,0},{4,7},{5,6},{6,5},{7,4},{8,11},{9,10},{10,... | collective-permute-start | bytes 98312 | tf_op jit(solution)/shard_map/ppermute | solution.py:40
  13.0 8.3 %collective-permute-start = (bf16[272,128]{1,0:T(8,128)(2,1)S(1)}, bf16[272,128]{1,0:T(8,128)(2,1)S(1)}, u32[]{:S(2)}, u32[]{:S(2)}) collective-permute-start(bf16[272,128]{1,0:T(8,128)(2,1)S(1)} %get-tuple-element.12), channel_id=1, source_target_pairs={{0,3},{1,2},{2,1},{3,0},{4,7},{5,6},{6,5},{7,4},{8,11},{9,10},{10,... | collective-permute-start | bytes 208904 | tf_op jit(solution)/shard_map/ppermute | solution.py:40
  16.8 6.0 %collective-permute-start.1 = (bf16[272,128]{1,0:T(8,128)(2,1)S(1)}, bf16[272,128]{1,0:T(8,128)(2,1)S(1)}, u32[]{:S(2)}, u32[]{:S(2)}) collective-permute-start(bf16[272,128]{1,0:T(8,128)(2,1)S(1)} %get-tuple-element.13), channel_id=1, source_target_pairs={{0,2},{1,3},{2,0},{3,1},{4,6},{5,7},{6,4},{7,5},{8,10},{9,11},{10,... | collective-permute-start | bytes 208904 | tf_op jit(solution)/shard_map/ppermute | solution.py:40
  18.9 4.6 %collective-permute-start.2 = (bf16[272,128]{1,0:T(8,128)(2,1)S(1)}, bf16[272,128]{1,0:T(8,128)(2,1)S(1)}, u32[]{:S(2)}, u32[]{:S(2)}) collective-permute-start(bf16[272,128]{1,0:T(8,128)(2,1)S(1)} %get-tuple-element.14), channel_id=1, source_target_pairs={{0,1},{1,0},{2,3},{3,2},{4,5},{5,4},{6,7},{7,6},{8,9},{9,8},{10,11... | collective-permute-start | bytes 208904 | tf_op jit(solution)/shard_map/ppermute | solution.py:40
  21.3 2.3 %copy-start.8 = (bf16[272,128]{1,0:T(8,128)(2,1)}, bf16[272,128]{1,0:T(8,128)(2,1)S(1)}, u32[]{:S(2)}) copy-start(bf16[272,128]{1,0:T(8,128)(2,1)S(1)} %collective-permute-done.rest_0_) | copy-start | bytes 208900
  22.8 0.8 %copy-start.9 = (bf16[272,128]{1,0:T(8,128)(2,1)}, bf16[272,128]{1,0:T(8,128)(2,1)S(1)}, u32[]{:S(2)}) copy-start(bf16[272,128]{1,0:T(8,128)(2,1)S(1)} %collective-permute-done.1.rest_1_) | copy-start | bytes 208900
  26.1 4.6 %collective-permute-start.16 = (bf16[64,512]{1,0:T(8,128)(2,1)}, bf16[64,512]{1,0:T(8,128)(2,1)S(1)}, u32[]{:S(2)}, u32[]{:S(2)}) collective-permute-start(bf16[64,512]{1,0:T(8,128)(2,1)} %combine.1.rest_4_), channel_id=1, source_target_pairs={{0,4},{4,0},{8,12},{12,8},{1,5},{5,1},{9,13},{13,9},{2,6},{6,2},{1... | collective-permute-start | bytes 196616 | tf_op jit(solution)/shard_map/ppermute | solution.py:40
  26.1 6.5 %collective-permute-start.14 = (bf16[64,512]{1,0:T(8,128)(2,1)}, bf16[64,512]{1,0:T(8,128)(2,1)S(1)}, u32[]{:S(2)}, u32[]{:S(2)}) collective-permute-start(bf16[64,512]{1,0:T(8,128)(2,1)} %combine.1.rest_4_), channel_id=1, source_target_pairs={{0,1},{1,0},{2,3},{3,2},{4,5},{5,4},{6,7},{7,6},{8,9},{9,8},{10,11... | collective-permute-start | bytes 196616 | tf_op jit(solution)/shard_map/ppermute | solution.py:40
  28.1 10.5 %collective-permute-start.7 = (bf16[128,512]{1,0:T(8,128)(2,1)S(1)}, bf16[128,512]{1,0:T(8,128)(2,1)S(1)}, u32[]{:S(2)}, u32[]{:S(2)}) collective-permute-start(bf16[128,512]{1,0:T(8,128)(2,1)S(1)} %bitcast.21), channel_id=1, source_target_pairs={{0,4},{4,0},{8,12},{12,8},{1,5},{5,1},{9,13},{13,9},{2,6},{6,2},{1... | collective-permute-start | bytes 393224 | tf_op jit(solution)/shard_map/ppermute | solution.py:40
  28.4 11.8 %collective-permute-start.6 = (bf16[128,512]{1,0:T(8,128)(2,1)S(1)}, bf16[128,512]{1,0:T(8,128)(2,1)S(1)}, u32[]{:S(2)}, u32[]{:S(2)}) collective-permute-start(bf16[128,512]{1,0:T(8,128)(2,1)S(1)} %bitcast.22), channel_id=1, source_target_pairs={{0,8},{4,12},{8,0},{12,4},{1,9},{5,13},{9,1},{13,5},{2,10},{6,14},... | collective-permute-start | bytes 393224 | tf_op jit(solution)/shard_map/ppermute | solution.py:40
  29.9 8.0 %collective-permute-start.12 = (bf16[64,512]{1,0:T(8,128)(2,1)}, bf16[64,512]{1,0:T(8,128)(2,1)S(1)}, u32[]{:S(2)}, u32[]{:S(2)}) collective-permute-start(bf16[64,512]{1,0:T(8,128)(2,1)} %combine.1.rest_4_), channel_id=1, source_target_pairs={{0,2},{1,3},{2,0},{3,1},{4,6},{5,7},{6,4},{7,5},{8,10},{9,11},{10,... | collective-permute-start | bytes 196616 | tf_op jit(solution)/shard_map/ppermute | solution.py:40
  30.7 7.3 %collective-permute-start.10 = (bf16[64,512]{1,0:T(8,128)(2,1)}, bf16[64,512]{1,0:T(8,128)(2,1)S(1)}, u32[]{:S(2)}, u32[]{:S(2)}) collective-permute-start(bf16[64,512]{1,0:T(8,128)(2,1)} %combine.1.rest_4_), channel_id=1, source_target_pairs={{0,3},{1,2},{2,1},{3,0},{4,7},{5,6},{6,5},{7,4},{8,11},{9,10},{10,... | collective-permute-start | bytes 196616 | tf_op jit(solution)/shard_map/ppermute | solution.py:40
  32.6 5.8 %collective-permute-start.9 = (bf16[64,512]{1,0:T(8,128)(2,1)}, bf16[64,512]{1,0:T(8,128)(2,1)S(1)}, u32[]{:S(2)}, u32[]{:S(2)}) collective-permute-start(bf16[64,512]{1,0:T(8,128)(2,1)} %combine.1.rest_4_), channel_id=1, source_target_pairs={{0,8},{4,12},{8,0},{12,4},{1,9},{5,13},{9,1},{13,5},{2,10},{6,14},... | collective-permute-start | bytes 196616 | tf_op jit(solution)/shard_map/ppermute | solution.py:40
  37.9 2.3 %collective-permute-start.22 = (bf16[64,512]{1,0:T(8,128)(2,1)S(1)}, bf16[64,512]{1,0:T(8,128)(2,1)S(1)}, u32[]{:S(2)}, u32[]{:S(2)}) collective-permute-start(bf16[64,512]{1,0:T(8,128)(2,1)S(1)} %collective-permute-done.14.rest_10_), channel_id=1, source_target_pairs={{0,4},{4,0},{8,12},{12,8},{1,5},{5,1},{9,13},{13,9},{2,6},{6,2},{1... | collective-permute-start | bytes 196616 | tf_op jit(solution)/shard_map/ppermute | solution.py:40
  37.9 4.9 %collective-permute-start.15 = (bf16[64,512]{1,0:T(8,128)(2,1)S(1)}, bf16[64,512]{1,0:T(8,128)(2,1)S(1)}, u32[]{:S(2)}, u32[]{:S(2)}) collective-permute-start(bf16[64,512]{1,0:T(8,128)(2,1)S(1)} %collective-permute-done.14.rest_10_), channel_id=1, source_target_pairs={{0,8},{4,12},{8,0},{12,4},{1,9},{5,13},{9,1},{13,5},{2,10},{6,14},... | collective-permute-start | bytes 196616 | tf_op jit(solution)/shard_map/ppermute | solution.py:40
  38.4 5.9 %collective-permute-start.20 = (bf16[64,512]{1,0:T(8,128)(2,1)S(1)}, bf16[64,512]{1,0:T(8,128)(2,1)S(1)}, u32[]{:S(2)}, u32[]{:S(2)}) collective-permute-start(bf16[64,512]{1,0:T(8,128)(2,1)S(1)} %collective-permute-done.12.rest_8_), channel_id=1, source_target_pairs={{0,4},{4,0},{8,12},{12,8},{1,5},{5,1},{9,13},{13,9},{2,6},{6,2},{1... | collective-permute-start | bytes 196616 | tf_op jit(solution)/shard_map/ppermute | solution.py:40
  38.6 6.2 %collective-permute-start.13 = (bf16[64,512]{1,0:T(8,128)(2,1)S(1)}, bf16[64,512]{1,0:T(8,128)(2,1)S(1)}, u32[]{:S(2)}, u32[]{:S(2)}) collective-permute-start(bf16[64,512]{1,0:T(8,128)(2,1)S(1)} %collective-permute-done.12.rest_8_), channel_id=1, source_target_pairs={{0,8},{4,12},{8,0},{12,4},{1,9},{5,13},{9,1},{13,5},{2,10},{6,14},... | collective-permute-start | bytes 196616 | tf_op jit(solution)/shard_map/ppermute | solution.py:40
  40.2 4.7 %collective-permute-start.18 = (bf16[64,512]{1,0:T(8,128)(2,1)S(1)}, bf16[64,512]{1,0:T(8,128)(2,1)S(1)}, u32[]{:S(2)}, u32[]{:S(2)}) collective-permute-start(bf16[64,512]{1,0:T(8,128)(2,1)S(1)} %collective-permute-done.10.rest_6_), channel_id=1, source_target_pairs={{0,4},{4,0},{8,12},{12,8},{1,5},{5,1},{9,13},{13,9},{2,6},{6,2},{1... | collective-permute-start | bytes 196616 | tf_op jit(solution)/shard_map/ppermute | solution.py:40
  40.2 5.1 %collective-permute-start.11 = (bf16[64,512]{1,0:T(8,128)(2,1)S(1)}, bf16[64,512]{1,0:T(8,128)(2,1)S(1)}, u32[]{:S(2)}, u32[]{:S(2)}) collective-permute-start(bf16[64,512]{1,0:T(8,128)(2,1)S(1)} %collective-permute-done.10.rest_6_), channel_id=1, source_target_pairs={{0,8},{4,12},{8,0},{12,4},{1,9},{5,13},{9,1},{13,5},{2,10},{6,14},... | collective-permute-start | bytes 196616 | tf_op jit(solution)/shard_map/ppermute | solution.py:40
  42.8 3.8 %collective-permute-start.8 = (bf16[128,512]{1,0:T(8,128)(2,1)S(1)}, bf16[128,512]{1,0:T(8,128)(2,1)S(1)}, u32[]{:S(2)}, u32[]{:S(2)}) collective-permute-start(bf16[128,512]{1,0:T(8,128)(2,1)S(1)} %collective-permute-done.6.rest_1_), channel_id=1, source_target_pairs={{0,4},{4,0},{8,12},{12,8},{1,5},{5,1},{9,13},{13,9},{2,6},{6,2},{1... | collective-permute-start | bytes 393224 | tf_op jit(solution)/shard_map/ppermute | solution.py:40
  44.2 1.5 %collective-permute-start.17 = (bf16[64,512]{1,0:T(8,128)(2,1)S(1)}, bf16[64,512]{1,0:T(8,128)(2,1)S(1)}, u32[]{:S(2)}, u32[]{:S(2)}) collective-permute-start(bf16[64,512]{1,0:T(8,128)(2,1)S(1)} %collective-permute-done.9.rest_5_), channel_id=1, source_target_pairs={{0,4},{4,0},{8,12},{12,8},{1,5},{5,1},{9,13},{13,9},{2,6},{6,2},{1... | collective-permute-start | bytes 196616 | tf_op jit(solution)/shard_map/ppermute | solution.py:40
  44.8 1.3 %collective-permute-start.23 = (bf16[64,512]{1,0:T(8,128)(2,1)S(1)}, bf16[64,512]{1,0:T(8,128)(2,1)S(1)}, u32[]{:S(2)}, u32[]{:S(2)}) collective-permute-start(bf16[64,512]{1,0:T(8,128)(2,1)S(1)} %collective-permute-done.15.rest_11_), channel_id=1, source_target_pairs={{0,4},{4,0},{8,12},{12,8},{1,5},{5,1},{9,13},{13,9},{2,6},{6,2},{1... | collective-permute-start | bytes 196616 | tf_op jit(solution)/shard_map/ppermute | solution.py:40
  44.9 1.3 %collective-permute-start.21 = (bf16[64,512]{1,0:T(8,128)(2,1)S(1)}, bf16[64,512]{1,0:T(8,128)(2,1)S(1)}, u32[]{:S(2)}, u32[]{:S(2)}) collective-permute-start(bf16[64,512]{1,0:T(8,128)(2,1)S(1)} %collective-permute-done.13.rest_9_), channel_id=1, source_target_pairs={{0,4},{4,0},{8,12},{12,8},{1,5},{5,1},{9,13},{13,9},{2,6},{6,2},{1... | collective-permute-start | bytes 196616 | tf_op jit(solution)/shard_map/ppermute | solution.py:40
  45.3 1.3 %collective-permute-start.19 = (bf16[64,512]{1,0:T(8,128)(2,1)S(1)}, bf16[64,512]{1,0:T(8,128)(2,1)S(1)}, u32[]{:S(2)}, u32[]{:S(2)}) collective-permute-start(bf16[64,512]{1,0:T(8,128)(2,1)S(1)} %collective-permute-done.11.rest_7_), channel_id=1, source_target_pairs={{0,4},{4,0},{8,12},{12,8},{1,5},{5,1},{9,13},{13,9},{2,6},{6,2},{1... | collective-permute-start | bytes 196616 | tf_op jit(solution)/shard_map/ppermute | solution.py:40
  46.6 0.8 %copy-start.5 = (bf16[64,512]{1,0:T(8,128)(2,1)S(1)}, bf16[64,512]{1,0:T(8,128)(2,1)}, u32[]{:S(2)}) copy-start(bf16[64,512]{1,0:T(8,128)(2,1)} %combine.1.rest_4_) | copy-start | bytes 196612
  (3 other events, 1.9 us)

commit v2 on v1

v2 whole, which is shorter than its diff:
```python
import functools
import math

import jax
import jax.numpy as jnp
from jax import lax
from jax.experimental import pallas as pl
from jax.experimental.pallas import tpu as pltpu
from jax.sharding import PartitionSpec as P

MODEL_WIDTH = 8192
QUERY_HEADS = 64
KEY_HEADS = 8
HEAD_SIZE = 128
SPAN_LENGTH = 256
EPS = 1e-05
NEGATIVE_LARGE = -1e30
GROUP = QUERY_HEADS // KEY_HEADS
KEY_COLUMNS = KEY_HEADS * HEAD_SIZE
BF16 = jnp.bfloat16
F32 = jnp.float32
VMEM = pl.BlockSpec(memory_space=pltpu.VMEM)
HBM = pl.BlockSpec(memory_space=pltpu.HBM)
SMEM = pl.BlockSpec(memory_space=pltpu.SMEM)


def peer(index, step, count):
    if count & (count - 1) == 0:
        return index ^ step
    return (index + step) % count


def source(index, step, count):
    if count & (count - 1) == 0:
        return index ^ step
    return (index + count - step) % count


def exchange(value, axis, step):
    count = lax.axis_size(axis)
    return lax.ppermute(value, axis, [(i, peer(i, step, count)) for i in range(count)])


def frequencies():
    base = 500000.0 ** (-(jnp.arange(HEAD_SIZE // 2).astype(F32) * 2.0) / HEAD_SIZE)
    wave = 2.0 * math.pi / base
    smooth = (8192.0 / wave - 1.0) / 3.0
    blended = (1.0 - smooth) * base / 8.0 + smooth * base
    return jnp.where(wave < 2048.0, base, jnp.where(wave > 8192.0, base / 8.0, blended))


def tables(positions):
    angles = positions.astype(F32)[:, None] * frequencies()[None, :]
    cosine, sine = jnp.cos(angles), jnp.sin(angles)
    return jnp.concatenate([cosine, cosine], -1), jnp.concatenate([-sine, sine], -1)


def turn(value, cosine, sine):
    return value * cosine + pltpu.roll(value, HEAD_SIZE // 2, 1) * sine


def diagonal(rows):
    shape = (rows, HEAD_SIZE)
    return lax.broadcasted_iota(jnp.int32, shape, 0) == lax.broadcasted_iota(jnp.int32, shape, 1)


def project_kernel(count, rows, heads, chunks, at_ref, hidden_ref, gain_ref, weight_ref, *rest):
    own_ref, square_ref = rest[:2]
    sends = rest[2 : 1 + count]
    hidden_buf, gain_buf, weight_buf, total, squares, sems = rest[1 + count :]
    depth = hidden_ref.shape[1]
    size = depth // chunks
    gain_copy = pltpu.make_async_copy(gain_ref, gain_buf, sems.at[2 * chunks])
    gain_copy.start()
    copies = []
    for c in range(chunks):
        part = pl.ds(c * size, size)
        copies.append(
            (
                pltpu.make_async_copy(hidden_ref.at[:, part], hidden_buf.at[:, part], sems.at[2 * c]),
                pltpu.make_async_copy(weight_ref.at[part, :], weight_buf.at[part, :], sems.at[2 * c + 1]),
            )
        )
        copies[-1][0].start()
        copies[-1][1].start()
    gain_copy.wait()
    for c in range(chunks):
        copies[c][0].wait()
        folded, scaled = None, []
        for lane in range(c * size, (c + 1) * size, HEAD_SIZE):
            hidden = hidden_buf[:, lane : lane + HEAD_SIZE].astype(F32)
            tile = lane // HEAD_SIZE
            scaled.append((hidden * gain_buf[tile : tile + 1, :].astype(F32)).astype(BF16))
            square = hidden * hidden
            folded = square if folded is None else folded + square
        copies[c][1].wait()
        part = jnp.dot(
            jnp.concatenate(scaled, axis=1),
            weight_buf[c * size : (c + 1) * size, :],
            preferred_element_type=F32,
        )
        if c == 0:
            total[...] = part
            squares[...] = folded
        else:
            total[...] += part
            squares[...] += folded
    me = at_ref[0]
    for k in range(count):
        to = pl.ds(pl.multiple_of(peer(me, k, count) * rows, rows), rows)
        column = jnp.sum(squares[to, :], axis=1, keepdims=True)
        if k == 0:
            square_ref[...] = jnp.broadcast_to(column, (rows, HEAD_SIZE))
            out = own_ref
        else:
            out = sends[k - 1]
            line = jnp.sum(jnp.where(diagonal(rows), column, 0.0), axis=0, keepdims=True)
            high = line.astype(BF16).astype(F32)
            low = line - high
            which = lax.broadcasted_iota(jnp.int32, (16, HEAD_SIZE), 0)
            tail = jnp.where(which == 0, high, jnp.where(which == 1, low, 0.0))
            out[heads * rows :, :] = tail.astype(BF16)
        for h in range(heads):
            piece = total[to, h * HEAD_SIZE : (h + 1) * HEAD_SIZE]
            out[h * rows : (h + 1) * rows, :] = piece.astype(out.dtype)


def project(at, span_hidden, norm_gain, key_value_weight, count):
    length, depth = span_hidden.shape
    width = key_value_weight.shape[1]
    rows, heads = length // count, width // HEAD_SIZE
    chunks = 4 if depth % (4 * HEAD_SIZE) == 0 else 1
    gain = norm_gain.reshape(-1, HEAD_SIZE)
    outs = [
        jax.ShapeDtypeStruct((heads * rows, HEAD_SIZE), F32),
        jax.ShapeDtypeStruct((rows, HEAD_SIZE), F32),
    ] + [jax.ShapeDtypeStruct((heads * rows + 16, HEAD_SIZE), BF16)] * (count - 1)
    return pl.pallas_call(
        functools.partial(project_kernel, count, rows, heads, chunks),
        in_specs=[SMEM, HBM, HBM, HBM],
        out_shape=outs,
        out_specs=[VMEM] * len(outs),
        scratch_shapes=[
            pltpu.VMEM((length, depth), BF16),
            pltpu.VMEM(gain.shape, BF16),
            pltpu.VMEM((depth, width), BF16),
            pltpu.VMEM((length, width), F32),
            pltpu.VMEM((length, HEAD_SIZE), F32),
            pltpu.SemaphoreType.DMA((2 * chunks + 1,)),
        ],
        compiler_params=pltpu.CompilerParams(vmem_limit_bytes=16 << 20),
        cost_estimate=pl.CostEstimate(
            flops=2 * length * depth * width, bytes_accessed=2 * depth * (length + width), transcendentals=0
        ),
        name="project",
    )(at, span_hidden, gain, key_value_weight)


def combine_kernel(rows, heads, first_ref, own_ref, square_ref, cosine_ref, sine_ref, *rest):
    got, out_ref = rest[:-1], rest[-1]
    line = jnp.zeros((1, HEAD_SIZE), F32)
    for ref in got:
        tail = ref[heads * rows :, :].astype(F32)
        line = line + tail[0:1, :] + tail[1:2, :]
    column = jnp.sum(jnp.where(diagonal(rows), line, 0.0), axis=1, keepdims=True)
    scale = lax.rsqrt((square_ref[...] + column) / MODEL_WIDTH + EPS)
    cosine, sine = cosine_ref[...], sine_ref[...]
    for h in range(heads):
        span = slice(h * rows, (h + 1) * rows)
        value = own_ref[span, :]
        for ref in got:
            value = value + ref[span, :].astype(F32)
        value = value * scale
        is_key = first_ref[0] + h < KEY_HEADS
        out = jnp.where(is_key, turn(value, cosine, sine), value)
        out_ref[:, h * HEAD_SIZE : (h + 1) * HEAD_SIZE] = out.astype(BF16)


def combine(first, own, square, cosine, sine, got):
    rows = square.shape[0]
    heads = own.shape[0] // rows
    return pl.pallas_call(
        functools.partial(combine_kernel, rows, heads),
        in_specs=[SMEM] + [VMEM] * (4 + len(got)),
        out_shape=jax.ShapeDtypeStruct((rows, heads * HEAD_SIZE), BF16),
        out_specs=VMEM,
        compiler_params=pltpu.CompilerParams(vmem_limit_bytes=4 << 20),
        name="combine",
    )(first, own, square, cosine, sine, *got)


def queries_kernel(query_ref, own_ref, cosine_ref, sine_ref, query_out, key_out):
    tokens = cosine_ref.shape[0]
    cosine, sine = cosine_ref[...], sine_ref[...]
    for h in range(KEY_HEADS):
        span = slice(h * HEAD_SIZE, (h + 1) * HEAD_SIZE)
        key_out[:, span] = turn(own_ref[:, span].astype(F32), cosine, sine).astype(BF16)
    factor = HEAD_SIZE**-0.5 * math.log2(math.e)
    cosine, sine = cosine * factor, sine * factor
    for h in range(QUERY_HEADS):
        span = slice(h * HEAD_SIZE, (h + 1) * HEAD_SIZE)
        turned = turn(query_ref[:, span].astype(F32), cosine, sine)
        query_out[h * tokens : (h + 1) * tokens, :] = turned.astype(BF16)


def queries(cont_query, own_rows, cosine, sine):
    tokens = cosine.shape[0]
    return pl.pallas_call(
        queries_kernel,
        in_specs=[VMEM] * 4,
        out_shape=[
            jax.ShapeDtypeStruct((QUERY_HEADS * tokens, HEAD_SIZE), BF16),
            jax.ShapeDtypeStruct((tokens, KEY_COLUMNS), BF16),
        ],
        out_specs=[VMEM, VMEM],
        compiler_params=pltpu.CompilerParams(vmem_limit_bytes=8 << 20),
        cost_estimate=pl.CostEstimate(flops=8 * cont_query.size, bytes_accessed=4 * cont_query.size, transcendentals=0),
        name="queries",
    )(cont_query, own_rows, cosine, sine)


def attend_kernel(sets, plan, first, last, spots_ref, query_ref, *rest):
    pieces, rest = rest[: len(plan)], rest[len(plan) :]
    if first:
        key_ref, own_ref = rest[:2]
        top_out, mixed_out, cache = rest[2:]
    elif last:
        top_ref, mixed_ref, out_ref, cache, staged, sems = rest
    else:
        top_ref, mixed_ref, top_out, mixed_out, cache = rest
    me, offset, length = spots_ref[0], spots_ref[1], spots_ref[2]
    width = cache.shape[2]
    heads = width // HEAD_SIZE
    block = query_ref.shape[0] // KEY_HEADS
    tokens = block // GROUP
    total_rows = cache.shape[1]
    for ref, (step, row) in zip(pieces, plan):
        cache[source(me, step, sets), row : row + ref.shape[0], :] = ref[...]
    if first:
        prompt_rows = total_rows - tokens
        for s in range(sets):
            mine = key_ref if s * width < KEY_COLUMNS else own_ref
            cache[s, prompt_rows:, :] = mine[:, s * width : (s + 1) * width]
        token = lax.broadcasted_iota(jnp.int32, (tokens, total_rows), 0)
        place = lax.broadcasted_iota(jnp.int32, (tokens, total_rows), 1)
        live = (place < offset) & (place < prompt_rows) | (place >= prompt_rows) & (place - prompt_rows <= token)
        bias = jnp.concatenate([jnp.where(live, 0.0, NEGATIVE_LARGE)] * GROUP, axis=0)
    if last:
        keep = lax.broadcasted_iota(jnp.int32, (tokens, HEAD_SIZE), 0) < length
    ones = jnp.ones((total_rows, HEAD_SIZE), BF16)
    copies = []
    for g in range(KEY_HEADS):
        lane = (g % heads) * HEAD_SIZE
        span = slice(g * block, (g + 1) * block)
        key = cache[g // heads, :, lane : lane + HEAD_SIZE]
        value = cache[sets // 2 + g // heads, :, lane : lane + HEAD_SIZE]
        scores = lax.dot_general(
            query_ref[span, :], key, (((1,), (1,)), ((), ())), preferred_element_type=F32
        )
        if first:
            scores = scores + bias
        top = jnp.max(scores, axis=1, keepdims=True)
        if not first:
            old = top_ref[span, :]
            top = jnp.maximum(old, top)
        weights = jnp.exp2(scores - top[:, :1]).astype(BF16)
        mixed = jnp.dot(weights, jnp.concatenate([value, ones], axis=1), preferred_element_type=F32)
        if not first:
            shrink = jnp.exp2(old - top)
            mixed = mixed + mixed_ref[span, :] * jnp.concatenate([shrink, shrink], axis=1)
        if last:
            mixed = mixed[:, :HEAD_SIZE] / mixed[:, HEAD_SIZE:]
            for j in range(GROUP):
                column = (g * GROUP + j) * HEAD_SIZE
                piece = jnp.where(keep, mixed[j * tokens : (j + 1) * tokens, :], 0.0)
                staged[:, column : column + HEAD_SIZE] = piece.astype(BF16)
            part = pl.ds(g * GROUP * HEAD_SIZE, GROUP * HEAD_SIZE)
            copies.append(pltpu.make_async_copy(staged.at[:, part], out_ref.at[:, part], sems.at[g]))
            copies[-1].start()
        else:
            top_out[span, :] = jnp.broadcast_to(top, (block, HEAD_SIZE))
            mixed_out[span, :] = mixed
    for copy in copies:
        copy.wait()


def attend(spots, query, sets, pieces, own=(), state=(), last=False):
    first = not state
    width = pieces[0][2].shape[1]
    block = query.shape[0] // KEY_HEADS
    tokens = block // GROUP
    total_rows = max(row + value.shape[0] for _, row, value in pieces) + (tokens if first else 0)
    plan = [(step, row) for step, row, _ in pieces]
    operands = [spots, query] + [value for _, _, value in pieces] + list(own) + list(state)
    scratch = [pltpu.VMEM((sets, total_rows, width), BF16)]
    if last:
        out_shape = jax.ShapeDtypeStruct((tokens, QUERY_HEADS * HEAD_SIZE), BF16)
        out_specs = HBM
        scratch += [pltpu.VMEM(out_shape.shape, BF16), pltpu.SemaphoreType.DMA((KEY_HEADS,))]
    else:
        out_shape = [
            jax.ShapeDtypeStruct((query.shape[0], HEAD_SIZE), F32),
            jax.ShapeDtypeStruct((query.shape[0], 2 * HEAD_SIZE), F32),
        ]
        out_specs = [VMEM, VMEM]
    name = "attend_own" if first else "attend_last" if last else "attend_more"
    return pl.pallas_call(
        functools.partial(attend_kernel, sets, plan, first, last),
        in_specs=[SMEM] + [VMEM] * (len(operands) - 1),
        out_shape=out_shape,
        out_specs=out_specs,
        scratch_shapes=scratch,
        input_output_aliases={} if first or last else {len(operands) - 2: 0, len(operands) - 1: 1},
        compiler_params=pltpu.CompilerParams(vmem_limit_bytes=16 << 20),
        cost_estimate=pl.CostEstimate(
            flops=4 * query.size * total_rows, bytes_accessed=4 * query.size, transcendentals=query.size
        ),
        name=name,
    )(*operands)


def on_device(
    span_hidden,
    norm_gain,
    key_value_weight,
    prompt_key_value,
    span_offset,
    cont_query,
    continuation_key_value,
    cont_lengths,
):
    offset = span_offset[0]
    sets, count = lax.axis_size("set"), lax.axis_size("seq")
    my_set, my_seq = lax.axis_index("set"), lax.axis_index("seq")
    width = key_value_weight.shape[1]
    rows = span_hidden.shape[0] // count
    tokens = cont_query.shape[1]
    low = 2 if sets % 2 == 0 else 1

    own, square, *sends = project(my_seq[None].astype(jnp.int32), span_hidden, norm_gain, key_value_weight, count)
    order = list(range(count - 1, 0, -1))
    got = [exchange(sends[k - 1], "seq", k) for k in order]

    span_cosine, span_sine = tables(offset + my_seq * rows + jnp.arange(rows, dtype=jnp.int32))
    self_cosine, self_sine = tables(offset + SPAN_LENGTH + jnp.arange(tokens, dtype=jnp.int32))
    query, key = queries(cont_query[0], continuation_key_value[0], self_cosine, self_sine)

    mine = lax.dynamic_slice_in_dim(prompt_key_value, my_set * width, width, 1)
    mine, _ = lax.optimization_barrier((mine, got[0]))
    parts = [mine] + [exchange(mine, "seq", k) for k in order]
    prompt = jnp.zeros((count,) + mine.shape, BF16)
    for part, place in zip(parts, [my_seq] + [source(my_seq, k, count) for k in order]):
        prompt = lax.dynamic_update_slice(prompt, part[None], (place, 0, 0))
    prompt = prompt.reshape(-1, width)

    first = (my_set * (width // HEAD_SIZE))[None].astype(jnp.int32)
    block = combine(first, own, square, span_cosine, span_sine, got)

    far = list(range(low, sets, low))
    beside = [exchange(block, "set", step) for step in far]
    across = [exchange(block, "seq", k) for k in order[:-1]]
    nearest = exchange(jnp.concatenate([block] + beside, axis=0), "seq", order[-1])
    prompt, _ = lax.optimization_barrier((prompt, beside))
    prompts = [prompt] + [exchange(prompt, "set", step) for step in far]
    columns = [(0, [block] + beside)]
    for k, value in zip(order[:-1], across):
        columns.append((k * rows, [value] + [exchange(value, "set", step) for step in far]))
    columns.append((order[-1] * rows, [nearest[i * rows : (i + 1) * rows] for i in range(1 + len(far))]))

    def with_core(first_row, values):
        steps = [0] + far
        pieces = [(step, first_row, value) for step, value in zip(steps, values)]
        if low == 2:
            length = values[0].shape[0]
            others = exchange(jnp.concatenate(values, axis=0), "set", 1)
            pieces += [
                (step ^ 1, first_row, others[i * length : (i + 1) * length]) for i, step in enumerate(steps)
            ]
        return pieces

    spots = jnp.stack([my_set.astype(jnp.int32), offset, cont_lengths[0]])
    state = attend(spots, query, sets, with_core(0, prompts), own=(key, continuation_key_value[0]))
    split = max(1, len(columns) // 2)
    shares = [columns[:split], columns[split:]]
    for share in shares:
        pieces, row = [], 0
        for _, values in share:
            pieces += with_core(row, values)
            row += rows
        state = attend(spots, query, sets, pieces, state=state, last=share is shares[-1])
    return block, state[None]


def solution(mesh):
    placed = (
        P("parts", "seq"),
        P("seq"),
        P("seq", "set"),
        P(("parts", "seq"), None),
        P("parts"),
        P(("parts", "set", "seq"), None, None),
        P(("parts", "set", "seq"), None, None),
        P(("parts", "set", "seq")),
    )
    return jax.shard_map(
        on_device,
        mesh=mesh,
        in_specs=placed,
        out_specs=(P(("parts", "seq"), "set"), P(("parts", "set", "seq"), None, None)),
        check_vma=False,
    )
```

time: 52.3 us -> 51.1 us (0.977)
  Pallas kernels: 8.79 us -> 14.9 us
  local copies, waits for them, and re-layouts: 6.51 us -> 3.68 us
  starting transfers between devices: 22.7 us -> 19.9 us
  waiting for transfers between devices: 10.6 us -> 8.64 us
    pallas_call x2 -> x4, Pallas kernels: 6.23 us -> 13.4 us  [the longest x3 11.7 us: attend(): pl.pallas_call(functools.partial(attend_kernel, sets, plan, first, last),...]
    ppermute x24 -> x18, starting transfers between devices: 22.7 us -> 19.9 us  [exchange(): lax.ppermute(value, axis, [(i, peer(i, step, count)) for i in range(count)])]
    unnamed x22 -> x14, local copies, waits for them, and re-layouts: 5.74 us -> 3.55 us
    ppermute x24 -> x18, waiting for transfers between devices: 10.6 us -> 8.64 us  [exchange(): lax.ppermute(value, axis, [(i, peer(i, step, count)) for i in range(count)])]
    pallas_call x1, Pallas kernels: 1.9 us -> 0.84 us  [combine(): pl.pallas_call(functools.partial(combine_kernel, rows, heads), in_specs=[...]
    concatenate x0 -> x4, other arithmetic: none -> 0.89 us  [the longest x1 0.85 us: on_device(): jnp.concatenate([block] + beside, axis=0)]
    broadcast_in_dim x1 -> x0, local copies, waits for them, and re-layouts: 0.73 us -> none  [project(): norm_gain[None, :]]
    concatenate x2, other arithmetic: 0.8 us -> 0.17 us  [tables(): jnp.concatenate([cosine, cosine], -1)]
  transfers between devices with their start and end apart: 24 -> 18, of which waited for: 9 -> 4; matrix products, arithmetic and copies ran while one was open for 2% -> 3% of each run, Pallas kernels for 5% -> 3%
where the time goes in v2:
time: 51.1 us; the launch traced here: 50.9 us
  starting transfers between devices  19.9 us (39%)
  Pallas kernels  14.9 us (29%)
  waiting for transfers between devices  8.64 us (17%)
  local copies, waits for them, and re-layouts  3.68 us (7%)
  between operations  2.29 us (4%)
  other arithmetic  1.47 us (3%)
    ppermute x18, starting transfers between devices, exchange(): lax.ppermute(value, axis, [(i, peer(i, step, count)) for i in range(count)])  19.9 us
    pallas_call x3, Pallas kernels, attend(): pl.pallas_call(functools.partial(attend_kernel, sets, plan, first, last),...  11.7 us
    ppermute x18, waiting for transfers between devices, exchange(): lax.ppermute(value, axis, [(i, peer(i, step, count)) for i in range(count)])  8.64 us
    unnamed x14, local copies, waits for them, and re-layouts  3.55 us
    pallas_call x1, Pallas kernels, project(): pl.pallas_call(functools.partial(project_kernel, count, rows, heads, chun...  1.76 us
  transfers between devices with their start and end apart: 18, of which 4 were waited for; matrix products, arithmetic and copies ran while one was open for 3% of the time, Pallas kernels for 3%

profile of v2, /device:TPU:0, one launch (start us, length us, event | category | flops | bytes accessed | tf_op | source)
XLA Modules:
  0.0 50.9 jit_solution(9718699039052020345)
XLA Ops:
  0.7 1.6 %copy-done.1 = bf16[2048,512]{1,0:T(8,128)(2,1)S(1)} copy-done((bf16[2048,512]{1,0:T(8,128)(2,1)S(1)}, bf16[2048,512]{1,0:T(8,128)(2,1)}, u32[]{:S(2)}) %copy-start.1) | copy-done | bytes 2097176
  2.3 1.2 %copy-done.4 = bf16[256,2048]{1,0:T(8,128)(2,1)S(1)} copy-done((bf16[256,2048]{1,0:T(8,128)(2,1)S(1)}, bf16[256,2048]{1,0:T(8,128)(2,1)}, u32[]{:S(2)}) %copy-start.4) | copy-done | bytes 1048600
  3.5 0.7 %copy-done.6 = bf16[2048]{0:T(1024)(128)(2,1)S(1)} copy-done((bf16[2048]{0:T(1024)(128)(2,1)S(1)}, bf16[2048]{0:T(1024)(128)(2,1)}, u32[]{:S(2)}) %copy-start.6) | copy-done | bytes 4120
  4.2 1.8 %project.1 = (f32[256,128]{1,0:T(8,128)S(1)}, f32[64,128]{1,0:T(8,128)S(1)}, bf16[272,128]{1,0:T(8,128)(2,1)S(1)}, bf16[272,128]{1,0:T(8,128)(2,1)S(1)}, bf16[272,128]{1,0:T(8,128)(2,1)S(1)}) custom-call(s32[1]{0:T(128)} %bitcast.1.at_ref, bf16[256,2048]{1,0:T(8,128)(2,1)S(1)} %copy-done.4, bf16[16,128]{1,0:T(8,128)(2,1)S(1)} %bitcast.25, ...), custom_call_target="tpu_custom_call" | custom-call | flops 536870912 | bytes 3145728 | tf_op jit(solution)/shard_map/project/pallas_call | solution.py:138
  6.0 5.1 %collective-permute-start = (bf16[272,128]{1,0:T(8,128)(2,1)S(1)}, bf16[272,128]{1,0:T(8,128)(2,1)S(1)}, u32[]{:S(2)}, u32[]{:S(2)}) collective-permute-start(bf16[272,128]{1,0:T(8,128)(2,1)S(1)} %get-tuple-element.17), channel_id=1, source_target_pairs={{0,3},{1,2},{2,1},{3,0},{4,7},{5,6},{6,5},{7,4},{8,11},{9,10},{10,... | collective-permute-start | bytes 208904 | tf_op jit(solution)/shard_map/ppermute | solution.py:41
  11.1 0.6 %collective-permute-start.2 = (bf16[272,128]{1,0:T(8,128)(2,1)S(1)}, bf16[272,128]{1,0:T(8,128)(2,1)S(1)}, u32[]{:S(2)}, u32[]{:S(2)}) collective-permute-start(bf16[272,128]{1,0:T(8,128)(2,1)S(1)} %get-tuple-element.19), channel_id=1, source_target_pairs={{0,1},{1,0},{2,3},{3,2},{4,5},{5,4},{6,7},{7,6},{8,9},{9,8},{10,11... | collective-permute-start | bytes 208904 | tf_op jit(solution)/shard_map/ppermute | solution.py:41
  13.1 0.3 fusion.1
  13.4 0.1 pad_maximum_fusion.4
  13.5 0.1 pad_maximum_fusion.6
  13.6 0.7 %queries.1 = (bf16[4096,128]{1,0:T(8,128)(2,1)S(1)}, bf16[64,1024]{1,0:T(8,128)(2,1)S(1)}) custom-call(bf16[64,8192]{1,0:T(8,128)(2,1)S(1)} %bitcast.22, bf16[64,2048]{1,0:T(8,128)(2,1)S(1)} %bitcast.23, f32[64,128]{1,0:T(8,128)S(1)} %get-tuple-element.51.cosine_ref, f32[64,128]{1,0:T(8,128)S(1)} %get-tuple-element.52.sine_ref), custom_call_target="tpu_custom_call" | custom-call | flops 4194304 | bytes 2097152 | tf_op jit(solution)/shard_map/queries/pallas_call | solution.py:208
  14.3 0.1 pad_add_fusion.spots_ref
  14.4 3.8 %collective-permute-start.13 = (bf16[32,512]{1,0:T(8,128)(2,1)S(1)}, bf16[32,512]{1,0:T(8,128)(2,1)S(1)}, u32[]{:S(2)}, u32[]{:S(2)}) collective-permute-start(bf16[32,512]{1,0:T(8,128)(2,1)S(1)} %constant_dynamic-slice_fusion), channel_id=1, source_target_pairs={{0,3},{1,2},{2,1},{3,0},{4,7},{5,6},{6,5},{7,4},{8,11},{9,10},{10,... | collective-permute-start | bytes 98312 | tf_op jit(solution)/shard_map/ppermute | solution.py:41
  18.2 0.6 %collective-permute-start.15 = (bf16[32,512]{1,0:T(8,128)(2,1)S(1)}, bf16[32,512]{1,0:T(8,128)(2,1)S(1)}, u32[]{:S(2)}, u32[]{:S(2)}) collective-permute-start(bf16[32,512]{1,0:T(8,128)(2,1)S(1)} %constant_dynamic-slice_fusion), channel_id=1, source_target_pairs={{0,1},{1,0},{2,3},{3,2},{4,5},{5,4},{6,7},{7,6},{8,9},{9,8},{10,11... | collective-permute-start | bytes 98312 | tf_op jit(solution)/shard_map/ppermute | solution.py:41
  18.8 0.8 %combine.1.rest_0_ = bf16[64,512]{1,0:T(8,128)(2,1)} custom-call(s32[1]{0:T(128)} %bitcast.first_ref, f32[256,128]{1,0:T(8,128)S(1)} %get-tuple-element.15.own_ref, f32[64,128]{1,0:T(8,128)S(1)} %get-tuple-element.16.square_ref, f32[64,128]{1,0:T(8,128)S(1)} %get-tuple-element.49.cosine_ref, f32[64,128]{1,0:T(8,128)S(1)} %get-tuple-element.50.sine_ref, ...), custom_call_target="tpu_custom_call" | custom-call | tf_op jit(solution)/shard_map/combine/pallas_call | solution.py:182
  19.6 1.6 %collective-permute-start.6 = (bf16[64,512]{1,0:T(8,128)(2,1)}, bf16[64,512]{1,0:T(8,128)(2,1)S(1)}, u32[]{:S(2)}, u32[]{:S(2)}) collective-permute-start(bf16[64,512]{1,0:T(8,128)(2,1)} %combine.1.rest_0_), channel_id=1, source_target_pairs={{0,8},{4,12},{8,0},{12,4},{1,9},{5,13},{9,1},{13,5},{2,10},{6,14},... | collective-permute-start | bytes 196616 | tf_op jit(solution)/shard_map/ppermute | solution.py:41
  21.3 3.6 %collective-permute-start.10 = (bf16[64,512]{1,0:T(8,128)(2,1)}, bf16[64,512]{1,0:T(8,128)(2,1)S(1)}, u32[]{:S(2)}, u32[]{:S(2)}) collective-permute-start(bf16[64,512]{1,0:T(8,128)(2,1)} %combine.1.rest_0_), channel_id=1, source_target_pairs={{0,3},{1,2},{2,1},{3,0},{4,7},{5,6},{6,5},{7,4},{8,11},{9,10},{10,... | collective-permute-start | bytes 196616 | tf_op jit(solution)/shard_map/ppermute | solution.py:41
  25.1 2.6 %collective-permute-done.10.rest_4_ = bf16[64,512]{1,0:T(8,128)(2,1)S(1)} collective-permute-done((bf16[64,512]{1,0:T(8,128)(2,1)}, bf16[64,512]{1,0:T(8,128)(2,1)S(1)}, u32[]{:S(2)}, u32[]{:S(2)}) %collective-permute-start.10) | collective-permute-done | bytes 65568 | tf_op jit(solution)/shard_map/ppermute | solution.py:41
  27.6 0.4 collective-permute-start.11
  28.0 0.8 %pad_maximum_fusion.2 = bf16[128,512]{1,0:T(8,128)(2,1)S(1)} fusion(bf16[64,512]{1,0:T(8,128)(2,1)S(1)} %collective-permute-done.6.rest_1_, bf16[64,512]{1,0:T(8,128)(2,1)} %combine.1.rest_0_), kind=kLoop, calls=%fused_computation.2 | loop fusion | flops 262144 | bytes 262144 | tf_op jit(solution)/shard_map/concatenate | solution.py:362
  28.9 0.1 collective-permute-start.9
  29.0 1.1 %collective-permute-start.7 = (bf16[128,512]{1,0:T(8,128)(2,1)S(1)}, bf16[128,512]{1,0:T(8,128)(2,1)S(1)}, u32[]{:S(2)}, u32[]{:S(2)}) collective-permute-start(bf16[128,512]{1,0:T(8,128)(2,1)S(1)} %pad_maximum_fusion.2), channel_id=1, source_target_pairs={{0,1},{1,0},{2,3},{3,2},{4,5},{5,4},{6,7},{7,6},{8,9},{9,8},{10,11... | collective-permute-start | bytes 393224 | tf_op jit(solution)/shard_map/ppermute | solution.py:41
  30.1 0.7 %collective-permute-start.16 = (bf16[128,512]{1,0:T(8,128)(2,1)S(1)}, bf16[128,512]{1,0:T(8,128)(2,1)S(1)}, u32[]{:S(2)}, u32[]{:S(2)}) collective-permute-start(bf16[128,512]{1,0:T(8,128)(2,1)S(1)} %bitcast.19), channel_id=1, source_target_pairs={{0,8},{4,12},{8,0},{12,4},{1,9},{5,13},{9,1},{13,5},{2,10},{6,14},... | collective-permute-start | bytes 393224 | tf_op jit(solution)/shard_map/ppermute | solution.py:41
  30.8 1.4 %collective-permute-start.4 = (bf16[64,512]{1,0:T(8,128)(2,1)S(1)}, bf16[64,512]{1,0:T(8,128)(2,1)S(1)}, u32[]{:S(2)}, u32[]{:S(2)}) collective-permute-start(bf16[64,512]{1,0:T(8,128)(2,1)S(1)} %collective-permute-done.3.rest_0_), channel_id=1, source_target_pairs={{0,8},{4,12},{8,0},{12,4},{1,9},{5,13},{9,1},{13,5},{2,10},{6,14},... | collective-permute-start | bytes 196616 | tf_op jit(solution)/shard_map/ppermute | solution.py:41
  32.2 4.8 %collective-permute-done.4.rest_1_ = bf16[64,512]{1,0:T(8,128)(2,1)S(1)} collective-permute-done((bf16[64,512]{1,0:T(8,128)(2,1)S(1)}, bf16[64,512]{1,0:T(8,128)(2,1)S(1)}, u32[]{:S(2)}, u32[]{:S(2)}) %collective-permute-start.4) | collective-permute-done | bytes 65568 | tf_op jit(solution)/shard_map/ppermute | solution.py:41
  37.1 0.1 collective-permute-start.5
  37.2 0.5 %collective-permute-start.17 = (bf16[256,512]{1,0:T(8,128)(2,1)S(1)}, bf16[256,512]{1,0:T(8,128)(2,1)S(1)}, u32[]{:S(2)}, u32[]{:S(2)}) collective-permute-start(bf16[256,512]{1,0:T(8,128)(2,1)S(1)} %pad_maximum_fusion), channel_id=1, source_target_pairs={{0,4},{4,0},{8,12},{12,8},{1,5},{5,1},{9,13},{13,9},{2,6},{6,2},{1... | collective-permute-start | bytes 786440 | tf_op jit(solution)/shard_map/ppermute | solution.py:41
  37.8 0.1 collective-permute-start.8
  37.9 0.6 %collective-permute-done.5 = bf16[128,512]{1,0:T(8,128)(2,1)S(1)} collective-permute-done((bf16[128,512]{1,0:T(8,128)(2,1)S(1)}, bf16[128,512]{1,0:T(8,128)(2,1)S(1)}, u32[]{:S(2)}, u32[]{:S(2)}) %collective-permute-start.5) | collective-permute-done | bytes 131104 | tf_op jit(solution)/shard_map/ppermute | solution.py:41
  38.5 0.6 %collective-permute-done.8 = bf16[128,512]{1,0:T(8,128)(2,1)S(1)} collective-permute-done((bf16[128,512]{1,0:T(8,128)(2,1)S(1)}, bf16[128,512]{1,0:T(8,128)(2,1)S(1)}, u32[]{:S(2)}, u32[]{:S(2)}) %collective-permute-start.8) | collective-permute-done | bytes 131104 | tf_op jit(solution)/shard_map/ppermute | solution.py:41
  39.2 2.3 %attend_own.1 = (f32[4096,128]{1,0:T(8,128)S(1)}, f32[4096,256]{1,0:T(8,128)S(1)}) custom-call(s32[3]{0:T(128)S(1)} %pad_add_fusion.spots_ref, bf16[4096,128]{1,0:T(8,128)(2,1)S(1)} %get-tuple-element.20.query_ref, bf16[128,512]{1,0:T(8,128)(2,1)S(1)} %bitcast.21, bf16[128,512]{1,0:T(8,128)(2,1)S(1)} %collective-permute-done.16.rest_1_, ...), custom_call_target="tpu_custom_call" | custom-call | flops 402653184 | bytes 2097152 | tf_op jit(solution)/shard_map/attend_own/pallas_call | solution.py:307
  41.5 5.1 %attend_more.1 = (f32[4096,128]{1,0:T(8,128)S(1)}, f32[4096,256]{1,0:T(8,128)S(1)}) custom-call(s32[3]{0:T(128)S(1)} %pad_add_fusion.spots_ref, bf16[4096,128]{1,0:T(8,128)(2,1)S(1)} %get-tuple-element.20.query_ref, bf16[64,512]{1,0:T(8,128)(2,1)S(1)} %copy-done.5, ...), custom_call_target="tpu_custom_call", output_to_operand_aliasing={{0}: (10, {}), {1}: (11, {})} | custom-call | flops 268435456 | bytes 2097152 | tf_op jit(solution)/shard_map/attend_more/pallas_call | solution.py:307
  46.6 4.3 %attend_last.1 = bf16[64,8192]{1,0:T(8,128)(2,1)} custom-call(s32[3]{0:T(128)S(1)} %pad_add_fusion.spots_ref, bf16[4096,128]{1,0:T(8,128)(2,1)S(1)} %get-tuple-element.20.query_ref, bf16[64,512]{1,0:T(8,128)(2,1)S(1)} %collective-permute-done.3.rest_0_, bf16[64,512]{1,0:T(8,128)(2,1)S(1)} %collective-permute-done.4.rest_1_, ...), custom_call_target="tpu_custom_call" | custom-call | flops 268435456 | bytes 2097152 | tf_op jit(solution)/shard_map/attend_last/pallas_call | solution.py:307
  (47 shorter events, 0.4 us)
Async XLA Ops:
  0.6 12.4 %copy-start = (bf16[32,2048]{1,0:T(8,128)(2,1)S(1)}, bf16[32,2048]{1,0:T(8,128)(2,1)}, u32[]{:S(2)}) copy-start(bf16[32,2048]{1,0:T(8,128)(2,1)} %param.11) | copy-start | bytes 393220
  0.7 1.6 %copy-start.1 = (bf16[2048,512]{1,0:T(8,128)(2,1)S(1)}, bf16[2048,512]{1,0:T(8,128)(2,1)}, u32[]{:S(2)}) copy-start(bf16[2048,512]{1,0:T(8,128)(2,1)} %weight_ref.1) | copy-start | bytes 6291460
  2.3 1.2 %copy-start.4 = (bf16[256,2048]{1,0:T(8,128)(2,1)S(1)}, bf16[256,2048]{1,0:T(8,128)(2,1)}, u32[]{:S(2)}) copy-start(bf16[256,2048]{1,0:T(8,128)(2,1)} %hidden_ref.1) | copy-start | bytes 3145732
  3.5 0.7 %copy-start.6 = (bf16[2048]{0:T(1024)(128)(2,1)S(1)}, bf16[2048]{0:T(1024)(128)(2,1)}, u32[]{:S(2)}) copy-start(bf16[2048]{0:T(1024)(128)(2,1)} %param.9) | copy-start | bytes 12292
  4.2 9.4 %copy-start.2 = (bf16[1,64,8192]{2,1,0:T(8,128)(2,1)S(1)}, bf16[1,64,8192]{2,1,0:T(8,128)(2,1)}, u32[]{:S(2)}) copy-start(bf16[1,64,8192]{2,1,0:T(8,128)(2,1)} %param.13) | copy-start | bytes 3145732
  4.2 9.4 %copy-start.3 = (bf16[1,64,2048]{2,1,0:T(8,128)(2,1)S(1)}, bf16[1,64,2048]{2,1,0:T(8,128)(2,1)}, u32[]{:S(2)}) copy-start(bf16[1,64,2048]{2,1,0:T(8,128)(2,1)} %param.14) | copy-start | bytes 786436
  6.0 8.4 %collective-permute-start = (bf16[272,128]{1,0:T(8,128)(2,1)S(1)}, bf16[272,128]{1,0:T(8,128)(2,1)S(1)}, u32[]{:S(2)}, u32[]{:S(2)}) collective-permute-start(bf16[272,128]{1,0:T(8,128)(2,1)S(1)} %get-tuple-element.17), channel_id=1, source_target_pairs={{0,3},{1,2},{2,1},{3,0},{4,7},{5,6},{6,5},{7,4},{8,11},{9,10},{10,... | collective-permute-start | bytes 208904 | tf_op jit(solution)/shard_map/ppermute | solution.py:41
  11.1 7.7 %collective-permute-start.1 = (bf16[272,128]{1,0:T(8,128)(2,1)S(1)}, bf16[272,128]{1,0:T(8,128)(2,1)S(1)}, u32[]{:S(2)}, u32[]{:S(2)}) collective-permute-start(bf16[272,128]{1,0:T(8,128)(2,1)S(1)} %get-tuple-element.18), channel_id=1, source_target_pairs={{0,2},{1,3},{2,0},{3,1},{4,6},{5,7},{6,4},{7,5},{8,10},{9,11},{10,... | collective-permute-start | bytes 208904 | tf_op jit(solution)/shard_map/ppermute | solution.py:41
  11.1 7.7 %collective-permute-start.2 = (bf16[272,128]{1,0:T(8,128)(2,1)S(1)}, bf16[272,128]{1,0:T(8,128)(2,1)S(1)}, u32[]{:S(2)}, u32[]{:S(2)}) collective-permute-start(bf16[272,128]{1,0:T(8,128)(2,1)S(1)} %get-tuple-element.19), channel_id=1, source_target_pairs={{0,1},{1,0},{2,3},{3,2},{4,5},{5,4},{6,7},{7,6},{8,9},{9,8},{10,11... | collective-permute-start | bytes 208904 | tf_op jit(solution)/shard_map/ppermute | solution.py:41
  14.4 10.5 %collective-permute-start.13 = (bf16[32,512]{1,0:T(8,128)(2,1)S(1)}, bf16[32,512]{1,0:T(8,128)(2,1)S(1)}, u32[]{:S(2)}, u32[]{:S(2)}) collective-permute-start(bf16[32,512]{1,0:T(8,128)(2,1)S(1)} %constant_dynamic-slice_fusion), channel_id=1, source_target_pairs={{0,3},{1,2},{2,1},{3,0},{4,7},{5,6},{6,5},{7,4},{8,11},{9,10},{10,... | collective-permute-start | bytes 98312 | tf_op jit(solution)/shard_map/ppermute | solution.py:41
  18.2 6.9 %collective-permute-start.14 = (bf16[32,512]{1,0:T(8,128)(2,1)S(1)}, bf16[32,512]{1,0:T(8,128)(2,1)S(1)}, u32[]{:S(2)}, u32[]{:S(2)}) collective-permute-start(bf16[32,512]{1,0:T(8,128)(2,1)S(1)} %constant_dynamic-slice_fusion), channel_id=1, source_target_pairs={{0,2},{1,3},{2,0},{3,1},{4,6},{5,7},{6,4},{7,5},{8,10},{9,11},{10,... | collective-permute-start | bytes 98312 | tf_op jit(solution)/shard_map/ppermute | solution.py:41
  18.2 6.9 %collective-permute-start.15 = (bf16[32,512]{1,0:T(8,128)(2,1)S(1)}, bf16[32,512]{1,0:T(8,128)(2,1)S(1)}, u32[]{:S(2)}, u32[]{:S(2)}) collective-permute-start(bf16[32,512]{1,0:T(8,128)(2,1)S(1)} %constant_dynamic-slice_fusion), channel_id=1, source_target_pairs={{0,1},{1,0},{2,3},{3,2},{4,5},{5,4},{6,7},{7,6},{8,9},{9,8},{10,11... | collective-permute-start | bytes 98312 | tf_op jit(solution)/shard_map/ppermute | solution.py:41
  19.6 8.4 %collective-permute-start.6 = (bf16[64,512]{1,0:T(8,128)(2,1)}, bf16[64,512]{1,0:T(8,128)(2,1)S(1)}, u32[]{:S(2)}, u32[]{:S(2)}) collective-permute-start(bf16[64,512]{1,0:T(8,128)(2,1)} %combine.1.rest_0_), channel_id=1, source_target_pairs={{0,8},{4,12},{8,0},{12,4},{1,9},{5,13},{9,1},{13,5},{2,10},{6,14},... | collective-permute-start | bytes 196616 | tf_op jit(solution)/shard_map/ppermute | solution.py:41
  21.3 6.4 %collective-permute-start.10 = (bf16[64,512]{1,0:T(8,128)(2,1)}, bf16[64,512]{1,0:T(8,128)(2,1)S(1)}, u32[]{:S(2)}, u32[]{:S(2)}) collective-permute-start(bf16[64,512]{1,0:T(8,128)(2,1)} %combine.1.rest_0_), channel_id=1, source_target_pairs={{0,3},{1,2},{2,1},{3,0},{4,7},{5,6},{6,5},{7,4},{8,11},{9,10},{10,... | collective-permute-start | bytes 196616 | tf_op jit(solution)/shard_map/ppermute | solution.py:41
  24.9 5.8 %collective-permute-start.3 = (bf16[64,512]{1,0:T(8,128)(2,1)}, bf16[64,512]{1,0:T(8,128)(2,1)S(1)}, u32[]{:S(2)}, u32[]{:S(2)}) collective-permute-start(bf16[64,512]{1,0:T(8,128)(2,1)} %combine.1.rest_0_), channel_id=1, source_target_pairs={{0,2},{1,3},{2,0},{3,1},{4,6},{5,7},{6,4},{7,5},{8,10},{9,11},{10,... | collective-permute-start | bytes 196616 | tf_op jit(solution)/shard_map/ppermute | solution.py:41
  27.6 4.5 %collective-permute-start.11 = (bf16[64,512]{1,0:T(8,128)(2,1)S(1)}, bf16[64,512]{1,0:T(8,128)(2,1)S(1)}, u32[]{:S(2)}, u32[]{:S(2)}) collective-permute-start(bf16[64,512]{1,0:T(8,128)(2,1)S(1)} %collective-permute-done.10.rest_4_), channel_id=1, source_target_pairs={{0,8},{4,12},{8,0},{12,4},{1,9},{5,13},{9,1},{13,5},{2,10},{6,14},... | collective-permute-start | bytes 196616 | tf_op jit(solution)/shard_map/ppermute | solution.py:41
  28.9 9.0 %collective-permute-start.9 = (bf16[128,512]{1,0:T(8,128)(2,1)S(1)}, bf16[128,512]{1,0:T(8,128)(2,1)S(1)}, u32[]{:S(2)}, u32[]{:S(2)}) collective-permute-start(bf16[128,512]{1,0:T(8,128)(2,1)S(1)} %pad_maximum_fusion.2), channel_id=1, source_target_pairs={{0,4},{4,0},{8,12},{12,8},{1,5},{5,1},{9,13},{13,9},{2,6},{6,2},{1... | collective-permute-start | bytes 393224 | tf_op jit(solution)/shard_map/ppermute | solution.py:41
  29.0 8.8 %collective-permute-start.7 = (bf16[128,512]{1,0:T(8,128)(2,1)S(1)}, bf16[128,512]{1,0:T(8,128)(2,1)S(1)}, u32[]{:S(2)}, u32[]{:S(2)}) collective-permute-start(bf16[128,512]{1,0:T(8,128)(2,1)S(1)} %pad_maximum_fusion.2), channel_id=1, source_target_pairs={{0,1},{1,0},{2,3},{3,2},{4,5},{5,4},{6,7},{7,6},{8,9},{9,8},{10,11... | collective-permute-start | bytes 393224 | tf_op jit(solution)/shard_map/ppermute | solution.py:41
  30.1 7.1 %collective-permute-start.16 = (bf16[128,512]{1,0:T(8,128)(2,1)S(1)}, bf16[128,512]{1,0:T(8,128)(2,1)S(1)}, u32[]{:S(2)}, u32[]{:S(2)}) collective-permute-start(bf16[128,512]{1,0:T(8,128)(2,1)S(1)} %bitcast.19), channel_id=1, source_target_pairs={{0,8},{4,12},{8,0},{12,4},{1,9},{5,13},{9,1},{13,5},{2,10},{6,14},... | collective-permute-start | bytes 393224 | tf_op jit(solution)/shard_map/ppermute | solution.py:41
  30.8 6.3 %collective-permute-start.4 = (bf16[64,512]{1,0:T(8,128)(2,1)S(1)}, bf16[64,512]{1,0:T(8,128)(2,1)S(1)}, u32[]{:S(2)}, u32[]{:S(2)}) collective-permute-start(bf16[64,512]{1,0:T(8,128)(2,1)S(1)} %collective-permute-done.3.rest_0_), channel_id=1, source_target_pairs={{0,8},{4,12},{8,0},{12,4},{1,9},{5,13},{9,1},{13,5},{2,10},{6,14},... | collective-permute-start | bytes 196616 | tf_op jit(solution)/shard_map/ppermute | solution.py:41
  32.1 5.8 %collective-permute-start.12 = (bf16[128,512]{1,0:T(8,128)(2,1)S(1)}, bf16[128,512]{1,0:T(8,128)(2,1)S(1)}, u32[]{:S(2)}, u32[]{:S(2)}) collective-permute-start(bf16[128,512]{1,0:T(8,128)(2,1)S(1)} %pad_maximum_fusion.3), channel_id=1, source_target_pairs={{0,4},{4,0},{8,12},{12,8},{1,5},{5,1},{9,13},{13,9},{2,6},{6,2},{1... | collective-permute-start | bytes 393224 | tf_op jit(solution)/shard_map/ppermute | solution.py:41
  37.1 4.4 %copy-start.5 = (bf16[64,512]{1,0:T(8,128)(2,1)S(1)}, bf16[64,512]{1,0:T(8,128)(2,1)}, u32[]{:S(2)}) copy-start(bf16[64,512]{1,0:T(8,128)(2,1)} %combine.1.rest_0_) | copy-start | bytes 196612
  37.1 1.4 %collective-permute-start.5 = (bf16[128,512]{1,0:T(8,128)(2,1)S(1)}, bf16[128,512]{1,0:T(8,128)(2,1)S(1)}, u32[]{:S(2)}, u32[]{:S(2)}) collective-permute-start(bf16[128,512]{1,0:T(8,128)(2,1)S(1)} %pad_maximum_fusion.1), channel_id=1, source_target_pairs={{0,4},{4,0},{8,12},{12,8},{1,5},{5,1},{9,13},{13,9},{2,6},{6,2},{1... | collective-permute-start | bytes 393224 | tf_op jit(solution)/shard_map/ppermute | solution.py:41
  37.2 1.9 %collective-permute-start.17 = (bf16[256,512]{1,0:T(8,128)(2,1)S(1)}, bf16[256,512]{1,0:T(8,128)(2,1)S(1)}, u32[]{:S(2)}, u32[]{:S(2)}) collective-permute-start(bf16[256,512]{1,0:T(8,128)(2,1)S(1)} %pad_maximum_fusion), channel_id=1, source_target_pairs={{0,4},{4,0},{8,12},{12,8},{1,5},{5,1},{9,13},{13,9},{2,6},{6,2},{1... | collective-permute-start | bytes 786440 | tf_op jit(solution)/shard_map/ppermute | solution.py:41
  37.8 1.3 %collective-permute-start.8 = (bf16[128,512]{1,0:T(8,128)(2,1)S(1)}, bf16[128,512]{1,0:T(8,128)(2,1)S(1)}, u32[]{:S(2)}, u32[]{:S(2)}) collective-permute-start(bf16[128,512]{1,0:T(8,128)(2,1)S(1)} %collective-permute-done.7), channel_id=1, source_target_pairs={{0,4},{4,0},{8,12},{12,8},{1,5},{5,1},{9,13},{13,9},{2,6},{6,2},{1... | collective-permute-start | bytes 393224 | tf_op jit(solution)/shard_map/ppermute | solution.py:41

commit v3 on v2

v3 whole, which is shorter than its diff:
```python
import functools
import math

import jax
import jax.numpy as jnp
from jax import lax
from jax.experimental import pallas as pl
from jax.experimental.pallas import tpu as pltpu
from jax.sharding import PartitionSpec as P

MODEL_WIDTH = 8192
QUERY_HEADS = 64
KEY_HEADS = 8
HEAD_SIZE = 128
SPAN_LENGTH = 256
EPS = 1e-05
NEGATIVE_LARGE = -1e30
GROUP = QUERY_HEADS // KEY_HEADS
KEY_COLUMNS = KEY_HEADS * HEAD_SIZE
BF16 = jnp.bfloat16
F32 = jnp.float32
VMEM = pl.BlockSpec(memory_space=pltpu.VMEM)
HBM = pl.BlockSpec(memory_space=pltpu.HBM)
SMEM = pl.BlockSpec(memory_space=pltpu.SMEM)


def peer(index, step, count):
    if count & (count - 1) == 0:
        return index ^ step
    return (index + step) % count


def source(index, step, count):
    if count & (count - 1) == 0:
        return index ^ step
    return (index + count - step) % count


def exchange(value, axis, step):
    count = lax.axis_size(axis)
    return lax.ppermute(value, axis, [(i, peer(i, step, count)) for i in range(count)])


def frequencies():
    base = 500000.0 ** (-(jnp.arange(HEAD_SIZE // 2).astype(F32) * 2.0) / HEAD_SIZE)
    wave = 2.0 * math.pi / base
    smooth = (8192.0 / wave - 1.0) / 3.0
    blended = (1.0 - smooth) * base / 8.0 + smooth * base
    return jnp.where(wave < 2048.0, base, jnp.where(wave > 8192.0, base / 8.0, blended))


def tables(positions):
    angles = positions.astype(F32)[:, None] * frequencies()[None, :]
    cosine, sine = jnp.cos(angles), jnp.sin(angles)
    return jnp.concatenate([cosine, cosine], -1), jnp.concatenate([-sine, sine], -1)


def turn(value, cosine, sine):
    return value * cosine + pltpu.roll(value, HEAD_SIZE // 2, 1) * sine


def diagonal(rows):
    shape = (rows, HEAD_SIZE)
    return lax.broadcasted_iota(jnp.int32, shape, 0) == lax.broadcasted_iota(jnp.int32, shape, 1)


def project_kernel(count, rows, heads, chunks, at_ref, hidden_ref, gain_ref, weight_ref, prompt_ref, *rest):
    own_ref, square_ref, mine_ref = rest[:3]
    sends = rest[3 : 2 + count]
    hidden_buf, gain_buf, weight_buf, total, squares, sems = rest[2 + count :]
    depth = hidden_ref.shape[1]
    size = depth // chunks
    width = weight_ref.shape[1]
    cached = prompt_ref.shape[0]
    gain_copy = pltpu.make_async_copy(gain_ref, gain_buf, sems.at[2 * chunks])
    gain_copy.start()
    columns = pl.ds(pl.multiple_of(at_ref[1] * width, HEAD_SIZE), width)
    prompt_copy = pltpu.make_async_copy(prompt_ref.at[:, columns], mine_ref, sems.at[2 * chunks + 1])
    copies = []
    for c in range(chunks):
        part = pl.ds(c * size, size)
        copies.append(
            (
                pltpu.make_async_copy(hidden_ref.at[:, part], hidden_buf.at[:, part], sems.at[2 * c]),
                pltpu.make_async_copy(weight_ref.at[part, :], weight_buf.at[part, :], sems.at[2 * c + 1]),
            )
        )
        copies[-1][0].start()
        copies[-1][1].start()
    prompt_copy.start()
    gain_copy.wait()
    for c in range(chunks):
        copies[c][0].wait()
        folded, scaled = None, []
        for lane in range(c * size, (c + 1) * size, HEAD_SIZE):
            hidden = hidden_buf[:, lane : lane + HEAD_SIZE].astype(F32)
            tile = lane // HEAD_SIZE
            scaled.append((hidden * gain_buf[tile : tile + 1, :].astype(F32)).astype(BF16))
            square = hidden * hidden
            folded = square if folded is None else folded + square
        copies[c][1].wait()
        part = jnp.dot(
            jnp.concatenate(scaled, axis=1),
            weight_buf[c * size : (c + 1) * size, :],
            preferred_element_type=F32,
        )
        if c == 0:
            total[...] = part
            squares[...] = folded
        else:
            total[...] += part
            squares[...] += folded
    prompt_copy.wait()
    me = at_ref[0]
    for k in range(count):
        to = pl.ds(pl.multiple_of(peer(me, k, count) * rows, rows), rows)
        column = jnp.sum(squares[to, :], axis=1, keepdims=True)
        if k == 0:
            square_ref[...] = jnp.broadcast_to(column, (rows, HEAD_SIZE))
            out = own_ref
        else:
            out = sends[k - 1]
            line = jnp.sum(jnp.where(diagonal(rows), column, 0.0), axis=0, keepdims=True)
            high = line.astype(BF16).astype(F32)
            low = line - high
            which = lax.broadcasted_iota(jnp.int32, (16, HEAD_SIZE), 0)
            tail = jnp.where(which == 0, high, jnp.where(which == 1, low, 0.0))
            out[heads * rows : heads * rows + 16, :] = tail.astype(BF16)
            for h in range(heads):
                first = heads * rows + 16 + h * cached
                out[first : first + cached, :] = mine_ref[:, h * HEAD_SIZE : (h + 1) * HEAD_SIZE]
        for h in range(heads):
            piece = total[to, h * HEAD_SIZE : (h + 1) * HEAD_SIZE]
            out[h * rows : (h + 1) * rows, :] = piece.astype(out.dtype)


def project(at, span_hidden, norm_gain, key_value_weight, prompt_rows, count):
    length, depth = span_hidden.shape
    width = key_value_weight.shape[1]
    rows, heads = length // count, width // HEAD_SIZE
    cached = prompt_rows.shape[0]
    chunks = 4 if depth % (4 * HEAD_SIZE) == 0 else 1
    gain = norm_gain.reshape(-1, HEAD_SIZE)
    outs = [
        jax.ShapeDtypeStruct((heads * rows, HEAD_SIZE), F32),
        jax.ShapeDtypeStruct((rows, HEAD_SIZE), F32),
        jax.ShapeDtypeStruct((cached, width), BF16),
    ] + [jax.ShapeDtypeStruct((heads * (rows + cached) + 16, HEAD_SIZE), BF16)] * (count - 1)
    stay = [pltpu.with_memory_space_constraint(x, pltpu.HBM) for x in (span_hidden, gain, key_value_weight, prompt_rows)]
    return pl.pallas_call(
        functools.partial(project_kernel, count, rows, heads, chunks),
        in_specs=[SMEM, HBM, HBM, HBM, HBM],
        out_shape=outs,
        out_specs=[VMEM] * len(outs),
        scratch_shapes=[
            pltpu.VMEM((length, depth), BF16),
            pltpu.VMEM(gain.shape, BF16),
            pltpu.VMEM((depth, width), BF16),
            pltpu.VMEM((length, width), F32),
            pltpu.VMEM((length, HEAD_SIZE), F32),
            pltpu.SemaphoreType.DMA((2 * chunks + 2,)),
        ],
        compiler_params=pltpu.CompilerParams(vmem_limit_bytes=16 << 20),
        cost_estimate=pl.CostEstimate(
            flops=2 * length * depth * width, bytes_accessed=2 * depth * (length + width), transcendentals=0
        ),
        name="project",
    )(at, *stay)


def combine_kernel(rows, heads, first_ref, own_ref, square_ref, mine_ref, cosine_ref, sine_ref, *rest):
    got, (out_ref, send_ref, prompt_ref) = rest[:-3], rest[-3:]
    cached = mine_ref.shape[0]
    line = jnp.zeros((1, HEAD_SIZE), F32)
    for ref in got:
        tail = ref[heads * rows : heads * rows + 16, :].astype(F32)
        line = line + tail[0:1, :] + tail[1:2, :]
    column = jnp.sum(jnp.where(diagonal(rows), line, 0.0), axis=1, keepdims=True)
    scale = lax.rsqrt((square_ref[...] + column) / MODEL_WIDTH + EPS)
    cosine, sine = cosine_ref[...], sine_ref[...]
    for h in range(heads):
        span = slice(h * rows, (h + 1) * rows)
        lanes = slice(h * HEAD_SIZE, (h + 1) * HEAD_SIZE)
        value = own_ref[span, :]
        for ref in got:
            value = value + ref[span, :].astype(F32)
        value = value * scale
        is_key = first_ref[0] + h < KEY_HEADS
        out = jnp.where(is_key, turn(value, cosine, sine), value).astype(BF16)
        out_ref[:, lanes] = out
        send_ref[:, lanes] = out
        for i, ref in enumerate(got):
            first = heads * rows + 16 + h * cached
            prompt_ref[(i + 1) * cached : (i + 2) * cached, lanes] = ref[first : first + cached, :]
    prompt_ref[:cached, :] = mine_ref[...]


def combine(first, own, square, mine, cosine, sine, got):
    rows = square.shape[0]
    heads = own.shape[0] // rows
    block = jax.ShapeDtypeStruct((rows, heads * HEAD_SIZE), BF16)
    prompt = jax.ShapeDtypeStruct(((1 + len(got)) * mine.shape[0], heads * HEAD_SIZE), BF16)
    return pl.pallas_call(
        functools.partial(combine_kernel, rows, heads),
        in_specs=[SMEM] + [VMEM] * (5 + len(got)),
        out_shape=[block, block, prompt],
        out_specs=[VMEM, VMEM, VMEM],
        compiler_params=pltpu.CompilerParams(vmem_limit_bytes=4 << 20),
        name="combine",
    )(first, own, square, mine, cosine, sine, *got)


def queries_kernel(query_ref, own_ref, cosine_ref, sine_ref, query_out, key_out):
    tokens = cosine_ref.shape[0]
    cosine, sine = cosine_ref[...], sine_ref[...]
    for h in range(KEY_HEADS):
        span = slice(h * HEAD_SIZE, (h + 1) * HEAD_SIZE)
        key_out[:, span] = turn(own_ref[:, span].astype(F32), cosine, sine).astype(BF16)
    factor = HEAD_SIZE**-0.5 * math.log2(math.e)
    cosine, sine = cosine * factor, sine * factor
    for h in range(QUERY_HEADS):
        span = slice(h * HEAD_SIZE, (h + 1) * HEAD_SIZE)
        turned = turn(query_ref[:, span].astype(F32), cosine, sine)
        query_out[h * tokens : (h + 1) * tokens, :] = turned.astype(BF16)


def queries(cont_query, own_rows, cosine, sine):
    tokens = cosine.shape[0]
    return pl.pallas_call(
        queries_kernel,
        in_specs=[VMEM] * 4,
        out_shape=[
            jax.ShapeDtypeStruct((QUERY_HEADS * tokens, HEAD_SIZE), BF16),
            jax.ShapeDtypeStruct((tokens, KEY_COLUMNS), BF16),
        ],
        out_specs=[VMEM, VMEM],
        compiler_params=pltpu.CompilerParams(vmem_limit_bytes=8 << 20),
        cost_estimate=pl.CostEstimate(flops=8 * cont_query.size, bytes_accessed=4 * cont_query.size, transcendentals=0),
        name="queries",
    )(cont_query, own_rows, cosine, sine)


def attend_kernel(sets, count, plan, tile, first, last, spots_ref, query_ref, *rest):
    operands = 1 + max(piece[0] for piece in plan)
    pieces, rest = rest[:operands], rest[operands:]
    if first:
        key_ref, own_ref, state_out, mixed_out, cache = rest
    elif last:
        state_ref, mixed_ref, out_ref, cache = rest
    else:
        state_ref, mixed_ref, state_out, mixed_out, cache = rest
    my_set, my_seq, offset, length = (spots_ref[i] for i in range(4))
    width = cache.shape[2]
    heads = width // HEAD_SIZE
    block = query_ref.shape[0] // KEY_HEADS
    tokens = block // GROUP
    total_rows = cache.shape[1]
    for operand, start, rows, step, place in plan:
        if isinstance(place, tuple):
            place = pl.multiple_of(source(my_seq, place[0], count) * rows, rows)
        cache[source(my_set, step, sets), pl.ds(place, rows), :] = pieces[operand][start : start + rows, :]
    if first:
        prompt_rows = total_rows - tokens
        for s in range(sets):
            mine = key_ref if s * width < KEY_COLUMNS else own_ref
            cache[s, prompt_rows:, :] = mine[:, s * width : (s + 1) * width]
        place = lax.broadcasted_iota(jnp.int32, (total_rows, tokens), 0)
        token = lax.broadcasted_iota(jnp.int32, (total_rows, tokens), 1)
        live = (place < offset) & (place < prompt_rows) | (place >= prompt_rows) & (place - prompt_rows <= token)
        bias = jnp.concatenate([jnp.where(live, 0.0, NEGATIVE_LARGE)] * (tile // tokens), axis=1)
    if last:
        keep = lax.broadcasted_iota(jnp.int32, (tokens, HEAD_SIZE), 0) < length
    units = [(g, start) for g in range(KEY_HEADS) for start in range(0, block, tile)]
    scored, weighed, mixtures = {}, {}, {}

    def score(unit):
        g, start = unit
        lane = (g % heads) * HEAD_SIZE
        key = cache[g // heads, :, lane : lane + HEAD_SIZE]
        query = query_ref[g * block + start : g * block + start + tile, :]
        scores = lax.dot_general(key, query, (((1,), (1,)), ((), ())), preferred_element_type=F32)
        scored[unit] = scores + bias if first else scores

    def weigh(unit):
        g, start = unit
        scores = scored.pop(unit)
        top, shrink = jnp.max(scores, axis=0, keepdims=True), None
        if not first:
            old = state_ref[g, 0:1, start : start + tile]
            top = jnp.maximum(old, top)
            shrink = jnp.exp2(old - top)
        weights = jnp.exp2(scores - top)
        total = jnp.sum(weights, axis=0, keepdims=True)
        if not first:
            total = total + state_ref[g, 1:2, start : start + tile] * shrink
        weighed[unit] = top, shrink, total
        lane = (g % heads) * HEAD_SIZE
        value = cache[sets // 2 + g // heads, :, lane : lane + HEAD_SIZE]
        mixtures[unit] = lax.dot_general(
            value, weights.astype(BF16), (((0,), (0,)), ((), ())), preferred_element_type=F32
        )

    def finish(unit):
        g, start = unit
        top, shrink, total = weighed.pop(unit)
        mixed = mixtures.pop(unit)
        if not first:
            mixed = mixed + mixed_ref[g, :, start : start + tile] * shrink
        if last:
            mixed = (mixed * (1.0 / total)).astype(BF16).T
            for j in range(tile // tokens):
                column = (g * GROUP + start // tokens + j) * HEAD_SIZE
                piece = mixed[j * tokens : (j + 1) * tokens, :]
                out_ref[:, column : column + HEAD_SIZE] = jnp.where(keep, piece, jnp.zeros_like(piece))
        else:
            state_out[g, 0:1, start : start + tile] = top
            state_out[g, 1:2, start : start + tile] = total
            mixed_out[g, :, start : start + tile] = mixed

    for i in range(len(units) + 2):
        if i < len(units):
            score(units[i])
        if 0 <= i - 1 < len(units):
            weigh(units[i - 1])
        if 0 <= i - 2 < len(units):
            finish(units[i - 2])


def attend(spots, query, sets, count, plan, pieces, own=(), state=(), last=False):
    first = not state
    width = pieces[0].shape[1]
    block = query.shape[0] // KEY_HEADS
    tokens = block // GROUP
    per_set = {}
    for _, _, rows, step, _ in plan:
        per_set[step] = per_set.get(step, 0) + rows
    total_rows = per_set[0] + (tokens if first else 0)
    tile = block if first else block // 2
    operands = [spots, query] + list(pieces) + list(own) + list(state)
    if last:
        out_shape = jax.ShapeDtypeStruct((tokens, QUERY_HEADS * HEAD_SIZE), BF16)
        out_specs = VMEM
    else:
        out_shape = [
            jax.ShapeDtypeStruct((KEY_HEADS, 8, block), F32),
            jax.ShapeDtypeStruct((KEY_HEADS, HEAD_SIZE, block), F32),
        ]
        out_specs = [VMEM, VMEM]
    name = "attend_own" if first else "attend_last" if last else "attend_more"
    return pl.pallas_call(
        functools.partial(attend_kernel, sets, count, plan, tile, first, last),
        in_specs=[SMEM] + [VMEM] * (len(operands) - 1),
        out_shape=out_shape,
        out_specs=out_specs,
        scratch_shapes=[pltpu.VMEM((sets, total_rows, width), BF16)],
        compiler_params=pltpu.CompilerParams(vmem_limit_bytes=16 << 20),
        name=name,
    )(*operands)


def on_device(
    span_hidden,
    norm_gain,
    key_value_weight,
    prompt_key_value,
    span_offset,
    cont_query,
    continuation_key_value,
    cont_lengths,
):
    offset = span_offset[0]
    sets, count = lax.axis_size("set"), lax.axis_size("seq")
    my_set, my_seq = lax.axis_index("set"), lax.axis_index("seq")
    width = key_value_weight.shape[1]
    rows = span_hidden.shape[0] // count
    tokens = cont_query.shape[1]
    low = 2 if sets % 2 == 0 else 1

    at = jnp.stack([my_seq, my_set]).astype(jnp.int32)
    own, square, mine, *sends = project(at, span_hidden, norm_gain, key_value_weight, prompt_key_value, count)
    order = list(range(count - 1, 0, -1))
    got = [exchange(sends[k - 1], "seq", k) for k in order]

    span_cosine, span_sine = tables(offset + my_seq * rows + jnp.arange(rows, dtype=jnp.int32))
    self_cosine, self_sine = tables(offset + SPAN_LENGTH + jnp.arange(tokens, dtype=jnp.int32))
    query, key = queries(cont_query[0], continuation_key_value[0], self_cosine, self_sine)
    query, key, span_cosine = lax.optimization_barrier((query, key, span_cosine))

    first = (my_set * (width // HEAD_SIZE))[None].astype(jnp.int32)
    block, send, prompt = combine(first, own, square, mine, span_cosine, span_sine, got)

    far = list(range(low, sets, low))
    steps = [0] + far
    beside = [exchange(send, "set", step) for step in far]
    across = [exchange(send, "seq", k) for k in order[:-1]]
    nearest = exchange(jnp.concatenate([send] + beside, axis=0), "seq", order[-1])
    prompt, _ = lax.optimization_barrier((prompt, beside))
    prompts = [prompt] + [exchange(prompt, "set", step) for step in far]
    stretches = [[send] + beside]
    for value in across:
        stretches.append([value] + [exchange(value, "set", step) for step in far])

    def gather(plan, pieces, stretch, places):
        length = stretch[0].shape[0]
        rows = length // len(places)
        for step, value in zip(steps, stretch):
            for i, place in enumerate(places):
                plan.append((len(pieces), i * rows, rows, step, place))
            pieces.append(value)
        if low == 2:
            for n, step in enumerate(steps):
                for i, place in enumerate(places):
                    plan.append((len(pieces), n * length + i * rows, rows, step ^ 1, place))
            pieces.append(exchange(jnp.concatenate(stretch, axis=0), "set", 1))

    spots = jnp.stack([my_set.astype(jnp.int32), my_seq.astype(jnp.int32), offset, cont_lengths[0]])
    plan, pieces = [], []
    gather(plan, pieces, prompts, [(k,) for k in [0] + order])
    state = attend(spots, query, sets, count, plan, pieces, own=(key, continuation_key_value[0]))

    split = max(1, count // 2)
    plan, pieces = [], []
    for i, stretch in enumerate(stretches[:split]):
        gather(plan, pieces, stretch, [i * rows])
    state = attend(spots, query, sets, count, plan, pieces, state=state)

    plan, pieces = [], []
    for i, stretch in enumerate(stretches[split:]):
        gather(plan, pieces, stretch, [i * rows])
    place = (count - 1 - split) * rows
    for n, step in enumerate(steps):
        plan.append((len(pieces), n * rows, rows, step, place))
    pieces.append(nearest)
    if low == 2:
        for n, step in enumerate(steps):
            plan.append((len(pieces), n * rows, rows, step ^ 1, place))
        pieces.append(exchange(nearest, "set", 1))
    attended = attend(spots, query, sets, count, plan, pieces, state=state, last=True)
    return block, attended[None]


def solution(mesh):
    placed = (
        P("parts", "seq"),
        P("seq"),
        P("seq", "set"),
        P(("parts", "seq"), None),
        P("parts"),
        P(("parts", "set", "seq"), None, None),
        P(("parts", "set", "seq"), None, None),
        P(("parts", "set", "seq")),
    )
    return jax.shard_map(
        on_device,
        mesh=mesh,
        in_specs=placed,
        out_specs=(P(("parts", "seq"), "set"), P(("parts", "set", "seq"), None, None)),
        check_vma=False,
    )
```

time: 51.1 us -> 42.1 us (0.82)
  Pallas kernels: 14.9 us -> 10.9 us
  starting transfers between devices: 19.9 us -> 16.1 us
  local copies, waits for them, and re-layouts: 3.68 us -> 0.02 us
  waiting for transfers between devices: 8.64 us -> 12.1 us
  other arithmetic: 1.47 us -> 0.77 us
    pallas_call x3, Pallas kernels: 11.7 us -> 6.22 us  [attend(): pl.pallas_call(functools.partial(attend_kernel, sets, count, plan, tile,...]
    ppermute x18 -> x15, starting transfers between devices: 19.9 us -> 16.1 us  [exchange(): lax.ppermute(value, axis, [(i, peer(i, step, count)) for i in range(count)])]
    unnamed x14 -> x5, local copies, waits for them, and re-layouts: 3.55 us -> 0.01 us
    ppermute x18 -> x15, waiting for transfers between devices: 8.64 us -> 12.1 us  [exchange(): lax.ppermute(value, axis, [(i, peer(i, step, count)) for i in range(count)])]
    pallas_call x1, Pallas kernels: 1.76 us -> 3.17 us  [project(): pl.pallas_call(functools.partial(project_kernel, count, rows, heads, chun...]
    concatenate x4, other arithmetic: 0.89 us -> 0.11 us  [the longest x1 0.08 us: tables(): jnp.concatenate([-sine, sine], -1)]
  transfers between devices with their start and end apart: 18 -> 15, of which waited for: 4 -> 6; matrix products, arithmetic and copies ran while one was open for 3% -> 2% of each run, Pallas kernels for 3% -> 10%
where the time goes in v3:
time: 42.1 us; the launch traced here: 42 us
  starting transfers between devices  16.1 us (38%)
  waiting for transfers between devices  12.1 us (29%)
  Pallas kernels  10.9 us (26%)
  between operations  2.13 us (5%)
  other arithmetic  0.77 us (2%)
    ppermute x15, starting transfers between devices, exchange(): lax.ppermute(value, axis, [(i, peer(i, step, count)) for i in range(count)])  16.1 us
    ppermute x15, waiting for transfers between devices, exchange(): lax.ppermute(value, axis, [(i, peer(i, step, count)) for i in range(count)])  12.1 us
    pallas_call x3, Pallas kernels, attend(): pl.pallas_call(functools.partial(attend_kernel, sets, count, plan, tile,...  6.22 us
    pallas_call x1, Pallas kernels, project(): pl.pallas_call(functools.partial(project_kernel, count, rows, heads, chun...  3.17 us
  transfers between devices with their start and end apart: 15, of which 6 were waited for; matrix products, arithmetic and copies ran while one was open for 2% of the time, Pallas kernels for 10%

profile of v3, /device:TPU:0, one launch (start us, length us, event | category | flops | bytes accessed | tf_op | source)
XLA Modules:
  0.0 42.0 jit_solution(10539800848708382546)
XLA Ops:
  0.7 0.1 pad_add_fusion.at_ref
  0.7 3.2 %project.1 = (f32[256,128]{1,0:T(8,128)S(1)}, f32[64,128]{1,0:T(8,128)S(1)}, bf16[32,512]{1,0:T(8,128)(2,1)S(1)}, bf16[400,128]{1,0:T(8,128)(2,1)S(1)}, bf16[400...) custom-call(s32[2]{0:T(128)S(1)} %pad_add_fusion.at_ref, bf16[256,2048]{1,0:T(8,128)(2,1)} %hidden_ref.1, ...), custom_call_target="tpu_custom_call" | custom-call | flops 536870912 | bytes 3145728 | tf_op jit(solution)/shard_map/project/pallas_call | solution.py:150
  3.9 5.1 %collective-permute-start = (bf16[400,128]{1,0:T(8,128)(2,1)S(1)}, bf16[400,128]{1,0:T(8,128)(2,1)S(1)}, u32[]{:S(2)}, u32[]{:S(2)}) collective-permute-start(bf16[400,128]{1,0:T(8,128)(2,1)S(1)} %get-tuple-element.27), channel_id=1, source_target_pairs={{0,3},{1,2},{2,1},{3,0},{4,7},{5,6},{6,5},{7,4},{8,11},{9,10},{10,... | collective-permute-start | bytes 307208 | tf_op jit(solution)/shard_map/ppermute | solution.py:41
  9.0 0.0 collective-permute-start.1
  9.0 0.6 %collective-permute-start.2 = (bf16[400,128]{1,0:T(8,128)(2,1)S(1)}, bf16[400,128]{1,0:T(8,128)(2,1)S(1)}, u32[]{:S(2)}, u32[]{:S(2)}) collective-permute-start(bf16[400,128]{1,0:T(8,128)(2,1)S(1)} %get-tuple-element.29), channel_id=1, source_target_pairs={{0,1},{1,0},{2,3},{3,2},{4,5},{5,4},{6,7},{7,6},{8,9},{9,8},{10,11... | collective-permute-start | bytes 307208 | tf_op jit(solution)/shard_map/ppermute | solution.py:41
  10.4 0.3 fusion.1
  10.7 0.1 pad_maximum_fusion.5.cosine_ref
  10.8 0.1 pad_maximum_fusion.3
  10.9 0.7 %queries.1 = (bf16[4096,128]{1,0:T(8,128)(2,1)S(1)}, bf16[64,1024]{1,0:T(8,128)(2,1)S(1)}) custom-call(bf16[64,8192]{1,0:T(8,128)(2,1)S(1)} %bitcast.10, bf16[64,2048]{1,0:T(8,128)(2,1)S(1)} %bitcast.11, f32[64,128]{1,0:T(8,128)S(1)} %get-tuple-element.49.cosine_ref, f32[64,128]{1,0:T(8,128)S(1)} %get-tuple-element.50.sine_ref), custom_call_target="tpu_custom_call" | custom-call | flops 4194304 | bytes 2097152 | tf_op jit(solution)/shard_map/queries/pallas_call | solution.py:229
  11.5 0.1 pad_maximum_fusion.6.sine_ref
  11.6 1.2 %collective-permute-done.rest_0_ = bf16[400,128]{1,0:T(8,128)(2,1)S(1)} collective-permute-done((bf16[400,128]{1,0:T(8,128)(2,1)S(1)}, bf16[400,128]{1,0:T(8,128)(2,1)S(1)}, u32[]{:S(2)}, u32[]{:S(2)}) %collective-permute-start) | collective-permute-done | bytes 102432 | tf_op jit(solution)/shard_map/ppermute | solution.py:41
  12.8 4.8 %collective-permute-done.1.rest_1_ = bf16[400,128]{1,0:T(8,128)(2,1)S(1)} collective-permute-done((bf16[400,128]{1,0:T(8,128)(2,1)S(1)}, bf16[400,128]{1,0:T(8,128)(2,1)S(1)}, u32[]{:S(2)}, u32[]{:S(2)}) %collective-permute-start.1) | collective-permute-done | bytes 102432 | tf_op jit(solution)/shard_map/ppermute | solution.py:41
  17.6 0.8 %combine.1 = (bf16[64,512]{1,0:T(8,128)(2,1)}, bf16[64,512]{1,0:T(8,128)(2,1)S(1)}, bf16[128,512]{1,0:T(8,128)(2,1)S(1)}) custom-call(s32[1]{0:T(128)} %bitcast.first_ref, f32[256,128]{1,0:T(8,128)S(1)} %get-tuple-element.21.own_ref, f32[64,128]{1,0:T(8,128)S(1)} %get-tuple-element.22.square_ref, bf16[32,512]{1,0:T(8,128)(2,1)S(1)} %get-tuple-element.23.mine_ref, ...), custom_call_target="tpu_custom_call" | custom-call | tf_op jit(solution)/shard_map/combine/pallas_call | solution.py:203
  18.5 1.5 %collective-permute-start.6 = (bf16[64,512]{1,0:T(8,128)(2,1)S(1)}, bf16[64,512]{1,0:T(8,128)(2,1)S(1)}, u32[]{:S(2)}, u32[]{:S(2)}) collective-permute-start(bf16[64,512]{1,0:T(8,128)(2,1)S(1)} %get-tuple-element.32.rest_0_), channel_id=1, source_target_pairs={{0,8},{4,12},{8,0},{12,4},{1,9},{5,13},{9,1},{13,5},{2,10},{6,14},... | collective-permute-start | bytes 196616 | tf_op jit(solution)/shard_map/ppermute | solution.py:41
  20.0 2.5 %collective-permute-start.10 = (bf16[64,512]{1,0:T(8,128)(2,1)S(1)}, bf16[64,512]{1,0:T(8,128)(2,1)S(1)}, u32[]{:S(2)}, u32[]{:S(2)}) collective-permute-start(bf16[64,512]{1,0:T(8,128)(2,1)S(1)} %get-tuple-element.32.rest_0_), channel_id=1, source_target_pairs={{0,3},{1,2},{2,1},{3,0},{4,7},{5,6},{6,5},{7,4},{8,11},{9,10},{10,... | collective-permute-start | bytes 196616 | tf_op jit(solution)/shard_map/ppermute | solution.py:41
  22.4 0.3 collective-permute-done.6.rest_1_
  22.7 1.5 %collective-permute-start.13 = (bf16[128,512]{1,0:T(8,128)(2,1)S(1)}, bf16[128,512]{1,0:T(8,128)(2,1)S(1)}, u32[]{:S(2)}, u32[]{:S(2)}) collective-permute-start(bf16[128,512]{1,0:T(8,128)(2,1)S(1)} %get-tuple-element.34.rest_0_), channel_id=1, source_target_pairs={{0,8},{4,12},{8,0},{12,4},{1,9},{5,13},{9,1},{13,5},{2,10},{6,14},... | collective-permute-start | bytes 393224 | tf_op jit(solution)/shard_map/ppermute | solution.py:41
  24.2 0.9 %collective-permute-start.3 = (bf16[64,512]{1,0:T(8,128)(2,1)S(1)}, bf16[64,512]{1,0:T(8,128)(2,1)S(1)}, u32[]{:S(2)}, u32[]{:S(2)}) collective-permute-start(bf16[64,512]{1,0:T(8,128)(2,1)S(1)} %get-tuple-element.32.rest_0_), channel_id=1, source_target_pairs={{0,2},{1,3},{2,0},{3,1},{4,6},{5,7},{6,4},{7,5},{8,10},{9,11},{10,... | collective-permute-start | bytes 196616 | tf_op jit(solution)/shard_map/ppermute | solution.py:41
  25.2 2.2 %collective-permute-start.7 = (bf16[128,512]{1,0:T(8,128)(2,1)S(1)}, bf16[128,512]{1,0:T(8,128)(2,1)S(1)}, u32[]{:S(2)}, u32[]{:S(2)}) collective-permute-start(bf16[128,512]{1,0:T(8,128)(2,1)S(1)} %constant_dynamic-update-slice_fusion), channel_id=1, source_target_pairs={{0,1},{1,0},{2,3},{3,2},{4,5},{5,4},{6,7},{7,6},{8,9},{9,8},{10,11... | collective-permute-start | bytes 393224 | tf_op jit(solution)/shard_map/ppermute | solution.py:41
  27.4 0.5 %collective-permute-start.11 = (bf16[64,512]{1,0:T(8,128)(2,1)S(1)}, bf16[64,512]{1,0:T(8,128)(2,1)S(1)}, u32[]{:S(2)}, u32[]{:S(2)}) collective-permute-start(bf16[64,512]{1,0:T(8,128)(2,1)S(1)} %collective-permute-done.10.rest_3_), channel_id=1, source_target_pairs={{0,8},{4,12},{8,0},{12,4},{1,9},{5,13},{9,1},{13,5},{2,10},{6,14},... | collective-permute-start | bytes 196616 | tf_op jit(solution)/shard_map/ppermute | solution.py:41
  27.9 2.2 %collective-permute-done.3.rest_0_ = bf16[64,512]{1,0:T(8,128)(2,1)S(1)} collective-permute-done((bf16[64,512]{1,0:T(8,128)(2,1)S(1)}, bf16[64,512]{1,0:T(8,128)(2,1)S(1)}, u32[]{:S(2)}, u32[]{:S(2)}) %collective-permute-start.3) | collective-permute-done | bytes 65568 | tf_op jit(solution)/shard_map/ppermute | solution.py:41
  30.1 0.5 %collective-permute-start.4 = (bf16[64,512]{1,0:T(8,128)(2,1)S(1)}, bf16[64,512]{1,0:T(8,128)(2,1)S(1)}, u32[]{:S(2)}, u32[]{:S(2)}) collective-permute-start(bf16[64,512]{1,0:T(8,128)(2,1)S(1)} %collective-permute-done.3.rest_0_), channel_id=1, source_target_pairs={{0,8},{4,12},{8,0},{12,4},{1,9},{5,13},{9,1},{13,5},{2,10},{6,14},... | collective-permute-start | bytes 196616 | tf_op jit(solution)/shard_map/ppermute | solution.py:41
  30.7 0.1 collective-permute-start.14
  30.7 1.5 %collective-permute-done.11.rest_4_ = bf16[64,512]{1,0:T(8,128)(2,1)S(1)} collective-permute-done((bf16[64,512]{1,0:T(8,128)(2,1)S(1)}, bf16[64,512]{1,0:T(8,128)(2,1)S(1)}, u32[]{:S(2)}, u32[]{:S(2)}) %collective-permute-start.11) | collective-permute-done | bytes 65568 | tf_op jit(solution)/shard_map/ppermute | solution.py:41
  32.2 0.1 collective-permute-start.12
  32.3 2.0 %collective-permute-done.4.rest_1_ = bf16[64,512]{1,0:T(8,128)(2,1)S(1)} collective-permute-done((bf16[64,512]{1,0:T(8,128)(2,1)S(1)}, bf16[64,512]{1,0:T(8,128)(2,1)S(1)}, u32[]{:S(2)}, u32[]{:S(2)}) %collective-permute-start.4) | collective-permute-done | bytes 65568 | tf_op jit(solution)/shard_map/ppermute | solution.py:41
  34.4 0.1 collective-permute-start.5
  34.5 0.5 %collective-permute-start.8 = (bf16[128,512]{1,0:T(8,128)(2,1)S(1)}, bf16[128,512]{1,0:T(8,128)(2,1)S(1)}, u32[]{:S(2)}, u32[]{:S(2)}) collective-permute-start(bf16[128,512]{1,0:T(8,128)(2,1)S(1)} %collective-permute-done.7.rest_3_), channel_id=1, source_target_pairs={{0,4},{4,0},{8,12},{12,8},{1,5},{5,1},{9,13},{13,9},{2,6},{6,2},{1... | collective-permute-start | bytes 393224 | tf_op jit(solution)/shard_map/ppermute | solution.py:41
  35.6 0.1 pad_add_fusion.1.spots_ref
  35.7 2.1 %attend_own.1 = (f32[8,8,512]{2,1,0:T(8,128)S(1)}, f32[8,128,512]{2,1,0:T(8,128)S(1)}) custom-call(s32[4]{0:T(128)S(1)} %pad_add_fusion.1.spots_ref, bf16[4096,128]{1,0:T(8,128)(2,1)S(1)} %get-tuple-element.31.query_ref, bf16[128,512]{1,0:T(8,128)(2,1)S(1)} %get-tuple-element.34.rest_0_, bf16[128,512]{1,0:T(8,128)(2,1)S(1)} %collective-permute-done.13.rest_1_, ...), custom_call_target="tpu_custom_call" | custom-call | tf_op jit(solution)/shard_map/attend_own/pallas_call | solution.py:350
  37.8 1.5 %attend_more.1 = (f32[8,8,512]{2,1,0:T(8,128)S(1)}, f32[8,128,512]{2,1,0:T(8,128)S(1)}) custom-call(s32[4]{0:T(128)S(1)} %pad_add_fusion.1.spots_ref, bf16[4096,128]{1,0:T(8,128)(2,1)S(1)} %get-tuple-element.31.query_ref, bf16[64,512]{1,0:T(8,128)(2,1)S(1)} %get-tuple-element.32.rest_0_, bf16[64,512]{1,0:T(8,128)(2,1)S(1)} %collective-permute-done.6.rest_1_, ...), custom_call_target="tpu_custom_call" | custom-call | tf_op jit(solution)/shard_map/attend_more/pallas_call | solution.py:350
  39.3 2.7 %attend_last.1 = bf16[64,8192]{1,0:T(8,128)(2,1)} custom-call(s32[4]{0:T(128)S(1)} %pad_add_fusion.1.spots_ref, bf16[4096,128]{1,0:T(8,128)(2,1)S(1)} %get-tuple-element.31.query_ref, bf16[64,512]{1,0:T(8,128)(2,1)S(1)} %collective-permute-done.3.rest_0_, bf16[64,512]{1,0:T(8,128)(2,1)S(1)} %collective-permute-done.4.rest_1_, ...), custom_call_target="tpu_custom_call" | custom-call | tf_op jit(solution)/shard_map/attend_last/pallas_call | solution.py:350
  (22 shorter events, 0.1 us)
Async XLA Ops:
  0.6 10.2 %copy-start.1 = (bf16[1,64,2048]{2,1,0:T(8,128)(2,1)S(1)}, bf16[1,64,2048]{2,1,0:T(8,128)(2,1)}, u32[]{:S(2)}) copy-start(bf16[1,64,2048]{2,1,0:T(8,128)(2,1)} %param.14) | copy-start | bytes 786436
  0.6 10.2 %copy-start = (bf16[1,64,8192]{2,1,0:T(8,128)(2,1)S(1)}, bf16[1,64,8192]{2,1,0:T(8,128)(2,1)}, u32[]{:S(2)}) copy-start(bf16[1,64,8192]{2,1,0:T(8,128)(2,1)} %param.13) | copy-start | bytes 3145732
  3.9 8.9 %collective-permute-start = (bf16[400,128]{1,0:T(8,128)(2,1)S(1)}, bf16[400,128]{1,0:T(8,128)(2,1)S(1)}, u32[]{:S(2)}, u32[]{:S(2)}) collective-permute-start(bf16[400,128]{1,0:T(8,128)(2,1)S(1)} %get-tuple-element.27), channel_id=1, source_target_pairs={{0,3},{1,2},{2,1},{3,0},{4,7},{5,6},{6,5},{7,4},{8,11},{9,10},{10,... | collective-permute-start | bytes 307208 | tf_op jit(solution)/shard_map/ppermute | solution.py:41
  9.0 8.6 %collective-permute-start.1 = (bf16[400,128]{1,0:T(8,128)(2,1)S(1)}, bf16[400,128]{1,0:T(8,128)(2,1)S(1)}, u32[]{:S(2)}, u32[]{:S(2)}) collective-permute-start(bf16[400,128]{1,0:T(8,128)(2,1)S(1)} %get-tuple-element.28), channel_id=1, source_target_pairs={{0,2},{1,3},{2,0},{3,1},{4,6},{5,7},{6,4},{7,5},{8,10},{9,11},{10,... | collective-permute-start | bytes 307208 | tf_op jit(solution)/shard_map/ppermute | solution.py:41
  9.0 8.6 %collective-permute-start.2 = (bf16[400,128]{1,0:T(8,128)(2,1)S(1)}, bf16[400,128]{1,0:T(8,128)(2,1)S(1)}, u32[]{:S(2)}, u32[]{:S(2)}) collective-permute-start(bf16[400,128]{1,0:T(8,128)(2,1)S(1)} %get-tuple-element.29), channel_id=1, source_target_pairs={{0,1},{1,0},{2,3},{3,2},{4,5},{5,4},{6,7},{7,6},{8,9},{9,8},{10,11... | collective-permute-start | bytes 307208 | tf_op jit(solution)/shard_map/ppermute | solution.py:41
  18.5 4.3 %collective-permute-start.6 = (bf16[64,512]{1,0:T(8,128)(2,1)S(1)}, bf16[64,512]{1,0:T(8,128)(2,1)S(1)}, u32[]{:S(2)}, u32[]{:S(2)}) collective-permute-start(bf16[64,512]{1,0:T(8,128)(2,1)S(1)} %get-tuple-element.32.rest_0_), channel_id=1, source_target_pairs={{0,8},{4,12},{8,0},{12,4},{1,9},{5,13},{9,1},{13,5},{2,10},{6,14},... | collective-permute-start | bytes 196616 | tf_op jit(solution)/shard_map/ppermute | solution.py:41
  20.0 7.4 %collective-permute-start.10 = (bf16[64,512]{1,0:T(8,128)(2,1)S(1)}, bf16[64,512]{1,0:T(8,128)(2,1)S(1)}, u32[]{:S(2)}, u32[]{:S(2)}) collective-permute-start(bf16[64,512]{1,0:T(8,128)(2,1)S(1)} %get-tuple-element.32.rest_0_), channel_id=1, source_target_pairs={{0,3},{1,2},{2,1},{3,0},{4,7},{5,6},{6,5},{7,4},{8,11},{9,10},{10,... | collective-permute-start | bytes 196616 | tf_op jit(solution)/shard_map/ppermute | solution.py:41
  22.7 7.9 %collective-permute-start.13 = (bf16[128,512]{1,0:T(8,128)(2,1)S(1)}, bf16[128,512]{1,0:T(8,128)(2,1)S(1)}, u32[]{:S(2)}, u32[]{:S(2)}) collective-permute-start(bf16[128,512]{1,0:T(8,128)(2,1)S(1)} %get-tuple-element.34.rest_0_), channel_id=1, source_target_pairs={{0,8},{4,12},{8,0},{12,4},{1,9},{5,13},{9,1},{13,5},{2,10},{6,14},... | collective-permute-start | bytes 393224 | tf_op jit(solution)/shard_map/ppermute | solution.py:41
  24.2 5.8 %collective-permute-start.3 = (bf16[64,512]{1,0:T(8,128)(2,1)S(1)}, bf16[64,512]{1,0:T(8,128)(2,1)S(1)}, u32[]{:S(2)}, u32[]{:S(2)}) collective-permute-start(bf16[64,512]{1,0:T(8,128)(2,1)S(1)} %get-tuple-element.32.rest_0_), channel_id=1, source_target_pairs={{0,2},{1,3},{2,0},{3,1},{4,6},{5,7},{6,4},{7,5},{8,10},{9,11},{10,... | collective-permute-start | bytes 196616 | tf_op jit(solution)/shard_map/ppermute | solution.py:41
  25.2 12.6 %collective-permute-start.9 = (bf16[128,512]{1,0:T(8,128)(2,1)S(1)}, bf16[128,512]{1,0:T(8,128)(2,1)S(1)}, u32[]{:S(2)}, u32[]{:S(2)}) collective-permute-start(bf16[128,512]{1,0:T(8,128)(2,1)S(1)} %constant_dynamic-update-slice_fusion), channel_id=1, source_target_pairs={{0,4},{4,0},{8,12},{12,8},{1,5},{5,1},{9,13},{13,9},{2,6},{6,2},{1... | collective-permute-start | bytes 393224 | tf_op jit(solution)/shard_map/ppermute | solution.py:41
  25.2 9.3 %collective-permute-start.7 = (bf16[128,512]{1,0:T(8,128)(2,1)S(1)}, bf16[128,512]{1,0:T(8,128)(2,1)S(1)}, u32[]{:S(2)}, u32[]{:S(2)}) collective-permute-start(bf16[128,512]{1,0:T(8,128)(2,1)S(1)} %constant_dynamic-update-slice_fusion), channel_id=1, source_target_pairs={{0,1},{1,0},{2,3},{3,2},{4,5},{5,4},{6,7},{7,6},{8,9},{9,8},{10,11... | collective-permute-start | bytes 393224 | tf_op jit(solution)/shard_map/ppermute | solution.py:41
  27.4 4.9 %collective-permute-start.11 = (bf16[64,512]{1,0:T(8,128)(2,1)S(1)}, bf16[64,512]{1,0:T(8,128)(2,1)S(1)}, u32[]{:S(2)}, u32[]{:S(2)}) collective-permute-start(bf16[64,512]{1,0:T(8,128)(2,1)S(1)} %collective-permute-done.10.rest_3_), channel_id=1, source_target_pairs={{0,8},{4,12},{8,0},{12,4},{1,9},{5,13},{9,1},{13,5},{2,10},{6,14},... | collective-permute-start | bytes 196616 | tf_op jit(solution)/shard_map/ppermute | solution.py:41
  30.1 4.3 %collective-permute-start.4 = (bf16[64,512]{1,0:T(8,128)(2,1)S(1)}, bf16[64,512]{1,0:T(8,128)(2,1)S(1)}, u32[]{:S(2)}, u32[]{:S(2)}) collective-permute-start(bf16[64,512]{1,0:T(8,128)(2,1)S(1)} %collective-permute-done.3.rest_0_), channel_id=1, source_target_pairs={{0,8},{4,12},{8,0},{12,4},{1,9},{5,13},{9,1},{13,5},{2,10},{6,14},... | collective-permute-start | bytes 196616 | tf_op jit(solution)/shard_map/ppermute | solution.py:41
  30.7 5.0 %collective-permute-start.14 = (bf16[256,512]{1,0:T(8,128)(2,1)S(1)}, bf16[256,512]{1,0:T(8,128)(2,1)S(1)}, u32[]{:S(2)}, u32[]{:S(2)}) collective-permute-start(bf16[256,512]{1,0:T(8,128)(2,1)S(1)} %pad_maximum_fusion), channel_id=1, source_target_pairs={{0,4},{4,0},{8,12},{12,8},{1,5},{5,1},{9,13},{13,9},{2,6},{6,2},{1... | collective-permute-start | bytes 786440 | tf_op jit(solution)/shard_map/ppermute | solution.py:41
  32.2 5.5 %collective-permute-start.12 = (bf16[128,512]{1,0:T(8,128)(2,1)S(1)}, bf16[128,512]{1,0:T(8,128)(2,1)S(1)}, u32[]{:S(2)}, u32[]{:S(2)}) collective-permute-start(bf16[128,512]{1,0:T(8,128)(2,1)S(1)} %pad_maximum_fusion.2), channel_id=1, source_target_pairs={{0,4},{4,0},{8,12},{12,8},{1,5},{5,1},{9,13},{13,9},{2,6},{6,2},{1... | collective-permute-start | bytes 393224 | tf_op jit(solution)/shard_map/ppermute | solution.py:41
  34.4 4.9 %collective-permute-start.5 = (bf16[128,512]{1,0:T(8,128)(2,1)S(1)}, bf16[128,512]{1,0:T(8,128)(2,1)S(1)}, u32[]{:S(2)}, u32[]{:S(2)}) collective-permute-start(bf16[128,512]{1,0:T(8,128)(2,1)S(1)} %pad_maximum_fusion.1), channel_id=1, source_target_pairs={{0,4},{4,0},{8,12},{12,8},{1,5},{5,1},{9,13},{13,9},{2,6},{6,2},{1... | collective-permute-start | bytes 393224 | tf_op jit(solution)/shard_map/ppermute | solution.py:41
  34.5 4.8 %collective-permute-start.8 = (bf16[128,512]{1,0:T(8,128)(2,1)S(1)}, bf16[128,512]{1,0:T(8,128)(2,1)S(1)}, u32[]{:S(2)}, u32[]{:S(2)}) collective-permute-start(bf16[128,512]{1,0:T(8,128)(2,1)S(1)} %collective-permute-done.7.rest_3_), channel_id=1, source_target_pairs={{0,4},{4,0},{8,12},{12,8},{1,5},{5,1},{9,13},{13,9},{2,6},{6,2},{1... | collective-permute-start | bytes 393224 | tf_op jit(solution)/shard_map/ppermute | solution.py:41

commit v4 on v3

--- a/solution.py
+++ b/solution.py
@@ -168,9 +168,15 @@
     )(at, *stay)
 
 
-def combine_kernel(rows, heads, first_ref, own_ref, square_ref, mine_ref, cosine_ref, sine_ref, *rest):
-    got, (out_ref, send_ref, prompt_ref) = rest[:-3], rest[-3:]
+def combine_kernel(rows, heads, at_ref, own_ref, square_ref, mine_ref, cosine_ref, sine_ref, *rest):
+    got, (out_ref, send_ref, packed_ref) = rest[:-3], rest[-3:]
     cached = mine_ref.shape[0]
+    count = 1 + len(got)
+    me, first = at_ref[0], at_ref[1] * heads
+
+    def prompt_rows(k):
+        return pl.ds(pl.multiple_of(rows + source(me, k, count) * cached, 16), cached)
+
     line = jnp.zeros((1, HEAD_SIZE), F32)
     for ref in got:
         tail = ref[heads * rows : heads * rows + 16, :].astype(F32)
@@ -185,37 +191,38 @@
         for ref in got:
             value = value + ref[span, :].astype(F32)
         value = value * scale
-        is_key = first_ref[0] + h < KEY_HEADS
-        out = jnp.where(is_key, turn(value, cosine, sine), value).astype(BF16)
+        out = jnp.where(first + h < KEY_HEADS, turn(value, cosine, sine), value).astype(BF16)
         out_ref[:, lanes] = out
         send_ref[:, lanes] = out
+        packed_ref[:rows, lanes] = out
         for i, ref in enumerate(got):
-            first = heads * rows + 16 + h * cached
-            prompt_ref[(i + 1) * cached : (i + 2) * cached, lanes] = ref[first : first + cached, :]
-    prompt_ref[:cached, :] = mine_ref[...]
-
-
-def combine(first, own, square, mine, cosine, sine, got):
+            start = heads * rows + 16 + h * cached
+            packed_ref[prompt_rows(count - 1 - i), lanes] = ref[start : start + cached, :]
+    packed_ref[prompt_rows(0), :] = mine_ref[...]
+
+
+def combine(at, own, square, mine, cosine, sine, got):
     rows = square.shape[0]
     heads = own.shape[0] // rows
     block = jax.ShapeDtypeStruct((rows, heads * HEAD_SIZE), BF16)
-    prompt = jax.ShapeDtypeStruct(((1 + len(got)) * mine.shape[0], heads * HEAD_SIZE), BF16)
+    packed = jax.ShapeDtypeStruct((rows + (1 + len(got)) * mine.shape[0], heads * HEAD_SIZE), BF16)
     return pl.pallas_call(
         functools.partial(combine_kernel, rows, heads),
         in_specs=[SMEM] + [VMEM] * (5 + len(got)),
-        out_shape=[block, block, prompt],
+        out_shape=[block, block, packed],
         out_specs=[VMEM, VMEM, VMEM],
         compiler_params=pltpu.CompilerParams(vmem_limit_bytes=4 << 20),
         name="combine",
-    )(first, own, square, mine, cosine, sine, *got)
-
-
-def queries_kernel(query_ref, own_ref, cosine_ref, sine_ref, query_out, key_out):
+    )(at, own, square, mine, cosine, sine, *got)
+
+
+def queries_kernel(query_ref, own_ref, cosine_ref, sine_ref, query_out, key_out, value_out):
     tokens = cosine_ref.shape[0]
     cosine, sine = cosine_ref[...], sine_ref[...]
     for h in range(KEY_HEADS):
         span = slice(h * HEAD_SIZE, (h + 1) * HEAD_SIZE)
         key_out[:, span] = turn(own_ref[:, span].astype(F32), cosine, sine).astype(BF16)
+    value_out[...] = own_ref[:, KEY_COLUMNS:]
     factor = HEAD_SIZE**-0.5 * math.log2(math.e)
     cosine, sine = cosine * factor, sine * factor
     for h in range(QUERY_HEADS):
@@ -232,51 +239,51 @@
         out_shape=[
             jax.ShapeDtypeStruct((QUERY_HEADS * tokens, HEAD_SIZE), BF16),
             jax.ShapeDtypeStruct((tokens, KEY_COLUMNS), BF16),
+            jax.ShapeDtypeStruct((tokens, KEY_COLUMNS), BF16),
         ],
-        out_specs=[VMEM, VMEM],
+        out_specs=[VMEM, VMEM, VMEM],
         compiler_params=pltpu.CompilerParams(vmem_limit_bytes=8 << 20),
         cost_estimate=pl.CostEstimate(flops=8 * cont_query.size, bytes_accessed=4 * cont_query.size, transcendentals=0),
         name="queries",
     )(cont_query, own_rows, cosine, sine)
 
 
-def attend_kernel(sets, count, plan, tile, first, last, spots_ref, query_ref, *rest):
-    operands = 1 + max(piece[0] for piece in plan)
-    pieces, rest = rest[:operands], rest[operands:]
+def attend_kernel(tile, span_rows, last, spots_ref, query_ref, cache_ref, *rest):
+    first = span_rows is not None
     if first:
-        key_ref, own_ref, state_out, mixed_out, cache = rest
+        key_ref, own_ref, state_out, mixed_out = rest
     elif last:
-        state_ref, mixed_ref, out_ref, cache = rest
+        state_ref, mixed_ref, out_ref = rest
     else:
-        state_ref, mixed_ref, state_out, mixed_out, cache = rest
-    my_set, my_seq, offset, length = (spots_ref[i] for i in range(4))
-    width = cache.shape[2]
+        state_ref, mixed_ref, state_out, mixed_out = rest
+    offset, length = spots_ref[0], spots_ref[1]
+    sets, cached_rows, width = cache_ref.shape
     heads = width // HEAD_SIZE
     block = query_ref.shape[0] // KEY_HEADS
     tokens = block // GROUP
-    total_rows = cache.shape[1]
-    for operand, start, rows, step, place in plan:
-        if isinstance(place, tuple):
-            place = pl.multiple_of(source(my_seq, place[0], count) * rows, rows)
-        cache[source(my_set, step, sets), pl.ds(place, rows), :] = pieces[operand][start : start + rows, :]
+    total_rows = cached_rows + (tokens if first else 0)
     if first:
-        prompt_rows = total_rows - tokens
-        for s in range(sets):
-            mine = key_ref if s * width < KEY_COLUMNS else own_ref
-            cache[s, prompt_rows:, :] = mine[:, s * width : (s + 1) * width]
         place = lax.broadcasted_iota(jnp.int32, (total_rows, tokens), 0)
         token = lax.broadcasted_iota(jnp.int32, (total_rows, tokens), 1)
-        live = (place < offset) & (place < prompt_rows) | (place >= prompt_rows) & (place - prompt_rows <= token)
+        cached = place - span_rows
+        seen = (place < span_rows) | (place < cached_rows) & (cached < offset)
+        live = seen | (place >= cached_rows) & (place - cached_rows <= token)
         bias = jnp.concatenate([jnp.where(live, 0.0, NEGATIVE_LARGE)] * (tile // tokens), axis=1)
     if last:
         keep = lax.broadcasted_iota(jnp.int32, (tokens, HEAD_SIZE), 0) < length
     units = [(g, start) for g in range(KEY_HEADS) for start in range(0, block, tile)]
     scored, weighed, mixtures = {}, {}, {}
 
+    def rows_of(g, at, ref):
+        lane = (g % heads) * HEAD_SIZE
+        rows = cache_ref[at + g // heads, :, lane : lane + HEAD_SIZE]
+        if first:
+            rows = jnp.concatenate([rows, ref[:, g * HEAD_SIZE : (g + 1) * HEAD_SIZE]], axis=0)
+        return rows
+
     def score(unit):
         g, start = unit
-        lane = (g % heads) * HEAD_SIZE
-        key = cache[g // heads, :, lane : lane + HEAD_SIZE]
+        key = rows_of(g, 0, key_ref if first else None)
         query = query_ref[g * block + start : g * block + start + tile, :]
         scores = lax.dot_general(key, query, (((1,), (1,)), ((), ())), preferred_element_type=F32)
         scored[unit] = scores + bias if first else scores
@@ -294,8 +301,7 @@
         if not first:
             total = total + state_ref[g, 1:2, start : start + tile] * shrink
         weighed[unit] = top, shrink, total
-        lane = (g % heads) * HEAD_SIZE
-        value = cache[sets // 2 + g // heads, :, lane : lane + HEAD_SIZE]
+        value = rows_of(g, sets // 2, own_ref if first else None)
         mixtures[unit] = lax.dot_general(
             value, weights.astype(BF16), (((0,), (0,)), ((), ())), preferred_element_type=F32
         )
@@ -326,17 +332,12 @@
             finish(units[i - 2])
 
 
-def attend(spots, query, sets, count, plan, pieces, own=(), state=(), last=False):
+def attend(spots, query, cache, span_rows=None, own=(), state=(), last=False):
     first = not state
-    width = pieces[0].shape[1]
     block = query.shape[0] // KEY_HEADS
     tokens = block // GROUP
-    per_set = {}
-    for _, _, rows, step, _ in plan:
-        per_set[step] = per_set.get(step, 0) + rows
-    total_rows = per_set[0] + (tokens if first else 0)
     tile = block if first else block // 2
-    operands = [spots, query] + list(pieces) + list(own) + list(state)
+    operands = [spots, query, cache] + list(own) + list(state)
     if last:
         out_shape = jax.ShapeDtypeStruct((tokens, QUERY_HEADS * HEAD_SIZE), BF16)
         out_specs = VMEM
@@ -348,11 +349,10 @@
         out_specs = [VMEM, VMEM]
     name = "attend_own" if first else "attend_last" if last else "attend_more"
     return pl.pallas_call(
-        functools.partial(attend_kernel, sets, count, plan, tile, first, last),
+        functools.partial(attend_kernel, tile, span_rows, last),
         in_specs=[SMEM] + [VMEM] * (len(operands) - 1),
         out_shape=out_shape,
         out_specs=out_specs,
-        scratch_shapes=[pltpu.VMEM((sets, total_rows, width), BF16)],
         compiler_params=pltpu.CompilerParams(vmem_limit_bytes=16 << 20),
         name=name,
     )(*operands)
@@ -383,59 +383,38 @@
 
     span_cosine, span_sine = tables(offset + my_seq * rows + jnp.arange(rows, dtype=jnp.int32))
     self_cosine, self_sine = tables(offset + SPAN_LENGTH + jnp.arange(tokens, dtype=jnp.int32))
-    query, key = queries(cont_query[0], continuation_key_value[0], self_cosine, self_sine)
-    query, key, span_cosine = lax.optimization_barrier((query, key, span_cosine))
-
-    first = (my_set * (width // HEAD_SIZE))[None].astype(jnp.int32)
-    block, send, prompt = combine(first, own, square, mine, span_cosine, span_sine, got)
+    query, key, value = queries(cont_query[0], continuation_key_value[0], self_cosine, self_sine)
+    query, key, value, span_cosine = lax.optimization_barrier((query, key, value, span_cosine))
+
+    block, send, packed = combine(at, own, square, mine, span_cosine, span_sine, got)
 
     far = list(range(low, sets, low))
     steps = [0] + far
-    beside = [exchange(send, "set", step) for step in far]
+    beside = [packed] + [exchange(packed, "set", step) for step in far]
     across = [exchange(send, "seq", k) for k in order[:-1]]
-    nearest = exchange(jnp.concatenate([send] + beside, axis=0), "seq", order[-1])
-    prompt, _ = lax.optimization_barrier((prompt, beside))
-    prompts = [prompt] + [exchange(prompt, "set", step) for step in far]
-    stretches = [[send] + beside]
-    for value in across:
-        stretches.append([value] + [exchange(value, "set", step) for step in far])
-
-    def gather(plan, pieces, stretch, places):
-        length = stretch[0].shape[0]
-        rows = length // len(places)
-        for step, value in zip(steps, stretch):
-            for i, place in enumerate(places):
-                plan.append((len(pieces), i * rows, rows, step, place))
-            pieces.append(value)
+    nearest = exchange(jnp.concatenate([send] + [x[:rows] for x in beside[1:]], axis=0), "seq", order[-1])
+    stretches = []
+    for arrived in across:
+        stretches.append([arrived] + [exchange(arrived, "set", step) for step in far])
+    stretches.append([nearest[i * rows : (i + 1) * rows] for i in range(len(steps))])
+
+    def gather(share, after=None):
+        held = [jnp.concatenate([stretch[n] for stretch in share], axis=0) for n in range(len(steps))]
+        if after is not None:
+            held, _ = lax.optimization_barrier((held, after))
+        size = held[0].shape[0]
+        held = list(zip(steps, held))
         if low == 2:
-            for n, step in enumerate(steps):
-                for i, place in enumerate(places):
-                    plan.append((len(pieces), n * length + i * rows, rows, step ^ 1, place))
-            pieces.append(exchange(jnp.concatenate(stretch, axis=0), "set", 1))
-
-    spots = jnp.stack([my_set.astype(jnp.int32), my_seq.astype(jnp.int32), offset, cont_lengths[0]])
-    plan, pieces = [], []
-    gather(plan, pieces, prompts, [(k,) for k in [0] + order])
-    state = attend(spots, query, sets, count, plan, pieces, own=(key, continuation_key_value[0]))
-
-    split = max(1, count // 2)
-    plan, pieces = [], []
-    for i, stretch in enumerate(stretches[:split]):
-        gather(plan, pieces, stretch, [i * rows])
-    state = attend(spots, query, sets, count, plan, pieces, state=state)
-
-    plan, pieces = [], []
-    for i, stretch in enumerate(stretches[split:]):
-        gather(plan, pieces, stretch, [i * rows])
-    place = (count - 1 - split) * rows
-    for n, step in enumerate(steps):
-        plan.append((len(pieces), n * rows, rows, step, place))
-    pieces.append(nearest)
-    if low == 2:
-        for n, step in enumerate(steps):
-            plan.append((len(pieces), n * rows, rows, step ^ 1, place))
-        pieces.append(exchange(nearest, "set", 1))
-    attended = attend(spots, query, sets, count, plan, pieces, state=state, last=True)
+            other = exchange(jnp.concatenate([part for _, part in held], axis=0), "set", 1)
+            held += [(step ^ 1, other[n * size : (n + 1) * size]) for n, step in enumerate(steps)]
+        cache = jnp.zeros((sets, size, width), BF16)
+        for step, part in held:
+            cache = lax.dynamic_update_slice(cache, part[None], (source(my_set, step, sets), 0, 0))
+        return cache
+
+    spots = jnp.stack([offset, cont_lengths[0]])
+    state = attend(spots, query, gather([beside]), span_rows=rows, own=(key, value))
+    attended = attend(spots, query, gather(stretches, state), state=state, last=True)
     return block, attended[None]
 
 

time: 42.1 us -> 41.2 us (0.979)
  starting transfers between devices: 16.1 us -> 13.1 us
  waiting for transfers between devices: 12.1 us -> 13.7 us
    ppermute x15 -> x11, starting transfers between devices: 16.1 us -> 13.1 us  [exchange(): lax.ppermute(value, axis, [(i, peer(i, step, count)) for i in range(count)])]
    ppermute x15 -> x11, waiting for transfers between devices: 12.1 us -> 13.7 us  [exchange(): lax.ppermute(value, axis, [(i, peer(i, step, count)) for i in range(count)])]
    pallas_call x3 -> x2, Pallas kernels: 6.22 us -> 5.66 us  [attend(): pl.pallas_call(functools.partial(attend_kernel, tile, span_rows, last), i...]
    pallas_call x1, Pallas kernels: 0.84 us -> 1.38 us  [combine(): pl.pallas_call(functools.partial(combine_kernel, rows, heads), in_specs=[...]
  transfers between devices with their start and end apart: 15 -> 11, of which waited for: 6 -> 5; matrix products, arithmetic and copies ran while one was open for 2% -> 2% of each run, Pallas kernels for 10% -> 2%
where the time goes in v4:
time: 41.2 us; the launch traced here: 41 us
  waiting for transfers between devices  13.7 us (33%)
  starting transfers between devices  13.1 us (32%)
  Pallas kernels  10.9 us (26%)
  between operations  2.21 us (5%)
  other arithmetic  0.83 us (2%)
    ppermute x11, waiting for transfers between devices, exchange(): lax.ppermute(value, axis, [(i, peer(i, step, count)) for i in range(count)])  13.7 us
    ppermute x11, starting transfers between devices, exchange(): lax.ppermute(value, axis, [(i, peer(i, step, count)) for i in range(count)])  13.1 us
    pallas_call x2, Pallas kernels, attend(): pl.pallas_call(functools.partial(attend_kernel, tile, span_rows, last), i...  5.66 us
    pallas_call x1, Pallas kernels, project(): pl.pallas_call(functools.partial(project_kernel, count, rows, heads, chun...  3.17 us
    pallas_call x1, Pallas kernels, combine(): pl.pallas_call(functools.partial(combine_kernel, rows, heads), in_specs=[...  1.38 us
  transfers between devices with their start and end apart: 11, of which 5 were waited for; matrix products, arithmetic and copies ran while one was open for 2% of the time, Pallas kernels for 2%

profile of v4, /device:TPU:0, one launch (start us, length us, event | category | flops | bytes accessed | tf_op | source)
XLA Modules:
  0.0 41.0 jit_solution(2711383278335968917)
XLA Ops:
  0.7 0.1 pad_add_fusion.at_ref
  0.7 3.2 %project.1 = (f32[256,128]{1,0:T(8,128)S(1)}, f32[64,128]{1,0:T(8,128)S(1)}, bf16[32,512]{1,0:T(8,128)(2,1)S(1)}, bf16[400,128]{1,0:T(8,128)(2,1)S(1)}, bf16[400...) custom-call(s32[2]{0:T(128)S(1)} %pad_add_fusion.at_ref, bf16[256,2048]{1,0:T(8,128)(2,1)} %hidden_ref.1, ...), custom_call_target="tpu_custom_call" | custom-call | flops 536870912 | bytes 3145728 | tf_op jit(solution)/shard_map/project/pallas_call | solution.py:150
  3.9 5.1 %collective-permute-start = (bf16[400,128]{1,0:T(8,128)(2,1)S(1)}, bf16[400,128]{1,0:T(8,128)(2,1)S(1)}, u32[]{:S(2)}, u32[]{:S(2)}) collective-permute-start(bf16[400,128]{1,0:T(8,128)(2,1)S(1)} %get-tuple-element.29), channel_id=1, source_target_pairs={{0,3},{1,2},{2,1},{3,0},{4,7},{5,6},{6,5},{7,4},{8,11},{9,10},{10,... | collective-permute-start | bytes 307208 | tf_op jit(solution)/shard_map/ppermute | solution.py:41
  9.0 0.0 collective-permute-start.1
  9.0 0.6 %collective-permute-start.2 = (bf16[400,128]{1,0:T(8,128)(2,1)S(1)}, bf16[400,128]{1,0:T(8,128)(2,1)S(1)}, u32[]{:S(2)}, u32[]{:S(2)}) collective-permute-start(bf16[400,128]{1,0:T(8,128)(2,1)S(1)} %get-tuple-element.31), channel_id=1, source_target_pairs={{0,1},{1,0},{2,3},{3,2},{4,5},{5,4},{6,7},{7,6},{8,9},{9,8},{10,11... | collective-permute-start | bytes 307208 | tf_op jit(solution)/shard_map/ppermute | solution.py:41
  11.0 0.3 fusion.5
  11.3 0.1 pad_maximum_fusion.7.cosine_ref
  11.4 0.1 pad_maximum_fusion.5
  11.5 0.7 %queries.1 = (bf16[4096,128]{1,0:T(8,128)(2,1)S(1)}, bf16[64,1024]{1,0:T(8,128)(2,1)S(1)}, bf16[64,1024]{1,0:T(8,128)(2,1)S(1)}) custom-call(bf16[64,8192]{1,0:T(8,128)(2,1)S(1)} %bitcast.33, bf16[64,2048]{1,0:T(8,128)(2,1)S(1)} %bitcast.34, f32[64,128]{1,0:T(8,128)S(1)} %get-tuple-element.53.cosine_ref, f32[64,128]{1,0:T(8,128)S(1)} %get-tuple-element.54.sine_ref), custom_call_target="tpu_custom_call" | custom-call | flops 4194304 | bytes 2097152 | tf_op jit(solution)/shard_map/queries/pallas_call | solution.py:236
  12.2 0.1 pad_maximum_fusion.8.sine_ref
  12.3 0.1 pad_add_fusion.1.spots_ref
  12.4 0.5 %collective-permute-done.rest_0_ = bf16[400,128]{1,0:T(8,128)(2,1)S(1)} collective-permute-done((bf16[400,128]{1,0:T(8,128)(2,1)S(1)}, bf16[400,128]{1,0:T(8,128)(2,1)S(1)}, u32[]{:S(2)}, u32[]{:S(2)}) %collective-permute-start) | collective-permute-done | bytes 102432 | tf_op jit(solution)/shard_map/ppermute | solution.py:41
  12.8 4.8 %collective-permute-done.1.rest_1_ = bf16[400,128]{1,0:T(8,128)(2,1)S(1)} collective-permute-done((bf16[400,128]{1,0:T(8,128)(2,1)S(1)}, bf16[400,128]{1,0:T(8,128)(2,1)S(1)}, u32[]{:S(2)}, u32[]{:S(2)}) %collective-permute-start.1) | collective-permute-done | bytes 102432 | tf_op jit(solution)/shard_map/ppermute | solution.py:41
  17.6 0.0 collective-permute-done.2.rest_2_
  17.6 1.4 %combine.1 = (bf16[64,512]{1,0:T(8,128)(2,1)}, bf16[64,512]{1,0:T(8,128)(2,1)S(1)}, bf16[192,512]{1,0:T(8,128)(2,1)S(1)}) custom-call(s32[2]{0:T(128)S(1)} %pad_add_fusion.at_ref, f32[256,128]{1,0:T(8,128)S(1)} %get-tuple-element.22.own_ref, f32[64,128]{1,0:T(8,128)S(1)} %get-tuple-element.23.square_ref, bf16[32,512]{1,0:T(8,128)(2,1)S(1)} %get-tuple-element.24.mine_ref, ...), custom_call_target="tpu_custom_call" | custom-call | tf_op jit(solution)/shard_map/combine/pallas_call | solution.py:209
  19.0 0.5 %collective-permute-start.4 = (bf16[64,512]{1,0:T(8,128)(2,1)S(1)}, bf16[64,512]{1,0:T(8,128)(2,1)S(1)}, u32[]{:S(2)}, u32[]{:S(2)}) collective-permute-start(bf16[64,512]{1,0:T(8,128)(2,1)S(1)} %get-tuple-element.34), channel_id=1, source_target_pairs={{0,2},{1,3},{2,0},{3,1},{4,6},{5,7},{6,4},{7,5},{8,10},{9,11},{10,... | collective-permute-start | bytes 196616 | tf_op jit(solution)/shard_map/ppermute | solution.py:41
  19.5 2.3 %collective-permute-start.3 = (bf16[64,512]{1,0:T(8,128)(2,1)S(1)}, bf16[64,512]{1,0:T(8,128)(2,1)S(1)}, u32[]{:S(2)}, u32[]{:S(2)}) collective-permute-start(bf16[64,512]{1,0:T(8,128)(2,1)S(1)} %get-tuple-element.34), channel_id=1, source_target_pairs={{0,3},{1,2},{2,1},{3,0},{4,7},{5,6},{6,5},{7,4},{8,11},{9,10},{10,... | collective-permute-start | bytes 196616 | tf_op jit(solution)/shard_map/ppermute | solution.py:41
  21.8 1.5 %collective-permute-start.5 = (bf16[192,512]{1,0:T(8,128)(2,1)S(1)}, bf16[192,512]{1,0:T(8,128)(2,1)S(1)}, u32[]{:S(2)}, u32[]{:S(2)}) collective-permute-start(bf16[192,512]{1,0:T(8,128)(2,1)S(1)} %get-tuple-element.35), channel_id=1, source_target_pairs={{0,8},{4,12},{8,0},{12,4},{1,9},{5,13},{9,1},{13,5},{2,10},{6,14},... | collective-permute-start | bytes 589832 | tf_op jit(solution)/shard_map/ppermute | solution.py:41
  23.3 0.1 broadcast.107.clone
  23.4 2.8 %collective-permute-done.4 = bf16[64,512]{1,0:T(8,128)(2,1)S(1)} collective-permute-done((bf16[64,512]{1,0:T(8,128)(2,1)S(1)}, bf16[64,512]{1,0:T(8,128)(2,1)S(1)}, u32[]{:S(2)}, u32[]{:S(2)}) %collective-permute-start.4) | collective-permute-done | bytes 65568 | tf_op jit(solution)/shard_map/ppermute | solution.py:41
  26.2 1.5 %collective-permute-start.8 = (bf16[64,512]{1,0:T(8,128)(2,1)S(1)}, bf16[64,512]{1,0:T(8,128)(2,1)S(1)}, u32[]{:S(2)}, u32[]{:S(2)}) collective-permute-start(bf16[64,512]{1,0:T(8,128)(2,1)S(1)} %collective-permute-done.4), channel_id=1, source_target_pairs={{0,8},{4,12},{8,0},{12,4},{1,9},{5,13},{9,1},{13,5},{2,10},{6,14},... | collective-permute-start | bytes 196616 | tf_op jit(solution)/shard_map/ppermute | solution.py:41
  27.7 0.5 %collective-permute-start.7 = (bf16[64,512]{1,0:T(8,128)(2,1)S(1)}, bf16[64,512]{1,0:T(8,128)(2,1)S(1)}, u32[]{:S(2)}, u32[]{:S(2)}) collective-permute-start(bf16[64,512]{1,0:T(8,128)(2,1)S(1)} %collective-permute-done.3), channel_id=1, source_target_pairs={{0,8},{4,12},{8,0},{12,4},{1,9},{5,13},{9,1},{13,5},{2,10},{6,14},... | collective-permute-start | bytes 196616 | tf_op jit(solution)/shard_map/ppermute | solution.py:41
  28.3 0.0 collective-permute-done.5
  28.3 0.9 %collective-permute-start.6 = (bf16[128,512]{1,0:T(8,128)(2,1)S(1)}, bf16[128,512]{1,0:T(8,128)(2,1)S(1)}, u32[]{:S(2)}, u32[]{:S(2)}) collective-permute-start(bf16[128,512]{1,0:T(8,128)(2,1)S(1)} %pad_maximum_fusion.4), channel_id=1, source_target_pairs={{0,1},{1,0},{2,3},{3,2},{4,5},{5,4},{6,7},{7,6},{8,9},{9,8},{10,11... | collective-permute-start | bytes 393224 | tf_op jit(solution)/shard_map/ppermute | solution.py:41
  29.2 0.1 collective-permute-start.9
  29.3 4.0 %collective-permute-done.6 = bf16[128,512]{1,0:T(8,128)(2,1)S(1)} collective-permute-done((bf16[128,512]{1,0:T(8,128)(2,1)S(1)}, bf16[128,512]{1,0:T(8,128)(2,1)S(1)}, u32[]{:S(2)}, u32[]{:S(2)}) %collective-permute-start.6) | collective-permute-done | bytes 131104 | tf_op jit(solution)/shard_map/ppermute | solution.py:41
  33.4 0.0 collective-permute-done.7
  33.5 2.2 %attend_own.1 = (f32[8,8,512]{2,1,0:T(8,128)S(1)}, f32[8,128,512]{2,1,0:T(8,128)S(1)}) custom-call(s32[2]{0:T(128)S(1)} %pad_add_fusion.1.spots_ref, bf16[4096,128]{1,0:T(8,128)(2,1)S(1)} %get-tuple-element.33.query_ref, bf16[4,192,512]{2,1,0:T(8,128)(2,1)S(1)} %fusion.2.cache_ref, bf16[64,1024]{1,0:T(8,128)(2,1)S(1)} %get-tuple-element.36.rest_0_, ...), custom_call_target="tpu_custom_call" | custom-call | tf_op jit(solution)/shard_map/attend_own/pallas_call | solution.py:351
  35.7 0.1 collective-permute-start.10
  35.8 0.1 broadcast.107
  35.9 1.6 %collective-permute-done.10 = bf16[384,512]{1,0:T(8,128)(2,1)S(1)} collective-permute-done((bf16[384,512]{1,0:T(8,128)(2,1)S(1)}, bf16[384,512]{1,0:T(8,128)(2,1)S(1)}, u32[]{:S(2)}, u32[]{:S(2)}) %collective-permute-start.10) | collective-permute-done | bytes 393248 | tf_op jit(solution)/shard_map/ppermute | solution.py:41
  37.5 3.5 %attend_last.1 = bf16[64,8192]{1,0:T(8,128)(2,1)} custom-call(s32[2]{0:T(128)S(1)} %pad_add_fusion.1.spots_ref, bf16[4096,128]{1,0:T(8,128)(2,1)S(1)} %get-tuple-element.33.query_ref, bf16[4,192,512]{2,1,0:T(8,128)(2,1)S(1)} %fusion.cache_ref, f32[8,8,512]{2,1,0:T(8,128)S(1)} %get-tuple-element.38.rest_0_, f32[8,128,512]{2,1,0:T(8,128)S(1)} %get-tuple-element.39.rest_1_), custom_call_target="tpu_custom_call" | custom-call | tf_op jit(solution)/shard_map/attend_last/pallas_call | solution.py:351
  (25 shorter events, 0.3 us)
Async XLA Ops:
  0.6 10.9 %copy-start.1 = (bf16[1,64,2048]{2,1,0:T(8,128)(2,1)S(1)}, bf16[1,64,2048]{2,1,0:T(8,128)(2,1)}, u32[]{:S(2)}) copy-start(bf16[1,64,2048]{2,1,0:T(8,128)(2,1)} %param.14) | copy-start | bytes 786436
  0.6 10.9 %copy-start = (bf16[1,64,8192]{2,1,0:T(8,128)(2,1)S(1)}, bf16[1,64,8192]{2,1,0:T(8,128)(2,1)}, u32[]{:S(2)}) copy-start(bf16[1,64,8192]{2,1,0:T(8,128)(2,1)} %param.13) | copy-start | bytes 3145732
  3.9 8.9 %collective-permute-start = (bf16[400,128]{1,0:T(8,128)(2,1)S(1)}, bf16[400,128]{1,0:T(8,128)(2,1)S(1)}, u32[]{:S(2)}, u32[]{:S(2)}) collective-permute-start(bf16[400,128]{1,0:T(8,128)(2,1)S(1)} %get-tuple-element.29), channel_id=1, source_target_pairs={{0,3},{1,2},{2,1},{3,0},{4,7},{5,6},{6,5},{7,4},{8,11},{9,10},{10,... | collective-permute-start | bytes 307208 | tf_op jit(solution)/shard_map/ppermute | solution.py:41
  9.0 8.6 %collective-permute-start.1 = (bf16[400,128]{1,0:T(8,128)(2,1)S(1)}, bf16[400,128]{1,0:T(8,128)(2,1)S(1)}, u32[]{:S(2)}, u32[]{:S(2)}) collective-permute-start(bf16[400,128]{1,0:T(8,128)(2,1)S(1)} %get-tuple-element.30), channel_id=1, source_target_pairs={{0,2},{1,3},{2,0},{3,1},{4,6},{5,7},{6,4},{7,5},{8,10},{9,11},{10,... | collective-permute-start | bytes 307208 | tf_op jit(solution)/shard_map/ppermute | solution.py:41
  9.0 8.6 %collective-permute-start.2 = (bf16[400,128]{1,0:T(8,128)(2,1)S(1)}, bf16[400,128]{1,0:T(8,128)(2,1)S(1)}, u32[]{:S(2)}, u32[]{:S(2)}) collective-permute-start(bf16[400,128]{1,0:T(8,128)(2,1)S(1)} %get-tuple-element.31), channel_id=1, source_target_pairs={{0,1},{1,0},{2,3},{3,2},{4,5},{5,4},{6,7},{7,6},{8,9},{9,8},{10,11... | collective-permute-start | bytes 307208 | tf_op jit(solution)/shard_map/ppermute | solution.py:41
  19.0 7.2 %collective-permute-start.4 = (bf16[64,512]{1,0:T(8,128)(2,1)S(1)}, bf16[64,512]{1,0:T(8,128)(2,1)S(1)}, u32[]{:S(2)}, u32[]{:S(2)}) collective-permute-start(bf16[64,512]{1,0:T(8,128)(2,1)S(1)} %get-tuple-element.34), channel_id=1, source_target_pairs={{0,2},{1,3},{2,0},{3,1},{4,6},{5,7},{6,4},{7,5},{8,10},{9,11},{10,... | collective-permute-start | bytes 196616 | tf_op jit(solution)/shard_map/ppermute | solution.py:41
  19.5 8.2 %collective-permute-start.3 = (bf16[64,512]{1,0:T(8,128)(2,1)S(1)}, bf16[64,512]{1,0:T(8,128)(2,1)S(1)}, u32[]{:S(2)}, u32[]{:S(2)}) collective-permute-start(bf16[64,512]{1,0:T(8,128)(2,1)S(1)} %get-tuple-element.34), channel_id=1, source_target_pairs={{0,3},{1,2},{2,1},{3,0},{4,7},{5,6},{6,5},{7,4},{8,11},{9,10},{10,... | collective-permute-start | bytes 196616 | tf_op jit(solution)/shard_map/ppermute | solution.py:41
  21.8 6.4 %collective-permute-start.5 = (bf16[192,512]{1,0:T(8,128)(2,1)S(1)}, bf16[192,512]{1,0:T(8,128)(2,1)S(1)}, u32[]{:S(2)}, u32[]{:S(2)}) collective-permute-start(bf16[192,512]{1,0:T(8,128)(2,1)S(1)} %get-tuple-element.35), channel_id=1, source_target_pairs={{0,8},{4,12},{8,0},{12,4},{1,9},{5,13},{9,1},{13,5},{2,10},{6,14},... | collective-permute-start | bytes 589832 | tf_op jit(solution)/shard_map/ppermute | solution.py:41
  26.2 7.1 %collective-permute-start.8 = (bf16[64,512]{1,0:T(8,128)(2,1)S(1)}, bf16[64,512]{1,0:T(8,128)(2,1)S(1)}, u32[]{:S(2)}, u32[]{:S(2)}) collective-permute-start(bf16[64,512]{1,0:T(8,128)(2,1)S(1)} %collective-permute-done.4), channel_id=1, source_target_pairs={{0,8},{4,12},{8,0},{12,4},{1,9},{5,13},{9,1},{13,5},{2,10},{6,14},... | collective-permute-start | bytes 196616 | tf_op jit(solution)/shard_map/ppermute | solution.py:41
  27.7 5.7 %collective-permute-start.7 = (bf16[64,512]{1,0:T(8,128)(2,1)S(1)}, bf16[64,512]{1,0:T(8,128)(2,1)S(1)}, u32[]{:S(2)}, u32[]{:S(2)}) collective-permute-start(bf16[64,512]{1,0:T(8,128)(2,1)S(1)} %collective-permute-done.3), channel_id=1, source_target_pairs={{0,8},{4,12},{8,0},{12,4},{1,9},{5,13},{9,1},{13,5},{2,10},{6,14},... | collective-permute-start | bytes 196616 | tf_op jit(solution)/shard_map/ppermute | solution.py:41
  28.3 5.0 %collective-permute-start.6 = (bf16[128,512]{1,0:T(8,128)(2,1)S(1)}, bf16[128,512]{1,0:T(8,128)(2,1)S(1)}, u32[]{:S(2)}, u32[]{:S(2)}) collective-permute-start(bf16[128,512]{1,0:T(8,128)(2,1)S(1)} %pad_maximum_fusion.4), channel_id=1, source_target_pairs={{0,1},{1,0},{2,3},{3,2},{4,5},{5,4},{6,7},{7,6},{8,9},{9,8},{10,11... | collective-permute-start | bytes 393224 | tf_op jit(solution)/shard_map/ppermute | solution.py:41
  29.2 4.2 %collective-permute-start.9 = (bf16[384,512]{1,0:T(8,128)(2,1)S(1)}, bf16[384,512]{1,0:T(8,128)(2,1)S(1)}, u32[]{:S(2)}, u32[]{:S(2)}) collective-permute-start(bf16[384,512]{1,0:T(8,128)(2,1)S(1)} %pad_maximum_fusion), channel_id=1, source_target_pairs={{0,4},{4,0},{8,12},{12,8},{1,5},{5,1},{9,13},{13,9},{2,6},{6,2},{1... | collective-permute-start | bytes 1179656 | tf_op jit(solution)/shard_map/ppermute | solution.py:41
  35.7 1.8 %collective-permute-start.10 = (bf16[384,512]{1,0:T(8,128)(2,1)S(1)}, bf16[384,512]{1,0:T(8,128)(2,1)S(1)}, u32[]{:S(2)}, u32[]{:S(2)}) collective-permute-start(bf16[384,512]{1,0:T(8,128)(2,1)S(1)} %pad_maximum_fusion.1), channel_id=1, source_target_pairs={{0,4},{4,0},{8,12},{12,8},{1,5},{5,1},{9,13},{13,9},{2,6},{6,2},{1... | collective-permute-start | bytes 1179656 | tf_op jit(solution)/shard_map/ppermute | solution.py:41

commit v5 on v4

--- a/solution.py
+++ b/solution.py
@@ -19,9 +19,9 @@
 KEY_COLUMNS = KEY_HEADS * HEAD_SIZE
 BF16 = jnp.bfloat16
 F32 = jnp.float32
+FLUSHES = 4
 VMEM = pl.BlockSpec(memory_space=pltpu.VMEM)
 HBM = pl.BlockSpec(memory_space=pltpu.HBM)
-SMEM = pl.BlockSpec(memory_space=pltpu.SMEM)
 
 
 def peer(index, step, count):
@@ -64,7 +64,7 @@
     return lax.broadcasted_iota(jnp.int32, shape, 0) == lax.broadcasted_iota(jnp.int32, shape, 1)
 
 
-def project_kernel(count, rows, heads, chunks, at_ref, hidden_ref, gain_ref, weight_ref, prompt_ref, *rest):
+def project_kernel(count, rows, heads, chunks, hidden_ref, gain_ref, weight_ref, prompt_ref, *rest):
     own_ref, square_ref, mine_ref = rest[:3]
     sends = rest[3 : 2 + count]
     hidden_buf, gain_buf, weight_buf, total, squares, sems = rest[2 + count :]
@@ -74,7 +74,7 @@
     cached = prompt_ref.shape[0]
     gain_copy = pltpu.make_async_copy(gain_ref, gain_buf, sems.at[2 * chunks])
     gain_copy.start()
-    columns = pl.ds(pl.multiple_of(at_ref[1] * width, HEAD_SIZE), width)
+    columns = pl.ds(pl.multiple_of(lax.axis_index("set") * width, HEAD_SIZE), width)
     prompt_copy = pltpu.make_async_copy(prompt_ref.at[:, columns], mine_ref, sems.at[2 * chunks + 1])
     copies = []
     for c in range(chunks):
@@ -111,7 +111,7 @@
             total[...] += part
             squares[...] += folded
     prompt_copy.wait()
-    me = at_ref[0]
+    me = lax.axis_index("seq")
     for k in range(count):
         to = pl.ds(pl.multiple_of(peer(me, k, count) * rows, rows), rows)
         column = jnp.sum(squares[to, :], axis=1, keepdims=True)
@@ -134,7 +134,7 @@
             out[h * rows : (h + 1) * rows, :] = piece.astype(out.dtype)
 
 
-def project(at, span_hidden, norm_gain, key_value_weight, prompt_rows, count):
+def project(span_hidden, norm_gain, key_value_weight, prompt_rows, count):
     length, depth = span_hidden.shape
     width = key_value_weight.shape[1]
     rows, heads = length // count, width // HEAD_SIZE
@@ -149,7 +149,7 @@
     stay = [pltpu.with_memory_space_constraint(x, pltpu.HBM) for x in (span_hidden, gain, key_value_weight, prompt_rows)]
     return pl.pallas_call(
         functools.partial(project_kernel, count, rows, heads, chunks),
-        in_specs=[SMEM, HBM, HBM, HBM, HBM],
+        in_specs=[HBM, HBM, HBM, HBM],
         out_shape=outs,
         out_specs=[VMEM] * len(outs),
         scratch_shapes=[
@@ -165,14 +165,14 @@
             flops=2 * length * depth * width, bytes_accessed=2 * depth * (length + width), transcendentals=0
         ),
         name="project",
-    )(at, *stay)
-
-
-def combine_kernel(rows, heads, at_ref, own_ref, square_ref, mine_ref, cosine_ref, sine_ref, *rest):
-    got, (out_ref, send_ref, packed_ref) = rest[:-3], rest[-3:]
+    )(*stay)
+
+
+def combine_kernel(rows, heads, own_ref, square_ref, mine_ref, cosine_ref, sine_ref, *rest):
+    got, (send_ref, packed_ref) = rest[:-2], rest[-2:]
     cached = mine_ref.shape[0]
     count = 1 + len(got)
-    me, first = at_ref[0], at_ref[1] * heads
+    me, first = lax.axis_index("seq"), lax.axis_index("set") * heads
 
     def prompt_rows(k):
         return pl.ds(pl.multiple_of(rows + source(me, k, count) * cached, 16), cached)
@@ -192,7 +192,6 @@
             value = value + ref[span, :].astype(F32)
         value = value * scale
         out = jnp.where(first + h < KEY_HEADS, turn(value, cosine, sine), value).astype(BF16)
-        out_ref[:, lanes] = out
         send_ref[:, lanes] = out
         packed_ref[:rows, lanes] = out
         for i, ref in enumerate(got):
@@ -201,19 +200,19 @@
     packed_ref[prompt_rows(0), :] = mine_ref[...]
 
 
-def combine(at, own, square, mine, cosine, sine, got):
+def combine(own, square, mine, cosine, sine, got):
     rows = square.shape[0]
     heads = own.shape[0] // rows
-    block = jax.ShapeDtypeStruct((rows, heads * HEAD_SIZE), BF16)
+    block = pltpu.VMEM((rows, heads * HEAD_SIZE), BF16)
     packed = jax.ShapeDtypeStruct((rows + (1 + len(got)) * mine.shape[0], heads * HEAD_SIZE), BF16)
     return pl.pallas_call(
         functools.partial(combine_kernel, rows, heads),
-        in_specs=[SMEM] + [VMEM] * (5 + len(got)),
-        out_shape=[block, block, packed],
-        out_specs=[VMEM, VMEM, VMEM],
+        in_specs=[VMEM] * (5 + len(got)),
+        out_shape=[block, packed],
+        out_specs=[VMEM, VMEM],
         compiler_params=pltpu.CompilerParams(vmem_limit_bytes=4 << 20),
         name="combine",
-    )(at, own, square, mine, cosine, sine, *got)
+    )(own, square, mine, cosine, sine, *got)
 
 
 def queries_kernel(query_ref, own_ref, cosine_ref, sine_ref, query_out, key_out, value_out):
@@ -248,69 +247,88 @@
     )(cont_query, own_rows, cosine, sine)
 
 
-def attend_kernel(tile, span_rows, last, spots_ref, query_ref, cache_ref, *rest):
-    first = span_rows is not None
-    if first:
+def attend_kernel(plan, sets, spans, tile, last, bounds_ref, query_ref, *rest):
+    own = plan is None
+    if own:
         key_ref, own_ref, state_out, mixed_out = rest
-    elif last:
-        state_ref, mixed_ref, out_ref = rest
     else:
-        state_ref, mixed_ref, state_out, mixed_out = rest
-    offset, length = spots_ref[0], spots_ref[1]
-    sets, cached_rows, width = cache_ref.shape
-    heads = width // HEAD_SIZE
+        operands = 1 + max(operand for stretch in plan for operand, _ in stretch.values())
+        pieces, rest = rest[:operands], rest[operands:]
+        if last:
+            state_ref, mixed_ref, final_ref, out_ref, sems = rest
+        else:
+            state_ref, mixed_ref, state_out, mixed_out = rest
+    my_set = lax.axis_index("set")
     block = query_ref.shape[0] // KEY_HEADS
     tokens = block // GROUP
-    total_rows = cached_rows + (tokens if first else 0)
-    if first:
-        place = lax.broadcasted_iota(jnp.int32, (total_rows, tokens), 0)
-        token = lax.broadcasted_iota(jnp.int32, (total_rows, tokens), 1)
-        cached = place - span_rows
-        seen = (place < span_rows) | (place < cached_rows) & (cached < offset)
-        live = seen | (place >= cached_rows) & (place - cached_rows <= token)
-        bias = jnp.concatenate([jnp.where(live, 0.0, NEGATIVE_LARGE)] * (tile // tokens), axis=1)
-    if last:
-        keep = lax.broadcasted_iota(jnp.int32, (tokens, HEAD_SIZE), 0) < length
+    offset, length = bounds_ref[0:1, :], bounds_ref[8:9, :]
+    total_rows = sum(rows for rows, _ in spans)
+    bias = None
+    if own:
+        place = lax.broadcasted_iota(jnp.int32, (tokens, tokens), 0)
+        token = lax.broadcasted_iota(jnp.int32, (tokens, tokens), 1)
+        bias = jnp.concatenate([jnp.where(place <= token, 0.0, NEGATIVE_LARGE)] * (tile // tokens), axis=1)
+    elif any(prompt for _, prompt in spans):
+        parts = []
+        for rows, prompt in spans:
+            place = lax.broadcasted_iota(jnp.int32, (rows, HEAD_SIZE), 0)
+            parts.append(jnp.where(place < offset, 0.0, NEGATIVE_LARGE) if prompt else jnp.zeros(place.shape, F32))
+        bias = jnp.concatenate([jnp.concatenate(parts, axis=0)] * (tile // HEAD_SIZE), axis=1)
+    keep = lax.broadcasted_iota(jnp.int32, (tokens, HEAD_SIZE), 0) < length
     units = [(g, start) for g in range(KEY_HEADS) for start in range(0, block, tile)]
-    scored, weighed, mixtures = {}, {}, {}
-
-    def rows_of(g, at, ref):
-        lane = (g % heads) * HEAD_SIZE
-        rows = cache_ref[at + g // heads, :, lane : lane + HEAD_SIZE]
-        if first:
-            rows = jnp.concatenate([rows, ref[:, g * HEAD_SIZE : (g + 1) * HEAD_SIZE]], axis=0)
-        return rows
+    held, scored, weighed, mixtures, copies = {}, {}, {}, {}, []
+
+    def rows_of(column):
+        if column not in held:
+            if own:
+                ref = key_ref if column < KEY_COLUMNS else own_ref
+                held[column] = ref[:, column % KEY_COLUMNS : column % KEY_COLUMNS + HEAD_SIZE]
+                return held[column]
+            width = pieces[0].shape[1]
+            lanes = slice(column % width, column % width + HEAD_SIZE)
+            parts = []
+            for stretch, (rows, _) in zip(plan, spans):
+                chosen = None
+                for step, (operand, first) in stretch.items():
+                    part = pieces[operand][first : first + rows, lanes]
+                    here = source(my_set, step, sets) == column // width
+                    chosen = part if chosen is None else jnp.where(here, part, chosen)
+                parts.append(chosen)
+            held[column] = jnp.concatenate(parts, axis=0)
+        return held[column]
 
     def score(unit):
         g, start = unit
-        key = rows_of(g, 0, key_ref if first else None)
         query = query_ref[g * block + start : g * block + start + tile, :]
+        key = rows_of(g * HEAD_SIZE)
         scores = lax.dot_general(key, query, (((1,), (1,)), ((), ())), preferred_element_type=F32)
-        scored[unit] = scores + bias if first else scores
+        scored[unit] = scores if bias is None else scores + bias
 
     def weigh(unit):
         g, start = unit
         scores = scored.pop(unit)
         top, shrink = jnp.max(scores, axis=0, keepdims=True), None
-        if not first:
+        if not own:
             old = state_ref[g, 0:1, start : start + tile]
             top = jnp.maximum(old, top)
             shrink = jnp.exp2(old - top)
         weights = jnp.exp2(scores - top)
         total = jnp.sum(weights, axis=0, keepdims=True)
-        if not first:
+        if not own:
             total = total + state_ref[g, 1:2, start : start + tile] * shrink
         weighed[unit] = top, shrink, total
-        value = rows_of(g, sets // 2, own_ref if first else None)
         mixtures[unit] = lax.dot_general(
-            value, weights.astype(BF16), (((0,), (0,)), ((), ())), preferred_element_type=F32
+            rows_of(KEY_COLUMNS + g * HEAD_SIZE),
+            weights.astype(BF16),
+            (((0,), (0,)), ((), ())),
+            preferred_element_type=F32,
         )
 
     def finish(unit):
         g, start = unit
         top, shrink, total = weighed.pop(unit)
         mixed = mixtures.pop(unit)
-        if not first:
+        if not own:
             mixed = mixed + mixed_ref[g, :, start : start + tile] * shrink
         if last:
             mixed = (mixed * (1.0 / total)).astype(BF16).T
@@ -323,6 +341,7 @@
             state_out[g, 1:2, start : start + tile] = total
             mixed_out[g, :, start : start + tile] = mixed
 
+    flush = len(units) // FLUSHES
     for i in range(len(units) + 2):
         if i < len(units):
             score(units[i])
@@ -330,31 +349,46 @@
             weigh(units[i - 1])
         if 0 <= i - 2 < len(units):
             finish(units[i - 2])
-
-
-def attend(spots, query, cache, span_rows=None, own=(), state=(), last=False):
-    first = not state
+            if last and (i - 1) % flush == 0:
+                wide = out_ref.shape[1] // FLUSHES
+                part = pl.ds(len(copies) * wide, wide)
+                copies.append(pltpu.make_async_copy(out_ref.at[:, part], final_ref.at[:, part], sems.at[len(copies)]))
+                copies[-1].start()
+    for copy in copies:
+        copy.wait()
+
+
+def attend(bounds, query, sets, own=None, plan=None, spans=(), pieces=(), state=(), last=False):
     block = query.shape[0] // KEY_HEADS
     tokens = block // GROUP
-    tile = block if first else block // 2
-    operands = [spots, query, cache] + list(own) + list(state)
+    spans = [(tokens, False)] if own else spans
+    total_rows = sum(rows for rows, _ in spans)
+    tile = block
+    operands = [bounds, query] + list(own or ()) + list(pieces) + list(state)
+    scratch = []
     if last:
         out_shape = jax.ShapeDtypeStruct((tokens, QUERY_HEADS * HEAD_SIZE), BF16)
-        out_specs = VMEM
+        out_specs = HBM
+        scratch = [pltpu.VMEM(out_shape.shape, BF16), pltpu.SemaphoreType.DMA((FLUSHES,))]
     else:
         out_shape = [
             jax.ShapeDtypeStruct((KEY_HEADS, 8, block), F32),
             jax.ShapeDtypeStruct((KEY_HEADS, HEAD_SIZE, block), F32),
         ]
         out_specs = [VMEM, VMEM]
-    name = "attend_own" if first else "attend_last" if last else "attend_more"
     return pl.pallas_call(
-        functools.partial(attend_kernel, tile, span_rows, last),
-        in_specs=[SMEM] + [VMEM] * (len(operands) - 1),
+        functools.partial(attend_kernel, plan, sets, spans, tile, last),
+        in_specs=[VMEM] * len(operands),
         out_shape=out_shape,
         out_specs=out_specs,
+        scratch_shapes=scratch,
         compiler_params=pltpu.CompilerParams(vmem_limit_bytes=16 << 20),
-        name=name,
+        cost_estimate=pl.CostEstimate(
+            flops=4 * query.size * total_rows,
+            bytes_accessed=4 * query.size,
+            transcendentals=query.shape[0] * total_rows,
+        ),
+        name="attend_own" if own else "attend_last" if last else "attend_more",
     )(*operands)
 
 
@@ -376,45 +410,52 @@
     tokens = cont_query.shape[1]
     low = 2 if sets % 2 == 0 else 1
 
-    at = jnp.stack([my_seq, my_set]).astype(jnp.int32)
-    own, square, mine, *sends = project(at, span_hidden, norm_gain, key_value_weight, prompt_key_value, count)
+    own, square, mine, *sends = project(span_hidden, norm_gain, key_value_weight, prompt_key_value, count)
     order = list(range(count - 1, 0, -1))
     got = [exchange(sends[k - 1], "seq", k) for k in order]
 
     span_cosine, span_sine = tables(offset + my_seq * rows + jnp.arange(rows, dtype=jnp.int32))
     self_cosine, self_sine = tables(offset + SPAN_LENGTH + jnp.arange(tokens, dtype=jnp.int32))
     query, key, value = queries(cont_query[0], continuation_key_value[0], self_cosine, self_sine)
-    query, key, value, span_cosine = lax.optimization_barrier((query, key, value, span_cosine))
-
-    block, send, packed = combine(at, own, square, mine, span_cosine, span_sine, got)
+    bounds = jnp.repeat(jnp.stack([offset, cont_lengths[0]]), 8)[:, None] * jnp.ones((1, HEAD_SIZE), jnp.int32)
+    state = attend(bounds, query, sets, own=(key, value))
+    query, state, span_cosine = lax.optimization_barrier((query, state, span_cosine))
+
+    block, packed = combine(own, square, mine, span_cosine, span_sine, got)
 
     far = list(range(low, sets, low))
     steps = [0] + far
     beside = [packed] + [exchange(packed, "set", step) for step in far]
-    across = [exchange(send, "seq", k) for k in order[:-1]]
-    nearest = exchange(jnp.concatenate([send] + [x[:rows] for x in beside[1:]], axis=0), "seq", order[-1])
-    stretches = []
-    for arrived in across:
-        stretches.append([arrived] + [exchange(arrived, "set", step) for step in far])
-    stretches.append([nearest[i * rows : (i + 1) * rows] for i in range(len(steps))])
-
-    def gather(share, after=None):
-        held = [jnp.concatenate([stretch[n] for stretch in share], axis=0) for n in range(len(steps))]
-        if after is not None:
-            held, _ = lax.optimization_barrier((held, after))
-        size = held[0].shape[0]
-        held = list(zip(steps, held))
+    across = [exchange(block, "seq", k) for k in order]
+    stretches = [[arrived] + [exchange(arrived, "set", step) for step in far] for arrived in across]
+
+    def share(values, spans):
+        plan, pieces = [], []
+        for lines, stretch_spans in zip(values, spans):
+            first = 0
+            for rows, _ in stretch_spans:
+                plan.append({step: (len(pieces) + n, first) for n, step in enumerate(steps)})
+                first += rows
+            pieces += lines
         if low == 2:
-            other = exchange(jnp.concatenate([part for _, part in held], axis=0), "set", 1)
-            held += [(step ^ 1, other[n * size : (n + 1) * size]) for n, step in enumerate(steps)]
-        cache = jnp.zeros((sets, size, width), BF16)
-        for step, part in held:
-            cache = lax.dynamic_update_slice(cache, part[None], (source(my_set, step, sets), 0, 0))
-        return cache
-
-    spots = jnp.stack([offset, cont_lengths[0]])
-    state = attend(spots, query, gather([beside]), span_rows=rows, own=(key, value))
-    attended = attend(spots, query, gather(stretches, state), state=state, last=True)
+            other = exchange(jnp.concatenate([line for lines in values for line in lines], axis=0), "set", 1)
+            top, at = 0, 0
+            for lines, stretch_spans in zip(values, spans):
+                size = lines[0].shape[0]
+                first = 0
+                for rows, _ in stretch_spans:
+                    for n, step in enumerate(steps):
+                        plan[at][step ^ 1] = (len(pieces), top + n * size + first)
+                    first += rows
+                    at += 1
+                top += size * len(lines)
+            pieces.append(other)
+        return dict(plan=plan, pieces=pieces, spans=[span for stretch_spans in spans for span in stretch_spans])
+
+    near = share([beside], [[(rows, False), (packed.shape[0] - rows, True)]])
+    state = attend(bounds, query, sets, state=state, **near)
+    rest = share(stretches, [[(rows, False)]] * len(stretches))
+    attended = attend(bounds, query, sets, state=state, last=True, **rest)
     return block, attended[None]
 
 

time: 41.2 us -> 36.5 us (0.89)
  waiting for transfers between devices: 13.7 us -> 8.7 us
  Pallas kernels: 10.9 us -> 8.65 us
  starting transfers between devices: 13.1 us -> 15.3 us
  local copies, waits for them, and re-layouts: 0.3 us -> 0.9 us
    ppermute x11 -> x12, waiting for transfers between devices: 13.7 us -> 8.7 us  [exchange(): lax.ppermute(value, axis, [(i, peer(i, step, count)) for i in range(count)])]
    ppermute x11 -> x12, starting transfers between devices: 13.1 us -> 15.3 us  [exchange(): lax.ppermute(value, axis, [(i, peer(i, step, count)) for i in range(count)])]
    pallas_call x1, Pallas kernels: 1.38 us -> 0.22 us  [combine(): pl.pallas_call(functools.partial(combine_kernel, rows, heads), in_specs=[...]
    unnamed x4 -> x10, local copies, waits for them, and re-layouts: 0.01 us -> 0.67 us
    pallas_call x2 -> x3, Pallas kernels: 5.66 us -> 5.05 us  [attend(): pl.pallas_call(functools.partial(attend_kernel, plan, sets, spans, tile,...]
    pallas_call x1, Pallas kernels: 3.17 us -> 2.73 us  [project(): pl.pallas_call(functools.partial(project_kernel, count, rows, heads, chun...]
  transfers between devices with their start and end apart: 11 -> 12, of which waited for: 5 -> 7; matrix products, arithmetic and copies ran while one was open for 2% -> 4% of each run, Pallas kernels for 2% -> 9%
where the time goes in v5:
time: 36.5 us; the launch traced here: 36.3 us
  starting transfers between devices  15.3 us (42%)
  waiting for transfers between devices  8.7 us (24%)
  Pallas kernels  8.65 us (24%)
  between operations  2.11 us (6%)
  local copies, waits for them, and re-layouts  0.9 us (2%)
  other arithmetic  0.68 us (2%)
    ppermute x12, starting transfers between devices, exchange(): lax.ppermute(value, axis, [(i, peer(i, step, count)) for i in range(count)])  15.3 us
    ppermute x12, waiting for transfers between devices, exchange(): lax.ppermute(value, axis, [(i, peer(i, step, count)) for i in range(count)])  8.7 us
    pallas_call x3, Pallas kernels, attend(): pl.pallas_call(functools.partial(attend_kernel, plan, sets, spans, tile,...  5.05 us
    pallas_call x1, Pallas kernels, project(): pl.pallas_call(functools.partial(project_kernel, count, rows, heads, chun...  2.73 us
  transfers between devices with their start and end apart: 12, of which 7 were waited for; matrix products, arithmetic and copies ran while one was open for 4% of the time, Pallas kernels for 9%

profile of v5, /device:TPU:0, one launch (start us, length us, event | category | flops | bytes accessed | tf_op | source)
XLA Modules:
  0.0 36.3 jit_solution(8475670219453254534)
XLA Ops:
  0.7 2.7 %project.1 = (f32[256,128]{1,0:T(8,128)S(1)}, f32[64,128]{1,0:T(8,128)S(1)}, bf16[32,512]{1,0:T(8,128)(2,1)S(1)}, bf16[400,128]{1,0:T(8,128)(2,1)S(1)}, bf16[400...) custom-call(bf16[256,2048]{1,0:T(8,128)(2,1)} %hidden_ref.1, bf16[16,128]{1,0:T(8,128)(2,1)} %bitcast.10, ...), custom_call_target="tpu_custom_call" | custom-call | flops 536870912 | bytes 3145728 | tf_op jit(solution)/shard_map/project/pallas_call | solution.py:150
  3.4 5.1 %collective-permute-start = (bf16[400,128]{1,0:T(8,128)(2,1)S(1)}, bf16[400,128]{1,0:T(8,128)(2,1)S(1)}, u32[]{:S(2)}, u32[]{:S(2)}) collective-permute-start(bf16[400,128]{1,0:T(8,128)(2,1)S(1)} %get-tuple-element.30), channel_id=1, source_target_pairs={{0,3},{1,2},{2,1},{3,0},{4,7},{5,6},{6,5},{7,4},{8,11},{9,10},{10,... | collective-permute-start | bytes 307208 | tf_op jit(solution)/shard_map/ppermute | solution.py:41
  8.5 0.6 %collective-permute-start.2 = (bf16[400,128]{1,0:T(8,128)(2,1)S(1)}, bf16[400,128]{1,0:T(8,128)(2,1)S(1)}, u32[]{:S(2)}, u32[]{:S(2)}) collective-permute-start(bf16[400,128]{1,0:T(8,128)(2,1)S(1)} %get-tuple-element.32), channel_id=1, source_target_pairs={{0,1},{1,0},{2,3},{3,2},{4,5},{5,4},{6,7},{7,6},{8,9},{9,8},{10,11... | collective-permute-start | bytes 307208 | tf_op jit(solution)/shard_map/ppermute | solution.py:41
  10.5 0.1 pad_add_fusion
  10.6 0.1 broadcast_in_dim.4
  10.7 0.1 mul.72
  10.7 0.3 fusion.1
  11.1 0.1 pad_maximum_fusion.3.cosine_ref
  11.1 0.1 pad_maximum_fusion.1
  11.2 0.7 %queries.1 = (bf16[4096,128]{1,0:T(8,128)(2,1)S(1)}, bf16[64,1024]{1,0:T(8,128)(2,1)S(1)}, bf16[64,1024]{1,0:T(8,128)(2,1)S(1)}) custom-call(bf16[64,8192]{1,0:T(8,128)(2,1)S(1)} %bitcast.7, bf16[64,2048]{1,0:T(8,128)(2,1)S(1)} %bitcast.8, f32[64,128]{1,0:T(8,128)S(1)} %get-tuple-element.49.cosine_ref, f32[64,128]{1,0:T(8,128)S(1)} %get-tuple-element.50.sine_ref), custom_call_target="tpu_custom_call" | custom-call | flops 4194304 | bytes 2097152 | tf_op jit(solution)/shard_map/queries/pallas_call | solution.py:235
  11.9 0.1 mul.73.bounds_ref
  12.0 1.1 %attend_own.1 = (f32[8,8,512]{2,1,0:T(8,128)S(1)}, f32[8,128,512]{2,1,0:T(8,128)S(1)}) custom-call(s32[16,128]{1,0:T(8,128)S(1)} %mul.73.bounds_ref, bf16[4096,128]{1,0:T(8,128)(2,1)S(1)} %get-tuple-element.34.query_ref, bf16[64,1024]{1,0:T(8,128)(2,1)S(1)} %get-tuple-element.25.rest_0_, bf16[64,1024]{1,0:T(8,128)(2,1)S(1)} %get-tuple-element.26.rest_1_), custom_call_target="tpu_custom_call" | custom-call | flops 134217728 | bytes 2097152 | tf_op jit(solution)/shard_map/attend_own/pallas_call | solution.py:379
  13.1 0.1 pad_maximum_fusion.4.sine_ref
  13.2 0.0 collective-permute-done.rest_0_
  13.2 3.9 %collective-permute-done.1.rest_1_ = bf16[400,128]{1,0:T(8,128)(2,1)S(1)} collective-permute-done((bf16[400,128]{1,0:T(8,128)(2,1)S(1)}, bf16[400,128]{1,0:T(8,128)(2,1)S(1)}, u32[]{:S(2)}, u32[]{:S(2)}) %collective-permute-start.1) | collective-permute-done | bytes 102432 | tf_op jit(solution)/shard_map/ppermute | solution.py:41
  17.1 0.2 combine.1
  17.3 2.5 %collective-permute-start.3 = (bf16[64,512]{1,0:T(8,128)(2,1)S(1)}, bf16[64,512]{1,0:T(8,128)(2,1)S(1)}, u32[]{:S(2)}, u32[]{:S(2)}) collective-permute-start(bf16[64,512]{1,0:T(8,128)(2,1)S(1)} %get-tuple-element.51), channel_id=1, source_target_pairs={{0,3},{1,2},{2,1},{3,0},{4,7},{5,6},{6,5},{7,4},{8,11},{9,10},{10,... | collective-permute-start | bytes 196616 | tf_op jit(solution)/shard_map/ppermute | solution.py:41
  19.9 1.9 %collective-permute-start.7 = (bf16[64,512]{1,0:T(8,128)(2,1)S(1)}, bf16[64,512]{1,0:T(8,128)(2,1)S(1)}, u32[]{:S(2)}, u32[]{:S(2)}) collective-permute-start(bf16[64,512]{1,0:T(8,128)(2,1)S(1)} %get-tuple-element.51), channel_id=1, source_target_pairs={{0,1},{1,0},{2,3},{3,2},{4,5},{5,4},{6,7},{7,6},{8,9},{9,8},{10,11... | collective-permute-start | bytes 196616 | tf_op jit(solution)/shard_map/ppermute | solution.py:41
  21.8 1.5 %collective-permute-start.10 = (bf16[192,512]{1,0:T(8,128)(2,1)S(1)}, bf16[192,512]{1,0:T(8,128)(2,1)S(1)}, u32[]{:S(2)}, u32[]{:S(2)}) collective-permute-start(bf16[192,512]{1,0:T(8,128)(2,1)S(1)} %get-tuple-element.35.rest_0_), channel_id=1, source_target_pairs={{0,8},{4,12},{8,0},{12,4},{1,9},{5,13},{9,1},{13,5},{2,10},{6,14},... | collective-permute-start | bytes 589832 | tf_op jit(solution)/shard_map/ppermute | solution.py:41
  23.3 0.7 %collective-permute-done.3.rest_0_ = bf16[64,512]{1,0:T(8,128)(2,1)S(1)} collective-permute-done((bf16[64,512]{1,0:T(8,128)(2,1)S(1)}, bf16[64,512]{1,0:T(8,128)(2,1)S(1)}, u32[]{:S(2)}, u32[]{:S(2)}) %collective-permute-start.3) | collective-permute-done | bytes 65568 | tf_op jit(solution)/shard_map/ppermute | solution.py:41
  24.0 1.5 %collective-permute-start.4 = (bf16[64,512]{1,0:T(8,128)(2,1)S(1)}, bf16[64,512]{1,0:T(8,128)(2,1)S(1)}, u32[]{:S(2)}, u32[]{:S(2)}) collective-permute-start(bf16[64,512]{1,0:T(8,128)(2,1)S(1)} %collective-permute-done.3.rest_0_), channel_id=1, source_target_pairs={{0,8},{4,12},{8,0},{12,4},{1,9},{5,13},{9,1},{13,5},{2,10},{6,14},... | collective-permute-start | bytes 196616 | tf_op jit(solution)/shard_map/ppermute | solution.py:41
  25.5 0.3 collective-permute-done.5.rest_2_
  25.8 1.5 %collective-permute-start.6 = (bf16[64,512]{1,0:T(8,128)(2,1)S(1)}, bf16[64,512]{1,0:T(8,128)(2,1)S(1)}, u32[]{:S(2)}, u32[]{:S(2)}) collective-permute-start(bf16[64,512]{1,0:T(8,128)(2,1)S(1)} %collective-permute-done.5.rest_2_), channel_id=1, source_target_pairs={{0,8},{4,12},{8,0},{12,4},{1,9},{5,13},{9,1},{13,5},{2,10},{6,14},... | collective-permute-start | bytes 196616 | tf_op jit(solution)/shard_map/ppermute | solution.py:41
  27.3 0.5 %collective-permute-start.8 = (bf16[64,512]{1,0:T(8,128)(2,1)S(1)}, bf16[64,512]{1,0:T(8,128)(2,1)S(1)}, u32[]{:S(2)}, u32[]{:S(2)}) collective-permute-start(bf16[64,512]{1,0:T(8,128)(2,1)S(1)} %collective-permute-done.7.rest_4_), channel_id=1, source_target_pairs={{0,8},{4,12},{8,0},{12,4},{1,9},{5,13},{9,1},{13,5},{2,10},{6,14},... | collective-permute-start | bytes 196616 | tf_op jit(solution)/shard_map/ppermute | solution.py:41
  27.8 0.9 %collective-permute-done.4.rest_1_ = bf16[64,512]{1,0:T(8,128)(2,1)S(1)} collective-permute-done((bf16[64,512]{1,0:T(8,128)(2,1)S(1)}, bf16[64,512]{1,0:T(8,128)(2,1)S(1)}, u32[]{:S(2)}, u32[]{:S(2)}) %collective-permute-start.4) | collective-permute-done | bytes 65568 | tf_op jit(solution)/shard_map/ppermute | solution.py:41
  28.7 1.8 %collective-permute-done.6.rest_3_ = bf16[64,512]{1,0:T(8,128)(2,1)S(1)} collective-permute-done((bf16[64,512]{1,0:T(8,128)(2,1)S(1)}, bf16[64,512]{1,0:T(8,128)(2,1)S(1)}, u32[]{:S(2)}, u32[]{:S(2)}) %collective-permute-start.6) | collective-permute-done | bytes 65568 | tf_op jit(solution)/shard_map/ppermute | solution.py:41
  30.6 0.1 collective-permute-start.11
  30.7 0.9 %collective-permute-done.8.rest_5_ = bf16[64,512]{1,0:T(8,128)(2,1)S(1)} collective-permute-done((bf16[64,512]{1,0:T(8,128)(2,1)S(1)}, bf16[64,512]{1,0:T(8,128)(2,1)S(1)}, u32[]{:S(2)}, u32[]{:S(2)}) %collective-permute-start.8) | collective-permute-done | bytes 65568 | tf_op jit(solution)/shard_map/ppermute | solution.py:41
  31.5 0.6 %copy.15 = bf16[64,512]{1,0:T(8,128)(2,1)} copy(bf16[64,512]{1,0:T(8,128)(2,1)S(1)} %get-tuple-element.51) | data formatting | bytes 131072
  32.2 0.2 collective-permute-done.11.rest_2_
  32.4 1.5 %attend_more.1 = (f32[8,8,512]{2,1,0:T(8,128)S(1)}, f32[8,128,512]{2,1,0:T(8,128)S(1)}) custom-call(s32[16,128]{1,0:T(8,128)S(1)} %mul.73.bounds_ref, bf16[4096,128]{1,0:T(8,128)(2,1)S(1)} %get-tuple-element.34.query_ref, bf16[192,512]{1,0:T(8,128)(2,1)S(1)} %get-tuple-element.35.rest_0_, bf16[192,512]{1,0:T(8,128)(2,1)S(1)} %collective-permute-done.10.rest_1_, ...), custom_call_target="tpu_custom_call" | custom-call | flops 402653184 | bytes 2097152 | tf_op jit(solution)/shard_map/attend_more/pallas_call | solution.py:379
  33.8 2.5 %attend_last.1 = bf16[64,8192]{1,0:T(8,128)(2,1)} custom-call(s32[16,128]{1,0:T(8,128)S(1)} %mul.73.bounds_ref, bf16[4096,128]{1,0:T(8,128)(2,1)S(1)} %get-tuple-element.34.query_ref, bf16[64,512]{1,0:T(8,128)(2,1)S(1)} %collective-permute-done.3.rest_0_, bf16[64,512]{1,0:T(8,128)(2,1)S(1)} %collective-permute-done.4.rest_1_, ...), custom_call_target="tpu_custom_call" | custom-call | flops 402653184 | bytes 2097152 | tf_op jit(solution)/shard_map/attend_last/pallas_call | solution.py:379
  (21 shorter events, 0.1 us)
Async XLA Ops:
  0.6 10.6 %copy-start = (bf16[1,64,8192]{2,1,0:T(8,128)(2,1)S(1)}, bf16[1,64,8192]{2,1,0:T(8,128)(2,1)}, u32[]{:S(2)}) copy-start(bf16[1,64,8192]{2,1,0:T(8,128)(2,1)} %param.13) | copy-start | bytes 3145732
  0.6 10.6 %copy-start.1 = (bf16[1,64,2048]{2,1,0:T(8,128)(2,1)S(1)}, bf16[1,64,2048]{2,1,0:T(8,128)(2,1)}, u32[]{:S(2)}) copy-start(bf16[1,64,2048]{2,1,0:T(8,128)(2,1)} %param.14) | copy-start | bytes 786436
  3.4 9.8 %collective-permute-start = (bf16[400,128]{1,0:T(8,128)(2,1)S(1)}, bf16[400,128]{1,0:T(8,128)(2,1)S(1)}, u32[]{:S(2)}, u32[]{:S(2)}) collective-permute-start(bf16[400,128]{1,0:T(8,128)(2,1)S(1)} %get-tuple-element.30), channel_id=1, source_target_pairs={{0,3},{1,2},{2,1},{3,0},{4,7},{5,6},{6,5},{7,4},{8,11},{9,10},{10,... | collective-permute-start | bytes 307208 | tf_op jit(solution)/shard_map/ppermute | solution.py:41
  8.5 8.6 %collective-permute-start.1 = (bf16[400,128]{1,0:T(8,128)(2,1)S(1)}, bf16[400,128]{1,0:T(8,128)(2,1)S(1)}, u32[]{:S(2)}, u32[]{:S(2)}) collective-permute-start(bf16[400,128]{1,0:T(8,128)(2,1)S(1)} %get-tuple-element.31), channel_id=1, source_target_pairs={{0,2},{1,3},{2,0},{3,1},{4,6},{5,7},{6,4},{7,5},{8,10},{9,11},{10,... | collective-permute-start | bytes 307208 | tf_op jit(solution)/shard_map/ppermute | solution.py:41
  8.5 8.6 %collective-permute-start.2 = (bf16[400,128]{1,0:T(8,128)(2,1)S(1)}, bf16[400,128]{1,0:T(8,128)(2,1)S(1)}, u32[]{:S(2)}, u32[]{:S(2)}) collective-permute-start(bf16[400,128]{1,0:T(8,128)(2,1)S(1)} %get-tuple-element.32), channel_id=1, source_target_pairs={{0,1},{1,0},{2,3},{3,2},{4,5},{5,4},{6,7},{7,6},{8,9},{9,8},{10,11... | collective-permute-start | bytes 307208 | tf_op jit(solution)/shard_map/ppermute | solution.py:41
  17.3 6.7 %collective-permute-start.3 = (bf16[64,512]{1,0:T(8,128)(2,1)S(1)}, bf16[64,512]{1,0:T(8,128)(2,1)S(1)}, u32[]{:S(2)}, u32[]{:S(2)}) collective-permute-start(bf16[64,512]{1,0:T(8,128)(2,1)S(1)} %get-tuple-element.51), channel_id=1, source_target_pairs={{0,3},{1,2},{2,1},{3,0},{4,7},{5,6},{6,5},{7,4},{8,11},{9,10},{10,... | collective-permute-start | bytes 196616 | tf_op jit(solution)/shard_map/ppermute | solution.py:41
  19.9 5.9 %collective-permute-start.5 = (bf16[64,512]{1,0:T(8,128)(2,1)S(1)}, bf16[64,512]{1,0:T(8,128)(2,1)S(1)}, u32[]{:S(2)}, u32[]{:S(2)}) collective-permute-start(bf16[64,512]{1,0:T(8,128)(2,1)S(1)} %get-tuple-element.51), channel_id=1, source_target_pairs={{0,2},{1,3},{2,0},{3,1},{4,6},{5,7},{6,4},{7,5},{8,10},{9,11},{10,... | collective-permute-start | bytes 196616 | tf_op jit(solution)/shard_map/ppermute | solution.py:41
  19.9 7.4 %collective-permute-start.7 = (bf16[64,512]{1,0:T(8,128)(2,1)S(1)}, bf16[64,512]{1,0:T(8,128)(2,1)S(1)}, u32[]{:S(2)}, u32[]{:S(2)}) collective-permute-start(bf16[64,512]{1,0:T(8,128)(2,1)S(1)} %get-tuple-element.51), channel_id=1, source_target_pairs={{0,1},{1,0},{2,3},{3,2},{4,5},{5,4},{6,7},{7,6},{8,9},{9,8},{10,11... | collective-permute-start | bytes 196616 | tf_op jit(solution)/shard_map/ppermute | solution.py:41
  21.8 8.7 %collective-permute-start.10 = (bf16[192,512]{1,0:T(8,128)(2,1)S(1)}, bf16[192,512]{1,0:T(8,128)(2,1)S(1)}, u32[]{:S(2)}, u32[]{:S(2)}) collective-permute-start(bf16[192,512]{1,0:T(8,128)(2,1)S(1)} %get-tuple-element.35.rest_0_), channel_id=1, source_target_pairs={{0,8},{4,12},{8,0},{12,4},{1,9},{5,13},{9,1},{13,5},{2,10},{6,14},... | collective-permute-start | bytes 589832 | tf_op jit(solution)/shard_map/ppermute | solution.py:41
  24.0 4.7 %collective-permute-start.4 = (bf16[64,512]{1,0:T(8,128)(2,1)S(1)}, bf16[64,512]{1,0:T(8,128)(2,1)S(1)}, u32[]{:S(2)}, u32[]{:S(2)}) collective-permute-start(bf16[64,512]{1,0:T(8,128)(2,1)S(1)} %collective-permute-done.3.rest_0_), channel_id=1, source_target_pairs={{0,8},{4,12},{8,0},{12,4},{1,9},{5,13},{9,1},{13,5},{2,10},{6,14},... | collective-permute-start | bytes 196616 | tf_op jit(solution)/shard_map/ppermute | solution.py:41
  25.8 4.8 %collective-permute-start.6 = (bf16[64,512]{1,0:T(8,128)(2,1)S(1)}, bf16[64,512]{1,0:T(8,128)(2,1)S(1)}, u32[]{:S(2)}, u32[]{:S(2)}) collective-permute-start(bf16[64,512]{1,0:T(8,128)(2,1)S(1)} %collective-permute-done.5.rest_2_), channel_id=1, source_target_pairs={{0,8},{4,12},{8,0},{12,4},{1,9},{5,13},{9,1},{13,5},{2,10},{6,14},... | collective-permute-start | bytes 196616 | tf_op jit(solution)/shard_map/ppermute | solution.py:41
  27.3 4.3 %collective-permute-start.8 = (bf16[64,512]{1,0:T(8,128)(2,1)S(1)}, bf16[64,512]{1,0:T(8,128)(2,1)S(1)}, u32[]{:S(2)}, u32[]{:S(2)}) collective-permute-start(bf16[64,512]{1,0:T(8,128)(2,1)S(1)} %collective-permute-done.7.rest_4_), channel_id=1, source_target_pairs={{0,8},{4,12},{8,0},{12,4},{1,9},{5,13},{9,1},{13,5},{2,10},{6,14},... | collective-permute-start | bytes 196616 | tf_op jit(solution)/shard_map/ppermute | solution.py:41
  30.6 1.8 %collective-permute-start.11 = (bf16[384,512]{1,0:T(8,128)(2,1)S(1)}, bf16[384,512]{1,0:T(8,128)(2,1)S(1)}, u32[]{:S(2)}, u32[]{:S(2)}) collective-permute-start(bf16[384,512]{1,0:T(8,128)(2,1)S(1)} %pad_maximum_fusion), channel_id=1, source_target_pairs={{0,4},{4,0},{8,12},{12,8},{1,5},{5,1},{9,13},{13,9},{2,6},{6,2},{1... | collective-permute-start | bytes 1179656 | tf_op jit(solution)/shard_map/ppermute | solution.py:41
  31.5 2.3 %collective-permute-start.9 = (bf16[384,512]{1,0:T(8,128)(2,1)S(1)}, bf16[384,512]{1,0:T(8,128)(2,1)S(1)}, u32[]{:S(2)}, u32[]{:S(2)}) collective-permute-start(bf16[384,512]{1,0:T(8,128)(2,1)S(1)} %constant_dynamic-update-slice_fusion), channel_id=1, source_target_pairs={{0,4},{4,0},{8,12},{12,8},{1,5},{5,1},{9,13},{13,9},{2,6},{6,2},{1... | collective-permute-start | bytes 1179656 | tf_op jit(solution)/shard_map/ppermute | solution.py:41

commit v6 on v5

--- a/solution.py
+++ b/solution.py
@@ -64,18 +64,14 @@
     return lax.broadcasted_iota(jnp.int32, shape, 0) == lax.broadcasted_iota(jnp.int32, shape, 1)
 
 
-def project_kernel(count, rows, heads, chunks, hidden_ref, gain_ref, weight_ref, prompt_ref, *rest):
-    own_ref, square_ref, mine_ref = rest[:3]
-    sends = rest[3 : 2 + count]
-    hidden_buf, gain_buf, weight_buf, total, squares, sems = rest[2 + count :]
+def project_kernel(count, rows, heads, chunks, hidden_ref, gain_ref, weight_ref, *rest):
+    own_ref, square_ref = rest[:2]
+    sends = rest[2 : 1 + count]
+    hidden_buf, gain_buf, weight_buf, total, squares, sems = rest[1 + count :]
     depth = hidden_ref.shape[1]
     size = depth // chunks
-    width = weight_ref.shape[1]
-    cached = prompt_ref.shape[0]
     gain_copy = pltpu.make_async_copy(gain_ref, gain_buf, sems.at[2 * chunks])
     gain_copy.start()
-    columns = pl.ds(pl.multiple_of(lax.axis_index("set") * width, HEAD_SIZE), width)
-    prompt_copy = pltpu.make_async_copy(prompt_ref.at[:, columns], mine_ref, sems.at[2 * chunks + 1])
     copies = []
     for c in range(chunks):
         part = pl.ds(c * size, size)
@@ -87,7 +83,6 @@
         )
         copies[-1][0].start()
         copies[-1][1].start()
-    prompt_copy.start()
     gain_copy.wait()
     for c in range(chunks):
         copies[c][0].wait()
@@ -110,7 +105,6 @@
         else:
             total[...] += part
             squares[...] += folded
-    prompt_copy.wait()
     me = lax.axis_index("seq")
     for k in range(count):
         to = pl.ds(pl.multiple_of(peer(me, k, count) * rows, rows), rows)
@@ -126,30 +120,25 @@
             which = lax.broadcasted_iota(jnp.int32, (16, HEAD_SIZE), 0)
             tail = jnp.where(which == 0, high, jnp.where(which == 1, low, 0.0))
             out[heads * rows : heads * rows + 16, :] = tail.astype(BF16)
-            for h in range(heads):
-                first = heads * rows + 16 + h * cached
-                out[first : first + cached, :] = mine_ref[:, h * HEAD_SIZE : (h + 1) * HEAD_SIZE]
         for h in range(heads):
             piece = total[to, h * HEAD_SIZE : (h + 1) * HEAD_SIZE]
             out[h * rows : (h + 1) * rows, :] = piece.astype(out.dtype)
 
 
-def project(span_hidden, norm_gain, key_value_weight, prompt_rows, count):
+def project(span_hidden, norm_gain, key_value_weight, count):
     length, depth = span_hidden.shape
     width = key_value_weight.shape[1]
     rows, heads = length // count, width // HEAD_SIZE
-    cached = prompt_rows.shape[0]
     chunks = 4 if depth % (4 * HEAD_SIZE) == 0 else 1
     gain = norm_gain.reshape(-1, HEAD_SIZE)
     outs = [
         jax.ShapeDtypeStruct((heads * rows, HEAD_SIZE), F32),
         jax.ShapeDtypeStruct((rows, HEAD_SIZE), F32),
-        jax.ShapeDtypeStruct((cached, width), BF16),
-    ] + [jax.ShapeDtypeStruct((heads * (rows + cached) + 16, HEAD_SIZE), BF16)] * (count - 1)
-    stay = [pltpu.with_memory_space_constraint(x, pltpu.HBM) for x in (span_hidden, gain, key_value_weight, prompt_rows)]
+    ] + [jax.ShapeDtypeStruct((heads * rows + 16, HEAD_SIZE), BF16)] * (count - 1)
+    stay = [pltpu.with_memory_space_constraint(x, pltpu.HBM) for x in (span_hidden, gain, key_value_weight)]
     return pl.pallas_call(
         functools.partial(project_kernel, count, rows, heads, chunks),
-        in_specs=[HBM, HBM, HBM, HBM],
+        in_specs=[HBM, HBM, HBM],
         out_shape=outs,
         out_specs=[VMEM] * len(outs),
         scratch_shapes=[
@@ -158,7 +147,7 @@
             pltpu.VMEM((depth, width), BF16),
             pltpu.VMEM((length, width), F32),
             pltpu.VMEM((length, HEAD_SIZE), F32),
-            pltpu.SemaphoreType.DMA((2 * chunks + 2,)),
+            pltpu.SemaphoreType.DMA((2 * chunks + 1,)),
         ],
         compiler_params=pltpu.CompilerParams(vmem_limit_bytes=16 << 20),
         cost_estimate=pl.CostEstimate(
@@ -168,15 +157,9 @@
     )(*stay)
 
 
-def combine_kernel(rows, heads, own_ref, square_ref, mine_ref, cosine_ref, sine_ref, *rest):
-    got, (send_ref, packed_ref) = rest[:-2], rest[-2:]
-    cached = mine_ref.shape[0]
-    count = 1 + len(got)
+def combine_kernel(rows, heads, count, places, own_ref, square_ref, cosine_ref, sine_ref, *rest):
+    got, prompts, (send_ref, packed_ref) = rest[: count - 1], rest[count - 1 : -2], rest[-2:]
     me, first = lax.axis_index("seq"), lax.axis_index("set") * heads
-
-    def prompt_rows(k):
-        return pl.ds(pl.multiple_of(rows + source(me, k, count) * cached, 16), cached)
-
     line = jnp.zeros((1, HEAD_SIZE), F32)
     for ref in got:
         tail = ref[heads * rows : heads * rows + 16, :].astype(F32)
@@ -194,25 +177,27 @@
         out = jnp.where(first + h < KEY_HEADS, turn(value, cosine, sine), value).astype(BF16)
         send_ref[:, lanes] = out
         packed_ref[:rows, lanes] = out
-        for i, ref in enumerate(got):
-            start = heads * rows + 16 + h * cached
-            packed_ref[prompt_rows(count - 1 - i), lanes] = ref[start : start + cached, :]
-    packed_ref[prompt_rows(0), :] = mine_ref[...]
-
-
-def combine(own, square, mine, cosine, sine, got):
+    cached = prompts[0].shape[0] // len(places[0])
+    for ref, steps in zip(prompts, places):
+        for i, step in enumerate(steps):
+            to = pl.ds(pl.multiple_of(rows + source(me, step, count) * cached, 16), cached)
+            packed_ref[to, :] = ref[i * cached : (i + 1) * cached, :]
+
+
+def combine(own, square, cosine, sine, got, prompts, places):
     rows = square.shape[0]
     heads = own.shape[0] // rows
     block = pltpu.VMEM((rows, heads * HEAD_SIZE), BF16)
-    packed = jax.ShapeDtypeStruct((rows + (1 + len(got)) * mine.shape[0], heads * HEAD_SIZE), BF16)
+    cached = sum(part.shape[0] for part in prompts)
+    packed = jax.ShapeDtypeStruct((rows + cached, heads * HEAD_SIZE), BF16)
     return pl.pallas_call(
-        functools.partial(combine_kernel, rows, heads),
-        in_specs=[VMEM] * (5 + len(got)),
+        functools.partial(combine_kernel, rows, heads, 1 + len(got), places),
+        in_specs=[VMEM] * (4 + len(got) + len(prompts)),
         out_shape=[block, packed],
         out_specs=[VMEM, VMEM],
         compiler_params=pltpu.CompilerParams(vmem_limit_bytes=4 << 20),
         name="combine",
-    )(own, square, mine, cosine, sine, *got)
+    )(own, square, cosine, sine, *got, *prompts)
 
 
 def queries_kernel(query_ref, own_ref, cosine_ref, sine_ref, query_out, key_out, value_out):
@@ -255,7 +240,7 @@
         operands = 1 + max(operand for stretch in plan for operand, _ in stretch.values())
         pieces, rest = rest[:operands], rest[operands:]
         if last:
-            state_ref, mixed_ref, final_ref, out_ref, sems = rest
+            state_ref, mixed_ref, block_ref, final_ref, block_out, out_ref, sems = rest
         else:
             state_ref, mixed_ref, state_out, mixed_out = rest
     my_set = lax.axis_index("set")
@@ -277,6 +262,9 @@
     keep = lax.broadcasted_iota(jnp.int32, (tokens, HEAD_SIZE), 0) < length
     units = [(g, start) for g in range(KEY_HEADS) for start in range(0, block, tile)]
     held, scored, weighed, mixtures, copies = {}, {}, {}, {}, []
+    if last:
+        block_copy = pltpu.make_async_copy(block_ref, block_out, sems.at[FLUSHES])
+        block_copy.start()
 
     def rows_of(column):
         if column not in held:
@@ -356,20 +344,23 @@
                 copies[-1].start()
     for copy in copies:
         copy.wait()
-
-
-def attend(bounds, query, sets, own=None, plan=None, spans=(), pieces=(), state=(), last=False):
+    if last:
+        block_copy.wait()
+
+
+def attend(bounds, query, sets, own=None, plan=None, spans=(), pieces=(), state=(), last=None):
     block = query.shape[0] // KEY_HEADS
     tokens = block // GROUP
     spans = [(tokens, False)] if own else spans
     total_rows = sum(rows for rows, _ in spans)
     tile = block
-    operands = [bounds, query] + list(own or ()) + list(pieces) + list(state)
+    operands = [bounds, query] + list(own or ()) + list(pieces) + list(state) + ([] if last is None else [last])
     scratch = []
-    if last:
-        out_shape = jax.ShapeDtypeStruct((tokens, QUERY_HEADS * HEAD_SIZE), BF16)
-        out_specs = HBM
-        scratch = [pltpu.VMEM(out_shape.shape, BF16), pltpu.SemaphoreType.DMA((FLUSHES,))]
+    if last is not None:
+        wide = (tokens, QUERY_HEADS * HEAD_SIZE)
+        out_shape = [jax.ShapeDtypeStruct(wide, BF16), jax.ShapeDtypeStruct(last.shape, BF16)]
+        out_specs = [HBM, HBM]
+        scratch = [pltpu.VMEM(wide, BF16), pltpu.SemaphoreType.DMA((FLUSHES + 1,))]
     else:
         out_shape = [
             jax.ShapeDtypeStruct((KEY_HEADS, 8, block), F32),
@@ -377,7 +368,7 @@
         ]
         out_specs = [VMEM, VMEM]
     return pl.pallas_call(
-        functools.partial(attend_kernel, plan, sets, spans, tile, last),
+        functools.partial(attend_kernel, plan, sets, spans, tile, last is not None),
         in_specs=[VMEM] * len(operands),
         out_shape=out_shape,
         out_specs=out_specs,
@@ -388,7 +379,7 @@
             bytes_accessed=4 * query.size,
             transcendentals=query.shape[0] * total_rows,
         ),
-        name="attend_own" if own else "attend_last" if last else "attend_more",
+        name="attend_own" if own else "attend_more" if last is None else "attend_last",
     )(*operands)
 
 
@@ -402,7 +393,6 @@
     continuation_key_value,
     cont_lengths,
 ):
-    offset = span_offset[0]
     sets, count = lax.axis_size("set"), lax.axis_size("seq")
     my_set, my_seq = lax.axis_index("set"), lax.axis_index("seq")
     width = key_value_weight.shape[1]
@@ -410,10 +400,27 @@
     tokens = cont_query.shape[1]
     low = 2 if sets % 2 == 0 else 1
 
-    own, square, mine, *sends = project(span_hidden, norm_gain, key_value_weight, prompt_key_value, count)
     order = list(range(count - 1, 0, -1))
+    mine = lax.dynamic_slice_in_dim(prompt_key_value, my_set * width, width, 1)
+    prompts, places = [mine], [[0]]
+    doubling = count & (count - 1) == 0
+    leaps = [count >> i for i in range(1, count.bit_length())] if doubling else order
+    early = [exchange(mine, "seq", k) for k in leaps[:1]]
+
+    own, square, *sends = project(span_hidden, norm_gain, key_value_weight, count)
     got = [exchange(sends[k - 1], "seq", k) for k in order]
 
+    for k in leaps:
+        come = [step ^ k for steps in places for step in steps] if doubling else [k]
+        if k != leaps[0]:
+            early.append(exchange(jnp.concatenate(prompts, axis=0) if doubling else mine, "seq", k))
+        prompts.append(early[-1])
+        places.append(come)
+
+    span_offset, cont_query, continuation_key_value, *_ = lax.optimization_barrier(
+        (span_offset, cont_query, continuation_key_value, prompts[1:2])
+    )
+    offset = span_offset[0]
     span_cosine, span_sine = tables(offset + my_seq * rows + jnp.arange(rows, dtype=jnp.int32))
     self_cosine, self_sine = tables(offset + SPAN_LENGTH + jnp.arange(tokens, dtype=jnp.int32))
     query, key, value = queries(cont_query[0], continuation_key_value[0], self_cosine, self_sine)
@@ -421,7 +428,7 @@
     state = attend(bounds, query, sets, own=(key, value))
     query, state, span_cosine = lax.optimization_barrier((query, state, span_cosine))
 
-    block, packed = combine(own, square, mine, span_cosine, span_sine, got)
+    block, packed = combine(own, square, span_cosine, span_sine, got, prompts, places)
 
     far = list(range(low, sets, low))
     steps = [0] + far
@@ -455,7 +462,7 @@
     near = share([beside], [[(rows, False), (packed.shape[0] - rows, True)]])
     state = attend(bounds, query, sets, state=state, **near)
     rest = share(stretches, [[(rows, False)]] * len(stretches))
-    attended = attend(bounds, query, sets, state=state, last=True, **rest)
+    attended, block = attend(bounds, query, sets, state=state, last=block, **rest)
     return block, attended[None]
 
 

time: 36.5 us -> 38 us (1.041)
  starting transfers between devices: 15.3 us -> 18.8 us
  waiting for transfers between devices: 8.7 us -> 6.63 us
    ppermute x12 -> x14, starting transfers between devices: 15.3 us -> 18.8 us  [exchange(): lax.ppermute(value, axis, [(i, peer(i, step, count)) for i in range(count)])]
    ppermute x12 -> x14, waiting for transfers between devices: 8.7 us -> 6.63 us  [exchange(): lax.ppermute(value, axis, [(i, peer(i, step, count)) for i in range(count)])]
    unnamed x10 -> x11, local copies, waits for them, and re-layouts: 0.67 us -> 0.91 us
  transfers between devices with their start and end apart: 12 -> 14, of which waited for: 7 -> 8; matrix products, arithmetic and copies ran while one was open for 4% -> 3% of each run, Pallas kernels for 9% -> 15%
where the time goes in v6:
time: 38 us; the launch traced here: 37.8 us
  starting transfers between devices  18.8 us (49%)
  Pallas kernels  8.46 us (22%)
  waiting for transfers between devices  6.63 us (17%)
  between operations  2.14 us (6%)
  local copies, waits for them, and re-layouts  1.15 us (3%)
  other arithmetic  0.69 us (2%)
    ppermute x14, starting transfers between devices, exchange(): lax.ppermute(value, axis, [(i, peer(i, step, count)) for i in range(count)])  18.8 us
    ppermute x14, waiting for transfers between devices, exchange(): lax.ppermute(value, axis, [(i, peer(i, step, count)) for i in range(count)])  6.63 us
    pallas_call x3, Pallas kernels, attend(): pl.pallas_call(functools.partial(attend_kernel, plan, sets, spans, tile,...  5.07 us
    pallas_call x1, Pallas kernels, project(): pl.pallas_call(functools.partial(project_kernel, count, rows, heads, chun...  2.53 us
    unnamed x11, local copies, waits for them, and re-layouts  0.91 us
  transfers between devices with their start and end apart: 14, of which 8 were waited for; matrix products, arithmetic and copies ran while one was open for 3% of the time, Pallas kernels for 15%

profile of v6, /device:TPU:0, one launch (start us, length us, event | category | flops | bytes accessed | tf_op | source)
XLA Modules:
  0.0 37.8 jit_solution(17569692413655087967)
XLA Ops:
  0.7 0.9 %copy-done = bf16[32,2048]{1,0:T(8,128)(2,1)S(1)} copy-done((bf16[32,2048]{1,0:T(8,128)(2,1)S(1)}, bf16[32,2048]{1,0:T(8,128)(2,1)}, u32[]{:S(2)}) %copy-start) | copy-done | bytes 131096
  1.5 4.0 %collective-permute-start = (bf16[32,512]{1,0:T(8,128)(2,1)S(1)}, bf16[32,512]{1,0:T(8,128)(2,1)S(1)}, u32[]{:S(2)}, u32[]{:S(2)}) collective-permute-start(bf16[32,512]{1,0:T(8,128)(2,1)S(1)} %constant_dynamic-slice_fusion.rest_3_), channel_id=1, source_target_pairs={{0,2},{1,3},{2,0},{3,1},{4,6},{5,7},{6,4},{7,5},{8,10},{9,11},{10,... | collective-permute-start | bytes 98312 | tf_op jit(solution)/shard_map/ppermute | solution.py:41
  5.6 2.5 %project.1 = (f32[256,128]{1,0:T(8,128)S(1)}, f32[64,128]{1,0:T(8,128)S(1)}, bf16[272,128]{1,0:T(8,128)(2,1)S(1)}, bf16[272,128]{1,0:T(8,128)(2,1)S(1)}, bf16[272,128]{1,0:T(8,128)(2,1)S(1)}) custom-call(bf16[256,2048]{1,0:T(8,128)(2,1)} %hidden_ref.1, bf16[16,128]{1,0:T(8,128)(2,1)} %bitcast.9, bf16[2048,512]{1,0:T(8,128)(2,1)} %weight_ref.1), custom_call_target="tpu_custom_call" | custom-call | flops 536870912 | bytes 3145728 | tf_op jit(solution)/shard_map/project/pallas_call | solution.py:139
  8.1 1.4 %collective-permute-start.1 = (bf16[272,128]{1,0:T(8,128)(2,1)S(1)}, bf16[272,128]{1,0:T(8,128)(2,1)S(1)}, u32[]{:S(2)}, u32[]{:S(2)}) collective-permute-start(bf16[272,128]{1,0:T(8,128)(2,1)S(1)} %get-tuple-element.37), channel_id=1, source_target_pairs={{0,3},{1,2},{2,1},{3,0},{4,7},{5,6},{6,5},{7,4},{8,11},{9,10},{10,... | collective-permute-start | bytes 208904 | tf_op jit(solution)/shard_map/ppermute | solution.py:41
  9.5 1.7 %collective-permute-start.2 = (bf16[272,128]{1,0:T(8,128)(2,1)S(1)}, bf16[272,128]{1,0:T(8,128)(2,1)S(1)}, u32[]{:S(2)}, u32[]{:S(2)}) collective-permute-start(bf16[272,128]{1,0:T(8,128)(2,1)S(1)} %get-tuple-element.38), channel_id=1, source_target_pairs={{0,2},{1,3},{2,0},{3,1},{4,6},{5,7},{6,4},{7,5},{8,10},{9,11},{10,... | collective-permute-start | bytes 208904 | tf_op jit(solution)/shard_map/ppermute | solution.py:41
  11.2 1.3 %collective-permute-start.3 = (bf16[272,128]{1,0:T(8,128)(2,1)S(1)}, bf16[272,128]{1,0:T(8,128)(2,1)S(1)}, u32[]{:S(2)}, u32[]{:S(2)}) collective-permute-start(bf16[272,128]{1,0:T(8,128)(2,1)S(1)} %get-tuple-element.39), channel_id=1, source_target_pairs={{0,1},{1,0},{2,3},{3,2},{4,5},{5,4},{6,7},{7,6},{8,9},{9,8},{10,11... | collective-permute-start | bytes 208904 | tf_op jit(solution)/shard_map/ppermute | solution.py:41
  13.3 0.3 fusion.1
  13.6 0.1 pad_maximum_fusion.4.cosine_ref
  13.7 0.1 pad_maximum_fusion.2
  13.8 0.1 pad_maximum_fusion.5.sine_ref
  14.5 0.7 %collective-permute-start.4 = (bf16[64,512]{1,0:T(8,128)(2,1)S(1)}, bf16[64,512]{1,0:T(8,128)(2,1)S(1)}, u32[]{:S(2)}, u32[]{:S(2)}) collective-permute-start(bf16[64,512]{1,0:T(8,128)(2,1)S(1)} %pad_maximum_fusion.1), channel_id=1, source_target_pairs={{0,1},{1,0},{2,3},{3,2},{4,5},{5,4},{6,7},{7,6},{8,9},{9,8},{10,11... | collective-permute-start | bytes 196616 | tf_op jit(solution)/shard_map/ppermute | solution.py:41
  15.3 0.1 pad_add_fusion
  15.4 0.1 mul.70
  15.5 0.7 %queries.1 = (bf16[4096,128]{1,0:T(8,128)(2,1)S(1)}, bf16[64,1024]{1,0:T(8,128)(2,1)S(1)}, bf16[64,1024]{1,0:T(8,128)(2,1)S(1)}) custom-call(bf16[64,8192]{1,0:T(8,128)(2,1)S(1)} %bitcast.7, bf16[64,2048]{1,0:T(8,128)(2,1)S(1)} %bitcast.8, f32[64,128]{1,0:T(8,128)S(1)} %get-tuple-element.57.cosine_ref, f32[64,128]{1,0:T(8,128)S(1)} %get-tuple-element.58.sine_ref), custom_call_target="tpu_custom_call" | custom-call | flops 4194304 | bytes 2097152 | tf_op jit(solution)/shard_map/queries/pallas_call | solution.py:220
  16.2 1.1 %attend_own.1 = (f32[8,8,512]{2,1,0:T(8,128)S(1)}, f32[8,128,512]{2,1,0:T(8,128)S(1)}) custom-call(s32[16,128]{1,0:T(8,128)S(1)} %mul.71.bounds_ref, bf16[4096,128]{1,0:T(8,128)(2,1)S(1)} %get-tuple-element.33.query_ref, bf16[64,1024]{1,0:T(8,128)(2,1)S(1)} %get-tuple-element.29.rest_0_, bf16[64,1024]{1,0:T(8,128)(2,1)S(1)} %get-tuple-element.30.rest_1_), custom_call_target="tpu_custom_call" | custom-call | flops 134217728 | bytes 2097152 | tf_op jit(solution)/shard_map/attend_own/pallas_call | solution.py:370
  17.4 1.4 %collective-permute-done.4.rest_5_ = bf16[64,512]{1,0:T(8,128)(2,1)S(1)} collective-permute-done((bf16[64,512]{1,0:T(8,128)(2,1)S(1)}, bf16[64,512]{1,0:T(8,128)(2,1)S(1)}, u32[]{:S(2)}, u32[]{:S(2)}) %collective-permute-start.4) | collective-permute-done | bytes 65568 | tf_op jit(solution)/shard_map/ppermute | solution.py:41
  18.9 0.2 combine.1
  19.1 1.4 %collective-permute-start.5 = (bf16[64,512]{1,0:T(8,128)(2,1)S(1)}, bf16[64,512]{1,0:T(8,128)(2,1)S(1)}, u32[]{:S(2)}, u32[]{:S(2)}) collective-permute-start(bf16[64,512]{1,0:T(8,128)(2,1)S(1)} %get-tuple-element.40.rest_9_), channel_id=1, source_target_pairs={{0,3},{1,2},{2,1},{3,0},{4,7},{5,6},{6,5},{7,4},{8,11},{9,10},{10,... | collective-permute-start | bytes 196616 | tf_op jit(solution)/shard_map/ppermute | solution.py:41
  20.5 0.8 %collective-permute-start.7 = (bf16[64,512]{1,0:T(8,128)(2,1)S(1)}, bf16[64,512]{1,0:T(8,128)(2,1)S(1)}, u32[]{:S(2)}, u32[]{:S(2)}) collective-permute-start(bf16[64,512]{1,0:T(8,128)(2,1)S(1)} %get-tuple-element.40.rest_9_), channel_id=1, source_target_pairs={{0,2},{1,3},{2,0},{3,1},{4,6},{5,7},{6,4},{7,5},{8,10},{9,11},{10,... | collective-permute-start | bytes 196616 | tf_op jit(solution)/shard_map/ppermute | solution.py:41
  21.3 2.2 %collective-permute-start.9 = (bf16[64,512]{1,0:T(8,128)(2,1)S(1)}, bf16[64,512]{1,0:T(8,128)(2,1)S(1)}, u32[]{:S(2)}, u32[]{:S(2)}) collective-permute-start(bf16[64,512]{1,0:T(8,128)(2,1)S(1)} %get-tuple-element.40.rest_9_), channel_id=1, source_target_pairs={{0,1},{1,0},{2,3},{3,2},{4,5},{5,4},{6,7},{7,6},{8,9},{9,8},{10,11... | collective-permute-start | bytes 196616 | tf_op jit(solution)/shard_map/ppermute | solution.py:41
  23.5 1.5 %collective-permute-start.12 = (bf16[192,512]{1,0:T(8,128)(2,1)S(1)}, bf16[192,512]{1,0:T(8,128)(2,1)S(1)}, u32[]{:S(2)}, u32[]{:S(2)}) collective-permute-start(bf16[192,512]{1,0:T(8,128)(2,1)S(1)} %get-tuple-element.41.rest_0_), channel_id=1, source_target_pairs={{0,8},{4,12},{8,0},{12,4},{1,9},{5,13},{9,1},{13,5},{2,10},{6,14},... | collective-permute-start | bytes 589832 | tf_op jit(solution)/shard_map/ppermute | solution.py:41
  25.0 0.3 collective-permute-done.5.rest_0_
  25.3 1.5 %collective-permute-start.6 = (bf16[64,512]{1,0:T(8,128)(2,1)S(1)}, bf16[64,512]{1,0:T(8,128)(2,1)S(1)}, u32[]{:S(2)}, u32[]{:S(2)}) collective-permute-start(bf16[64,512]{1,0:T(8,128)(2,1)S(1)} %collective-permute-done.5.rest_0_), channel_id=1, source_target_pairs={{0,8},{4,12},{8,0},{12,4},{1,9},{5,13},{9,1},{13,5},{2,10},{6,14},... | collective-permute-start | bytes 196616 | tf_op jit(solution)/shard_map/ppermute | solution.py:41
  26.8 0.3 collective-permute-done.7.rest_2_
  27.1 1.5 %collective-permute-start.8 = (bf16[64,512]{1,0:T(8,128)(2,1)S(1)}, bf16[64,512]{1,0:T(8,128)(2,1)S(1)}, u32[]{:S(2)}, u32[]{:S(2)}) collective-permute-start(bf16[64,512]{1,0:T(8,128)(2,1)S(1)} %collective-permute-done.7.rest_2_), channel_id=1, source_target_pairs={{0,8},{4,12},{8,0},{12,4},{1,9},{5,13},{9,1},{13,5},{2,10},{6,14},... | collective-permute-start | bytes 196616 | tf_op jit(solution)/shard_map/ppermute | solution.py:41
  28.6 0.5 %collective-permute-start.10 = (bf16[64,512]{1,0:T(8,128)(2,1)S(1)}, bf16[64,512]{1,0:T(8,128)(2,1)S(1)}, u32[]{:S(2)}, u32[]{:S(2)}) collective-permute-start(bf16[64,512]{1,0:T(8,128)(2,1)S(1)} %collective-permute-done.9.rest_4_), channel_id=1, source_target_pairs={{0,8},{4,12},{8,0},{12,4},{1,9},{5,13},{9,1},{13,5},{2,10},{6,14},... | collective-permute-start | bytes 196616 | tf_op jit(solution)/shard_map/ppermute | solution.py:41
  29.1 1.9 %collective-permute-done.6.rest_1_ = bf16[64,512]{1,0:T(8,128)(2,1)S(1)} collective-permute-done((bf16[64,512]{1,0:T(8,128)(2,1)S(1)}, bf16[64,512]{1,0:T(8,128)(2,1)S(1)}, u32[]{:S(2)}, u32[]{:S(2)}) %collective-permute-start.6) | collective-permute-done | bytes 65568 | tf_op jit(solution)/shard_map/ppermute | solution.py:41
  31.0 1.0 %collective-permute-done.8.rest_3_ = bf16[64,512]{1,0:T(8,128)(2,1)S(1)} collective-permute-done((bf16[64,512]{1,0:T(8,128)(2,1)S(1)}, bf16[64,512]{1,0:T(8,128)(2,1)S(1)}, u32[]{:S(2)}, u32[]{:S(2)}) %collective-permute-start.8) | collective-permute-done | bytes 65568 | tf_op jit(solution)/shard_map/ppermute | solution.py:41
  32.2 0.7 %collective-permute-done.10.rest_5_ = bf16[64,512]{1,0:T(8,128)(2,1)S(1)} collective-permute-done((bf16[64,512]{1,0:T(8,128)(2,1)S(1)}, bf16[64,512]{1,0:T(8,128)(2,1)S(1)}, u32[]{:S(2)}, u32[]{:S(2)}) %collective-permute-start.10) | collective-permute-done | bytes 65568 | tf_op jit(solution)/shard_map/ppermute | solution.py:41
  32.9 1.0 %collective-permute-done.13.rest_2_ = bf16[384,512]{1,0:T(8,128)(2,1)S(1)} collective-permute-done((bf16[384,512]{1,0:T(8,128)(2,1)S(1)}, bf16[384,512]{1,0:T(8,128)(2,1)S(1)}, u32[]{:S(2)}, u32[]{:S(2)}) %collective-permute-start.13) | collective-permute-done | bytes 393248 | tf_op jit(solution)/shard_map/ppermute | solution.py:41
  33.9 1.5 %attend_more.1 = (f32[8,8,512]{2,1,0:T(8,128)S(1)}, f32[8,128,512]{2,1,0:T(8,128)S(1)}) custom-call(s32[16,128]{1,0:T(8,128)S(1)} %mul.71.bounds_ref, bf16[4096,128]{1,0:T(8,128)(2,1)S(1)} %get-tuple-element.33.query_ref, bf16[192,512]{1,0:T(8,128)(2,1)S(1)} %get-tuple-element.41.rest_0_, bf16[192,512]{1,0:T(8,128)(2,1)S(1)} %collective-permute-done.12.rest_1_, ...), custom_call_target="tpu_custom_call" | custom-call | flops 402653184 | bytes 2097152 | tf_op jit(solution)/shard_map/attend_more/pallas_call | solution.py:370
  35.4 2.5 %attend_last.1 = (bf16[64,8192]{1,0:T(8,128)(2,1)}, bf16[64,512]{1,0:T(8,128)(2,1)}) custom-call(s32[16,128]{1,0:T(8,128)S(1)} %mul.71.bounds_ref, bf16[4096,128]{1,0:T(8,128)(2,1)S(1)} %get-tuple-element.33.query_ref, bf16[64,512]{1,0:T(8,128)(2,1)S(1)} %collective-permute-done.5.rest_0_, bf16[64,512]{1,0:T(8,128)(2,1)S(1)} %collective-permute-done.6.rest_1_, ...), custom_call_target="tpu_custom_call" | custom-call | flops 402653184 | bytes 2097152 | tf_op jit(solution)/shard_map/attend_last/pallas_call | solution.py:370
  (28 shorter events, 0.4 us)
Async XLA Ops:
  0.6 0.9 %copy-start = (bf16[32,2048]{1,0:T(8,128)(2,1)S(1)}, bf16[32,2048]{1,0:T(8,128)(2,1)}, u32[]{:S(2)}) copy-start(bf16[32,2048]{1,0:T(8,128)(2,1)} %param.11) | copy-start | bytes 393220
  0.6 14.9 %copy-start.1 = (bf16[1,64,8192]{2,1,0:T(8,128)(2,1)S(1)}, bf16[1,64,8192]{2,1,0:T(8,128)(2,1)}, u32[]{:S(2)}) copy-start(bf16[1,64,8192]{2,1,0:T(8,128)(2,1)} %param.13) | copy-start | bytes 3145732
  0.7 14.9 %copy-start.2 = (bf16[1,64,2048]{2,1,0:T(8,128)(2,1)S(1)}, bf16[1,64,2048]{2,1,0:T(8,128)(2,1)}, u32[]{:S(2)}) copy-start(bf16[1,64,2048]{2,1,0:T(8,128)(2,1)} %param.14) | copy-start | bytes 786436
  1.5 13.0 %collective-permute-start = (bf16[32,512]{1,0:T(8,128)(2,1)S(1)}, bf16[32,512]{1,0:T(8,128)(2,1)S(1)}, u32[]{:S(2)}, u32[]{:S(2)}) collective-permute-start(bf16[32,512]{1,0:T(8,128)(2,1)S(1)} %constant_dynamic-slice_fusion.rest_3_), channel_id=1, source_target_pairs={{0,2},{1,3},{2,0},{3,1},{4,6},{5,7},{6,4},{7,5},{8,10},{9,11},{10,... | collective-permute-start | bytes 98312 | tf_op jit(solution)/shard_map/ppermute | solution.py:41
  8.1 9.3 %collective-permute-start.1 = (bf16[272,128]{1,0:T(8,128)(2,1)S(1)}, bf16[272,128]{1,0:T(8,128)(2,1)S(1)}, u32[]{:S(2)}, u32[]{:S(2)}) collective-permute-start(bf16[272,128]{1,0:T(8,128)(2,1)S(1)} %get-tuple-element.37), channel_id=1, source_target_pairs={{0,3},{1,2},{2,1},{3,0},{4,7},{5,6},{6,5},{7,4},{8,11},{9,10},{10,... | collective-permute-start | bytes 208904 | tf_op jit(solution)/shard_map/ppermute | solution.py:41
  9.5 7.9 %collective-permute-start.2 = (bf16[272,128]{1,0:T(8,128)(2,1)S(1)}, bf16[272,128]{1,0:T(8,128)(2,1)S(1)}, u32[]{:S(2)}, u32[]{:S(2)}) collective-permute-start(bf16[272,128]{1,0:T(8,128)(2,1)S(1)} %get-tuple-element.38), channel_id=1, source_target_pairs={{0,2},{1,3},{2,0},{3,1},{4,6},{5,7},{6,4},{7,5},{8,10},{9,11},{10,... | collective-permute-start | bytes 208904 | tf_op jit(solution)/shard_map/ppermute | solution.py:41
  11.2 6.2 %collective-permute-start.3 = (bf16[272,128]{1,0:T(8,128)(2,1)S(1)}, bf16[272,128]{1,0:T(8,128)(2,1)S(1)}, u32[]{:S(2)}, u32[]{:S(2)}) collective-permute-start(bf16[272,128]{1,0:T(8,128)(2,1)S(1)} %get-tuple-element.39), channel_id=1, source_target_pairs={{0,1},{1,0},{2,3},{3,2},{4,5},{5,4},{6,7},{7,6},{8,9},{9,8},{10,11... | collective-permute-start | bytes 208904 | tf_op jit(solution)/shard_map/ppermute | solution.py:41
  14.5 4.3 %collective-permute-start.4 = (bf16[64,512]{1,0:T(8,128)(2,1)S(1)}, bf16[64,512]{1,0:T(8,128)(2,1)S(1)}, u32[]{:S(2)}, u32[]{:S(2)}) collective-permute-start(bf16[64,512]{1,0:T(8,128)(2,1)S(1)} %pad_maximum_fusion.1), channel_id=1, source_target_pairs={{0,1},{1,0},{2,3},{3,2},{4,5},{5,4},{6,7},{7,6},{8,9},{9,8},{10,11... | collective-permute-start | bytes 196616 | tf_op jit(solution)/shard_map/ppermute | solution.py:41
  19.1 6.3 %collective-permute-start.5 = (bf16[64,512]{1,0:T(8,128)(2,1)S(1)}, bf16[64,512]{1,0:T(8,128)(2,1)S(1)}, u32[]{:S(2)}, u32[]{:S(2)}) collective-permute-start(bf16[64,512]{1,0:T(8,128)(2,1)S(1)} %get-tuple-element.40.rest_9_), channel_id=1, source_target_pairs={{0,3},{1,2},{2,1},{3,0},{4,7},{5,6},{6,5},{7,4},{8,11},{9,10},{10,... | collective-permute-start | bytes 196616 | tf_op jit(solution)/shard_map/ppermute | solution.py:41
  20.5 6.6 %collective-permute-start.7 = (bf16[64,512]{1,0:T(8,128)(2,1)S(1)}, bf16[64,512]{1,0:T(8,128)(2,1)S(1)}, u32[]{:S(2)}, u32[]{:S(2)}) collective-permute-start(bf16[64,512]{1,0:T(8,128)(2,1)S(1)} %get-tuple-element.40.rest_9_), channel_id=1, source_target_pairs={{0,2},{1,3},{2,0},{3,1},{4,6},{5,7},{6,4},{7,5},{8,10},{9,11},{10,... | collective-permute-start | bytes 196616 | tf_op jit(solution)/shard_map/ppermute | solution.py:41
  21.3 7.3 %collective-permute-start.9 = (bf16[64,512]{1,0:T(8,128)(2,1)S(1)}, bf16[64,512]{1,0:T(8,128)(2,1)S(1)}, u32[]{:S(2)}, u32[]{:S(2)}) collective-permute-start(bf16[64,512]{1,0:T(8,128)(2,1)S(1)} %get-tuple-element.40.rest_9_), channel_id=1, source_target_pairs={{0,1},{1,0},{2,3},{3,2},{4,5},{5,4},{6,7},{7,6},{8,9},{9,8},{10,11... | collective-permute-start | bytes 196616 | tf_op jit(solution)/shard_map/ppermute | solution.py:41
  23.5 8.5 %collective-permute-start.12 = (bf16[192,512]{1,0:T(8,128)(2,1)S(1)}, bf16[192,512]{1,0:T(8,128)(2,1)S(1)}, u32[]{:S(2)}, u32[]{:S(2)}) collective-permute-start(bf16[192,512]{1,0:T(8,128)(2,1)S(1)} %get-tuple-element.41.rest_0_), channel_id=1, source_target_pairs={{0,8},{4,12},{8,0},{12,4},{1,9},{5,13},{9,1},{13,5},{2,10},{6,14},... | collective-permute-start | bytes 589832 | tf_op jit(solution)/shard_map/ppermute | solution.py:41
  25.3 5.7 %collective-permute-start.6 = (bf16[64,512]{1,0:T(8,128)(2,1)S(1)}, bf16[64,512]{1,0:T(8,128)(2,1)S(1)}, u32[]{:S(2)}, u32[]{:S(2)}) collective-permute-start(bf16[64,512]{1,0:T(8,128)(2,1)S(1)} %collective-permute-done.5.rest_0_), channel_id=1, source_target_pairs={{0,8},{4,12},{8,0},{12,4},{1,9},{5,13},{9,1},{13,5},{2,10},{6,14},... | collective-permute-start | bytes 196616 | tf_op jit(solution)/shard_map/ppermute | solution.py:41
  27.1 4.9 %collective-permute-start.8 = (bf16[64,512]{1,0:T(8,128)(2,1)S(1)}, bf16[64,512]{1,0:T(8,128)(2,1)S(1)}, u32[]{:S(2)}, u32[]{:S(2)}) collective-permute-start(bf16[64,512]{1,0:T(8,128)(2,1)S(1)} %collective-permute-done.7.rest_2_), channel_id=1, source_target_pairs={{0,8},{4,12},{8,0},{12,4},{1,9},{5,13},{9,1},{13,5},{2,10},{6,14},... | collective-permute-start | bytes 196616 | tf_op jit(solution)/shard_map/ppermute | solution.py:41
  28.6 4.3 %collective-permute-start.10 = (bf16[64,512]{1,0:T(8,128)(2,1)S(1)}, bf16[64,512]{1,0:T(8,128)(2,1)S(1)}, u32[]{:S(2)}, u32[]{:S(2)}) collective-permute-start(bf16[64,512]{1,0:T(8,128)(2,1)S(1)} %collective-permute-done.9.rest_4_), channel_id=1, source_target_pairs={{0,8},{4,12},{8,0},{12,4},{1,9},{5,13},{9,1},{13,5},{2,10},{6,14},... | collective-permute-start | bytes 196616 | tf_op jit(solution)/shard_map/ppermute | solution.py:41
  32.1 1.8 %collective-permute-start.13 = (bf16[384,512]{1,0:T(8,128)(2,1)S(1)}, bf16[384,512]{1,0:T(8,128)(2,1)S(1)}, u32[]{:S(2)}, u32[]{:S(2)}) collective-permute-start(bf16[384,512]{1,0:T(8,128)(2,1)S(1)} %pad_maximum_fusion), channel_id=1, source_target_pairs={{0,4},{4,0},{8,12},{12,8},{1,5},{5,1},{9,13},{13,9},{2,6},{6,2},{1... | collective-permute-start | bytes 1179656 | tf_op jit(solution)/shard_map/ppermute | solution.py:41
  32.9 2.5 %collective-permute-start.11 = (bf16[384,512]{1,0:T(8,128)(2,1)S(1)}, bf16[384,512]{1,0:T(8,128)(2,1)S(1)}, u32[]{:S(2)}, u32[]{:S(2)}) collective-permute-start(bf16[384,512]{1,0:T(8,128)(2,1)S(1)} %constant_dynamic-update-slice_fusion), channel_id=1, source_target_pairs={{0,4},{4,0},{8,12},{12,8},{1,5},{5,1},{9,13},{13,9},{2,6},{6,2},{1... | collective-permute-start | bytes 1179656 | tf_op jit(solution)/shard_map/ppermute | solution.py:41

commit v7 on v6

--- a/solution.py
+++ b/solution.py
@@ -3,6 +3,7 @@
 
 import jax
 import jax.numpy as jnp
+import numpy as np
 from jax import lax
 from jax.experimental import pallas as pl
 from jax.experimental.pallas import tpu as pltpu
@@ -20,6 +21,7 @@
 BF16 = jnp.bfloat16
 F32 = jnp.float32
 FLUSHES = 4
+SMEM = pl.BlockSpec(memory_space=pltpu.SMEM)
 VMEM = pl.BlockSpec(memory_space=pltpu.VMEM)
 HBM = pl.BlockSpec(memory_space=pltpu.HBM)
 
@@ -42,17 +44,12 @@
 
 
 def frequencies():
-    base = 500000.0 ** (-(jnp.arange(HEAD_SIZE // 2).astype(F32) * 2.0) / HEAD_SIZE)
+    base = 500000.0 ** (-(np.arange(HEAD_SIZE // 2) * 2.0) / HEAD_SIZE)
     wave = 2.0 * math.pi / base
     smooth = (8192.0 / wave - 1.0) / 3.0
     blended = (1.0 - smooth) * base / 8.0 + smooth * base
-    return jnp.where(wave < 2048.0, base, jnp.where(wave > 8192.0, base / 8.0, blended))
-
-
-def tables(positions):
-    angles = positions.astype(F32)[:, None] * frequencies()[None, :]
-    cosine, sine = jnp.cos(angles), jnp.sin(angles)
-    return jnp.concatenate([cosine, cosine], -1), jnp.concatenate([-sine, sine], -1)
+    rescaled = np.where(wave < 2048.0, base, np.where(wave > 8192.0, base / 8.0, blended))
+    return jnp.asarray(np.tile(rescaled, 2)[None], F32)
 
 
 def turn(value, cosine, sine):
@@ -157,82 +154,90 @@
     )(*stay)
 
 
-def combine_kernel(rows, heads, count, places, own_ref, square_ref, cosine_ref, sine_ref, *rest):
-    got, prompts, (send_ref, packed_ref) = rest[: count - 1], rest[count - 1 : -2], rest[-2:]
-    me, first = lax.axis_index("seq"), lax.axis_index("set") * heads
+def combine_kernel(rows, heads, own_ref, square_ref, cosine_ref, sine_ref, *rest):
+    got, out_ref = rest[:-1], rest[-1]
+    first = lax.axis_index("set") * heads
     line = jnp.zeros((1, HEAD_SIZE), F32)
     for ref in got:
-        tail = ref[heads * rows : heads * rows + 16, :].astype(F32)
+        tail = ref[heads * rows :, :].astype(F32)
         line = line + tail[0:1, :] + tail[1:2, :]
     column = jnp.sum(jnp.where(diagonal(rows), line, 0.0), axis=1, keepdims=True)
     scale = lax.rsqrt((square_ref[...] + column) / MODEL_WIDTH + EPS)
     cosine, sine = cosine_ref[...], sine_ref[...]
     for h in range(heads):
         span = slice(h * rows, (h + 1) * rows)
-        lanes = slice(h * HEAD_SIZE, (h + 1) * HEAD_SIZE)
         value = own_ref[span, :]
         for ref in got:
             value = value + ref[span, :].astype(F32)
         value = value * scale
-        out = jnp.where(first + h < KEY_HEADS, turn(value, cosine, sine), value).astype(BF16)
-        send_ref[:, lanes] = out
-        packed_ref[:rows, lanes] = out
-    cached = prompts[0].shape[0] // len(places[0])
-    for ref, steps in zip(prompts, places):
-        for i, step in enumerate(steps):
-            to = pl.ds(pl.multiple_of(rows + source(me, step, count) * cached, 16), cached)
-            packed_ref[to, :] = ref[i * cached : (i + 1) * cached, :]
-
-
-def combine(own, square, cosine, sine, got, prompts, places):
+        out = jnp.where(first + h < KEY_HEADS, turn(value, cosine, sine), value)
+        out_ref[:, h * HEAD_SIZE : (h + 1) * HEAD_SIZE] = out.astype(BF16)
+
+
+def combine(own, square, cosine, sine, got):
     rows = square.shape[0]
     heads = own.shape[0] // rows
-    block = pltpu.VMEM((rows, heads * HEAD_SIZE), BF16)
-    cached = sum(part.shape[0] for part in prompts)
-    packed = jax.ShapeDtypeStruct((rows + cached, heads * HEAD_SIZE), BF16)
     return pl.pallas_call(
-        functools.partial(combine_kernel, rows, heads, 1 + len(got), places),
-        in_specs=[VMEM] * (4 + len(got) + len(prompts)),
-        out_shape=[block, packed],
-        out_specs=[VMEM, VMEM],
+        functools.partial(combine_kernel, rows, heads),
+        in_specs=[VMEM] * (4 + len(got)),
+        out_shape=pltpu.VMEM((rows, heads * HEAD_SIZE), BF16),
+        out_specs=VMEM,
         compiler_params=pltpu.CompilerParams(vmem_limit_bytes=4 << 20),
         name="combine",
-    )(own, square, cosine, sine, *got, *prompts)
-
-
-def queries_kernel(query_ref, own_ref, cosine_ref, sine_ref, query_out, key_out, value_out):
-    tokens = cosine_ref.shape[0]
-    cosine, sine = cosine_ref[...], sine_ref[...]
+    )(own, square, cosine, sine, *got)
+
+
+def prepare_kernel(
+    sets, tile, offset_ref, length_ref, frequency_ref, query_ref, own_ref, cosine_out, sine_out, query_out, state_out, mixed_out, key_buf, value_buf
+):
+    def table(rows, first):
+        place = lax.broadcasted_iota(jnp.int32, (rows, HEAD_SIZE), 0) + first
+        angles = place.astype(F32) * frequency_ref[...]
+        front = lax.broadcasted_iota(jnp.int32, (rows, HEAD_SIZE), 1) < HEAD_SIZE // 2
+        return jnp.cos(angles), jnp.where(front, -1.0, 1.0) * jnp.sin(angles)
+
+    offset = offset_ref[0]
+    rows, tokens = cosine_out.shape[0], query_ref.shape[0]
+    cosine_out[...], sine_out[...] = table(rows, offset + lax.axis_index("seq") * rows)
+    cosine, sine = table(tokens, offset + SPAN_LENGTH)
     for h in range(KEY_HEADS):
         span = slice(h * HEAD_SIZE, (h + 1) * HEAD_SIZE)
-        key_out[:, span] = turn(own_ref[:, span].astype(F32), cosine, sine).astype(BF16)
-    value_out[...] = own_ref[:, KEY_COLUMNS:]
+        key_buf[:, span] = turn(own_ref[:, span].astype(F32), cosine, sine).astype(BF16)
+    value_buf[...] = own_ref[:, KEY_COLUMNS:]
     factor = HEAD_SIZE**-0.5 * math.log2(math.e)
     cosine, sine = cosine * factor, sine * factor
     for h in range(QUERY_HEADS):
         span = slice(h * HEAD_SIZE, (h + 1) * HEAD_SIZE)
         turned = turn(query_ref[:, span].astype(F32), cosine, sine)
         query_out[h * tokens : (h + 1) * tokens, :] = turned.astype(BF16)
-
-
-def queries(cont_query, own_rows, cosine, sine):
-    tokens = cosine.shape[0]
+    attend_kernel(
+        None, sets, [(tokens, ())], tile, False, offset_ref, length_ref, query_out, key_buf, value_buf, state_out, mixed_out
+    )
+
+
+def state_shapes(block):
+    return [
+        jax.ShapeDtypeStruct((KEY_HEADS, 8, block), F32),
+        jax.ShapeDtypeStruct((KEY_HEADS, HEAD_SIZE, block), F32),
+    ]
+
+
+def prepare(offset, length, cont_query, own_rows, sets, rows):
+    tokens = cont_query.shape[0]
+    block = GROUP * tokens
+    table = jax.ShapeDtypeStruct((rows, HEAD_SIZE), F32)
     return pl.pallas_call(
-        queries_kernel,
-        in_specs=[VMEM] * 4,
-        out_shape=[
-            jax.ShapeDtypeStruct((QUERY_HEADS * tokens, HEAD_SIZE), BF16),
-            jax.ShapeDtypeStruct((tokens, KEY_COLUMNS), BF16),
-            jax.ShapeDtypeStruct((tokens, KEY_COLUMNS), BF16),
-        ],
-        out_specs=[VMEM, VMEM, VMEM],
-        compiler_params=pltpu.CompilerParams(vmem_limit_bytes=8 << 20),
-        cost_estimate=pl.CostEstimate(flops=8 * cont_query.size, bytes_accessed=4 * cont_query.size, transcendentals=0),
-        name="queries",
-    )(cont_query, own_rows, cosine, sine)
-
-
-def attend_kernel(plan, sets, spans, tile, last, bounds_ref, query_ref, *rest):
+        functools.partial(prepare_kernel, sets, block),
+        in_specs=[SMEM, SMEM, VMEM, VMEM, VMEM],
+        out_shape=[table, table, jax.ShapeDtypeStruct((QUERY_HEADS * tokens, HEAD_SIZE), BF16)] + state_shapes(block),
+        out_specs=[VMEM] * 5,
+        scratch_shapes=[pltpu.VMEM((tokens, KEY_COLUMNS), BF16)] * 2,
+        compiler_params=pltpu.CompilerParams(vmem_limit_bytes=16 << 20),
+        name="prepare",
+    )(offset, length, frequencies(), cont_query, own_rows)
+
+
+def attend_kernel(plan, sets, spans, tile, last, offset_ref, length_ref, query_ref, *rest):
     own = plan is None
     if own:
         key_ref, own_ref, state_out, mixed_out = rest
@@ -246,18 +251,25 @@
     my_set = lax.axis_index("set")
     block = query_ref.shape[0] // KEY_HEADS
     tokens = block // GROUP
-    offset, length = bounds_ref[0:1, :], bounds_ref[8:9, :]
+    offset, length = offset_ref[0], length_ref[0]
     total_rows = sum(rows for rows, _ in spans)
     bias = None
     if own:
         place = lax.broadcasted_iota(jnp.int32, (tokens, tokens), 0)
         token = lax.broadcasted_iota(jnp.int32, (tokens, tokens), 1)
         bias = jnp.concatenate([jnp.where(place <= token, 0.0, NEGATIVE_LARGE)] * (tile // tokens), axis=1)
-    elif any(prompt for _, prompt in spans):
+    elif any(leaps for _, leaps in spans):
         parts = []
-        for rows, prompt in spans:
+        for rows, leaps in spans:
             place = lax.broadcasted_iota(jnp.int32, (rows, HEAD_SIZE), 0)
-            parts.append(jnp.where(place < offset, 0.0, NEGATIVE_LARGE) if prompt else jnp.zeros(place.shape, F32))
+            dead = jnp.zeros(place.shape, F32)
+            if leaps:
+                size = rows // len(leaps)
+                for i, step in enumerate(leaps):
+                    first = source(lax.axis_index("seq"), step, len(leaps)) * size - i * size
+                    here = (place >= i * size) & (place < (i + 1) * size)
+                    dead = jnp.where(here & (place + first >= offset), NEGATIVE_LARGE, dead)
+            parts.append(dead)
         bias = jnp.concatenate([jnp.concatenate(parts, axis=0)] * (tile // HEAD_SIZE), axis=1)
     keep = lax.broadcasted_iota(jnp.int32, (tokens, HEAD_SIZE), 0) < length
     units = [(g, start) for g in range(KEY_HEADS) for start in range(0, block, tile)]
@@ -348,39 +360,26 @@
         block_copy.wait()
 
 
-def attend(bounds, query, sets, own=None, plan=None, spans=(), pieces=(), state=(), last=None):
+def attend(offset, length, query, sets, plan, spans, pieces, state, last=None):
     block = query.shape[0] // KEY_HEADS
     tokens = block // GROUP
-    spans = [(tokens, False)] if own else spans
     total_rows = sum(rows for rows, _ in spans)
-    tile = block
-    operands = [bounds, query] + list(own or ()) + list(pieces) + list(state) + ([] if last is None else [last])
-    scratch = []
+    tile = block if total_rows % 128 else block // 2
+    operands = [query] + list(pieces) + list(state) + ([] if last is None else [last])
+    out_shape, scratch = state_shapes(block), []
     if last is not None:
         wide = (tokens, QUERY_HEADS * HEAD_SIZE)
         out_shape = [jax.ShapeDtypeStruct(wide, BF16), jax.ShapeDtypeStruct(last.shape, BF16)]
-        out_specs = [HBM, HBM]
         scratch = [pltpu.VMEM(wide, BF16), pltpu.SemaphoreType.DMA((FLUSHES + 1,))]
-    else:
-        out_shape = [
-            jax.ShapeDtypeStruct((KEY_HEADS, 8, block), F32),
-            jax.ShapeDtypeStruct((KEY_HEADS, HEAD_SIZE, block), F32),
-        ]
-        out_specs = [VMEM, VMEM]
     return pl.pallas_call(
         functools.partial(attend_kernel, plan, sets, spans, tile, last is not None),
-        in_specs=[VMEM] * len(operands),
+        in_specs=[SMEM, SMEM] + [VMEM] * len(operands),
         out_shape=out_shape,
-        out_specs=out_specs,
+        out_specs=[VMEM, VMEM] if last is None else [HBM, HBM],
         scratch_shapes=scratch,
         compiler_params=pltpu.CompilerParams(vmem_limit_bytes=16 << 20),
-        cost_estimate=pl.CostEstimate(
-            flops=4 * query.size * total_rows,
-            bytes_accessed=4 * query.size,
-            transcendentals=query.shape[0] * total_rows,
-        ),
-        name="attend_own" if own else "attend_more" if last is None else "attend_last",
-    )(*operands)
+        name="attend_more" if last is None else "attend_last",
+    )(offset, length, *operands)
 
 
 def on_device(
@@ -394,75 +393,68 @@
     cont_lengths,
 ):
     sets, count = lax.axis_size("set"), lax.axis_size("seq")
-    my_set, my_seq = lax.axis_index("set"), lax.axis_index("seq")
-    width = key_value_weight.shape[1]
     rows = span_hidden.shape[0] // count
-    tokens = cont_query.shape[1]
     low = 2 if sets % 2 == 0 else 1
 
     order = list(range(count - 1, 0, -1))
+    my_set, width = lax.axis_index("set"), key_value_weight.shape[1]
     mine = lax.dynamic_slice_in_dim(prompt_key_value, my_set * width, width, 1)
-    prompts, places = [mine], [[0]]
     doubling = count & (count - 1) == 0
     leaps = [count >> i for i in range(1, count.bit_length())] if doubling else order
-    early = [exchange(mine, "seq", k) for k in leaps[:1]]
+    come = exchange(mine, "seq", leaps[0])
 
     own, square, *sends = project(span_hidden, norm_gain, key_value_weight, count)
     got = [exchange(sends[k - 1], "seq", k) for k in order]
 
-    for k in leaps:
-        come = [step ^ k for steps in places for step in steps] if doubling else [k]
-        if k != leaps[0]:
-            early.append(exchange(jnp.concatenate(prompts, axis=0) if doubling else mine, "seq", k))
-        prompts.append(early[-1])
-        places.append(come)
-
-    span_offset, cont_query, continuation_key_value, *_ = lax.optimization_barrier(
-        (span_offset, cont_query, continuation_key_value, prompts[1:2])
+    prompt, places = jnp.concatenate([mine, come], axis=0), [0, leaps[0]]
+    prompt, mine, _ = lax.optimization_barrier((prompt, mine, own))
+    cont_query, _ = lax.optimization_barrier((cont_query, prompt))
+    for k in leaps[1:]:
+        come = exchange(prompt if doubling else mine, "seq", k)
+        prompt = jnp.concatenate([prompt, come], axis=0)
+        places += [place ^ k for place in places] if doubling else [k]
+
+    cosine, sine, query, *state = prepare(
+        span_offset, cont_lengths, cont_query[0], continuation_key_value[0], sets, rows
     )
-    offset = span_offset[0]
-    span_cosine, span_sine = tables(offset + my_seq * rows + jnp.arange(rows, dtype=jnp.int32))
-    self_cosine, self_sine = tables(offset + SPAN_LENGTH + jnp.arange(tokens, dtype=jnp.int32))
-    query, key, value = queries(cont_query[0], continuation_key_value[0], self_cosine, self_sine)
-    bounds = jnp.repeat(jnp.stack([offset, cont_lengths[0]]), 8)[:, None] * jnp.ones((1, HEAD_SIZE), jnp.int32)
-    state = attend(bounds, query, sets, own=(key, value))
-    query, state, span_cosine = lax.optimization_barrier((query, state, span_cosine))
-
-    block, packed = combine(own, square, span_cosine, span_sine, got, prompts, places)
+    block = combine(own, square, cosine, sine, got)
+    block, prompt = lax.optimization_barrier((block, prompt))
 
     far = list(range(low, sets, low))
     steps = [0] + far
-    beside = [packed] + [exchange(packed, "set", step) for step in far]
-    across = [exchange(block, "seq", k) for k in order]
-    stretches = [[arrived] + [exchange(arrived, "set", step) for step in far] for arrived in across]
+    half = max(1, (count - 1) // 2)
+    beside = [exchange(block, "set", step) for step in far]
+    across = [exchange(block, "seq", k) for k in order[:half]]
+    both = jnp.concatenate([block] + beside, axis=0)
+    together = [exchange(both, "seq", k) for k in order[half:]]
+    prompts = [prompt] + [exchange(prompt, "set", step) for step in far]
+    stretches = [[block] + beside]
+    for arrived in across:
+        stretches.append([arrived] + [exchange(arrived, "set", step) for step in far])
+    stretches += [[arrived] for arrived in together]
 
     def share(values, spans):
         plan, pieces = [], []
-        for lines, stretch_spans in zip(values, spans):
-            first = 0
-            for rows, _ in stretch_spans:
-                plan.append({step: (len(pieces) + n, first) for n, step in enumerate(steps)})
-                first += rows
+        for lines, (size, _) in zip(values, spans):
+            whole = len(lines) == 1
+            plan.append({step: (len(pieces) + (0 if whole else n), n * size if whole else 0) for n, step in enumerate(steps)})
             pieces += lines
         if low == 2:
             other = exchange(jnp.concatenate([line for lines in values for line in lines], axis=0), "set", 1)
-            top, at = 0, 0
-            for lines, stretch_spans in zip(values, spans):
-                size = lines[0].shape[0]
-                first = 0
-                for rows, _ in stretch_spans:
-                    for n, step in enumerate(steps):
-                        plan[at][step ^ 1] = (len(pieces), top + n * size + first)
-                    first += rows
-                    at += 1
-                top += size * len(lines)
+            first = 0
+            for stretch, (size, _) in zip(plan, spans):
+                for step in steps:
+                    stretch[step ^ 1] = (len(pieces), first)
+                    first += size
             pieces.append(other)
-        return dict(plan=plan, pieces=pieces, spans=[span for stretch_spans in spans for span in stretch_spans])
-
-    near = share([beside], [[(rows, False), (packed.shape[0] - rows, True)]])
-    state = attend(bounds, query, sets, state=state, **near)
-    rest = share(stretches, [[(rows, False)]] * len(stretches))
-    attended, block = attend(bounds, query, sets, state=state, last=block, **rest)
+        return dict(plan=plan, pieces=pieces, spans=spans)
+
+    ends = span_offset, cont_lengths
+    state = attend(*ends, query, sets, state=state, **share([prompts], [(prompt.shape[0], places)]))
+    near = stretches[: 1 + half]
+    state = attend(*ends, query, sets, state=state, **share(near, [(rows, ())] * len(near)))
+    rest = stretches[1 + half :]
+    attended, block = attend(*ends, query, sets, state=state, last=block, **share(rest, [(rows, ())] * len(rest)))
     return block, attended[None]
 
 

time: 38 us -> 36 us (0.947)
  starting transfers between devices: 18.8 us -> 17.2 us
  other arithmetic: 0.69 us -> 0.07 us
  waiting for transfers between devices: 6.63 us -> 7.03 us
    ppermute x14, starting transfers between devices: 18.8 us -> 17.2 us  [exchange(): lax.ppermute(value, axis, [(i, peer(i, step, count)) for i in range(count)])]
    pallas_call x2, Pallas kernels: 0.87 us -> 1.93 us  [the longest x1 1.73 us: prepare(): pl.pallas_call(functools.partial(prepare_kernel, sets, block), in_specs=[...]
    pallas_call x3, Pallas kernels: 5.07 us -> 4.02 us  [attend(): pl.pallas_call(functools.partial(attend_kernel, plan, sets, spans, tile,...]
    ppermute x14, waiting for transfers between devices: 6.63 us -> 7.03 us  [exchange(): lax.ppermute(value, axis, [(i, peer(i, step, count)) for i in range(count)])]
    unnamed x11 -> x9, local copies, waits for them, and re-layouts: 0.91 us -> 0.89 us
  transfers between devices with their start and end apart: 14 -> 14, of which waited for: 8 -> 4; matrix products, arithmetic and copies ran while one was open for 3% -> 0% of each run, Pallas kernels for 15% -> 18%
where the time goes in v7:
time: 36 us; the launch traced here: 35.8 us
  starting transfers between devices  17.2 us (48%)
  Pallas kernels  8.47 us (24%)
  waiting for transfers between devices  7.03 us (20%)
  between operations  2.11 us (6%)
  local copies, waits for them, and re-layouts  0.89 us (2%)
    ppermute x14, starting transfers between devices, exchange(): lax.ppermute(value, axis, [(i, peer(i, step, count)) for i in range(count)])  17.2 us
    ppermute x14, waiting for transfers between devices, exchange(): lax.ppermute(value, axis, [(i, peer(i, step, count)) for i in range(count)])  7.03 us
    pallas_call x3, Pallas kernels, attend(): pl.pallas_call(functools.partial(attend_kernel, plan, sets, spans, tile,...  4.02 us
    pallas_call x1, Pallas kernels, project(): pl.pallas_call(functools.partial(project_kernel, count, rows, heads, chun...  2.53 us
    pallas_call x1, Pallas kernels, prepare(): pl.pallas_call(functools.partial(prepare_kernel, sets, block), in_specs=[...  1.73 us
    unnamed x9, local copies, waits for them, and re-layouts  0.89 us
  transfers between devices with their start and end apart: 14, of which 4 were waited for; matrix products, arithmetic and copies ran while one was open for 0% of the time, Pallas kernels for 18%

profile of v7, /device:TPU:0, one launch (start us, length us, event | category | flops | bytes accessed | tf_op | source)
XLA Modules:
  0.0 35.8 jit_solution(12290619535929809916)
XLA Ops:
  0.6 0.0 copy-start
  0.6 0.0 copy-start.3
  0.7 0.9 %copy-done = bf16[32,2048]{1,0:T(8,128)(2,1)S(1)} copy-done((bf16[32,2048]{1,0:T(8,128)(2,1)S(1)}, bf16[32,2048]{1,0:T(8,128)(2,1)}, u32[]{:S(2)}) %copy-start) | copy-done | bytes 131096
  1.5 4.0 %collective-permute-start = (bf16[32,512]{1,0:T(8,128)(2,1)S(1)}, bf16[32,512]{1,0:T(8,128)(2,1)S(1)}, u32[]{:S(2)}, u32[]{:S(2)}) collective-permute-start(bf16[32,512]{1,0:T(8,128)(2,1)S(1)} %constant_dynamic-slice_fusion), channel_id=1, source_target_pairs={{0,2},{1,3},{2,0},{3,1},{4,6},{5,7},{6,4},{7,5},{8,10},{9,11},{10,... | collective-permute-start | bytes 98312 | tf_op jit(solution)/shard_map/ppermute | solution.py:43
  5.6 2.5 %project.1 = (f32[256,128]{1,0:T(8,128)S(1)}, f32[64,128]{1,0:T(8,128)S(1)}, bf16[272,128]{1,0:T(8,128)(2,1)S(1)}, bf16[272,128]{1,0:T(8,128)(2,1)S(1)}, bf16[272,128]{1,0:T(8,128)(2,1)S(1)}) custom-call(bf16[256,2048]{1,0:T(8,128)(2,1)} %hidden_ref.1, bf16[16,128]{1,0:T(8,128)(2,1)} %bitcast.6, bf16[2048,512]{1,0:T(8,128)(2,1)} %weight_ref.1), custom_call_target="tpu_custom_call" | custom-call | flops 536870912 | bytes 3145728 | tf_op jit(solution)/shard_map/project/pallas_call | solution.py:136
  8.1 1.4 %collective-permute-start.1 = (bf16[272,128]{1,0:T(8,128)(2,1)S(1)}, bf16[272,128]{1,0:T(8,128)(2,1)S(1)}, u32[]{:S(2)}, u32[]{:S(2)}) collective-permute-start(bf16[272,128]{1,0:T(8,128)(2,1)S(1)} %get-tuple-element.29), channel_id=1, source_target_pairs={{0,3},{1,2},{2,1},{3,0},{4,7},{5,6},{6,5},{7,4},{8,11},{9,10},{10,... | collective-permute-start | bytes 208904 | tf_op jit(solution)/shard_map/ppermute | solution.py:43
  9.5 1.7 %collective-permute-start.2 = (bf16[272,128]{1,0:T(8,128)(2,1)S(1)}, bf16[272,128]{1,0:T(8,128)(2,1)S(1)}, u32[]{:S(2)}, u32[]{:S(2)}) collective-permute-start(bf16[272,128]{1,0:T(8,128)(2,1)S(1)} %get-tuple-element.30), channel_id=1, source_target_pairs={{0,2},{1,3},{2,0},{3,1},{4,6},{5,7},{6,4},{7,5},{8,10},{9,11},{10,... | collective-permute-start | bytes 208904 | tf_op jit(solution)/shard_map/ppermute | solution.py:43
  11.2 1.3 %collective-permute-start.3 = (bf16[272,128]{1,0:T(8,128)(2,1)S(1)}, bf16[272,128]{1,0:T(8,128)(2,1)S(1)}, u32[]{:S(2)}, u32[]{:S(2)}) collective-permute-start(bf16[272,128]{1,0:T(8,128)(2,1)S(1)} %get-tuple-element.31), channel_id=1, source_target_pairs={{0,1},{1,0},{2,3},{3,2},{4,5},{5,4},{6,7},{7,6},{8,9},{9,8},{10,11... | collective-permute-start | bytes 208904 | tf_op jit(solution)/shard_map/ppermute | solution.py:43
  12.6 0.0 collective-permute-done
  12.6 0.7 %collective-permute-start.4 = (bf16[64,512]{1,0:T(8,128)(2,1)S(1)}, bf16[64,512]{1,0:T(8,128)(2,1)S(1)}, u32[]{:S(2)}, u32[]{:S(2)}) collective-permute-start(bf16[64,512]{1,0:T(8,128)(2,1)S(1)} %pad_maximum_fusion.4), channel_id=1, source_target_pairs={{0,1},{1,0},{2,3},{3,2},{4,5},{5,4},{6,7},{7,6},{8,9},{9,8},{10,11... | collective-permute-start | bytes 196616 | tf_op jit(solution)/shard_map/ppermute | solution.py:43
  14.7 1.7 %prepare.1 = (f32[64,128]{1,0:T(8,128)S(1)}, f32[64,128]{1,0:T(8,128)S(1)}, bf16[4096,128]{1,0:T(8,128)(2,1)S(1)}, f32[8,8,512]{2,1,0:T(8,128)S(1)}, f32[8,128,512]{2,1,0:T(8,128)S(1)}) custom-call(s32[1]{0:T(128)S(6)} %copy.12.offset_ref, s32[1]{0:T(128)S(6)} %copy.13.length_ref, f32[1,128]{1,0:T(1,128)S(1)} %copy-done.3, bf16[64,8192]{1,0:T(8,128)(2,1)S(1)} %bitcast.4, ...), custom_call_target="tpu_custom_call" | custom-call | tf_op jit(solution)/shard_map/prepare/pallas_call | solution.py:229
  16.4 1.0 %collective-permute-done.2.rest_1_ = bf16[272,128]{1,0:T(8,128)(2,1)S(1)} collective-permute-done((bf16[272,128]{1,0:T(8,128)(2,1)S(1)}, bf16[272,128]{1,0:T(8,128)(2,1)S(1)}, u32[]{:S(2)}, u32[]{:S(2)}) %collective-permute-start.2) | collective-permute-done | bytes 69664 | tf_op jit(solution)/shard_map/ppermute | solution.py:43
  17.4 0.2 combine.1.rest_0_.rest_5_
  17.6 0.4 %collective-permute-done.4 = bf16[64,512]{1,0:T(8,128)(2,1)S(1)} collective-permute-done((bf16[64,512]{1,0:T(8,128)(2,1)S(1)}, bf16[64,512]{1,0:T(8,128)(2,1)S(1)}, u32[]{:S(2)}, u32[]{:S(2)}) %collective-permute-start.4) | collective-permute-done | bytes 65568 | tf_op jit(solution)/shard_map/ppermute | solution.py:43
  18.1 1.4 %collective-permute-start.9 = (bf16[64,512]{1,0:T(8,128)(2,1)S(1)}, bf16[64,512]{1,0:T(8,128)(2,1)S(1)}, u32[]{:S(2)}, u32[]{:S(2)}) collective-permute-start(bf16[64,512]{1,0:T(8,128)(2,1)S(1)} %combine.1.rest_0_.rest_5_), channel_id=1, source_target_pairs={{0,3},{1,2},{2,1},{3,0},{4,7},{5,6},{6,5},{7,4},{8,11},{9,10},{10,... | collective-permute-start | bytes 196616 | tf_op jit(solution)/shard_map/ppermute | solution.py:43
  19.5 1.5 %collective-permute-start.5 = (bf16[64,512]{1,0:T(8,128)(2,1)S(1)}, bf16[64,512]{1,0:T(8,128)(2,1)S(1)}, u32[]{:S(2)}, u32[]{:S(2)}) collective-permute-start(bf16[64,512]{1,0:T(8,128)(2,1)S(1)} %combine.1.rest_0_.rest_5_), channel_id=1, source_target_pairs={{0,8},{4,12},{8,0},{12,4},{1,9},{5,13},{9,1},{13,5},{2,10},{6,14},... | collective-permute-start | bytes 196616 | tf_op jit(solution)/shard_map/ppermute | solution.py:43
  21.0 0.5 %collective-permute-start.12 = (bf16[128,512]{1,0:T(8,128)(2,1)S(1)}, bf16[128,512]{1,0:T(8,128)(2,1)S(1)}, u32[]{:S(2)}, u32[]{:S(2)}) collective-permute-start(bf16[128,512]{1,0:T(8,128)(2,1)S(1)} %pad_maximum_fusion.3.rest_0_), channel_id=1, source_target_pairs={{0,8},{4,12},{8,0},{12,4},{1,9},{5,13},{9,1},{13,5},{2,10},{6,14},... | collective-permute-start | bytes 393224 | tf_op jit(solution)/shard_map/ppermute | solution.py:43
  21.5 2.9 %collective-permute-done.5.rest_1_ = bf16[64,512]{1,0:T(8,128)(2,1)S(1)} collective-permute-done((bf16[64,512]{1,0:T(8,128)(2,1)S(1)}, bf16[64,512]{1,0:T(8,128)(2,1)S(1)}, u32[]{:S(2)}, u32[]{:S(2)}) %collective-permute-start.5) | collective-permute-done | bytes 65568 | tf_op jit(solution)/shard_map/ppermute | solution.py:43
  24.4 0.2 collective-permute-start.6
  24.6 2.2 %collective-permute-start.7 = (bf16[128,512]{1,0:T(8,128)(2,1)S(1)}, bf16[128,512]{1,0:T(8,128)(2,1)S(1)}, u32[]{:S(2)}, u32[]{:S(2)}) collective-permute-start(bf16[128,512]{1,0:T(8,128)(2,1)S(1)} %constant_dynamic-update-slice_fusion), channel_id=1, source_target_pairs={{0,1},{1,0},{2,3},{3,2},{4,5},{5,4},{6,7},{7,6},{8,9},{9,8},{10,11... | collective-permute-start | bytes 393224 | tf_op jit(solution)/shard_map/ppermute | solution.py:43
  26.8 1.5 %collective-permute-start.10 = (bf16[64,512]{1,0:T(8,128)(2,1)S(1)}, bf16[64,512]{1,0:T(8,128)(2,1)S(1)}, u32[]{:S(2)}, u32[]{:S(2)}) collective-permute-start(bf16[64,512]{1,0:T(8,128)(2,1)S(1)} %collective-permute-done.9.rest_2_), channel_id=1, source_target_pairs={{0,8},{4,12},{8,0},{12,4},{1,9},{5,13},{9,1},{13,5},{2,10},{6,14},... | collective-permute-start | bytes 196616 | tf_op jit(solution)/shard_map/ppermute | solution.py:43
  28.3 0.0 collective-permute-done.12.rest_1_
  28.3 0.1 collective-permute-start.13
  28.4 2.7 %collective-permute-done.10.rest_3_ = bf16[64,512]{1,0:T(8,128)(2,1)S(1)} collective-permute-done((bf16[64,512]{1,0:T(8,128)(2,1)S(1)}, bf16[64,512]{1,0:T(8,128)(2,1)S(1)}, u32[]{:S(2)}, u32[]{:S(2)}) %collective-permute-start.10) | collective-permute-done | bytes 65568 | tf_op jit(solution)/shard_map/ppermute | solution.py:43
  31.1 0.1 collective-permute-start.11
  31.2 0.0 collective-permute-done.7.rest_1_
  31.2 0.5 %collective-permute-start.8 = (bf16[256,512]{1,0:T(8,128)(2,1)S(1)}, bf16[256,512]{1,0:T(8,128)(2,1)S(1)}, u32[]{:S(2)}, u32[]{:S(2)}) collective-permute-start(bf16[256,512]{1,0:T(8,128)(2,1)S(1)} %pad_maximum_fusion), channel_id=1, source_target_pairs={{0,4},{4,0},{8,12},{12,8},{1,5},{5,1},{9,13},{13,9},{2,6},{6,2},{1... | collective-permute-start | bytes 786440 | tf_op jit(solution)/shard_map/ppermute | solution.py:43
  31.8 0.0 collective-permute-done.13.rest_2_
  31.8 1.1 %attend_more.2 = (f32[8,8,512]{2,1,0:T(8,128)S(1)}, f32[8,128,512]{2,1,0:T(8,128)S(1)}) custom-call(s32[1]{0:T(128)S(6)} %copy.12.offset_ref, s32[1]{0:T(128)S(6)} %copy.13.length_ref, bf16[4096,128]{1,0:T(8,128)(2,1)S(1)} %get-tuple-element.25.query_ref, bf16[128,512]{1,0:T(8,128)(2,1)S(1)} %pad_maximum_fusion.3.rest_0_, ...), custom_call_target="tpu_custom_call" | custom-call | tf_op jit(solution)/shard_map/attend_more/pallas_call | solution.py:374
  32.8 1.0 %attend_more.3 = (f32[8,8,512]{2,1,0:T(8,128)S(1)}, f32[8,128,512]{2,1,0:T(8,128)S(1)}) custom-call(s32[1]{0:T(128)S(6)} %copy.12.offset_ref, s32[1]{0:T(128)S(6)} %copy.13.length_ref, bf16[4096,128]{1,0:T(8,128)(2,1)S(1)} %get-tuple-element.25.query_ref, bf16[64,512]{1,0:T(8,128)(2,1)S(1)} %combine.1.rest_0_.rest_5_, ...), custom_call_target="tpu_custom_call" | custom-call | tf_op jit(solution)/shard_map/attend_more/pallas_call | solution.py:374
  33.8 0.0 collective-permute-done.8.rest_2_
  33.9 2.0 %attend_last.1 = (bf16[64,8192]{1,0:T(8,128)(2,1)}, bf16[64,512]{1,0:T(8,128)(2,1)}) custom-call(s32[1]{0:T(128)S(6)} %copy.12.offset_ref, s32[1]{0:T(128)S(6)} %copy.13.length_ref, bf16[4096,128]{1,0:T(8,128)(2,1)S(1)} %get-tuple-element.25.query_ref, bf16[128,512]{1,0:T(8,128)(2,1)S(1)} %collective-permute-done.6.rest_0_, ...), custom_call_target="tpu_custom_call" | custom-call | tf_op jit(solution)/shard_map/attend_last/pallas_call | solution.py:374
  (18 shorter events, 0.1 us)
Async XLA Ops:
  0.6 0.9 %copy-start = (bf16[32,2048]{1,0:T(8,128)(2,1)S(1)}, bf16[32,2048]{1,0:T(8,128)(2,1)}, u32[]{:S(2)}) copy-start(bf16[32,2048]{1,0:T(8,128)(2,1)} %param.12) | copy-start | bytes 393220
  0.6 14.0 %copy-start.3 = (f32[1,128]{1,0:T(1,128)S(1)}, f32[1,128]{1,0:T(1,128)}, u32[]{:S(2)}) copy-start(f32[1,128]{1,0:T(1,128)} %constant.13.clone.frequency_ref) | copy-start | bytes 1540
  0.7 14.0 %copy-start.1 = (bf16[1,64,8192]{2,1,0:T(8,128)(2,1)S(1)}, bf16[1,64,8192]{2,1,0:T(8,128)(2,1)}, u32[]{:S(2)}) copy-start(bf16[1,64,8192]{2,1,0:T(8,128)(2,1)} %param.14) | copy-start | bytes 3145732
  0.7 14.0 %copy-start.2 = (bf16[1,64,2048]{2,1,0:T(8,128)(2,1)S(1)}, bf16[1,64,2048]{2,1,0:T(8,128)(2,1)}, u32[]{:S(2)}) copy-start(bf16[1,64,2048]{2,1,0:T(8,128)(2,1)} %param.15) | copy-start | bytes 786436
  1.5 11.0 %collective-permute-start = (bf16[32,512]{1,0:T(8,128)(2,1)S(1)}, bf16[32,512]{1,0:T(8,128)(2,1)S(1)}, u32[]{:S(2)}, u32[]{:S(2)}) collective-permute-start(bf16[32,512]{1,0:T(8,128)(2,1)S(1)} %constant_dynamic-slice_fusion), channel_id=1, source_target_pairs={{0,2},{1,3},{2,0},{3,1},{4,6},{5,7},{6,4},{7,5},{8,10},{9,11},{10,... | collective-permute-start | bytes 98312 | tf_op jit(solution)/shard_map/ppermute | solution.py:43
  8.1 8.3 %collective-permute-start.1 = (bf16[272,128]{1,0:T(8,128)(2,1)S(1)}, bf16[272,128]{1,0:T(8,128)(2,1)S(1)}, u32[]{:S(2)}, u32[]{:S(2)}) collective-permute-start(bf16[272,128]{1,0:T(8,128)(2,1)S(1)} %get-tuple-element.29), channel_id=1, source_target_pairs={{0,3},{1,2},{2,1},{3,0},{4,7},{5,6},{6,5},{7,4},{8,11},{9,10},{10,... | collective-permute-start | bytes 208904 | tf_op jit(solution)/shard_map/ppermute | solution.py:43
  9.5 7.9 %collective-permute-start.2 = (bf16[272,128]{1,0:T(8,128)(2,1)S(1)}, bf16[272,128]{1,0:T(8,128)(2,1)S(1)}, u32[]{:S(2)}, u32[]{:S(2)}) collective-permute-start(bf16[272,128]{1,0:T(8,128)(2,1)S(1)} %get-tuple-element.30), channel_id=1, source_target_pairs={{0,2},{1,3},{2,0},{3,1},{4,6},{5,7},{6,4},{7,5},{8,10},{9,11},{10,... | collective-permute-start | bytes 208904 | tf_op jit(solution)/shard_map/ppermute | solution.py:43
  11.2 6.2 %collective-permute-start.3 = (bf16[272,128]{1,0:T(8,128)(2,1)S(1)}, bf16[272,128]{1,0:T(8,128)(2,1)S(1)}, u32[]{:S(2)}, u32[]{:S(2)}) collective-permute-start(bf16[272,128]{1,0:T(8,128)(2,1)S(1)} %get-tuple-element.31), channel_id=1, source_target_pairs={{0,1},{1,0},{2,3},{3,2},{4,5},{5,4},{6,7},{7,6},{8,9},{9,8},{10,11... | collective-permute-start | bytes 208904 | tf_op jit(solution)/shard_map/ppermute | solution.py:43
  12.6 5.5 %collective-permute-start.4 = (bf16[64,512]{1,0:T(8,128)(2,1)S(1)}, bf16[64,512]{1,0:T(8,128)(2,1)S(1)}, u32[]{:S(2)}, u32[]{:S(2)}) collective-permute-start(bf16[64,512]{1,0:T(8,128)(2,1)S(1)} %pad_maximum_fusion.4), channel_id=1, source_target_pairs={{0,1},{1,0},{2,3},{3,2},{4,5},{5,4},{6,7},{7,6},{8,9},{9,8},{10,11... | collective-permute-start | bytes 196616 | tf_op jit(solution)/shard_map/ppermute | solution.py:43
  18.1 8.7 %collective-permute-start.9 = (bf16[64,512]{1,0:T(8,128)(2,1)S(1)}, bf16[64,512]{1,0:T(8,128)(2,1)S(1)}, u32[]{:S(2)}, u32[]{:S(2)}) collective-permute-start(bf16[64,512]{1,0:T(8,128)(2,1)S(1)} %combine.1.rest_0_.rest_5_), channel_id=1, source_target_pairs={{0,3},{1,2},{2,1},{3,0},{4,7},{5,6},{6,5},{7,4},{8,11},{9,10},{10,... | collective-permute-start | bytes 196616 | tf_op jit(solution)/shard_map/ppermute | solution.py:43
  19.5 4.9 %collective-permute-start.5 = (bf16[64,512]{1,0:T(8,128)(2,1)S(1)}, bf16[64,512]{1,0:T(8,128)(2,1)S(1)}, u32[]{:S(2)}, u32[]{:S(2)}) collective-permute-start(bf16[64,512]{1,0:T(8,128)(2,1)S(1)} %combine.1.rest_0_.rest_5_), channel_id=1, source_target_pairs={{0,8},{4,12},{8,0},{12,4},{1,9},{5,13},{9,1},{13,5},{2,10},{6,14},... | collective-permute-start | bytes 196616 | tf_op jit(solution)/shard_map/ppermute | solution.py:43
  21.0 7.3 %collective-permute-start.12 = (bf16[128,512]{1,0:T(8,128)(2,1)S(1)}, bf16[128,512]{1,0:T(8,128)(2,1)S(1)}, u32[]{:S(2)}, u32[]{:S(2)}) collective-permute-start(bf16[128,512]{1,0:T(8,128)(2,1)S(1)} %pad_maximum_fusion.3.rest_0_), channel_id=1, source_target_pairs={{0,8},{4,12},{8,0},{12,4},{1,9},{5,13},{9,1},{13,5},{2,10},{6,14},... | collective-permute-start | bytes 393224 | tf_op jit(solution)/shard_map/ppermute | solution.py:43
  24.4 6.7 %collective-permute-start.6 = (bf16[128,512]{1,0:T(8,128)(2,1)S(1)}, bf16[128,512]{1,0:T(8,128)(2,1)S(1)}, u32[]{:S(2)}, u32[]{:S(2)}) collective-permute-start(bf16[128,512]{1,0:T(8,128)(2,1)S(1)} %constant_dynamic-update-slice_fusion), channel_id=1, source_target_pairs={{0,2},{1,3},{2,0},{3,1},{4,6},{5,7},{6,4},{7,5},{8,10},{9,11},{10,... | collective-permute-start | bytes 393224 | tf_op jit(solution)/shard_map/ppermute | solution.py:43
  24.6 6.6 %collective-permute-start.7 = (bf16[128,512]{1,0:T(8,128)(2,1)S(1)}, bf16[128,512]{1,0:T(8,128)(2,1)S(1)}, u32[]{:S(2)}, u32[]{:S(2)}) collective-permute-start(bf16[128,512]{1,0:T(8,128)(2,1)S(1)} %constant_dynamic-update-slice_fusion), channel_id=1, source_target_pairs={{0,1},{1,0},{2,3},{3,2},{4,5},{5,4},{6,7},{7,6},{8,9},{9,8},{10,11... | collective-permute-start | bytes 393224 | tf_op jit(solution)/shard_map/ppermute | solution.py:43
  26.8 4.3 %collective-permute-start.10 = (bf16[64,512]{1,0:T(8,128)(2,1)S(1)}, bf16[64,512]{1,0:T(8,128)(2,1)S(1)}, u32[]{:S(2)}, u32[]{:S(2)}) collective-permute-start(bf16[64,512]{1,0:T(8,128)(2,1)S(1)} %collective-permute-done.9.rest_2_), channel_id=1, source_target_pairs={{0,8},{4,12},{8,0},{12,4},{1,9},{5,13},{9,1},{13,5},{2,10},{6,14},... | collective-permute-start | bytes 196616 | tf_op jit(solution)/shard_map/ppermute | solution.py:43
  28.3 3.4 %collective-permute-start.13 = (bf16[256,512]{1,0:T(8,128)(2,1)S(1)}, bf16[256,512]{1,0:T(8,128)(2,1)S(1)}, u32[]{:S(2)}, u32[]{:S(2)}) collective-permute-start(bf16[256,512]{1,0:T(8,128)(2,1)S(1)} %pad_maximum_fusion.2), channel_id=1, source_target_pairs={{0,4},{4,0},{8,12},{12,8},{1,5},{5,1},{9,13},{13,9},{2,6},{6,2},{1... | collective-permute-start | bytes 786440 | tf_op jit(solution)/shard_map/ppermute | solution.py:43
  31.1 1.7 %collective-permute-start.11 = (bf16[256,512]{1,0:T(8,128)(2,1)S(1)}, bf16[256,512]{1,0:T(8,128)(2,1)S(1)}, u32[]{:S(2)}, u32[]{:S(2)}) collective-permute-start(bf16[256,512]{1,0:T(8,128)(2,1)S(1)} %pad_maximum_fusion.1), channel_id=1, source_target_pairs={{0,4},{4,0},{8,12},{12,8},{1,5},{5,1},{9,13},{13,9},{2,6},{6,2},{1... | collective-permute-start | bytes 786440 | tf_op jit(solution)/shard_map/ppermute | solution.py:43
  31.2 2.6 %collective-permute-start.8 = (bf16[256,512]{1,0:T(8,128)(2,1)S(1)}, bf16[256,512]{1,0:T(8,128)(2,1)S(1)}, u32[]{:S(2)}, u32[]{:S(2)}) collective-permute-start(bf16[256,512]{1,0:T(8,128)(2,1)S(1)} %pad_maximum_fusion), channel_id=1, source_target_pairs={{0,4},{4,0},{8,12},{12,8},{1,5},{5,1},{9,13},{13,9},{2,6},{6,2},{1... | collective-permute-start | bytes 786440 | tf_op jit(solution)/shard_map/ppermute | solution.py:43

commit v8 on v7

--- a/solution.py
+++ b/solution.py
@@ -61,14 +61,18 @@
     return lax.broadcasted_iota(jnp.int32, shape, 0) == lax.broadcasted_iota(jnp.int32, shape, 1)
 
 
-def project_kernel(count, rows, heads, chunks, hidden_ref, gain_ref, weight_ref, *rest):
-    own_ref, square_ref = rest[:2]
-    sends = rest[2 : 1 + count]
-    hidden_buf, gain_buf, weight_buf, total, squares, sems = rest[1 + count :]
+def project_kernel(count, rows, heads, chunks, hidden_ref, gain_ref, weight_ref, prompt_ref, *rest):
+    own_ref, square_ref, mine_ref = rest[:3]
+    sends = rest[3 : 2 + count]
+    hidden_buf, gain_buf, weight_buf, total, squares, sems = rest[2 + count :]
     depth = hidden_ref.shape[1]
     size = depth // chunks
+    width = weight_ref.shape[1]
+    cached = prompt_ref.shape[0]
     gain_copy = pltpu.make_async_copy(gain_ref, gain_buf, sems.at[2 * chunks])
     gain_copy.start()
+    columns = pl.ds(pl.multiple_of(lax.axis_index("set") * width, HEAD_SIZE), width)
+    prompt_copy = pltpu.make_async_copy(prompt_ref.at[:, columns], mine_ref, sems.at[2 * chunks + 1])
     copies = []
     for c in range(chunks):
         part = pl.ds(c * size, size)
@@ -80,6 +84,7 @@
         )
         copies[-1][0].start()
         copies[-1][1].start()
+    prompt_copy.start()
     gain_copy.wait()
     for c in range(chunks):
         copies[c][0].wait()
@@ -102,6 +107,7 @@
         else:
             total[...] += part
             squares[...] += folded
+    prompt_copy.wait()
     me = lax.axis_index("seq")
     for k in range(count):
         to = pl.ds(pl.multiple_of(peer(me, k, count) * rows, rows), rows)
@@ -117,25 +123,30 @@
             which = lax.broadcasted_iota(jnp.int32, (16, HEAD_SIZE), 0)
             tail = jnp.where(which == 0, high, jnp.where(which == 1, low, 0.0))
             out[heads * rows : heads * rows + 16, :] = tail.astype(BF16)
+            for h in range(heads):
+                first = heads * rows + 16 + h * cached
+                out[first : first + cached, :] = mine_ref[:, h * HEAD_SIZE : (h + 1) * HEAD_SIZE]
         for h in range(heads):
             piece = total[to, h * HEAD_SIZE : (h + 1) * HEAD_SIZE]
             out[h * rows : (h + 1) * rows, :] = piece.astype(out.dtype)
 
 
-def project(span_hidden, norm_gain, key_value_weight, count):
+def project(span_hidden, norm_gain, key_value_weight, prompt_rows, count):
     length, depth = span_hidden.shape
     width = key_value_weight.shape[1]
     rows, heads = length // count, width // HEAD_SIZE
+    cached = prompt_rows.shape[0]
     chunks = 4 if depth % (4 * HEAD_SIZE) == 0 else 1
     gain = norm_gain.reshape(-1, HEAD_SIZE)
     outs = [
         jax.ShapeDtypeStruct((heads * rows, HEAD_SIZE), F32),
         jax.ShapeDtypeStruct((rows, HEAD_SIZE), F32),
-    ] + [jax.ShapeDtypeStruct((heads * rows + 16, HEAD_SIZE), BF16)] * (count - 1)
-    stay = [pltpu.with_memory_space_constraint(x, pltpu.HBM) for x in (span_hidden, gain, key_value_weight)]
+        jax.ShapeDtypeStruct((cached, width), BF16),
+    ] + [jax.ShapeDtypeStruct((heads * (rows + cached) + 16, HEAD_SIZE), BF16)] * (count - 1)
+    stay = [pltpu.with_memory_space_constraint(x, pltpu.HBM) for x in (span_hidden, gain, key_value_weight, prompt_rows)]
     return pl.pallas_call(
         functools.partial(project_kernel, count, rows, heads, chunks),
-        in_specs=[HBM, HBM, HBM],
+        in_specs=[HBM, HBM, HBM, HBM],
         out_shape=outs,
         out_specs=[VMEM] * len(outs),
         scratch_shapes=[
@@ -144,7 +155,7 @@
             pltpu.VMEM((depth, width), BF16),
             pltpu.VMEM((length, width), F32),
             pltpu.VMEM((length, HEAD_SIZE), F32),
-            pltpu.SemaphoreType.DMA((2 * chunks + 1,)),
+            pltpu.SemaphoreType.DMA((2 * chunks + 2,)),
         ],
         compiler_params=pltpu.CompilerParams(vmem_limit_bytes=16 << 20),
         cost_estimate=pl.CostEstimate(
@@ -154,37 +165,50 @@
     )(*stay)
 
 
-def combine_kernel(rows, heads, own_ref, square_ref, cosine_ref, sine_ref, *rest):
-    got, out_ref = rest[:-1], rest[-1]
-    first = lax.axis_index("set") * heads
+def combine_kernel(rows, heads, own_ref, square_ref, mine_ref, cosine_ref, sine_ref, *rest):
+    got, (send_ref, prompt_ref) = rest[:-2], rest[-2:]
+    cached = mine_ref.shape[0]
+    count = 1 + len(got)
+    me, first = lax.axis_index("seq"), lax.axis_index("set") * heads
+
+    def prompt_rows(k):
+        return pl.ds(pl.multiple_of(source(me, k, count) * cached, 16), cached)
+
     line = jnp.zeros((1, HEAD_SIZE), F32)
     for ref in got:
-        tail = ref[heads * rows :, :].astype(F32)
+        tail = ref[heads * rows : heads * rows + 16, :].astype(F32)
         line = line + tail[0:1, :] + tail[1:2, :]
     column = jnp.sum(jnp.where(diagonal(rows), line, 0.0), axis=1, keepdims=True)
     scale = lax.rsqrt((square_ref[...] + column) / MODEL_WIDTH + EPS)
     cosine, sine = cosine_ref[...], sine_ref[...]
     for h in range(heads):
         span = slice(h * rows, (h + 1) * rows)
+        lanes = slice(h * HEAD_SIZE, (h + 1) * HEAD_SIZE)
         value = own_ref[span, :]
         for ref in got:
             value = value + ref[span, :].astype(F32)
         value = value * scale
-        out = jnp.where(first + h < KEY_HEADS, turn(value, cosine, sine), value)
-        out_ref[:, h * HEAD_SIZE : (h + 1) * HEAD_SIZE] = out.astype(BF16)
-
-
-def combine(own, square, cosine, sine, got):
+        out = jnp.where(first + h < KEY_HEADS, turn(value, cosine, sine), value).astype(BF16)
+        send_ref[:, lanes] = out
+        for i, ref in enumerate(got):
+            start = heads * rows + 16 + h * cached
+            prompt_ref[prompt_rows(count - 1 - i), lanes] = ref[start : start + cached, :]
+    prompt_ref[prompt_rows(0), :] = mine_ref[...]
+
+
+def combine(own, square, mine, cosine, sine, got):
     rows = square.shape[0]
     heads = own.shape[0] // rows
+    block = pltpu.VMEM((rows, heads * HEAD_SIZE), BF16)
+    prompt = jax.ShapeDtypeStruct(((1 + len(got)) * mine.shape[0], heads * HEAD_SIZE), BF16)
     return pl.pallas_call(
         functools.partial(combine_kernel, rows, heads),
-        in_specs=[VMEM] * (4 + len(got)),
-        out_shape=pltpu.VMEM((rows, heads * HEAD_SIZE), BF16),
-        out_specs=VMEM,
+        in_specs=[VMEM] * (5 + len(got)),
+        out_shape=[block, prompt],
+        out_specs=[VMEM, VMEM],
         compiler_params=pltpu.CompilerParams(vmem_limit_bytes=4 << 20),
         name="combine",
-    )(own, square, cosine, sine, *got)
+    )(own, square, mine, cosine, sine, *got)
 
 
 def prepare_kernel(
@@ -211,7 +235,7 @@
         turned = turn(query_ref[:, span].astype(F32), cosine, sine)
         query_out[h * tokens : (h + 1) * tokens, :] = turned.astype(BF16)
     attend_kernel(
-        None, sets, [(tokens, ())], tile, False, offset_ref, length_ref, query_out, key_buf, value_buf, state_out, mixed_out
+        None, sets, [(tokens, False)], tile, False, offset_ref, length_ref, query_out, key_buf, value_buf, state_out, mixed_out
     )
 
 
@@ -258,18 +282,11 @@
         place = lax.broadcasted_iota(jnp.int32, (tokens, tokens), 0)
         token = lax.broadcasted_iota(jnp.int32, (tokens, tokens), 1)
         bias = jnp.concatenate([jnp.where(place <= token, 0.0, NEGATIVE_LARGE)] * (tile // tokens), axis=1)
-    elif any(leaps for _, leaps in spans):
+    elif any(prompt for _, prompt in spans):
         parts = []
-        for rows, leaps in spans:
+        for rows, prompt in spans:
             place = lax.broadcasted_iota(jnp.int32, (rows, HEAD_SIZE), 0)
-            dead = jnp.zeros(place.shape, F32)
-            if leaps:
-                size = rows // len(leaps)
-                for i, step in enumerate(leaps):
-                    first = source(lax.axis_index("seq"), step, len(leaps)) * size - i * size
-                    here = (place >= i * size) & (place < (i + 1) * size)
-                    dead = jnp.where(here & (place + first >= offset), NEGATIVE_LARGE, dead)
-            parts.append(dead)
+            parts.append(jnp.where(place < offset, 0.0, NEGATIVE_LARGE) if prompt else jnp.zeros(place.shape, F32))
         bias = jnp.concatenate([jnp.concatenate(parts, axis=0)] * (tile // HEAD_SIZE), axis=1)
     keep = lax.broadcasted_iota(jnp.int32, (tokens, HEAD_SIZE), 0) < length
     units = [(g, start) for g in range(KEY_HEADS) for start in range(0, block, tile)]
@@ -396,29 +413,14 @@
     rows = span_hidden.shape[0] // count
     low = 2 if sets % 2 == 0 else 1
 
+    own, square, mine, *sends = project(span_hidden, norm_gain, key_value_weight, prompt_key_value, count)
     order = list(range(count - 1, 0, -1))
-    my_set, width = lax.axis_index("set"), key_value_weight.shape[1]
-    mine = lax.dynamic_slice_in_dim(prompt_key_value, my_set * width, width, 1)
-    doubling = count & (count - 1) == 0
-    leaps = [count >> i for i in range(1, count.bit_length())] if doubling else order
-    come = exchange(mine, "seq", leaps[0])
-
-    own, square, *sends = project(span_hidden, norm_gain, key_value_weight, count)
     got = [exchange(sends[k - 1], "seq", k) for k in order]
-
-    prompt, places = jnp.concatenate([mine, come], axis=0), [0, leaps[0]]
-    prompt, mine, _ = lax.optimization_barrier((prompt, mine, own))
-    cont_query, _ = lax.optimization_barrier((cont_query, prompt))
-    for k in leaps[1:]:
-        come = exchange(prompt if doubling else mine, "seq", k)
-        prompt = jnp.concatenate([prompt, come], axis=0)
-        places += [place ^ k for place in places] if doubling else [k]
 
     cosine, sine, query, *state = prepare(
         span_offset, cont_lengths, cont_query[0], continuation_key_value[0], sets, rows
     )
-    block = combine(own, square, cosine, sine, got)
-    block, prompt = lax.optimization_barrier((block, prompt))
+    block, prompt = combine(own, square, mine, cosine, sine, got)
 
     far = list(range(low, sets, low))
     steps = [0] + far
@@ -450,11 +452,11 @@
         return dict(plan=plan, pieces=pieces, spans=spans)
 
     ends = span_offset, cont_lengths
-    state = attend(*ends, query, sets, state=state, **share([prompts], [(prompt.shape[0], places)]))
+    state = attend(*ends, query, sets, state=state, **share([prompts], [(prompt.shape[0], True)]))
     near = stretches[: 1 + half]
-    state = attend(*ends, query, sets, state=state, **share(near, [(rows, ())] * len(near)))
+    state = attend(*ends, query, sets, state=state, **share(near, [(rows, False)] * len(near)))
     rest = stretches[1 + half :]
-    attended, block = attend(*ends, query, sets, state=state, last=block, **share(rest, [(rows, ())] * len(rest)))
+    attended, block = attend(*ends, query, sets, state=state, last=block, **share(rest, [(rows, False)] * len(rest)))
     return block, attended[None]
 
 

time: 36 us -> 35.8 us (level)
  waiting for transfers between devices: 7.03 us -> 10.4 us
  starting transfers between devices: 17.2 us -> 14.4 us
  local copies, waits for them, and re-layouts: 0.89 us -> 0.03 us
    ppermute x14 -> x12, waiting for transfers between devices: 7.03 us -> 10.4 us  [exchange(): lax.ppermute(value, axis, [(i, peer(i, step, count)) for i in range(count)])]
    ppermute x14 -> x12, starting transfers between devices: 17.2 us -> 14.4 us  [exchange(): lax.ppermute(value, axis, [(i, peer(i, step, count)) for i in range(count)])]
    unnamed x9 -> x7, local copies, waits for them, and re-layouts: 0.89 us -> 0.02 us
  transfers between devices with their start and end apart: 14 -> 12, of which waited for: 4 -> 4; matrix products, arithmetic and copies ran while one was open for 0% -> 0% of each run, Pallas kernels for 18% -> 11%
where the time goes in v8:
time: 35.8 us; the launch traced here: 35.6 us
  starting transfers between devices  14.4 us (40%)
  waiting for transfers between devices  10.4 us (29%)
  Pallas kernels  8.7 us (24%)
  between operations  2.09 us (6%)
    ppermute x12, starting transfers between devices, exchange(): lax.ppermute(value, axis, [(i, peer(i, step, count)) for i in range(count)])  14.4 us
    ppermute x12, waiting for transfers between devices, exchange(): lax.ppermute(value, axis, [(i, peer(i, step, count)) for i in range(count)])  10.4 us
    pallas_call x3, Pallas kernels, attend(): pl.pallas_call(functools.partial(attend_kernel, plan, sets, spans, tile,...  4.02 us
    pallas_call x1, Pallas kernels, project(): pl.pallas_call(functools.partial(project_kernel, count, rows, heads, chun...  2.73 us
    pallas_call x1, Pallas kernels, prepare(): pl.pallas_call(functools.partial(prepare_kernel, sets, block), in_specs=[...  1.74 us
  transfers between devices with their start and end apart: 12, of which 4 were waited for; matrix products, arithmetic and copies ran while one was open for 0% of the time, Pallas kernels for 11%

profile of v8, /device:TPU:0, one launch (start us, length us, event | category | flops | bytes accessed | tf_op | source)
XLA Modules:
  0.0 35.6 jit_solution(12196949872790778253)
XLA Ops:
  0.6 0.0 copy-start.2
  0.6 0.0 copy-start
  0.7 2.7 %project.1 = (f32[256,128]{1,0:T(8,128)S(1)}, f32[64,128]{1,0:T(8,128)S(1)}, bf16[32,512]{1,0:T(8,128)(2,1)S(1)}, bf16[400,128]{1,0:T(8,128)(2,1)S(1)}, bf16[400...) custom-call(bf16[256,2048]{1,0:T(8,128)(2,1)} %hidden_ref.1, bf16[16,128]{1,0:T(8,128)(2,1)} %bitcast.6, ...), custom_call_target="tpu_custom_call" | custom-call | flops 536870912 | bytes 3145728 | tf_op jit(solution)/shard_map/project/pallas_call | solution.py:147
  3.4 5.1 %collective-permute-start = (bf16[400,128]{1,0:T(8,128)(2,1)S(1)}, bf16[400,128]{1,0:T(8,128)(2,1)S(1)}, u32[]{:S(2)}, u32[]{:S(2)}) collective-permute-start(bf16[400,128]{1,0:T(8,128)(2,1)S(1)} %get-tuple-element.27), channel_id=1, source_target_pairs={{0,3},{1,2},{2,1},{3,0},{4,7},{5,6},{6,5},{7,4},{8,11},{9,10},{10,... | collective-permute-start | bytes 307208 | tf_op jit(solution)/shard_map/ppermute | solution.py:43
  8.5 0.0 collective-permute-start.1
  8.5 0.6 %collective-permute-start.2 = (bf16[400,128]{1,0:T(8,128)(2,1)S(1)}, bf16[400,128]{1,0:T(8,128)(2,1)S(1)}, u32[]{:S(2)}, u32[]{:S(2)}) collective-permute-start(bf16[400,128]{1,0:T(8,128)(2,1)S(1)} %get-tuple-element.29), channel_id=1, source_target_pairs={{0,1},{1,0},{2,3},{3,2},{4,5},{5,4},{6,7},{7,6},{8,9},{9,8},{10,11... | collective-permute-start | bytes 307208 | tf_op jit(solution)/shard_map/ppermute | solution.py:43
  10.5 1.7 %prepare.1 = (f32[64,128]{1,0:T(8,128)S(1)}, f32[64,128]{1,0:T(8,128)S(1)}, bf16[4096,128]{1,0:T(8,128)(2,1)S(1)}, f32[8,8,512]{2,1,0:T(8,128)S(1)}, f32[8,128,512]{2,1,0:T(8,128)S(1)}) custom-call(s32[1]{0:T(128)S(6)} %copy.12.offset_ref, s32[1]{0:T(128)S(6)} %copy.13.length_ref, f32[1,128]{1,0:T(1,128)S(1)} %copy-done.2, bf16[64,8192]{1,0:T(8,128)(2,1)S(1)} %bitcast.4, ...), custom_call_target="tpu_custom_call" | custom-call | tf_op jit(solution)/shard_map/prepare/pallas_call | solution.py:253
  12.2 0.1 collective-permute-done.rest_0_
  12.3 4.8 %collective-permute-done.1.rest_1_ = bf16[400,128]{1,0:T(8,128)(2,1)S(1)} collective-permute-done((bf16[400,128]{1,0:T(8,128)(2,1)S(1)}, bf16[400,128]{1,0:T(8,128)(2,1)S(1)}, u32[]{:S(2)}, u32[]{:S(2)}) %collective-permute-start.1) | collective-permute-done | bytes 102432 | tf_op jit(solution)/shard_map/ppermute | solution.py:43
  17.1 0.0 collective-permute-done.2.rest_2_
  17.1 0.2 combine.1
  17.4 2.5 %collective-permute-start.7 = (bf16[64,512]{1,0:T(8,128)(2,1)S(1)}, bf16[64,512]{1,0:T(8,128)(2,1)S(1)}, u32[]{:S(2)}, u32[]{:S(2)}) collective-permute-start(bf16[64,512]{1,0:T(8,128)(2,1)S(1)} %get-tuple-element.30.rest_0_.rest_5_), channel_id=1, source_target_pairs={{0,3},{1,2},{2,1},{3,0},{4,7},{5,6},{6,5},{7,4},{8,11},{9,10},{10,... | collective-permute-start | bytes 196616 | tf_op jit(solution)/shard_map/ppermute | solution.py:43
  19.9 1.5 %collective-permute-start.3 = (bf16[64,512]{1,0:T(8,128)(2,1)S(1)}, bf16[64,512]{1,0:T(8,128)(2,1)S(1)}, u32[]{:S(2)}, u32[]{:S(2)}) collective-permute-start(bf16[64,512]{1,0:T(8,128)(2,1)S(1)} %get-tuple-element.30.rest_0_.rest_5_), channel_id=1, source_target_pairs={{0,8},{4,12},{8,0},{12,4},{1,9},{5,13},{9,1},{13,5},{2,10},{6,14},... | collective-permute-start | bytes 196616 | tf_op jit(solution)/shard_map/ppermute | solution.py:43
  21.4 0.5 %collective-permute-start.10 = (bf16[128,512]{1,0:T(8,128)(2,1)S(1)}, bf16[128,512]{1,0:T(8,128)(2,1)S(1)}, u32[]{:S(2)}, u32[]{:S(2)}) collective-permute-start(bf16[128,512]{1,0:T(8,128)(2,1)S(1)} %get-tuple-element.31.rest_0_), channel_id=1, source_target_pairs={{0,8},{4,12},{8,0},{12,4},{1,9},{5,13},{9,1},{13,5},{2,10},{6,14},... | collective-permute-start | bytes 393224 | tf_op jit(solution)/shard_map/ppermute | solution.py:43
  21.9 2.3 %collective-permute-done.3.rest_1_ = bf16[64,512]{1,0:T(8,128)(2,1)S(1)} collective-permute-done((bf16[64,512]{1,0:T(8,128)(2,1)S(1)}, bf16[64,512]{1,0:T(8,128)(2,1)S(1)}, u32[]{:S(2)}, u32[]{:S(2)}) %collective-permute-start.3) | collective-permute-done | bytes 65568 | tf_op jit(solution)/shard_map/ppermute | solution.py:43
  24.2 0.0 collective-permute-start.4
  24.2 2.4 %collective-permute-start.5 = (bf16[128,512]{1,0:T(8,128)(2,1)S(1)}, bf16[128,512]{1,0:T(8,128)(2,1)S(1)}, u32[]{:S(2)}, u32[]{:S(2)}) collective-permute-start(bf16[128,512]{1,0:T(8,128)(2,1)S(1)} %constant_dynamic-update-slice_fusion), channel_id=1, source_target_pairs={{0,1},{1,0},{2,3},{3,2},{4,5},{5,4},{6,7},{7,6},{8,9},{9,8},{10,11... | collective-permute-start | bytes 393224 | tf_op jit(solution)/shard_map/ppermute | solution.py:43
  26.6 0.0 collective-permute-done.7.rest_2_
  26.6 1.0 %collective-permute-start.8 = (bf16[64,512]{1,0:T(8,128)(2,1)S(1)}, bf16[64,512]{1,0:T(8,128)(2,1)S(1)}, u32[]{:S(2)}, u32[]{:S(2)}) collective-permute-start(bf16[64,512]{1,0:T(8,128)(2,1)S(1)} %collective-permute-done.7.rest_2_), channel_id=1, source_target_pairs={{0,8},{4,12},{8,0},{12,4},{1,9},{5,13},{9,1},{13,5},{2,10},{6,14},... | collective-permute-start | bytes 196616 | tf_op jit(solution)/shard_map/ppermute | solution.py:43
  27.6 0.0 collective-permute-done.10.rest_1_
  27.6 0.1 collective-permute-start.11
  27.7 3.2 %collective-permute-done.8.rest_3_ = bf16[64,512]{1,0:T(8,128)(2,1)S(1)} collective-permute-done((bf16[64,512]{1,0:T(8,128)(2,1)S(1)}, bf16[64,512]{1,0:T(8,128)(2,1)S(1)}, u32[]{:S(2)}, u32[]{:S(2)}) %collective-permute-start.8) | collective-permute-done | bytes 65568 | tf_op jit(solution)/shard_map/ppermute | solution.py:43
  30.9 0.1 collective-permute-start.9
  31.0 0.0 collective-permute-done.4.rest_0_
  31.0 0.0 collective-permute-done.5.rest_1_
  31.0 0.5 %collective-permute-start.6 = (bf16[256,512]{1,0:T(8,128)(2,1)S(1)}, bf16[256,512]{1,0:T(8,128)(2,1)S(1)}, u32[]{:S(2)}, u32[]{:S(2)}) collective-permute-start(bf16[256,512]{1,0:T(8,128)(2,1)S(1)} %pad_maximum_fusion), channel_id=1, source_target_pairs={{0,4},{4,0},{8,12},{12,8},{1,5},{5,1},{9,13},{13,9},{2,6},{6,2},{1... | collective-permute-start | bytes 786440 | tf_op jit(solution)/shard_map/ppermute | solution.py:43
  31.5 0.0 collective-permute-done.11.rest_2_
  31.6 1.1 %attend_more.2 = (f32[8,8,512]{2,1,0:T(8,128)S(1)}, f32[8,128,512]{2,1,0:T(8,128)S(1)}) custom-call(s32[1]{0:T(128)S(6)} %copy.12.offset_ref, s32[1]{0:T(128)S(6)} %copy.13.length_ref, bf16[4096,128]{1,0:T(8,128)(2,1)S(1)} %get-tuple-element.21.query_ref, bf16[128,512]{1,0:T(8,128)(2,1)S(1)} %get-tuple-element.31.rest_0_, ...), custom_call_target="tpu_custom_call" | custom-call | tf_op jit(solution)/shard_map/attend_more/pallas_call | solution.py:391
  32.6 0.0 collective-permute-done.9.rest_4_
  32.6 1.0 %attend_more.3 = (f32[8,8,512]{2,1,0:T(8,128)S(1)}, f32[8,128,512]{2,1,0:T(8,128)S(1)}) custom-call(s32[1]{0:T(128)S(6)} %copy.12.offset_ref, s32[1]{0:T(128)S(6)} %copy.13.length_ref, bf16[4096,128]{1,0:T(8,128)(2,1)S(1)} %get-tuple-element.21.query_ref, bf16[64,512]{1,0:T(8,128)(2,1)S(1)} %get-tuple-element.30.rest_0_.rest_5_, ...), custom_call_target="tpu_custom_call" | custom-call | tf_op jit(solution)/shard_map/attend_more/pallas_call | solution.py:391
  33.6 0.0 collective-permute-done.6.rest_2_
  33.6 2.0 %attend_last.1 = (bf16[64,8192]{1,0:T(8,128)(2,1)}, bf16[64,512]{1,0:T(8,128)(2,1)}) custom-call(s32[1]{0:T(128)S(6)} %copy.12.offset_ref, s32[1]{0:T(128)S(6)} %copy.13.length_ref, bf16[4096,128]{1,0:T(8,128)(2,1)S(1)} %get-tuple-element.21.query_ref, bf16[128,512]{1,0:T(8,128)(2,1)S(1)} %collective-permute-done.4.rest_0_, ...), custom_call_target="tpu_custom_call" | custom-call | tf_op jit(solution)/shard_map/attend_last/pallas_call | solution.py:391
  (9 shorter events, 0.1 us)
Async XLA Ops:
  0.6 9.8 %copy-start.2 = (f32[1,128]{1,0:T(1,128)S(1)}, f32[1,128]{1,0:T(1,128)}, u32[]{:S(2)}) copy-start(f32[1,128]{1,0:T(1,128)} %constant.2.clone.frequency_ref) | copy-start | bytes 1540
  0.6 9.8 %copy-start = (bf16[1,64,8192]{2,1,0:T(8,128)(2,1)S(1)}, bf16[1,64,8192]{2,1,0:T(8,128)(2,1)}, u32[]{:S(2)}) copy-start(bf16[1,64,8192]{2,1,0:T(8,128)(2,1)} %param.14) | copy-start | bytes 3145732
  0.7 9.8 %copy-start.1 = (bf16[1,64,2048]{2,1,0:T(8,128)(2,1)S(1)}, bf16[1,64,2048]{2,1,0:T(8,128)(2,1)}, u32[]{:S(2)}) copy-start(bf16[1,64,2048]{2,1,0:T(8,128)(2,1)} %param.15) | copy-start | bytes 786436
  3.4 8.9 %collective-permute-start = (bf16[400,128]{1,0:T(8,128)(2,1)S(1)}, bf16[400,128]{1,0:T(8,128)(2,1)S(1)}, u32[]{:S(2)}, u32[]{:S(2)}) collective-permute-start(bf16[400,128]{1,0:T(8,128)(2,1)S(1)} %get-tuple-element.27), channel_id=1, source_target_pairs={{0,3},{1,2},{2,1},{3,0},{4,7},{5,6},{6,5},{7,4},{8,11},{9,10},{10,... | collective-permute-start | bytes 307208 | tf_op jit(solution)/shard_map/ppermute | solution.py:43
  8.5 8.6 %collective-permute-start.1 = (bf16[400,128]{1,0:T(8,128)(2,1)S(1)}, bf16[400,128]{1,0:T(8,128)(2,1)S(1)}, u32[]{:S(2)}, u32[]{:S(2)}) collective-permute-start(bf16[400,128]{1,0:T(8,128)(2,1)S(1)} %get-tuple-element.28), channel_id=1, source_target_pairs={{0,2},{1,3},{2,0},{3,1},{4,6},{5,7},{6,4},{7,5},{8,10},{9,11},{10,... | collective-permute-start | bytes 307208 | tf_op jit(solution)/shard_map/ppermute | solution.py:43
  8.5 8.6 %collective-permute-start.2 = (bf16[400,128]{1,0:T(8,128)(2,1)S(1)}, bf16[400,128]{1,0:T(8,128)(2,1)S(1)}, u32[]{:S(2)}, u32[]{:S(2)}) collective-permute-start(bf16[400,128]{1,0:T(8,128)(2,1)S(1)} %get-tuple-element.29), channel_id=1, source_target_pairs={{0,1},{1,0},{2,3},{3,2},{4,5},{5,4},{6,7},{7,6},{8,9},{9,8},{10,11... | collective-permute-start | bytes 307208 | tf_op jit(solution)/shard_map/ppermute | solution.py:43
  17.4 9.2 %collective-permute-start.7 = (bf16[64,512]{1,0:T(8,128)(2,1)S(1)}, bf16[64,512]{1,0:T(8,128)(2,1)S(1)}, u32[]{:S(2)}, u32[]{:S(2)}) collective-permute-start(bf16[64,512]{1,0:T(8,128)(2,1)S(1)} %get-tuple-element.30.rest_0_.rest_5_), channel_id=1, source_target_pairs={{0,3},{1,2},{2,1},{3,0},{4,7},{5,6},{6,5},{7,4},{8,11},{9,10},{10,... | collective-permute-start | bytes 196616 | tf_op jit(solution)/shard_map/ppermute | solution.py:43
  19.9 4.3 %collective-permute-start.3 = (bf16[64,512]{1,0:T(8,128)(2,1)S(1)}, bf16[64,512]{1,0:T(8,128)(2,1)S(1)}, u32[]{:S(2)}, u32[]{:S(2)}) collective-permute-start(bf16[64,512]{1,0:T(8,128)(2,1)S(1)} %get-tuple-element.30.rest_0_.rest_5_), channel_id=1, source_target_pairs={{0,8},{4,12},{8,0},{12,4},{1,9},{5,13},{9,1},{13,5},{2,10},{6,14},... | collective-permute-start | bytes 196616 | tf_op jit(solution)/shard_map/ppermute | solution.py:43
  21.4 6.2 %collective-permute-start.10 = (bf16[128,512]{1,0:T(8,128)(2,1)S(1)}, bf16[128,512]{1,0:T(8,128)(2,1)S(1)}, u32[]{:S(2)}, u32[]{:S(2)}) collective-permute-start(bf16[128,512]{1,0:T(8,128)(2,1)S(1)} %get-tuple-element.31.rest_0_), channel_id=1, source_target_pairs={{0,8},{4,12},{8,0},{12,4},{1,9},{5,13},{9,1},{13,5},{2,10},{6,14},... | collective-permute-start | bytes 393224 | tf_op jit(solution)/shard_map/ppermute | solution.py:43
  24.2 6.8 %collective-permute-start.4 = (bf16[128,512]{1,0:T(8,128)(2,1)S(1)}, bf16[128,512]{1,0:T(8,128)(2,1)S(1)}, u32[]{:S(2)}, u32[]{:S(2)}) collective-permute-start(bf16[128,512]{1,0:T(8,128)(2,1)S(1)} %constant_dynamic-update-slice_fusion), channel_id=1, source_target_pairs={{0,2},{1,3},{2,0},{3,1},{4,6},{5,7},{6,4},{7,5},{8,10},{9,11},{10,... | collective-permute-start | bytes 393224 | tf_op jit(solution)/shard_map/ppermute | solution.py:43
  24.2 6.8 %collective-permute-start.5 = (bf16[128,512]{1,0:T(8,128)(2,1)S(1)}, bf16[128,512]{1,0:T(8,128)(2,1)S(1)}, u32[]{:S(2)}, u32[]{:S(2)}) collective-permute-start(bf16[128,512]{1,0:T(8,128)(2,1)S(1)} %constant_dynamic-update-slice_fusion), channel_id=1, source_target_pairs={{0,1},{1,0},{2,3},{3,2},{4,5},{5,4},{6,7},{7,6},{8,9},{9,8},{10,11... | collective-permute-start | bytes 393224 | tf_op jit(solution)/shard_map/ppermute | solution.py:43
  26.6 4.3 %collective-permute-start.8 = (bf16[64,512]{1,0:T(8,128)(2,1)S(1)}, bf16[64,512]{1,0:T(8,128)(2,1)S(1)}, u32[]{:S(2)}, u32[]{:S(2)}) collective-permute-start(bf16[64,512]{1,0:T(8,128)(2,1)S(1)} %collective-permute-done.7.rest_2_), channel_id=1, source_target_pairs={{0,8},{4,12},{8,0},{12,4},{1,9},{5,13},{9,1},{13,5},{2,10},{6,14},... | collective-permute-start | bytes 196616 | tf_op jit(solution)/shard_map/ppermute | solution.py:43
  27.6 4.0 %collective-permute-start.11 = (bf16[256,512]{1,0:T(8,128)(2,1)S(1)}, bf16[256,512]{1,0:T(8,128)(2,1)S(1)}, u32[]{:S(2)}, u32[]{:S(2)}) collective-permute-start(bf16[256,512]{1,0:T(8,128)(2,1)S(1)} %pad_maximum_fusion.2), channel_id=1, source_target_pairs={{0,4},{4,0},{8,12},{12,8},{1,5},{5,1},{9,13},{13,9},{2,6},{6,2},{1... | collective-permute-start | bytes 786440 | tf_op jit(solution)/shard_map/ppermute | solution.py:43
  30.9 1.8 %collective-permute-start.9 = (bf16[256,512]{1,0:T(8,128)(2,1)S(1)}, bf16[256,512]{1,0:T(8,128)(2,1)S(1)}, u32[]{:S(2)}, u32[]{:S(2)}) collective-permute-start(bf16[256,512]{1,0:T(8,128)(2,1)S(1)} %pad_maximum_fusion.1), channel_id=1, source_target_pairs={{0,4},{4,0},{8,12},{12,8},{1,5},{5,1},{9,13},{13,9},{2,6},{6,2},{1... | collective-permute-start | bytes 786440 | tf_op jit(solution)/shard_map/ppermute | solution.py:43
  31.0 2.6 %collective-permute-start.6 = (bf16[256,512]{1,0:T(8,128)(2,1)S(1)}, bf16[256,512]{1,0:T(8,128)(2,1)S(1)}, u32[]{:S(2)}, u32[]{:S(2)}) collective-permute-start(bf16[256,512]{1,0:T(8,128)(2,1)S(1)} %pad_maximum_fusion), channel_id=1, source_target_pairs={{0,4},{4,0},{8,12},{12,8},{1,5},{5,1},{9,13},{13,9},{2,6},{6,2},{1... | collective-permute-start | bytes 786440 | tf_op jit(solution)/shard_map/ppermute | solution.py:43

commit v9 on v8

--- a/solution.py
+++ b/solution.py
@@ -452,10 +452,9 @@
         return dict(plan=plan, pieces=pieces, spans=spans)
 
     ends = span_offset, cont_lengths
-    state = attend(*ends, query, sets, state=state, **share([prompts], [(prompt.shape[0], True)]))
-    near = stretches[: 1 + half]
-    state = attend(*ends, query, sets, state=state, **share(near, [(rows, False)] * len(near)))
-    rest = stretches[1 + half :]
+    near = share([stretches[0], prompts], [(rows, False), (prompt.shape[0], True)])
+    state = attend(*ends, query, sets, state=state, **near)
+    rest = stretches[1:]
     attended, block = attend(*ends, query, sets, state=state, last=block, **share(rest, [(rows, False)] * len(rest)))
     return block, attended[None]
 

time: 35.8 us -> 34.9 us (0.975)
  waiting for transfers between devices: 10.4 us -> 9.5 us
    ppermute x12 -> x11, waiting for transfers between devices: 10.4 us -> 9.5 us  [exchange(): lax.ppermute(value, axis, [(i, peer(i, step, count)) for i in range(count)])]
    ppermute x12 -> x11, starting transfers between devices: 14.4 us -> 14.7 us  [exchange(): lax.ppermute(value, axis, [(i, peer(i, step, count)) for i in range(count)])]
    pallas_call x3 -> x2, Pallas kernels: 4.02 us -> 3.74 us  [attend(): pl.pallas_call(functools.partial(attend_kernel, plan, sets, spans, tile,...]
  transfers between devices with their start and end apart: 12 -> 11, of which waited for: 4 -> 6; matrix products, arithmetic and copies ran while one was open for 0% -> 0% of each run, Pallas kernels for 11% -> 9%
where the time goes in v9:
time: 34.9 us; the launch traced here: 34.7 us
  starting transfers between devices  14.7 us (42%)
  waiting for transfers between devices  9.5 us (27%)
  Pallas kernels  8.42 us (24%)
  between operations  2.05 us (6%)
    ppermute x11, starting transfers between devices, exchange(): lax.ppermute(value, axis, [(i, peer(i, step, count)) for i in range(count)])  14.7 us
    ppermute x11, waiting for transfers between devices, exchange(): lax.ppermute(value, axis, [(i, peer(i, step, count)) for i in range(count)])  9.5 us
    pallas_call x2, Pallas kernels, attend(): pl.pallas_call(functools.partial(attend_kernel, plan, sets, spans, tile,...  3.74 us
    pallas_call x1, Pallas kernels, project(): pl.pallas_call(functools.partial(project_kernel, count, rows, heads, chun...  2.73 us
    pallas_call x1, Pallas kernels, prepare(): pl.pallas_call(functools.partial(prepare_kernel, sets, block), in_specs=[...  1.74 us
  transfers between devices with their start and end apart: 11, of which 6 were waited for; matrix products, arithmetic and copies ran while one was open for 0% of the time, Pallas kernels for 9%

profile of v9, /device:TPU:0, one launch (start us, length us, event | category | flops | bytes accessed | tf_op | source)
XLA Modules:
  0.0 34.7 jit_solution(18211378013839398431)
XLA Ops:
  0.6 0.0 copy-start.2
  0.6 0.0 copy-start
  0.7 0.0 copy-start.1
  0.7 2.7 %project.1 = (f32[256,128]{1,0:T(8,128)S(1)}, f32[64,128]{1,0:T(8,128)S(1)}, bf16[32,512]{1,0:T(8,128)(2,1)S(1)}, bf16[400,128]{1,0:T(8,128)(2,1)S(1)}, bf16[400...) custom-call(bf16[256,2048]{1,0:T(8,128)(2,1)} %hidden_ref.1, bf16[16,128]{1,0:T(8,128)(2,1)} %bitcast.6, ...), custom_call_target="tpu_custom_call" | custom-call | flops 536870912 | bytes 3145728 | tf_op jit(solution)/shard_map/project/pallas_call | solution.py:147
  3.4 5.1 %collective-permute-start = (bf16[400,128]{1,0:T(8,128)(2,1)S(1)}, bf16[400,128]{1,0:T(8,128)(2,1)S(1)}, u32[]{:S(2)}, u32[]{:S(2)}) collective-permute-start(bf16[400,128]{1,0:T(8,128)(2,1)S(1)} %get-tuple-element.25), channel_id=1, source_target_pairs={{0,3},{1,2},{2,1},{3,0},{4,7},{5,6},{6,5},{7,4},{8,11},{9,10},{10,... | collective-permute-start | bytes 307208 | tf_op jit(solution)/shard_map/ppermute | solution.py:43
  8.5 0.0 collective-permute-start.1
  8.5 0.6 %collective-permute-start.2 = (bf16[400,128]{1,0:T(8,128)(2,1)S(1)}, bf16[400,128]{1,0:T(8,128)(2,1)S(1)}, u32[]{:S(2)}, u32[]{:S(2)}) collective-permute-start(bf16[400,128]{1,0:T(8,128)(2,1)S(1)} %get-tuple-element.27), channel_id=1, source_target_pairs={{0,1},{1,0},{2,3},{3,2},{4,5},{5,4},{6,7},{7,6},{8,9},{9,8},{10,11... | collective-permute-start | bytes 307208 | tf_op jit(solution)/shard_map/ppermute | solution.py:43
  10.5 0.0 copy-done.2
  10.5 0.0 copy-done
  10.5 1.7 %prepare.1 = (f32[64,128]{1,0:T(8,128)S(1)}, f32[64,128]{1,0:T(8,128)S(1)}, bf16[4096,128]{1,0:T(8,128)(2,1)S(1)}, f32[8,8,512]{2,1,0:T(8,128)S(1)}, f32[8,128,512]{2,1,0:T(8,128)S(1)}) custom-call(s32[1]{0:T(128)S(6)} %copy.12.offset_ref, s32[1]{0:T(128)S(6)} %copy.13.length_ref, f32[1,128]{1,0:T(1,128)S(1)} %copy-done.2, bf16[64,8192]{1,0:T(8,128)(2,1)S(1)} %bitcast.4, ...), custom_call_target="tpu_custom_call" | custom-call | tf_op jit(solution)/shard_map/prepare/pallas_call | solution.py:253
  12.2 0.1 collective-permute-done.rest_0_
  12.3 4.8 %collective-permute-done.1.rest_1_ = bf16[400,128]{1,0:T(8,128)(2,1)S(1)} collective-permute-done((bf16[400,128]{1,0:T(8,128)(2,1)S(1)}, bf16[400,128]{1,0:T(8,128)(2,1)S(1)}, u32[]{:S(2)}, u32[]{:S(2)}) %collective-permute-start.1) | collective-permute-done | bytes 102432 | tf_op jit(solution)/shard_map/ppermute | solution.py:43
  17.1 0.0 collective-permute-done.2.rest_2_
  17.1 0.2 combine.1
  17.4 1.6 %collective-permute-start.5 = (bf16[64,512]{1,0:T(8,128)(2,1)S(1)}, bf16[64,512]{1,0:T(8,128)(2,1)S(1)}, u32[]{:S(2)}, u32[]{:S(2)}) collective-permute-start(bf16[64,512]{1,0:T(8,128)(2,1)S(1)} %get-tuple-element.28.rest_0_.rest_7_), channel_id=1, source_target_pairs={{0,8},{4,12},{8,0},{12,4},{1,9},{5,13},{9,1},{13,5},{2,10},{6,14},... | collective-permute-start | bytes 196616 | tf_op jit(solution)/shard_map/ppermute | solution.py:43
  18.9 0.5 %collective-permute-start.9 = (bf16[128,512]{1,0:T(8,128)(2,1)S(1)}, bf16[128,512]{1,0:T(8,128)(2,1)S(1)}, u32[]{:S(2)}, u32[]{:S(2)}) collective-permute-start(bf16[128,512]{1,0:T(8,128)(2,1)S(1)} %get-tuple-element.29.rest_2_), channel_id=1, source_target_pairs={{0,8},{4,12},{8,0},{12,4},{1,9},{5,13},{9,1},{13,5},{2,10},{6,14},... | collective-permute-start | bytes 393224 | tf_op jit(solution)/shard_map/ppermute | solution.py:43
  19.4 2.5 %collective-permute-start.3 = (bf16[64,512]{1,0:T(8,128)(2,1)S(1)}, bf16[64,512]{1,0:T(8,128)(2,1)S(1)}, u32[]{:S(2)}, u32[]{:S(2)}) collective-permute-start(bf16[64,512]{1,0:T(8,128)(2,1)S(1)} %get-tuple-element.28.rest_0_.rest_7_), channel_id=1, source_target_pairs={{0,3},{1,2},{2,1},{3,0},{4,7},{5,6},{6,5},{7,4},{8,11},{9,10},{10,... | collective-permute-start | bytes 196616 | tf_op jit(solution)/shard_map/ppermute | solution.py:43
  21.9 0.4 %collective-permute-done.5.rest_1_ = bf16[64,512]{1,0:T(8,128)(2,1)S(1)} collective-permute-done((bf16[64,512]{1,0:T(8,128)(2,1)S(1)}, bf16[64,512]{1,0:T(8,128)(2,1)S(1)}, u32[]{:S(2)}, u32[]{:S(2)}) %collective-permute-start.5) | collective-permute-done | bytes 65568 | tf_op jit(solution)/shard_map/ppermute | solution.py:43
  22.3 0.0 collective-permute-start.6
  22.3 2.7 %collective-permute-start.7 = (bf16[128,512]{1,0:T(8,128)(2,1)S(1)}, bf16[128,512]{1,0:T(8,128)(2,1)S(1)}, u32[]{:S(2)}, u32[]{:S(2)}) collective-permute-start(bf16[128,512]{1,0:T(8,128)(2,1)S(1)} %constant_dynamic-update-slice_fusion), channel_id=1, source_target_pairs={{0,1},{1,0},{2,3},{3,2},{4,5},{5,4},{6,7},{7,6},{8,9},{9,8},{10,11... | collective-permute-start | bytes 393224 | tf_op jit(solution)/shard_map/ppermute | solution.py:43
  25.0 1.2 %collective-permute-done.3.rest_0_ = bf16[64,512]{1,0:T(8,128)(2,1)S(1)} collective-permute-done((bf16[64,512]{1,0:T(8,128)(2,1)S(1)}, bf16[64,512]{1,0:T(8,128)(2,1)S(1)}, u32[]{:S(2)}, u32[]{:S(2)}) %collective-permute-start.3) | collective-permute-done | bytes 65568 | tf_op jit(solution)/shard_map/ppermute | solution.py:43
  26.3 1.5 %collective-permute-start.4 = (bf16[64,512]{1,0:T(8,128)(2,1)S(1)}, bf16[64,512]{1,0:T(8,128)(2,1)S(1)}, u32[]{:S(2)}, u32[]{:S(2)}) collective-permute-start(bf16[64,512]{1,0:T(8,128)(2,1)S(1)} %collective-permute-done.3.rest_0_), channel_id=1, source_target_pairs={{0,8},{4,12},{8,0},{12,4},{1,9},{5,13},{9,1},{13,5},{2,10},{6,14},... | collective-permute-start | bytes 196616 | tf_op jit(solution)/shard_map/ppermute | solution.py:43
  27.8 0.0 collective-permute-done.9.rest_3_
  27.8 0.1 collective-permute-start.10
  27.9 2.7 %collective-permute-done.4.rest_1_ = bf16[64,512]{1,0:T(8,128)(2,1)S(1)} collective-permute-done((bf16[64,512]{1,0:T(8,128)(2,1)S(1)}, bf16[64,512]{1,0:T(8,128)(2,1)S(1)}, u32[]{:S(2)}, u32[]{:S(2)}) %collective-permute-start.4) | collective-permute-done | bytes 65568 | tf_op jit(solution)/shard_map/ppermute | solution.py:43
  30.5 0.0 collective-permute-done.6.rest_2_
  30.6 0.0 collective-permute-done.7.rest_3_
  30.6 0.1 collective-permute-start.8
  30.7 0.0 collective-permute-done.10.rest_4_
  30.7 1.4 %attend_more.1 = (f32[8,8,512]{2,1,0:T(8,128)S(1)}, f32[8,128,512]{2,1,0:T(8,128)S(1)}) custom-call(s32[1]{0:T(128)S(6)} %copy.12.offset_ref, s32[1]{0:T(128)S(6)} %copy.13.length_ref, bf16[4096,128]{1,0:T(8,128)(2,1)S(1)} %get-tuple-element.19.query_ref, bf16[64,512]{1,0:T(8,128)(2,1)S(1)} %get-tuple-element.28.rest_0_.rest_7_, ...), custom_call_target="tpu_custom_call" | custom-call | tf_op jit(solution)/shard_map/attend_more/pallas_call | solution.py:391
  32.1 0.3 collective-permute-done.8.rest_4_
  32.4 2.3 %attend_last.1 = (bf16[64,8192]{1,0:T(8,128)(2,1)}, bf16[64,512]{1,0:T(8,128)(2,1)}) custom-call(s32[1]{0:T(128)S(6)} %copy.12.offset_ref, s32[1]{0:T(128)S(6)} %copy.13.length_ref, bf16[4096,128]{1,0:T(8,128)(2,1)S(1)} %get-tuple-element.19.query_ref, bf16[64,512]{1,0:T(8,128)(2,1)S(1)} %collective-permute-done.3.rest_0_, ...), custom_call_target="tpu_custom_call" | custom-call | tf_op jit(solution)/shard_map/attend_last/pallas_call | solution.py:391
  (5 shorter events, 0.1 us)
Async XLA Ops:
  0.6 9.8 %copy-start.2 = (f32[1,128]{1,0:T(1,128)S(1)}, f32[1,128]{1,0:T(1,128)}, u32[]{:S(2)}) copy-start(f32[1,128]{1,0:T(1,128)} %constant.2.clone.frequency_ref) | copy-start | bytes 1540
  0.6 9.8 %copy-start = (bf16[1,64,8192]{2,1,0:T(8,128)(2,1)S(1)}, bf16[1,64,8192]{2,1,0:T(8,128)(2,1)}, u32[]{:S(2)}) copy-start(bf16[1,64,8192]{2,1,0:T(8,128)(2,1)} %param.14) | copy-start | bytes 3145732
  0.7 9.8 %copy-start.1 = (bf16[1,64,2048]{2,1,0:T(8,128)(2,1)S(1)}, bf16[1,64,2048]{2,1,0:T(8,128)(2,1)}, u32[]{:S(2)}) copy-start(bf16[1,64,2048]{2,1,0:T(8,128)(2,1)} %param.15) | copy-start | bytes 786436
  3.4 8.9 %collective-permute-start = (bf16[400,128]{1,0:T(8,128)(2,1)S(1)}, bf16[400,128]{1,0:T(8,128)(2,1)S(1)}, u32[]{:S(2)}, u32[]{:S(2)}) collective-permute-start(bf16[400,128]{1,0:T(8,128)(2,1)S(1)} %get-tuple-element.25), channel_id=1, source_target_pairs={{0,3},{1,2},{2,1},{3,0},{4,7},{5,6},{6,5},{7,4},{8,11},{9,10},{10,... | collective-permute-start | bytes 307208 | tf_op jit(solution)/shard_map/ppermute | solution.py:43
  8.5 8.6 %collective-permute-start.1 = (bf16[400,128]{1,0:T(8,128)(2,1)S(1)}, bf16[400,128]{1,0:T(8,128)(2,1)S(1)}, u32[]{:S(2)}, u32[]{:S(2)}) collective-permute-start(bf16[400,128]{1,0:T(8,128)(2,1)S(1)} %get-tuple-element.26), channel_id=1, source_target_pairs={{0,2},{1,3},{2,0},{3,1},{4,6},{5,7},{6,4},{7,5},{8,10},{9,11},{10,... | collective-permute-start | bytes 307208 | tf_op jit(solution)/shard_map/ppermute | solution.py:43
  8.5 8.6 %collective-permute-start.2 = (bf16[400,128]{1,0:T(8,128)(2,1)S(1)}, bf16[400,128]{1,0:T(8,128)(2,1)S(1)}, u32[]{:S(2)}, u32[]{:S(2)}) collective-permute-start(bf16[400,128]{1,0:T(8,128)(2,1)S(1)} %get-tuple-element.27), channel_id=1, source_target_pairs={{0,1},{1,0},{2,3},{3,2},{4,5},{5,4},{6,7},{7,6},{8,9},{9,8},{10,11... | collective-permute-start | bytes 307208 | tf_op jit(solution)/shard_map/ppermute | solution.py:43
  17.4 5.0 %collective-permute-start.5 = (bf16[64,512]{1,0:T(8,128)(2,1)S(1)}, bf16[64,512]{1,0:T(8,128)(2,1)S(1)}, u32[]{:S(2)}, u32[]{:S(2)}) collective-permute-start(bf16[64,512]{1,0:T(8,128)(2,1)S(1)} %get-tuple-element.28.rest_0_.rest_7_), channel_id=1, source_target_pairs={{0,8},{4,12},{8,0},{12,4},{1,9},{5,13},{9,1},{13,5},{2,10},{6,14},... | collective-permute-start | bytes 196616 | tf_op jit(solution)/shard_map/ppermute | solution.py:43
  18.9 8.9 %collective-permute-start.9 = (bf16[128,512]{1,0:T(8,128)(2,1)S(1)}, bf16[128,512]{1,0:T(8,128)(2,1)S(1)}, u32[]{:S(2)}, u32[]{:S(2)}) collective-permute-start(bf16[128,512]{1,0:T(8,128)(2,1)S(1)} %get-tuple-element.29.rest_2_), channel_id=1, source_target_pairs={{0,8},{4,12},{8,0},{12,4},{1,9},{5,13},{9,1},{13,5},{2,10},{6,14},... | collective-permute-start | bytes 393224 | tf_op jit(solution)/shard_map/ppermute | solution.py:43
  19.4 6.8 %collective-permute-start.3 = (bf16[64,512]{1,0:T(8,128)(2,1)S(1)}, bf16[64,512]{1,0:T(8,128)(2,1)S(1)}, u32[]{:S(2)}, u32[]{:S(2)}) collective-permute-start(bf16[64,512]{1,0:T(8,128)(2,1)S(1)} %get-tuple-element.28.rest_0_.rest_7_), channel_id=1, source_target_pairs={{0,3},{1,2},{2,1},{3,0},{4,7},{5,6},{6,5},{7,4},{8,11},{9,10},{10,... | collective-permute-start | bytes 196616 | tf_op jit(solution)/shard_map/ppermute | solution.py:43
  22.3 8.2 %collective-permute-start.6 = (bf16[128,512]{1,0:T(8,128)(2,1)S(1)}, bf16[128,512]{1,0:T(8,128)(2,1)S(1)}, u32[]{:S(2)}, u32[]{:S(2)}) collective-permute-start(bf16[128,512]{1,0:T(8,128)(2,1)S(1)} %constant_dynamic-update-slice_fusion), channel_id=1, source_target_pairs={{0,2},{1,3},{2,0},{3,1},{4,6},{5,7},{6,4},{7,5},{8,10},{9,11},{10,... | collective-permute-start | bytes 393224 | tf_op jit(solution)/shard_map/ppermute | solution.py:43
  22.3 8.2 %collective-permute-start.7 = (bf16[128,512]{1,0:T(8,128)(2,1)S(1)}, bf16[128,512]{1,0:T(8,128)(2,1)S(1)}, u32[]{:S(2)}, u32[]{:S(2)}) collective-permute-start(bf16[128,512]{1,0:T(8,128)(2,1)S(1)} %constant_dynamic-update-slice_fusion), channel_id=1, source_target_pairs={{0,1},{1,0},{2,3},{3,2},{4,5},{5,4},{6,7},{7,6},{8,9},{9,8},{10,11... | collective-permute-start | bytes 393224 | tf_op jit(solution)/shard_map/ppermute | solution.py:43
  26.3 4.3 %collective-permute-start.4 = (bf16[64,512]{1,0:T(8,128)(2,1)S(1)}, bf16[64,512]{1,0:T(8,128)(2,1)S(1)}, u32[]{:S(2)}, u32[]{:S(2)}) collective-permute-start(bf16[64,512]{1,0:T(8,128)(2,1)S(1)} %collective-permute-done.3.rest_0_), channel_id=1, source_target_pairs={{0,8},{4,12},{8,0},{12,4},{1,9},{5,13},{9,1},{13,5},{2,10},{6,14},... | collective-permute-start | bytes 196616 | tf_op jit(solution)/shard_map/ppermute | solution.py:43
  27.8 2.9 %collective-permute-start.10 = (bf16[384,512]{1,0:T(8,128)(2,1)S(1)}, bf16[384,512]{1,0:T(8,128)(2,1)S(1)}, u32[]{:S(2)}, u32[]{:S(2)}) collective-permute-start(bf16[384,512]{1,0:T(8,128)(2,1)S(1)} %pad_maximum_fusion.1), channel_id=1, source_target_pairs={{0,4},{4,0},{8,12},{12,8},{1,5},{5,1},{9,13},{13,9},{2,6},{6,2},{1... | collective-permute-start | bytes 1179656 | tf_op jit(solution)/shard_map/ppermute | solution.py:43
  30.6 1.8 %collective-permute-start.8 = (bf16[384,512]{1,0:T(8,128)(2,1)S(1)}, bf16[384,512]{1,0:T(8,128)(2,1)S(1)}, u32[]{:S(2)}, u32[]{:S(2)}) collective-permute-start(bf16[384,512]{1,0:T(8,128)(2,1)S(1)} %pad_maximum_fusion), channel_id=1, source_target_pairs={{0,4},{4,0},{8,12},{12,8},{1,5},{5,1},{9,13},{13,9},{2,6},{6,2},{1... | collective-permute-start | bytes 1179656 | tf_op jit(solution)/shard_map/ppermute | solution.py:43

commit v10 on v9

--- a/solution.py
+++ b/solution.py
@@ -165,7 +165,7 @@
     )(*stay)
 
 
-def combine_kernel(rows, heads, own_ref, square_ref, mine_ref, cosine_ref, sine_ref, *rest):
+def combine_kernel(rows, heads, order, own_ref, square_ref, mine_ref, cosine_ref, sine_ref, *rest):
     got, (send_ref, prompt_ref) = rest[:-2], rest[-2:]
     cached = mine_ref.shape[0]
     count = 1 + len(got)
@@ -192,17 +192,17 @@
         send_ref[:, lanes] = out
         for i, ref in enumerate(got):
             start = heads * rows + 16 + h * cached
-            prompt_ref[prompt_rows(count - 1 - i), lanes] = ref[start : start + cached, :]
+            prompt_ref[prompt_rows(order[i]), lanes] = ref[start : start + cached, :]
     prompt_ref[prompt_rows(0), :] = mine_ref[...]
 
 
-def combine(own, square, mine, cosine, sine, got):
+def combine(own, square, mine, cosine, sine, got, order):
     rows = square.shape[0]
     heads = own.shape[0] // rows
     block = pltpu.VMEM((rows, heads * HEAD_SIZE), BF16)
     prompt = jax.ShapeDtypeStruct(((1 + len(got)) * mine.shape[0], heads * HEAD_SIZE), BF16)
     return pl.pallas_call(
-        functools.partial(combine_kernel, rows, heads),
+        functools.partial(combine_kernel, rows, heads, order),
         in_specs=[VMEM] * (5 + len(got)),
         out_shape=[block, prompt],
         out_specs=[VMEM, VMEM],
@@ -415,12 +415,13 @@
 
     own, square, mine, *sends = project(span_hidden, norm_gain, key_value_weight, prompt_key_value, count)
     order = list(range(count - 1, 0, -1))
-    got = [exchange(sends[k - 1], "seq", k) for k in order]
+    sums = order[1:] + order[:1]
+    got = [exchange(sends[k - 1], "seq", k) for k in sums]
 
     cosine, sine, query, *state = prepare(
         span_offset, cont_lengths, cont_query[0], continuation_key_value[0], sets, rows
     )
-    block, prompt = combine(own, square, mine, cosine, sine, got)
+    block, prompt = combine(own, square, mine, cosine, sine, got, sums)
 
     far = list(range(low, sets, low))
     steps = [0] + far
@@ -428,7 +429,7 @@
     beside = [exchange(block, "set", step) for step in far]
     across = [exchange(block, "seq", k) for k in order[:half]]
     both = jnp.concatenate([block] + beside, axis=0)
-    together = [exchange(both, "seq", k) for k in order[half:]]
+    together = [exchange(both, "seq", k) for k in reversed(order[half:])]
     prompts = [prompt] + [exchange(prompt, "set", step) for step in far]
     stretches = [[block] + beside]
     for arrived in across:

time: 34.9 us -> 33.6 us (0.963)
  waiting for transfers between devices: 9.5 us -> 7.23 us
  starting transfers between devices: 14.7 us -> 15.6 us
    ppermute x11, waiting for transfers between devices: 9.5 us -> 7.23 us  [exchange(): lax.ppermute(value, axis, [(i, peer(i, step, count)) for i in range(count)])]
    ppermute x11, starting transfers between devices: 14.7 us -> 15.6 us  [exchange(): lax.ppermute(value, axis, [(i, peer(i, step, count)) for i in range(count)])]
where the time goes in v10:
time: 33.6 us; the launch traced here: 33.4 us
  starting transfers between devices  15.6 us (46%)
  Pallas kernels  8.42 us (25%)
  waiting for transfers between devices  7.23 us (22%)
  between operations  2.04 us (6%)
    ppermute x11, starting transfers between devices, exchange(): lax.ppermute(value, axis, [(i, peer(i, step, count)) for i in range(count)])  15.6 us
    ppermute x11, waiting for transfers between devices, exchange(): lax.ppermute(value, axis, [(i, peer(i, step, count)) for i in range(count)])  7.23 us
    pallas_call x2, Pallas kernels, attend(): pl.pallas_call(functools.partial(attend_kernel, plan, sets, spans, tile,...  3.74 us
    pallas_call x1, Pallas kernels, project(): pl.pallas_call(functools.partial(project_kernel, count, rows, heads, chun...  2.73 us
    pallas_call x1, Pallas kernels, prepare(): pl.pallas_call(functools.partial(prepare_kernel, sets, block), in_specs=[...  1.75 us
  transfers between devices with their start and end apart: 11, of which 6 were waited for; matrix products, arithmetic and copies ran while one was open for 0% of the time, Pallas kernels for 9%

profile of v10, /device:TPU:0, one launch (start us, length us, event | category | flops | bytes accessed | tf_op | source)
XLA Modules:
  0.0 33.4 jit_solution(5096774834514442531)
XLA Ops:
  0.6 0.0 copy-start.2
  0.6 0.0 copy-start
  0.7 0.0 copy-start.1
  0.7 2.7 %project.1 = (f32[256,128]{1,0:T(8,128)S(1)}, f32[64,128]{1,0:T(8,128)S(1)}, bf16[32,512]{1,0:T(8,128)(2,1)S(1)}, bf16[400,128]{1,0:T(8,128)(2,1)S(1)}, bf16[400...) custom-call(bf16[256,2048]{1,0:T(8,128)(2,1)} %hidden_ref.1, bf16[16,128]{1,0:T(8,128)(2,1)} %bitcast.6, ...), custom_call_target="tpu_custom_call" | custom-call | flops 536870912 | bytes 3145728 | tf_op jit(solution)/shard_map/project/pallas_call | solution.py:147
  3.4 4.1 %collective-permute-start = (bf16[400,128]{1,0:T(8,128)(2,1)S(1)}, bf16[400,128]{1,0:T(8,128)(2,1)S(1)}, u32[]{:S(2)}, u32[]{:S(2)}) collective-permute-start(bf16[400,128]{1,0:T(8,128)(2,1)S(1)} %get-tuple-element.25), channel_id=1, source_target_pairs={{0,2},{1,3},{2,0},{3,1},{4,6},{5,7},{6,4},{7,5},{8,10},{9,11},{10,... | collective-permute-start | bytes 307208 | tf_op jit(solution)/shard_map/ppermute | solution.py:43
  7.5 1.6 %collective-permute-start.1 = (bf16[400,128]{1,0:T(8,128)(2,1)S(1)}, bf16[400,128]{1,0:T(8,128)(2,1)S(1)}, u32[]{:S(2)}, u32[]{:S(2)}) collective-permute-start(bf16[400,128]{1,0:T(8,128)(2,1)S(1)} %get-tuple-element.26), channel_id=1, source_target_pairs={{0,1},{1,0},{2,3},{3,2},{4,5},{5,4},{6,7},{7,6},{8,9},{9,8},{10,11... | collective-permute-start | bytes 307208 | tf_op jit(solution)/shard_map/ppermute | solution.py:43
  9.1 0.0 collective-permute-start.2
  10.4 0.0 copy-done.2
  10.4 0.0 copy-done
  10.4 1.7 %prepare.1 = (f32[64,128]{1,0:T(8,128)S(1)}, f32[64,128]{1,0:T(8,128)S(1)}, bf16[4096,128]{1,0:T(8,128)(2,1)S(1)}, f32[8,8,512]{2,1,0:T(8,128)S(1)}, f32[8,128,512]{2,1,0:T(8,128)S(1)}) custom-call(s32[1]{0:T(128)S(6)} %copy.12.offset_ref, s32[1]{0:T(128)S(6)} %copy.13.length_ref, f32[1,128]{1,0:T(1,128)S(1)} %copy-done.2, bf16[64,8192]{1,0:T(8,128)(2,1)S(1)} %bitcast.4, ...), custom_call_target="tpu_custom_call" | custom-call | tf_op jit(solution)/shard_map/prepare/pallas_call | solution.py:253
  12.2 1.8 %collective-permute-done.rest_0_ = bf16[400,128]{1,0:T(8,128)(2,1)S(1)} collective-permute-done((bf16[400,128]{1,0:T(8,128)(2,1)S(1)}, bf16[400,128]{1,0:T(8,128)(2,1)S(1)}, u32[]{:S(2)}, u32[]{:S(2)}) %collective-permute-start) | collective-permute-done | bytes 102432 | tf_op jit(solution)/shard_map/ppermute | solution.py:43
  14.0 0.0 collective-permute-done.1.rest_1_
  14.0 1.9 %collective-permute-done.2.rest_2_ = bf16[400,128]{1,0:T(8,128)(2,1)S(1)} collective-permute-done((bf16[400,128]{1,0:T(8,128)(2,1)S(1)}, bf16[400,128]{1,0:T(8,128)(2,1)S(1)}, u32[]{:S(2)}, u32[]{:S(2)}) %collective-permute-start.2) | collective-permute-done | bytes 102432 | tf_op jit(solution)/shard_map/ppermute | solution.py:43
  15.9 0.2 combine.1
  16.2 1.5 %collective-permute-start.5 = (bf16[64,512]{1,0:T(8,128)(2,1)S(1)}, bf16[64,512]{1,0:T(8,128)(2,1)S(1)}, u32[]{:S(2)}, u32[]{:S(2)}) collective-permute-start(bf16[64,512]{1,0:T(8,128)(2,1)S(1)} %get-tuple-element.28.rest_0_.rest_7_), channel_id=1, source_target_pairs={{0,8},{4,12},{8,0},{12,4},{1,9},{5,13},{9,1},{13,5},{2,10},{6,14},... | collective-permute-start | bytes 196616 | tf_op jit(solution)/shard_map/ppermute | solution.py:43
  17.7 0.6 %collective-permute-start.9 = (bf16[128,512]{1,0:T(8,128)(2,1)S(1)}, bf16[128,512]{1,0:T(8,128)(2,1)S(1)}, u32[]{:S(2)}, u32[]{:S(2)}) collective-permute-start(bf16[128,512]{1,0:T(8,128)(2,1)S(1)} %get-tuple-element.29.rest_2_), channel_id=1, source_target_pairs={{0,8},{4,12},{8,0},{12,4},{1,9},{5,13},{9,1},{13,5},{2,10},{6,14},... | collective-permute-start | bytes 393224 | tf_op jit(solution)/shard_map/ppermute | solution.py:43
  18.3 2.4 %collective-permute-start.3 = (bf16[64,512]{1,0:T(8,128)(2,1)S(1)}, bf16[64,512]{1,0:T(8,128)(2,1)S(1)}, u32[]{:S(2)}, u32[]{:S(2)}) collective-permute-start(bf16[64,512]{1,0:T(8,128)(2,1)S(1)} %get-tuple-element.28.rest_0_.rest_7_), channel_id=1, source_target_pairs={{0,3},{1,2},{2,1},{3,0},{4,7},{5,6},{6,5},{7,4},{8,11},{9,10},{10,... | collective-permute-start | bytes 196616 | tf_op jit(solution)/shard_map/ppermute | solution.py:43
  20.7 0.4 %collective-permute-done.5.rest_1_ = bf16[64,512]{1,0:T(8,128)(2,1)S(1)} collective-permute-done((bf16[64,512]{1,0:T(8,128)(2,1)S(1)}, bf16[64,512]{1,0:T(8,128)(2,1)S(1)}, u32[]{:S(2)}, u32[]{:S(2)}) %collective-permute-start.5) | collective-permute-done | bytes 65568 | tf_op jit(solution)/shard_map/ppermute | solution.py:43
  21.2 1.5 %collective-permute-start.6 = (bf16[128,512]{1,0:T(8,128)(2,1)S(1)}, bf16[128,512]{1,0:T(8,128)(2,1)S(1)}, u32[]{:S(2)}, u32[]{:S(2)}) collective-permute-start(bf16[128,512]{1,0:T(8,128)(2,1)S(1)} %constant_dynamic-update-slice_fusion), channel_id=1, source_target_pairs={{0,1},{1,0},{2,3},{3,2},{4,5},{5,4},{6,7},{7,6},{8,9},{9,8},{10,11... | collective-permute-start | bytes 393224 | tf_op jit(solution)/shard_map/ppermute | solution.py:43
  22.7 2.0 %collective-permute-start.7 = (bf16[128,512]{1,0:T(8,128)(2,1)S(1)}, bf16[128,512]{1,0:T(8,128)(2,1)S(1)}, u32[]{:S(2)}, u32[]{:S(2)}) collective-permute-start(bf16[128,512]{1,0:T(8,128)(2,1)S(1)} %constant_dynamic-update-slice_fusion), channel_id=1, source_target_pairs={{0,2},{1,3},{2,0},{3,1},{4,6},{5,7},{6,4},{7,5},{8,10},{9,11},{10,... | collective-permute-start | bytes 393224 | tf_op jit(solution)/shard_map/ppermute | solution.py:43
  24.7 0.0 collective-permute-done.3.rest_0_
  24.7 1.7 %collective-permute-start.4 = (bf16[64,512]{1,0:T(8,128)(2,1)S(1)}, bf16[64,512]{1,0:T(8,128)(2,1)S(1)}, u32[]{:S(2)}, u32[]{:S(2)}) collective-permute-start(bf16[64,512]{1,0:T(8,128)(2,1)S(1)} %collective-permute-done.3.rest_0_), channel_id=1, source_target_pairs={{0,8},{4,12},{8,0},{12,4},{1,9},{5,13},{9,1},{13,5},{2,10},{6,14},... | collective-permute-start | bytes 196616 | tf_op jit(solution)/shard_map/ppermute | solution.py:43
  26.4 0.0 collective-permute-done.9.rest_3_
  26.4 0.1 collective-permute-start.10
  26.5 2.4 %collective-permute-done.4.rest_1_ = bf16[64,512]{1,0:T(8,128)(2,1)S(1)} collective-permute-done((bf16[64,512]{1,0:T(8,128)(2,1)S(1)}, bf16[64,512]{1,0:T(8,128)(2,1)S(1)}, u32[]{:S(2)}, u32[]{:S(2)}) %collective-permute-start.4) | collective-permute-done | bytes 65568 | tf_op jit(solution)/shard_map/ppermute | solution.py:43
  28.9 0.0 collective-permute-done.6.rest_2_
  29.0 0.3 collective-permute-done.7.rest_3_
  29.3 0.1 collective-permute-start.8
  29.4 0.0 collective-permute-done.10.rest_4_
  29.4 1.4 %attend_more.1 = (f32[8,8,512]{2,1,0:T(8,128)S(1)}, f32[8,128,512]{2,1,0:T(8,128)S(1)}) custom-call(s32[1]{0:T(128)S(6)} %copy.12.offset_ref, s32[1]{0:T(128)S(6)} %copy.13.length_ref, bf16[4096,128]{1,0:T(8,128)(2,1)S(1)} %get-tuple-element.19.query_ref, bf16[64,512]{1,0:T(8,128)(2,1)S(1)} %get-tuple-element.28.rest_0_.rest_7_, ...), custom_call_target="tpu_custom_call" | custom-call | tf_op jit(solution)/shard_map/attend_more/pallas_call | solution.py:391
  30.8 0.3 collective-permute-done.8.rest_4_
  31.1 2.3 %attend_last.1 = (bf16[64,8192]{1,0:T(8,128)(2,1)}, bf16[64,512]{1,0:T(8,128)(2,1)}) custom-call(s32[1]{0:T(128)S(6)} %copy.12.offset_ref, s32[1]{0:T(128)S(6)} %copy.13.length_ref, bf16[4096,128]{1,0:T(8,128)(2,1)S(1)} %get-tuple-element.19.query_ref, bf16[64,512]{1,0:T(8,128)(2,1)S(1)} %collective-permute-done.3.rest_0_, ...), custom_call_target="tpu_custom_call" | custom-call | tf_op jit(solution)/shard_map/attend_last/pallas_call | solution.py:391
  (5 shorter events, 0.1 us)
Async XLA Ops:
  0.6 9.8 %copy-start.2 = (f32[1,128]{1,0:T(1,128)S(1)}, f32[1,128]{1,0:T(1,128)}, u32[]{:S(2)}) copy-start(f32[1,128]{1,0:T(1,128)} %constant.2.clone.frequency_ref) | copy-start | bytes 1540
  0.6 9.8 %copy-start = (bf16[1,64,8192]{2,1,0:T(8,128)(2,1)S(1)}, bf16[1,64,8192]{2,1,0:T(8,128)(2,1)}, u32[]{:S(2)}) copy-start(bf16[1,64,8192]{2,1,0:T(8,128)(2,1)} %param.14) | copy-start | bytes 3145732
  0.7 9.8 %copy-start.1 = (bf16[1,64,2048]{2,1,0:T(8,128)(2,1)S(1)}, bf16[1,64,2048]{2,1,0:T(8,128)(2,1)}, u32[]{:S(2)}) copy-start(bf16[1,64,2048]{2,1,0:T(8,128)(2,1)} %param.15) | copy-start | bytes 786436
  3.4 10.6 %collective-permute-start = (bf16[400,128]{1,0:T(8,128)(2,1)S(1)}, bf16[400,128]{1,0:T(8,128)(2,1)S(1)}, u32[]{:S(2)}, u32[]{:S(2)}) collective-permute-start(bf16[400,128]{1,0:T(8,128)(2,1)S(1)} %get-tuple-element.25), channel_id=1, source_target_pairs={{0,2},{1,3},{2,0},{3,1},{4,6},{5,7},{6,4},{7,5},{8,10},{9,11},{10,... | collective-permute-start | bytes 307208 | tf_op jit(solution)/shard_map/ppermute | solution.py:43
  7.5 6.5 %collective-permute-start.1 = (bf16[400,128]{1,0:T(8,128)(2,1)S(1)}, bf16[400,128]{1,0:T(8,128)(2,1)S(1)}, u32[]{:S(2)}, u32[]{:S(2)}) collective-permute-start(bf16[400,128]{1,0:T(8,128)(2,1)S(1)} %get-tuple-element.26), channel_id=1, source_target_pairs={{0,1},{1,0},{2,3},{3,2},{4,5},{5,4},{6,7},{7,6},{8,9},{9,8},{10,11... | collective-permute-start | bytes 307208 | tf_op jit(solution)/shard_map/ppermute | solution.py:43
  9.1 6.9 %collective-permute-start.2 = (bf16[400,128]{1,0:T(8,128)(2,1)S(1)}, bf16[400,128]{1,0:T(8,128)(2,1)S(1)}, u32[]{:S(2)}, u32[]{:S(2)}) collective-permute-start(bf16[400,128]{1,0:T(8,128)(2,1)S(1)} %get-tuple-element.27), channel_id=1, source_target_pairs={{0,3},{1,2},{2,1},{3,0},{4,7},{5,6},{6,5},{7,4},{8,11},{9,10},{10,... | collective-permute-start | bytes 307208 | tf_op jit(solution)/shard_map/ppermute | solution.py:43
  16.2 5.0 %collective-permute-start.5 = (bf16[64,512]{1,0:T(8,128)(2,1)S(1)}, bf16[64,512]{1,0:T(8,128)(2,1)S(1)}, u32[]{:S(2)}, u32[]{:S(2)}) collective-permute-start(bf16[64,512]{1,0:T(8,128)(2,1)S(1)} %get-tuple-element.28.rest_0_.rest_7_), channel_id=1, source_target_pairs={{0,8},{4,12},{8,0},{12,4},{1,9},{5,13},{9,1},{13,5},{2,10},{6,14},... | collective-permute-start | bytes 196616 | tf_op jit(solution)/shard_map/ppermute | solution.py:43
  17.7 8.7 %collective-permute-start.9 = (bf16[128,512]{1,0:T(8,128)(2,1)S(1)}, bf16[128,512]{1,0:T(8,128)(2,1)S(1)}, u32[]{:S(2)}, u32[]{:S(2)}) collective-permute-start(bf16[128,512]{1,0:T(8,128)(2,1)S(1)} %get-tuple-element.29.rest_2_), channel_id=1, source_target_pairs={{0,8},{4,12},{8,0},{12,4},{1,9},{5,13},{9,1},{13,5},{2,10},{6,14},... | collective-permute-start | bytes 393224 | tf_op jit(solution)/shard_map/ppermute | solution.py:43
  18.3 6.4 %collective-permute-start.3 = (bf16[64,512]{1,0:T(8,128)(2,1)S(1)}, bf16[64,512]{1,0:T(8,128)(2,1)S(1)}, u32[]{:S(2)}, u32[]{:S(2)}) collective-permute-start(bf16[64,512]{1,0:T(8,128)(2,1)S(1)} %get-tuple-element.28.rest_0_.rest_7_), channel_id=1, source_target_pairs={{0,3},{1,2},{2,1},{3,0},{4,7},{5,6},{6,5},{7,4},{8,11},{9,10},{10,... | collective-permute-start | bytes 196616 | tf_op jit(solution)/shard_map/ppermute | solution.py:43
  21.2 7.8 %collective-permute-start.6 = (bf16[128,512]{1,0:T(8,128)(2,1)S(1)}, bf16[128,512]{1,0:T(8,128)(2,1)S(1)}, u32[]{:S(2)}, u32[]{:S(2)}) collective-permute-start(bf16[128,512]{1,0:T(8,128)(2,1)S(1)} %constant_dynamic-update-slice_fusion), channel_id=1, source_target_pairs={{0,1},{1,0},{2,3},{3,2},{4,5},{5,4},{6,7},{7,6},{8,9},{9,8},{10,11... | collective-permute-start | bytes 393224 | tf_op jit(solution)/shard_map/ppermute | solution.py:43
  22.7 6.6 %collective-permute-start.7 = (bf16[128,512]{1,0:T(8,128)(2,1)S(1)}, bf16[128,512]{1,0:T(8,128)(2,1)S(1)}, u32[]{:S(2)}, u32[]{:S(2)}) collective-permute-start(bf16[128,512]{1,0:T(8,128)(2,1)S(1)} %constant_dynamic-update-slice_fusion), channel_id=1, source_target_pairs={{0,2},{1,3},{2,0},{3,1},{4,6},{5,7},{6,4},{7,5},{8,10},{9,11},{10,... | collective-permute-start | bytes 393224 | tf_op jit(solution)/shard_map/ppermute | solution.py:43
  24.7 4.3 %collective-permute-start.4 = (bf16[64,512]{1,0:T(8,128)(2,1)S(1)}, bf16[64,512]{1,0:T(8,128)(2,1)S(1)}, u32[]{:S(2)}, u32[]{:S(2)}) collective-permute-start(bf16[64,512]{1,0:T(8,128)(2,1)S(1)} %collective-permute-done.3.rest_0_), channel_id=1, source_target_pairs={{0,8},{4,12},{8,0},{12,4},{1,9},{5,13},{9,1},{13,5},{2,10},{6,14},... | collective-permute-start | bytes 196616 | tf_op jit(solution)/shard_map/ppermute | solution.py:43
  26.4 2.9 %collective-permute-start.10 = (bf16[384,512]{1,0:T(8,128)(2,1)S(1)}, bf16[384,512]{1,0:T(8,128)(2,1)S(1)}, u32[]{:S(2)}, u32[]{:S(2)}) collective-permute-start(bf16[384,512]{1,0:T(8,128)(2,1)S(1)} %pad_maximum_fusion.1), channel_id=1, source_target_pairs={{0,4},{4,0},{8,12},{12,8},{1,5},{5,1},{9,13},{13,9},{2,6},{6,2},{1... | collective-permute-start | bytes 1179656 | tf_op jit(solution)/shard_map/ppermute | solution.py:43
  29.3 1.8 %collective-permute-start.8 = (bf16[384,512]{1,0:T(8,128)(2,1)S(1)}, bf16[384,512]{1,0:T(8,128)(2,1)S(1)}, u32[]{:S(2)}, u32[]{:S(2)}) collective-permute-start(bf16[384,512]{1,0:T(8,128)(2,1)S(1)} %pad_maximum_fusion), channel_id=1, source_target_pairs={{0,4},{4,0},{8,12},{12,8},{1,5},{5,1},{9,13},{13,9},{2,6},{6,2},{1... | collective-permute-start | bytes 1179656 | tf_op jit(solution)/shard_map/ppermute | solution.py:43

commit v11 on v10

--- a/solution.py
+++ b/solution.py
@@ -110,7 +110,7 @@
     prompt_copy.wait()
     me = lax.axis_index("seq")
     for k in range(count):
-        to = pl.ds(pl.multiple_of(peer(me, k, count) * rows, rows), rows)
+        to = pl.ds(pl.multiple_of(lax.rem(me + k, count) * rows, rows), rows)
         column = jnp.sum(squares[to, :], axis=1, keepdims=True)
         if k == 0:
             square_ref[...] = jnp.broadcast_to(column, (rows, HEAD_SIZE))
@@ -172,7 +172,7 @@
     me, first = lax.axis_index("seq"), lax.axis_index("set") * heads
 
     def prompt_rows(k):
-        return pl.ds(pl.multiple_of(source(me, k, count) * cached, 16), cached)
+        return pl.ds(pl.multiple_of(lax.rem(me + count - k, count) * cached, 16), cached)
 
     line = jnp.zeros((1, HEAD_SIZE), F32)
     for ref in got:
@@ -416,7 +416,7 @@
     own, square, mine, *sends = project(span_hidden, norm_gain, key_value_weight, prompt_key_value, count)
     order = list(range(count - 1, 0, -1))
     sums = order[1:] + order[:1]
-    got = [exchange(sends[k - 1], "seq", k) for k in sums]
+    got = [lax.ppermute(sends[k - 1], "seq", [(i, (i + k) % count) for i in range(count)]) for k in sums]
 
     cosine, sine, query, *state = prepare(
         span_offset, cont_lengths, cont_query[0], continuation_key_value[0], sets, rows

time: 33.6 us -> 33.6 us (level)
  starting transfers between devices: 15.6 us -> 16.9 us
  waiting for transfers between devices: 7.23 us -> 5.97 us
    ppermute x0 -> x3, starting transfers between devices: none -> 7.92 us  [on_device(): lax.ppermute(sends[k - 1], 'seq', [(i, (i + k) % count) for i in range(co...]
    ppermute x11 -> x8, starting transfers between devices: 15.6 us -> 8.99 us  [exchange(): lax.ppermute(value, axis, [(i, peer(i, step, count)) for i in range(count)])]
    ppermute x11 -> x8, waiting for transfers between devices: 7.23 us -> 4.01 us  [exchange(): lax.ppermute(value, axis, [(i, peer(i, step, count)) for i in range(count)])]
    ppermute x0 -> x3, waiting for transfers between devices: none -> 1.96 us  [on_device(): lax.ppermute(sends[k - 1], 'seq', [(i, (i + k) % count) for i in range(co...]
  transfers between devices with their start and end apart: 11 -> 11, of which waited for: 6 -> 7; matrix products, arithmetic and copies ran while one was open for 0% -> 0% of each run, Pallas kernels for 9% -> 9%
where the time goes in v11:
time: 33.6 us; the launch traced here: 33.4 us
  starting transfers between devices  16.9 us (50%)
  Pallas kernels  8.43 us (25%)
  waiting for transfers between devices  5.97 us (18%)
  between operations  2.04 us (6%)
    ppermute x8, starting transfers between devices, exchange(): lax.ppermute(value, axis, [(i, peer(i, step, count)) for i in range(count)])  8.99 us
    ppermute x3, starting transfers between devices, on_device(): lax.ppermute(sends[k - 1], 'seq', [(i, (i + k) % count) for i in range(co...  7.92 us
    ppermute x8, waiting for transfers between devices, exchange(): lax.ppermute(value, axis, [(i, peer(i, step, count)) for i in range(count)])  4.01 us
    pallas_call x2, Pallas kernels, attend(): pl.pallas_call(functools.partial(attend_kernel, plan, sets, spans, tile,...  3.74 us
    pallas_call x1, Pallas kernels, project(): pl.pallas_call(functools.partial(project_kernel, count, rows, heads, chun...  2.73 us
    ppermute x3, waiting for transfers between devices, on_device(): lax.ppermute(sends[k - 1], 'seq', [(i, (i + k) % count) for i in range(co...  1.96 us
    pallas_call x1, Pallas kernels, prepare(): pl.pallas_call(functools.partial(prepare_kernel, sets, block), in_specs=[...  1.74 us
  transfers between devices with their start and end apart: 11, of which 7 were waited for; matrix products, arithmetic and copies ran while one was open for 0% of the time, Pallas kernels for 9%

profile of v11, /device:TPU:0, one launch (start us, length us, event | category | flops | bytes accessed | tf_op | source)
XLA Modules:
  0.0 33.4 jit_solution(15131696081987630976)
XLA Ops:
  0.6 0.0 copy-start.2
  0.6 0.0 copy-start
  0.7 0.0 copy-start.1
  0.7 2.7 %project.1 = (f32[256,128]{1,0:T(8,128)S(1)}, f32[64,128]{1,0:T(8,128)S(1)}, bf16[32,512]{1,0:T(8,128)(2,1)S(1)}, bf16[400,128]{1,0:T(8,128)(2,1)S(1)}, bf16[400...) custom-call(bf16[256,2048]{1,0:T(8,128)(2,1)} %hidden_ref.1, bf16[16,128]{1,0:T(8,128)(2,1)} %bitcast.6, ...), custom_call_target="tpu_custom_call" | custom-call | flops 536870912 | bytes 3145728 | tf_op jit(solution)/shard_map/project/pallas_call | solution.py:147
  3.4 4.1 %collective-permute-start = (bf16[400,128]{1,0:T(8,128)(2,1)S(1)}, bf16[400,128]{1,0:T(8,128)(2,1)S(1)}, u32[]{:S(2)}, u32[]{:S(2)}) collective-permute-start(bf16[400,128]{1,0:T(8,128)(2,1)S(1)} %get-tuple-element.25), channel_id=1, source_target_pairs={{0,2},{1,3},{2,0},{3,1},{4,6},{5,7},{6,4},{7,5},{8,10},{9,11},{10,... | collective-permute-start | bytes 307208 | tf_op jit(solution)/shard_map/ppermute | solution.py:419
  7.5 1.6 %collective-permute-start.1 = (bf16[400,128]{1,0:T(8,128)(2,1)S(1)}, bf16[400,128]{1,0:T(8,128)(2,1)S(1)}, u32[]{:S(2)}, u32[]{:S(2)}) collective-permute-start(bf16[400,128]{1,0:T(8,128)(2,1)S(1)} %get-tuple-element.26), channel_id=1, source_target_pairs={{0,1},{1,2},{2,3},{3,0},{4,5},{5,6},{6,7},{7,4},{8,9},{9,10},{10,1... | collective-permute-start | bytes 307208 | tf_op jit(solution)/shard_map/ppermute | solution.py:419
  9.1 2.2 %collective-permute-start.2 = (bf16[400,128]{1,0:T(8,128)(2,1)S(1)}, bf16[400,128]{1,0:T(8,128)(2,1)S(1)}, u32[]{:S(2)}, u32[]{:S(2)}) collective-permute-start(bf16[400,128]{1,0:T(8,128)(2,1)S(1)} %get-tuple-element.27), channel_id=1, source_target_pairs={{0,3},{1,0},{2,1},{3,2},{4,7},{5,4},{6,5},{7,6},{8,11},{9,8},{10,9... | collective-permute-start | bytes 307208 | tf_op jit(solution)/shard_map/ppermute | solution.py:419
  12.6 0.0 copy-done.2
  12.6 0.0 copy-done
  12.7 1.7 %prepare.1 = (f32[64,128]{1,0:T(8,128)S(1)}, f32[64,128]{1,0:T(8,128)S(1)}, bf16[4096,128]{1,0:T(8,128)(2,1)S(1)}, f32[8,8,512]{2,1,0:T(8,128)S(1)}, f32[8,128,512]{2,1,0:T(8,128)S(1)}) custom-call(s32[1]{0:T(128)S(6)} %copy.12.offset_ref, s32[1]{0:T(128)S(6)} %copy.13.length_ref, f32[1,128]{1,0:T(1,128)S(1)} %copy-done.2, bf16[64,8192]{1,0:T(8,128)(2,1)S(1)} %bitcast.4, ...), custom_call_target="tpu_custom_call" | custom-call | tf_op jit(solution)/shard_map/prepare/pallas_call | solution.py:253
  14.4 1.2 %collective-permute-done.rest_0_ = bf16[400,128]{1,0:T(8,128)(2,1)S(1)} collective-permute-done((bf16[400,128]{1,0:T(8,128)(2,1)S(1)}, bf16[400,128]{1,0:T(8,128)(2,1)S(1)}, u32[]{:S(2)}, u32[]{:S(2)}) %collective-permute-start) | collective-permute-done | bytes 102432 | tf_op jit(solution)/shard_map/ppermute | solution.py:419
  15.7 0.0 collective-permute-done.1.rest_1_
  15.7 0.7 %collective-permute-done.2.rest_2_ = bf16[400,128]{1,0:T(8,128)(2,1)S(1)} collective-permute-done((bf16[400,128]{1,0:T(8,128)(2,1)S(1)}, bf16[400,128]{1,0:T(8,128)(2,1)S(1)}, u32[]{:S(2)}, u32[]{:S(2)}) %collective-permute-start.2) | collective-permute-done | bytes 102432 | tf_op jit(solution)/shard_map/ppermute | solution.py:419
  16.4 0.2 combine.1
  16.6 1.6 %collective-permute-start.5 = (bf16[64,512]{1,0:T(8,128)(2,1)S(1)}, bf16[64,512]{1,0:T(8,128)(2,1)S(1)}, u32[]{:S(2)}, u32[]{:S(2)}) collective-permute-start(bf16[64,512]{1,0:T(8,128)(2,1)S(1)} %get-tuple-element.28.rest_0_.rest_7_), channel_id=1, source_target_pairs={{0,8},{4,12},{8,0},{12,4},{1,9},{5,13},{9,1},{13,5},{2,10},{6,14},... | collective-permute-start | bytes 196616 | tf_op jit(solution)/shard_map/ppermute | solution.py:43
  18.2 0.5 %collective-permute-start.9 = (bf16[128,512]{1,0:T(8,128)(2,1)S(1)}, bf16[128,512]{1,0:T(8,128)(2,1)S(1)}, u32[]{:S(2)}, u32[]{:S(2)}) collective-permute-start(bf16[128,512]{1,0:T(8,128)(2,1)S(1)} %get-tuple-element.29.rest_2_), channel_id=1, source_target_pairs={{0,8},{4,12},{8,0},{12,4},{1,9},{5,13},{9,1},{13,5},{2,10},{6,14},... | collective-permute-start | bytes 393224 | tf_op jit(solution)/shard_map/ppermute | solution.py:43
  18.7 2.1 %collective-permute-start.3 = (bf16[64,512]{1,0:T(8,128)(2,1)S(1)}, bf16[64,512]{1,0:T(8,128)(2,1)S(1)}, u32[]{:S(2)}, u32[]{:S(2)}) collective-permute-start(bf16[64,512]{1,0:T(8,128)(2,1)S(1)} %get-tuple-element.28.rest_0_.rest_7_), channel_id=1, source_target_pairs={{0,3},{1,2},{2,1},{3,0},{4,7},{5,6},{6,5},{7,4},{8,11},{9,10},{10,... | collective-permute-start | bytes 196616 | tf_op jit(solution)/shard_map/ppermute | solution.py:43
  20.7 0.8 %collective-permute-done.5.rest_1_ = bf16[64,512]{1,0:T(8,128)(2,1)S(1)} collective-permute-done((bf16[64,512]{1,0:T(8,128)(2,1)S(1)}, bf16[64,512]{1,0:T(8,128)(2,1)S(1)}, u32[]{:S(2)}, u32[]{:S(2)}) %collective-permute-start.5) | collective-permute-done | bytes 65568 | tf_op jit(solution)/shard_map/ppermute | solution.py:43
  21.6 1.1 %collective-permute-start.6 = (bf16[128,512]{1,0:T(8,128)(2,1)S(1)}, bf16[128,512]{1,0:T(8,128)(2,1)S(1)}, u32[]{:S(2)}, u32[]{:S(2)}) collective-permute-start(bf16[128,512]{1,0:T(8,128)(2,1)S(1)} %constant_dynamic-update-slice_fusion), channel_id=1, source_target_pairs={{0,1},{1,0},{2,3},{3,2},{4,5},{5,4},{6,7},{7,6},{8,9},{9,8},{10,11... | collective-permute-start | bytes 393224 | tf_op jit(solution)/shard_map/ppermute | solution.py:43
  22.7 2.0 %collective-permute-start.7 = (bf16[128,512]{1,0:T(8,128)(2,1)S(1)}, bf16[128,512]{1,0:T(8,128)(2,1)S(1)}, u32[]{:S(2)}, u32[]{:S(2)}) collective-permute-start(bf16[128,512]{1,0:T(8,128)(2,1)S(1)} %constant_dynamic-update-slice_fusion), channel_id=1, source_target_pairs={{0,2},{1,3},{2,0},{3,1},{4,6},{5,7},{6,4},{7,5},{8,10},{9,11},{10,... | collective-permute-start | bytes 393224 | tf_op jit(solution)/shard_map/ppermute | solution.py:43
  24.7 0.2 collective-permute-done.3.rest_0_
  24.8 1.6 %collective-permute-start.4 = (bf16[64,512]{1,0:T(8,128)(2,1)S(1)}, bf16[64,512]{1,0:T(8,128)(2,1)S(1)}, u32[]{:S(2)}, u32[]{:S(2)}) collective-permute-start(bf16[64,512]{1,0:T(8,128)(2,1)S(1)} %collective-permute-done.3.rest_0_), channel_id=1, source_target_pairs={{0,8},{4,12},{8,0},{12,4},{1,9},{5,13},{9,1},{13,5},{2,10},{6,14},... | collective-permute-start | bytes 196616 | tf_op jit(solution)/shard_map/ppermute | solution.py:43
  26.4 0.0 collective-permute-done.9.rest_3_
  26.5 0.1 collective-permute-start.10
  26.5 2.6 %collective-permute-done.4.rest_1_ = bf16[64,512]{1,0:T(8,128)(2,1)S(1)} collective-permute-done((bf16[64,512]{1,0:T(8,128)(2,1)S(1)}, bf16[64,512]{1,0:T(8,128)(2,1)S(1)}, u32[]{:S(2)}, u32[]{:S(2)}) %collective-permute-start.4) | collective-permute-done | bytes 65568 | tf_op jit(solution)/shard_map/ppermute | solution.py:43
  29.1 0.0 collective-permute-done.6.rest_2_
  29.1 0.2 collective-permute-done.7.rest_3_
  29.3 0.1 collective-permute-start.8
  29.4 0.0 collective-permute-done.10.rest_4_
  29.4 1.4 %attend_more.1 = (f32[8,8,512]{2,1,0:T(8,128)S(1)}, f32[8,128,512]{2,1,0:T(8,128)S(1)}) custom-call(s32[1]{0:T(128)S(6)} %copy.12.offset_ref, s32[1]{0:T(128)S(6)} %copy.13.length_ref, bf16[4096,128]{1,0:T(8,128)(2,1)S(1)} %get-tuple-element.19.query_ref, bf16[64,512]{1,0:T(8,128)(2,1)S(1)} %get-tuple-element.28.rest_0_.rest_7_, ...), custom_call_target="tpu_custom_call" | custom-call | tf_op jit(solution)/shard_map/attend_more/pallas_call | solution.py:391
  30.8 0.3 collective-permute-done.8.rest_4_
  31.1 2.3 %attend_last.1 = (bf16[64,8192]{1,0:T(8,128)(2,1)}, bf16[64,512]{1,0:T(8,128)(2,1)}) custom-call(s32[1]{0:T(128)S(6)} %copy.12.offset_ref, s32[1]{0:T(128)S(6)} %copy.13.length_ref, bf16[4096,128]{1,0:T(8,128)(2,1)S(1)} %get-tuple-element.19.query_ref, bf16[64,512]{1,0:T(8,128)(2,1)S(1)} %collective-permute-done.3.rest_0_, ...), custom_call_target="tpu_custom_call" | custom-call | tf_op jit(solution)/shard_map/attend_last/pallas_call | solution.py:391
  (5 shorter events, 0.1 us)
Async XLA Ops:
  0.6 12.0 %copy-start.2 = (f32[1,128]{1,0:T(1,128)S(1)}, f32[1,128]{1,0:T(1,128)}, u32[]{:S(2)}) copy-start(f32[1,128]{1,0:T(1,128)} %constant.2.clone.frequency_ref) | copy-start | bytes 1540
  0.6 12.0 %copy-start = (bf16[1,64,8192]{2,1,0:T(8,128)(2,1)S(1)}, bf16[1,64,8192]{2,1,0:T(8,128)(2,1)}, u32[]{:S(2)}) copy-start(bf16[1,64,8192]{2,1,0:T(8,128)(2,1)} %param.14) | copy-start | bytes 3145732
  0.7 12.0 %copy-start.1 = (bf16[1,64,2048]{2,1,0:T(8,128)(2,1)S(1)}, bf16[1,64,2048]{2,1,0:T(8,128)(2,1)}, u32[]{:S(2)}) copy-start(bf16[1,64,2048]{2,1,0:T(8,128)(2,1)} %param.15) | copy-start | bytes 786436
  3.4 12.2 %collective-permute-start = (bf16[400,128]{1,0:T(8,128)(2,1)S(1)}, bf16[400,128]{1,0:T(8,128)(2,1)S(1)}, u32[]{:S(2)}, u32[]{:S(2)}) collective-permute-start(bf16[400,128]{1,0:T(8,128)(2,1)S(1)} %get-tuple-element.25), channel_id=1, source_target_pairs={{0,2},{1,3},{2,0},{3,1},{4,6},{5,7},{6,4},{7,5},{8,10},{9,11},{10,... | collective-permute-start | bytes 307208 | tf_op jit(solution)/shard_map/ppermute | solution.py:419
  7.5 8.2 %collective-permute-start.1 = (bf16[400,128]{1,0:T(8,128)(2,1)S(1)}, bf16[400,128]{1,0:T(8,128)(2,1)S(1)}, u32[]{:S(2)}, u32[]{:S(2)}) collective-permute-start(bf16[400,128]{1,0:T(8,128)(2,1)S(1)} %get-tuple-element.26), channel_id=1, source_target_pairs={{0,1},{1,2},{2,3},{3,0},{4,5},{5,6},{6,7},{7,4},{8,9},{9,10},{10,1... | collective-permute-start | bytes 307208 | tf_op jit(solution)/shard_map/ppermute | solution.py:419
  9.1 7.3 %collective-permute-start.2 = (bf16[400,128]{1,0:T(8,128)(2,1)S(1)}, bf16[400,128]{1,0:T(8,128)(2,1)S(1)}, u32[]{:S(2)}, u32[]{:S(2)}) collective-permute-start(bf16[400,128]{1,0:T(8,128)(2,1)S(1)} %get-tuple-element.27), channel_id=1, source_target_pairs={{0,3},{1,0},{2,1},{3,2},{4,7},{5,4},{6,5},{7,6},{8,11},{9,8},{10,9... | collective-permute-start | bytes 307208 | tf_op jit(solution)/shard_map/ppermute | solution.py:419
  16.6 5.0 %collective-permute-start.5 = (bf16[64,512]{1,0:T(8,128)(2,1)S(1)}, bf16[64,512]{1,0:T(8,128)(2,1)S(1)}, u32[]{:S(2)}, u32[]{:S(2)}) collective-permute-start(bf16[64,512]{1,0:T(8,128)(2,1)S(1)} %get-tuple-element.28.rest_0_.rest_7_), channel_id=1, source_target_pairs={{0,8},{4,12},{8,0},{12,4},{1,9},{5,13},{9,1},{13,5},{2,10},{6,14},... | collective-permute-start | bytes 196616 | tf_op jit(solution)/shard_map/ppermute | solution.py:43
  18.2 8.2 %collective-permute-start.9 = (bf16[128,512]{1,0:T(8,128)(2,1)S(1)}, bf16[128,512]{1,0:T(8,128)(2,1)S(1)}, u32[]{:S(2)}, u32[]{:S(2)}) collective-permute-start(bf16[128,512]{1,0:T(8,128)(2,1)S(1)} %get-tuple-element.29.rest_2_), channel_id=1, source_target_pairs={{0,8},{4,12},{8,0},{12,4},{1,9},{5,13},{9,1},{13,5},{2,10},{6,14},... | collective-permute-start | bytes 393224 | tf_op jit(solution)/shard_map/ppermute | solution.py:43
  18.7 6.2 %collective-permute-start.3 = (bf16[64,512]{1,0:T(8,128)(2,1)S(1)}, bf16[64,512]{1,0:T(8,128)(2,1)S(1)}, u32[]{:S(2)}, u32[]{:S(2)}) collective-permute-start(bf16[64,512]{1,0:T(8,128)(2,1)S(1)} %get-tuple-element.28.rest_0_.rest_7_), channel_id=1, source_target_pairs={{0,3},{1,2},{2,1},{3,0},{4,7},{5,6},{6,5},{7,4},{8,11},{9,10},{10,... | collective-permute-start | bytes 196616 | tf_op jit(solution)/shard_map/ppermute | solution.py:43
  21.6 7.6 %collective-permute-start.6 = (bf16[128,512]{1,0:T(8,128)(2,1)S(1)}, bf16[128,512]{1,0:T(8,128)(2,1)S(1)}, u32[]{:S(2)}, u32[]{:S(2)}) collective-permute-start(bf16[128,512]{1,0:T(8,128)(2,1)S(1)} %constant_dynamic-update-slice_fusion), channel_id=1, source_target_pairs={{0,1},{1,0},{2,3},{3,2},{4,5},{5,4},{6,7},{7,6},{8,9},{9,8},{10,11... | collective-permute-start | bytes 393224 | tf_op jit(solution)/shard_map/ppermute | solution.py:43
  22.7 6.6 %collective-permute-start.7 = (bf16[128,512]{1,0:T(8,128)(2,1)S(1)}, bf16[128,512]{1,0:T(8,128)(2,1)S(1)}, u32[]{:S(2)}, u32[]{:S(2)}) collective-permute-start(bf16[128,512]{1,0:T(8,128)(2,1)S(1)} %constant_dynamic-update-slice_fusion), channel_id=1, source_target_pairs={{0,2},{1,3},{2,0},{3,1},{4,6},{5,7},{6,4},{7,5},{8,10},{9,11},{10,... | collective-permute-start | bytes 393224 | tf_op jit(solution)/shard_map/ppermute | solution.py:43
  24.8 4.3 %collective-permute-start.4 = (bf16[64,512]{1,0:T(8,128)(2,1)S(1)}, bf16[64,512]{1,0:T(8,128)(2,1)S(1)}, u32[]{:S(2)}, u32[]{:S(2)}) collective-permute-start(bf16[64,512]{1,0:T(8,128)(2,1)S(1)} %collective-permute-done.3.rest_0_), channel_id=1, source_target_pairs={{0,8},{4,12},{8,0},{12,4},{1,9},{5,13},{9,1},{13,5},{2,10},{6,14},... | collective-permute-start | bytes 196616 | tf_op jit(solution)/shard_map/ppermute | solution.py:43
  26.5 2.9 %collective-permute-start.10 = (bf16[384,512]{1,0:T(8,128)(2,1)S(1)}, bf16[384,512]{1,0:T(8,128)(2,1)S(1)}, u32[]{:S(2)}, u32[]{:S(2)}) collective-permute-start(bf16[384,512]{1,0:T(8,128)(2,1)S(1)} %pad_maximum_fusion.1), channel_id=1, source_target_pairs={{0,4},{4,0},{8,12},{12,8},{1,5},{5,1},{9,13},{13,9},{2,6},{6,2},{1... | collective-permute-start | bytes 1179656 | tf_op jit(solution)/shard_map/ppermute | solution.py:43
  29.3 1.8 %collective-permute-start.8 = (bf16[384,512]{1,0:T(8,128)(2,1)S(1)}, bf16[384,512]{1,0:T(8,128)(2,1)S(1)}, u32[]{:S(2)}, u32[]{:S(2)}) collective-permute-start(bf16[384,512]{1,0:T(8,128)(2,1)S(1)} %pad_maximum_fusion), channel_id=1, source_target_pairs={{0,4},{4,0},{8,12},{12,8},{1,5},{5,1},{9,13},{13,9},{2,6},{6,2},{1... | collective-permute-start | bytes 1179656 | tf_op jit(solution)/shard_map/ppermute | solution.py:43

commit v12 on v11

--- a/solution.py
+++ b/solution.py
@@ -20,7 +20,7 @@
 KEY_COLUMNS = KEY_HEADS * HEAD_SIZE
 BF16 = jnp.bfloat16
 F32 = jnp.float32
-FLUSHES = 4
+FLUSHES = 8
 SMEM = pl.BlockSpec(memory_space=pltpu.SMEM)
 VMEM = pl.BlockSpec(memory_space=pltpu.VMEM)
 HBM = pl.BlockSpec(memory_space=pltpu.HBM)
@@ -415,7 +415,7 @@
 
     own, square, mine, *sends = project(span_hidden, norm_gain, key_value_weight, prompt_key_value, count)
     order = list(range(count - 1, 0, -1))
-    sums = order[1:] + order[:1]
+    sums = [order[1], order[0]] + order[2:]
     got = [lax.ppermute(sends[k - 1], "seq", [(i, (i + k) % count) for i in range(count)]) for k in sums]
 
     cosine, sine, query, *state = prepare(

time: 33.6 us -> 33.6 us (level)
  starting transfers between devices: 16.9 us -> 16.5 us
  waiting for transfers between devices: 5.97 us -> 6.36 us
    ppermute x3, starting transfers between devices: 7.92 us -> 6.13 us  [on_device(): lax.ppermute(sends[k - 1], 'seq', [(i, (i + k) % count) for i in range(co...]
    ppermute x8, starting transfers between devices: 8.99 us -> 10.4 us  [exchange(): lax.ppermute(value, axis, [(i, peer(i, step, count)) for i in range(count)])]
    ppermute x3, waiting for transfers between devices: 1.96 us -> 3.32 us  [on_device(): lax.ppermute(sends[k - 1], 'seq', [(i, (i + k) % count) for i in range(co...]
    ppermute x8, waiting for transfers between devices: 4.01 us -> 3.03 us  [exchange(): lax.ppermute(value, axis, [(i, peer(i, step, count)) for i in range(count)])]
  transfers between devices with their start and end apart: 11 -> 11, of which waited for: 7 -> 5; matrix products, arithmetic and copies ran while one was open for 0% -> 0% of each run, Pallas kernels for 9% -> 9%
where the time goes in v12:
time: 33.6 us; the launch traced here: 33.4 us
  starting transfers between devices  16.5 us (49%)
  Pallas kernels  8.42 us (25%)
  waiting for transfers between devices  6.36 us (19%)
  between operations  2.04 us (6%)
    ppermute x8, starting transfers between devices, exchange(): lax.ppermute(value, axis, [(i, peer(i, step, count)) for i in range(count)])  10.4 us
    ppermute x3, starting transfers between devices, on_device(): lax.ppermute(sends[k - 1], 'seq', [(i, (i + k) % count) for i in range(co...  6.13 us
    pallas_call x2, Pallas kernels, attend(): pl.pallas_call(functools.partial(attend_kernel, plan, sets, spans, tile,...  3.72 us
    ppermute x3, waiting for transfers between devices, on_device(): lax.ppermute(sends[k - 1], 'seq', [(i, (i + k) % count) for i in range(co...  3.32 us
    ppermute x8, waiting for transfers between devices, exchange(): lax.ppermute(value, axis, [(i, peer(i, step, count)) for i in range(count)])  3.03 us
    pallas_call x1, Pallas kernels, project(): pl.pallas_call(functools.partial(project_kernel, count, rows, heads, chun...  2.73 us
    pallas_call x1, Pallas kernels, prepare(): pl.pallas_call(functools.partial(prepare_kernel, sets, block), in_specs=[...  1.76 us
  transfers between devices with their start and end apart: 11, of which 5 were waited for; matrix products, arithmetic and copies ran while one was open for 0% of the time, Pallas kernels for 9%

profile of v12, /device:TPU:0, one launch (start us, length us, event | category | flops | bytes accessed | tf_op | source)
XLA Modules:
  0.0 33.4 jit_solution(3653012055050119365)
XLA Ops:
  0.6 0.0 copy-start.2
  0.6 0.0 copy-start
  0.7 0.0 copy-start.1
  0.7 2.7 %project.1 = (f32[256,128]{1,0:T(8,128)S(1)}, f32[64,128]{1,0:T(8,128)S(1)}, bf16[32,512]{1,0:T(8,128)(2,1)S(1)}, bf16[400,128]{1,0:T(8,128)(2,1)S(1)}, bf16[400...) custom-call(bf16[256,2048]{1,0:T(8,128)(2,1)} %hidden_ref.1, bf16[16,128]{1,0:T(8,128)(2,1)} %bitcast.6, ...), custom_call_target="tpu_custom_call" | custom-call | flops 536870912 | bytes 3145728 | tf_op jit(solution)/shard_map/project/pallas_call | solution.py:147
  3.4 4.1 %collective-permute-start = (bf16[400,128]{1,0:T(8,128)(2,1)S(1)}, bf16[400,128]{1,0:T(8,128)(2,1)S(1)}, u32[]{:S(2)}, u32[]{:S(2)}) collective-permute-start(bf16[400,128]{1,0:T(8,128)(2,1)S(1)} %get-tuple-element.25), channel_id=1, source_target_pairs={{0,2},{1,3},{2,0},{3,1},{4,6},{5,7},{6,4},{7,5},{8,10},{9,11},{10,... | collective-permute-start | bytes 307208 | tf_op jit(solution)/shard_map/ppermute | solution.py:419
  7.5 1.3 %collective-permute-start.1 = (bf16[400,128]{1,0:T(8,128)(2,1)S(1)}, bf16[400,128]{1,0:T(8,128)(2,1)S(1)}, u32[]{:S(2)}, u32[]{:S(2)}) collective-permute-start(bf16[400,128]{1,0:T(8,128)(2,1)S(1)} %get-tuple-element.26), channel_id=1, source_target_pairs={{0,3},{1,0},{2,1},{3,2},{4,7},{5,4},{6,5},{7,6},{8,11},{9,8},{10,9... | collective-permute-start | bytes 307208 | tf_op jit(solution)/shard_map/ppermute | solution.py:419
  8.9 0.7 %collective-permute-start.2 = (bf16[400,128]{1,0:T(8,128)(2,1)S(1)}, bf16[400,128]{1,0:T(8,128)(2,1)S(1)}, u32[]{:S(2)}, u32[]{:S(2)}) collective-permute-start(bf16[400,128]{1,0:T(8,128)(2,1)S(1)} %get-tuple-element.27), channel_id=1, source_target_pairs={{0,1},{1,2},{2,3},{3,0},{4,5},{5,6},{6,7},{7,4},{8,9},{9,10},{10,1... | collective-permute-start | bytes 307208 | tf_op jit(solution)/shard_map/ppermute | solution.py:419
  10.8 0.0 copy-done.2
  10.8 0.0 copy-done
  10.9 1.8 %prepare.1 = (f32[64,128]{1,0:T(8,128)S(1)}, f32[64,128]{1,0:T(8,128)S(1)}, bf16[4096,128]{1,0:T(8,128)(2,1)S(1)}, f32[8,8,512]{2,1,0:T(8,128)S(1)}, f32[8,128,512]{2,1,0:T(8,128)S(1)}) custom-call(s32[1]{0:T(128)S(6)} %copy.12.offset_ref, s32[1]{0:T(128)S(6)} %copy.13.length_ref, f32[1,128]{1,0:T(1,128)S(1)} %copy-done.2, bf16[64,8192]{1,0:T(8,128)(2,1)S(1)} %bitcast.4, ...), custom_call_target="tpu_custom_call" | custom-call | tf_op jit(solution)/shard_map/prepare/pallas_call | solution.py:253
  12.6 1.6 %collective-permute-done.rest_0_ = bf16[400,128]{1,0:T(8,128)(2,1)S(1)} collective-permute-done((bf16[400,128]{1,0:T(8,128)(2,1)S(1)}, bf16[400,128]{1,0:T(8,128)(2,1)S(1)}, u32[]{:S(2)}, u32[]{:S(2)}) %collective-permute-start) | collective-permute-done | bytes 102432 | tf_op jit(solution)/shard_map/ppermute | solution.py:419
  14.2 0.0 collective-permute-done.1.rest_1_
  14.2 1.7 %collective-permute-done.2.rest_2_ = bf16[400,128]{1,0:T(8,128)(2,1)S(1)} collective-permute-done((bf16[400,128]{1,0:T(8,128)(2,1)S(1)}, bf16[400,128]{1,0:T(8,128)(2,1)S(1)}, u32[]{:S(2)}, u32[]{:S(2)}) %collective-permute-start.2) | collective-permute-done | bytes 102432 | tf_op jit(solution)/shard_map/ppermute | solution.py:419
  15.9 0.2 combine.1
  16.2 1.5 %collective-permute-start.5 = (bf16[64,512]{1,0:T(8,128)(2,1)S(1)}, bf16[64,512]{1,0:T(8,128)(2,1)S(1)}, u32[]{:S(2)}, u32[]{:S(2)}) collective-permute-start(bf16[64,512]{1,0:T(8,128)(2,1)S(1)} %get-tuple-element.28.rest_0_.rest_7_), channel_id=1, source_target_pairs={{0,8},{4,12},{8,0},{12,4},{1,9},{5,13},{9,1},{13,5},{2,10},{6,14},... | collective-permute-start | bytes 196616 | tf_op jit(solution)/shard_map/ppermute | solution.py:43
  17.7 0.5 %collective-permute-start.9 = (bf16[128,512]{1,0:T(8,128)(2,1)S(1)}, bf16[128,512]{1,0:T(8,128)(2,1)S(1)}, u32[]{:S(2)}, u32[]{:S(2)}) collective-permute-start(bf16[128,512]{1,0:T(8,128)(2,1)S(1)} %get-tuple-element.29.rest_2_), channel_id=1, source_target_pairs={{0,8},{4,12},{8,0},{12,4},{1,9},{5,13},{9,1},{13,5},{2,10},{6,14},... | collective-permute-start | bytes 393224 | tf_op jit(solution)/shard_map/ppermute | solution.py:43
  18.3 2.7 %collective-permute-start.3 = (bf16[64,512]{1,0:T(8,128)(2,1)S(1)}, bf16[64,512]{1,0:T(8,128)(2,1)S(1)}, u32[]{:S(2)}, u32[]{:S(2)}) collective-permute-start(bf16[64,512]{1,0:T(8,128)(2,1)S(1)} %get-tuple-element.28.rest_0_.rest_7_), channel_id=1, source_target_pairs={{0,3},{1,2},{2,1},{3,0},{4,7},{5,6},{6,5},{7,4},{8,11},{9,10},{10,... | collective-permute-start | bytes 196616 | tf_op jit(solution)/shard_map/ppermute | solution.py:43
  21.0 0.0 collective-permute-done.5.rest_1_
  21.0 1.7 %collective-permute-start.6 = (bf16[128,512]{1,0:T(8,128)(2,1)S(1)}, bf16[128,512]{1,0:T(8,128)(2,1)S(1)}, u32[]{:S(2)}, u32[]{:S(2)}) collective-permute-start(bf16[128,512]{1,0:T(8,128)(2,1)S(1)} %constant_dynamic-update-slice_fusion), channel_id=1, source_target_pairs={{0,1},{1,0},{2,3},{3,2},{4,5},{5,4},{6,7},{7,6},{8,9},{9,8},{10,11... | collective-permute-start | bytes 393224 | tf_op jit(solution)/shard_map/ppermute | solution.py:43
  22.7 2.0 %collective-permute-start.7 = (bf16[128,512]{1,0:T(8,128)(2,1)S(1)}, bf16[128,512]{1,0:T(8,128)(2,1)S(1)}, u32[]{:S(2)}, u32[]{:S(2)}) collective-permute-start(bf16[128,512]{1,0:T(8,128)(2,1)S(1)} %constant_dynamic-update-slice_fusion), channel_id=1, source_target_pairs={{0,2},{1,3},{2,0},{3,1},{4,6},{5,7},{6,4},{7,5},{8,10},{9,11},{10,... | collective-permute-start | bytes 393224 | tf_op jit(solution)/shard_map/ppermute | solution.py:43
  24.7 0.0 collective-permute-done.3.rest_0_
  24.7 1.7 %collective-permute-start.4 = (bf16[64,512]{1,0:T(8,128)(2,1)S(1)}, bf16[64,512]{1,0:T(8,128)(2,1)S(1)}, u32[]{:S(2)}, u32[]{:S(2)}) collective-permute-start(bf16[64,512]{1,0:T(8,128)(2,1)S(1)} %collective-permute-done.3.rest_0_), channel_id=1, source_target_pairs={{0,8},{4,12},{8,0},{12,4},{1,9},{5,13},{9,1},{13,5},{2,10},{6,14},... | collective-permute-start | bytes 196616 | tf_op jit(solution)/shard_map/ppermute | solution.py:43
  26.4 0.0 collective-permute-done.9.rest_3_
  26.5 0.1 collective-permute-start.10
  26.5 2.4 %collective-permute-done.4.rest_1_ = bf16[64,512]{1,0:T(8,128)(2,1)S(1)} collective-permute-done((bf16[64,512]{1,0:T(8,128)(2,1)S(1)}, bf16[64,512]{1,0:T(8,128)(2,1)S(1)}, u32[]{:S(2)}, u32[]{:S(2)}) %collective-permute-start.4) | collective-permute-done | bytes 65568 | tf_op jit(solution)/shard_map/ppermute | solution.py:43
  29.0 0.0 collective-permute-done.6.rest_2_
  29.0 0.3 collective-permute-done.7.rest_3_
  29.3 0.1 collective-permute-start.8
  29.4 0.0 collective-permute-done.10.rest_4_
  29.4 1.4 %attend_more.1 = (f32[8,8,512]{2,1,0:T(8,128)S(1)}, f32[8,128,512]{2,1,0:T(8,128)S(1)}) custom-call(s32[1]{0:T(128)S(6)} %copy.12.offset_ref, s32[1]{0:T(128)S(6)} %copy.13.length_ref, bf16[4096,128]{1,0:T(8,128)(2,1)S(1)} %get-tuple-element.19.query_ref, bf16[64,512]{1,0:T(8,128)(2,1)S(1)} %get-tuple-element.28.rest_0_.rest_7_, ...), custom_call_target="tpu_custom_call" | custom-call | tf_op jit(solution)/shard_map/attend_more/pallas_call | solution.py:391
  30.8 0.3 collective-permute-done.8.rest_4_
  31.1 2.3 %attend_last.1 = (bf16[64,8192]{1,0:T(8,128)(2,1)}, bf16[64,512]{1,0:T(8,128)(2,1)}) custom-call(s32[1]{0:T(128)S(6)} %copy.12.offset_ref, s32[1]{0:T(128)S(6)} %copy.13.length_ref, bf16[4096,128]{1,0:T(8,128)(2,1)S(1)} %get-tuple-element.19.query_ref, bf16[64,512]{1,0:T(8,128)(2,1)S(1)} %collective-permute-done.3.rest_0_, ...), custom_call_target="tpu_custom_call" | custom-call | tf_op jit(solution)/shard_map/attend_last/pallas_call | solution.py:391
  (5 shorter events, 0.1 us)
Async XLA Ops:
  0.6 10.2 %copy-start.2 = (f32[1,128]{1,0:T(1,128)S(1)}, f32[1,128]{1,0:T(1,128)}, u32[]{:S(2)}) copy-start(f32[1,128]{1,0:T(1,128)} %constant.2.clone.frequency_ref) | copy-start | bytes 1540
  0.6 10.2 %copy-start = (bf16[1,64,8192]{2,1,0:T(8,128)(2,1)S(1)}, bf16[1,64,8192]{2,1,0:T(8,128)(2,1)}, u32[]{:S(2)}) copy-start(bf16[1,64,8192]{2,1,0:T(8,128)(2,1)} %param.14) | copy-start | bytes 3145732
  0.7 10.2 %copy-start.1 = (bf16[1,64,2048]{2,1,0:T(8,128)(2,1)S(1)}, bf16[1,64,2048]{2,1,0:T(8,128)(2,1)}, u32[]{:S(2)}) copy-start(bf16[1,64,2048]{2,1,0:T(8,128)(2,1)} %param.15) | copy-start | bytes 786436
  3.4 10.8 %collective-permute-start = (bf16[400,128]{1,0:T(8,128)(2,1)S(1)}, bf16[400,128]{1,0:T(8,128)(2,1)S(1)}, u32[]{:S(2)}, u32[]{:S(2)}) collective-permute-start(bf16[400,128]{1,0:T(8,128)(2,1)S(1)} %get-tuple-element.25), channel_id=1, source_target_pairs={{0,2},{1,3},{2,0},{3,1},{4,6},{5,7},{6,4},{7,5},{8,10},{9,11},{10,... | collective-permute-start | bytes 307208 | tf_op jit(solution)/shard_map/ppermute | solution.py:419
  7.5 6.7 %collective-permute-start.1 = (bf16[400,128]{1,0:T(8,128)(2,1)S(1)}, bf16[400,128]{1,0:T(8,128)(2,1)S(1)}, u32[]{:S(2)}, u32[]{:S(2)}) collective-permute-start(bf16[400,128]{1,0:T(8,128)(2,1)S(1)} %get-tuple-element.26), channel_id=1, source_target_pairs={{0,3},{1,0},{2,1},{3,2},{4,7},{5,4},{6,5},{7,6},{8,11},{9,8},{10,9... | collective-permute-start | bytes 307208 | tf_op jit(solution)/shard_map/ppermute | solution.py:419
  8.9 7.1 %collective-permute-start.2 = (bf16[400,128]{1,0:T(8,128)(2,1)S(1)}, bf16[400,128]{1,0:T(8,128)(2,1)S(1)}, u32[]{:S(2)}, u32[]{:S(2)}) collective-permute-start(bf16[400,128]{1,0:T(8,128)(2,1)S(1)} %get-tuple-element.27), channel_id=1, source_target_pairs={{0,1},{1,2},{2,3},{3,0},{4,5},{5,6},{6,7},{7,4},{8,9},{9,10},{10,1... | collective-permute-start | bytes 307208 | tf_op jit(solution)/shard_map/ppermute | solution.py:419
  16.2 4.8 %collective-permute-start.5 = (bf16[64,512]{1,0:T(8,128)(2,1)S(1)}, bf16[64,512]{1,0:T(8,128)(2,1)S(1)}, u32[]{:S(2)}, u32[]{:S(2)}) collective-permute-start(bf16[64,512]{1,0:T(8,128)(2,1)S(1)} %get-tuple-element.28.rest_0_.rest_7_), channel_id=1, source_target_pairs={{0,8},{4,12},{8,0},{12,4},{1,9},{5,13},{9,1},{13,5},{2,10},{6,14},... | collective-permute-start | bytes 196616 | tf_op jit(solution)/shard_map/ppermute | solution.py:43
  17.7 8.7 %collective-permute-start.9 = (bf16[128,512]{1,0:T(8,128)(2,1)S(1)}, bf16[128,512]{1,0:T(8,128)(2,1)S(1)}, u32[]{:S(2)}, u32[]{:S(2)}) collective-permute-start(bf16[128,512]{1,0:T(8,128)(2,1)S(1)} %get-tuple-element.29.rest_2_), channel_id=1, source_target_pairs={{0,8},{4,12},{8,0},{12,4},{1,9},{5,13},{9,1},{13,5},{2,10},{6,14},... | collective-permute-start | bytes 393224 | tf_op jit(solution)/shard_map/ppermute | solution.py:43
  18.3 6.4 %collective-permute-start.3 = (bf16[64,512]{1,0:T(8,128)(2,1)S(1)}, bf16[64,512]{1,0:T(8,128)(2,1)S(1)}, u32[]{:S(2)}, u32[]{:S(2)}) collective-permute-start(bf16[64,512]{1,0:T(8,128)(2,1)S(1)} %get-tuple-element.28.rest_0_.rest_7_), channel_id=1, source_target_pairs={{0,3},{1,2},{2,1},{3,0},{4,7},{5,6},{6,5},{7,4},{8,11},{9,10},{10,... | collective-permute-start | bytes 196616 | tf_op jit(solution)/shard_map/ppermute | solution.py:43
  21.0 7.9 %collective-permute-start.6 = (bf16[128,512]{1,0:T(8,128)(2,1)S(1)}, bf16[128,512]{1,0:T(8,128)(2,1)S(1)}, u32[]{:S(2)}, u32[]{:S(2)}) collective-permute-start(bf16[128,512]{1,0:T(8,128)(2,1)S(1)} %constant_dynamic-update-slice_fusion), channel_id=1, source_target_pairs={{0,1},{1,0},{2,3},{3,2},{4,5},{5,4},{6,7},{7,6},{8,9},{9,8},{10,11... | collective-permute-start | bytes 393224 | tf_op jit(solution)/shard_map/ppermute | solution.py:43
  22.7 6.6 %collective-permute-start.7 = (bf16[128,512]{1,0:T(8,128)(2,1)S(1)}, bf16[128,512]{1,0:T(8,128)(2,1)S(1)}, u32[]{:S(2)}, u32[]{:S(2)}) collective-permute-start(bf16[128,512]{1,0:T(8,128)(2,1)S(1)} %constant_dynamic-update-slice_fusion), channel_id=1, source_target_pairs={{0,2},{1,3},{2,0},{3,1},{4,6},{5,7},{6,4},{7,5},{8,10},{9,11},{10,... | collective-permute-start | bytes 393224 | tf_op jit(solution)/shard_map/ppermute | solution.py:43
  24.7 4.3 %collective-permute-start.4 = (bf16[64,512]{1,0:T(8,128)(2,1)S(1)}, bf16[64,512]{1,0:T(8,128)(2,1)S(1)}, u32[]{:S(2)}, u32[]{:S(2)}) collective-permute-start(bf16[64,512]{1,0:T(8,128)(2,1)S(1)} %collective-permute-done.3.rest_0_), channel_id=1, source_target_pairs={{0,8},{4,12},{8,0},{12,4},{1,9},{5,13},{9,1},{13,5},{2,10},{6,14},... | collective-permute-start | bytes 196616 | tf_op jit(solution)/shard_map/ppermute | solution.py:43
  26.5 2.9 %collective-permute-start.10 = (bf16[384,512]{1,0:T(8,128)(2,1)S(1)}, bf16[384,512]{1,0:T(8,128)(2,1)S(1)}, u32[]{:S(2)}, u32[]{:S(2)}) collective-permute-start(bf16[384,512]{1,0:T(8,128)(2,1)S(1)} %pad_maximum_fusion.1), channel_id=1, source_target_pairs={{0,4},{4,0},{8,12},{12,8},{1,5},{5,1},{9,13},{13,9},{2,6},{6,2},{1... | collective-permute-start | bytes 1179656 | tf_op jit(solution)/shard_map/ppermute | solution.py:43
  29.3 1.8 %collective-permute-start.8 = (bf16[384,512]{1,0:T(8,128)(2,1)S(1)}, bf16[384,512]{1,0:T(8,128)(2,1)S(1)}, u32[]{:S(2)}, u32[]{:S(2)}) collective-permute-start(bf16[384,512]{1,0:T(8,128)(2,1)S(1)} %pad_maximum_fusion), channel_id=1, source_target_pairs={{0,4},{4,0},{8,12},{12,8},{1,5},{5,1},{9,13},{13,9},{2,6},{6,2},{1... | collective-permute-start | bytes 1179656 | tf_op jit(solution)/shard_map/ppermute | solution.py:43
